TPU v7x, 32 devices: a whole 2x2x4 slice. The times are simulated.
32 devices in a mesh: groups: 2 (over x), et: 16 (over z, y, core).
Axes of the slice: x: 2, y: 2, z: 4, core: 2. Of those that a mesh axis runs over, the one named last changes fastest.
Arguments:
- tokens: bfloat16 [4096, 6144], P(('groups', 'et')), parts along dimension 0, may hold values from -6 to 6
- out_grad: bfloat16 [4096, 6144], P(('groups', 'et')), parts along dimension 0, may hold values from -6 to 6
- expert_ids: int32 [4096, 4], P(('groups', 'et')), parts along dimension 0, may hold values from 0 to 15, as said below
- gate_vals: bfloat16 [4096, 4], P(('groups', 'et')), parts along dimension 0, may hold values from 0.19921875 to 1
- w_gate: bfloat16 [6144, 5376], P(None, 'et'), may hold values from -0.078125 to 0.078125
- w_up: bfloat16 [6144, 5376], P(None, 'et'), may hold values from -0.078125 to 0.078125
- w_down: bfloat16 [5376, 6144], P('et'), may hold values from -0.078125 to 0.078125
Outputs:
- mixed: bfloat16 [4096, 6144], P(('groups', 'et')), parts along dimension 0
- grad_tokens: bfloat16 [4096, 6144], P(('groups', 'et')), parts along dimension 0
- grad_gate: bfloat16 [12288, 5376], P('groups', 'et'), parts along dimension 0
- grad_up: bfloat16 [12288, 5376], P('groups', 'et'), parts along dimension 0
- grad_down: bfloat16 [10752, 6144], P(('groups', 'et')), parts along dimension 0
There are 2 independent parts, one for each index of `groups`. A program takes and returns all parts, laid end to end along the dimension named above; an argument that names none is the same for every part. Nothing has to cross between parts.
Inputs may be any that keep to these rules, and one draw needn't show every extreme that they name: `expert_ids`: each row names 4 different experts of 0 to 15; among the 128 rows of one index of et at most 16 name expert 0, and some index has exactly 16.
All inputs are finite; a program needn't handle non-finite values.
Results may differ from a plain program's by a relative error of at most 0.0051.
Values may be sent and summed in bfloat16 or wider, within the bound.
No kernel may reach another device: no remote copies, remote signals or barrier semaphores. Data moves between devices by JAX's collectives and lax.ppermute only.
A program may use at most 128 MiB of HBM per device.

v0:
```python
import jax
import jax.numpy as jnp
from jax import lax
from jax.sharding import PartitionSpec as P

CAP = 16


def forward_rows(rows_x, rows_coef, w_gate, w_up):
    coef = rows_coef.astype(jnp.float32)[:, None]
    gate = jnp.dot(rows_x, w_gate, preferred_element_type=jnp.float32)
    up = jnp.dot(rows_x, w_up, preferred_element_type=jnp.float32)
    sig = jax.nn.sigmoid(gate)
    hidden = (coef * gate * sig * up).astype(jnp.bfloat16)
    return (coef, gate, up, hidden)


def backward_rows(rows_dy, coef, gate, up, w_gate, w_up, w_down):
    sig = jax.nn.sigmoid(gate)
    act = gate * sig
    scaled = coef * jnp.dot(rows_dy, w_down.T, preferred_element_type=jnp.float32)
    dgate = (scaled * up * sig * (1.0 + gate * (1.0 - sig))).astype(jnp.bfloat16)
    dup = (scaled * act).astype(jnp.bfloat16)
    dx_rows = jnp.dot(dgate, w_gate.T, preferred_element_type=jnp.float32) + jnp.dot(
        dup, w_up.T, preferred_element_type=jnp.float32
    )
    return (dgate, dup, dx_rows)


def per_device(tokens, out_grad, expert_ids, gate_vals, w_gate, w_up, w_down):
    landed = expert_ids == 0
    coef = jnp.sum(jnp.where(landed, gate_vals.astype(jnp.float32), 0.0), axis=1).astype(
        jnp.bfloat16
    )
    routed = jnp.any(landed, axis=1)
    slot = jnp.cumsum(routed.astype(jnp.int32)) - 1
    select = (slot[None, :] == jnp.arange(CAP, dtype=jnp.int32)[:, None]) & routed[None, :]
    select_bf = select.astype(jnp.bfloat16)
    slot_x = jnp.dot(select_bf, tokens, preferred_element_type=jnp.float32).astype(jnp.bfloat16)
    slot_dy = jnp.dot(select_bf, out_grad, preferred_element_type=jnp.float32).astype(jnp.bfloat16)
    slot_coef = jnp.dot(select_bf, coef[:, None], preferred_element_type=jnp.float32)[:, 0].astype(
        jnp.bfloat16
    )
    rows_x = lax.all_gather(slot_x, "et", axis=0, tiled=True)
    rows_dy = lax.all_gather(slot_dy, "et", axis=0, tiled=True)
    rows_coef = lax.all_gather(slot_coef, "et", axis=0, tiled=True)
    row_coef, gate, up, hidden = forward_rows(rows_x, rows_coef, w_gate, w_up)
    out_rows = jnp.dot(hidden, w_down, preferred_element_type=jnp.float32)
    dgate, dup, dx_rows = backward_rows(rows_dy, row_coef, gate, up, w_gate, w_up, w_down)
    out_slots, dx_slots = (
        lax.psum_scatter(out_rows, "et", scatter_dimension=0, tiled=True),
        lax.psum_scatter(dx_rows, "et", scatter_dimension=0, tiled=True),
    )
    spread = select.astype(jnp.float32).T
    mixed = jnp.dot(spread, out_slots, precision=lax.Precision.HIGHEST)
    grad_tokens = jnp.dot(spread, dx_slots, precision=lax.Precision.HIGHEST)
    grad_down = jnp.dot(hidden.T, rows_dy, preferred_element_type=jnp.float32).astype(jnp.bfloat16)
    grad_gate = jnp.dot(rows_x.T, dgate, preferred_element_type=jnp.float32).astype(jnp.bfloat16)
    grad_up = jnp.dot(rows_x.T, dup, preferred_element_type=jnp.float32).astype(jnp.bfloat16)
    return (
        mixed.astype(jnp.bfloat16),
        grad_tokens.astype(jnp.bfloat16),
        grad_gate,
        grad_up,
        grad_down,
    )


def solution(mesh):
    placed = (
        P(("groups", "et"), None),
        P(("groups", "et"), None),
        P(("groups", "et"), None),
        P(("groups", "et"), None),
        P(None, "et"),
        P(None, "et"),
        P("et", None),
    )
    return jax.shard_map(
        per_device,
        mesh=mesh,
        in_specs=placed,
        out_specs=(
            P(("groups", "et"), None),
            P(("groups", "et"), None),
            P("groups", "et"),
            P("groups", "et"),
            P(("groups", "et"), None),
        ),
        check_vma=False,
    )
```

profile of v0, /device:TPU:0, one launch (start us, length us, event | category | flops | bytes accessed | tf_op | source)
XLA Modules:
  0.0 300.4 jit_solution(15251528895076155866)
XLA Ops:
  7.2 0.0 copy-start
  7.2 0.0 copy-start.6
  7.2 0.0 all-gather.3.cloned.1.call-start
  7.2 0.8 select_reduce_fusion
  8.1 0.1 copy.13
  8.2 0.2 reduce-window.8
  8.4 0.1 add_reduce_fusion
  8.5 0.1 copy-done
  8.6 1.0 convolution_convert_fusion.6
  9.6 0.0 all-gather.3.cloned.1.call-update
  9.6 0.0 all-gather.5.cloned.1.call-start
  9.7 2.4 convolution_convert_fusion.5
  12.1 0.0 all-gather.5.cloned.1.call-update
  12.1 0.0 reduce-scatter.5.cloned.1.call-start
  12.2 0.0 copy-done.6
  12.2 0.6 dynamic-slice
  13.4 0.1 fusion
  13.5 0.2 dynamic-update-slice
  13.7 35.3 %all-reduce = bf16[256]{0:T(256)(128)(2,1)S(1)} all-reduce(bf16[256]{0:T(256)(128)(2,1)S(1)} %dynamic-update-slice), channel_id=1, replica_groups=mesh['groups'=2,'et'=16] {'et'}, use_global_device_ids=true, to_apply=%add | all-reduce | flops 256 | bytes 1024
  49.0 9.8 %all-gather.3.cloned.1.call-done = bf16[256,6144]{1,0:T(8,128)(2,1)} async-done(((bf16[16,6144]{1,0:T(8,128)(2,1)}), bf16[256,6144]{1,0:T(8,128)(2,1)}) %all-gather.3.cloned.1.call-update) | async-done | bytes 3145744 | tf_op jit(solution)/shard_map/all_gather | solution.py:44
  58.8 0.0 copy-start.1
  58.8 0.0 copy-start.4
  58.8 4.5 %fusion.17 = f32[256,336]{0,1:T(8,128)S(1)} fusion(bf16[256,6144]{1,0:T(8,128)(2,1)} %all-gather.3.cloned.1.call-done, bf16[6144,336]{0,1:T(8,128)(2,1)} %param.11), kind=kOutput, calls=%fused_computation.32 | convolution fusion | flops 1056964608 | bytes 7618560 | tf_op jit(solution)/shard_map/dot_general | solution.py:11
  63.3 0.0 copy-done.1
  63.4 0.7 copy-done.4
  64.1 1.3 fusion.18
  65.3 40.4 %all-gather.5.cloned.1.call-done = bf16[256,6144]{1,0:T(8,128)(2,1)} async-done(((bf16[16,6144]{1,0:T(8,128)(2,1)}), bf16[256,6144]{1,0:T(8,128)(2,1)}) %all-gather.5.cloned.1.call-update) | async-done | bytes 3145744 | tf_op jit(solution)/shard_map/all_gather | solution.py:45
  105.8 0.0 copy-start.3
  105.8 4.6 %multiply_convert_fusion = (bf16[256,336]{0,1:T(8,128)(2,1)S(1)}, bf16[256,336]{0,1:T(8,128)(2,1)S(1)}, bf16[256,336]{0,1:T(8,128)(2,1)S(1)}) fusion(f32[256,336]{0,1:T(8,128)S(1)} %fusion.17, f32[256,336]{0,1:T(8,128)S(1)} %fusion.18, f32[256]{0:T(256)S(1)} %convert_element_type.66, bf16[256,6144]{1,0:T(8,128)(2,1)} %all-gather.5.cloned.1.call-done, ...), kind=kOutput, calls=%fused_computation.11 | convolution fusion | flops 1058512896 | bytes 8479744 | tf_op jit(solution)/shard_map/dot_general | solution.py:21
  110.4 0.0 copy-done.3
  110.4 0.0 copy-start.5
  110.4 1.8 fusion.20
  112.2 0.3 copy-done.5
  112.6 4.5 %convolution_add_fusion = f32[256,6144]{1,0:T(8,128)} fusion(f32[256,6144]{1,0:T(8,128)S(1)} %fusion.20, bf16[256,336]{0,1:T(8,128)(2,1)S(1)} %get-tuple-element.7, bf16[6144,336]{0,1:T(8,128)(2,1)S(1)} %copy-done.5), kind=kOutput, calls=%fused_computation | convolution fusion | flops 1058537472 | bytes 16883712 | tf_op jit(solution)/shard_map/dot_general | solution.py:24
  117.0 0.0 reduce-scatter.5.cloned.1.call-update
  117.1 0.2 reduce-scatter.3.cloned.1.call-start
  117.3 6.7 %fusion.19 = f32[256,6144]{1,0:T(8,128)} fusion(bf16[256,336]{0,1:T(8,128)(2,1)S(1)} %get-tuple-element.9, bf16[336,6144]{1,0:T(8,128)(2,1)} %param.13), kind=kOutput, calls=%fused_computation.34 | convolution fusion | flops 1056964608 | bytes 10592256 | tf_op jit(solution)/shard_map/dot_general | solution.py:48
  124.0 0.0 reduce-scatter.3.cloned.1.call-update
  124.0 0.0 copy-start.2
  124.0 5.5 %convolution_convert_fusion.2 = bf16[336,6144]{1,0:T(8,128)(2,1)} fusion(bf16[256,336]{0,1:T(8,128)(2,1)S(1)} %get-tuple-element.9, bf16[256,6144]{1,0:T(8,128)(2,1)} %all-gather.5.cloned.1.call-done), kind=kOutput, calls=%fused_computation.3 | convolution fusion | flops 1059028992 | bytes 7446528 | tf_op jit(solution)/shard_map/dot_general | solution.py:57
  129.5 0.0 copy-done.2
  129.5 3.2 %convolution_convert_fusion = bf16[6144,336]{0,1:T(8,128)(2,1)} fusion(bf16[256,336]{0,1:T(8,128)(2,1)S(1)} %get-tuple-element.7, bf16[256,6144]{1,0:T(8,128)(2,1)S(1)} %copy-done.2), kind=kOutput, calls=%fused_computation.1 | convolution fusion | flops 1059028992 | bytes 7446528 | tf_op jit(solution)/shard_map/dot_general | solution.py:59
  132.7 3.2 %convolution_convert_fusion.1 = bf16[6144,336]{0,1:T(8,128)(2,1)} fusion(bf16[256,336]{0,1:T(8,128)(2,1)S(1)} %get-tuple-element.8, bf16[256,6144]{1,0:T(8,128)(2,1)S(1)} %copy-done.2), kind=kOutput, calls=%fused_computation.2 | convolution fusion | flops 1059028992 | bytes 7446528 | tf_op jit(solution)/shard_map/dot_general | solution.py:58
  136.0 65.3 %reduce-scatter.5.cloned.1.call-done = f32[16,6144]{1,0:T(8,128)} async-done(((f32[256,6144]{1,0:T(8,128)}), f32[16,6144]{1,0:T(8,128)}) %reduce-scatter.5.cloned.1.call-update) | async-done | bytes 393232 | tf_op jit(solution)/shard_map/reduce_scatter | solution.py:52
  201.3 3.6 %convolution_convert_fusion.3 = bf16[128,6144]{1,0:T(8,128)(2,1)} fusion(f32[16,6144]{1,0:T(8,128)} %reduce-scatter.5.cloned.1.call-done, s32[128]{0:T(128)S(1)} %add_reduce_fusion, pred[128]{0:T(512)(128)(4,1)S(1)} %reduce_or.9), kind=kOutput, calls=%fused_computation.4 | convolution fusion | flops 151785472 | bytes 1966720 | tf_op jit(solution)/shard_map/dot_general | solution.py:56
  204.8 85.5 %reduce-scatter.3.cloned.1.call-done = f32[16,6144]{1,0:T(8,128)} async-done(((f32[256,6144]{1,0:T(8,128)}), f32[16,6144]{1,0:T(8,128)}) %reduce-scatter.3.cloned.1.call-update) | async-done | bytes 393232 | tf_op jit(solution)/shard_map/reduce_scatter | solution.py:51
  290.3 3.6 %convolution_convert_fusion.4 = bf16[128,6144]{1,0:T(8,128)(2,1)} fusion(f32[16,6144]{1,0:T(8,128)} %reduce-scatter.3.cloned.1.call-done, s32[128]{0:T(128)S(1)} %add_reduce_fusion, pred[128]{0:T(512)(128)(4,1)S(1)} %reduce_or.9), kind=kOutput, calls=%fused_computation.5 | convolution fusion | flops 151785472 | bytes 1966720 | tf_op jit(solution)/shard_map/dot_general | solution.py:55
  (4 shorter events, 0.0 us)
Async XLA Ops:
  7.2 1.4 copy-start
  7.2 5.0 %copy-start.6 = (u32[32]{0:T(128)S(1)}, u32[32]{0:T(128)}, u32[]{:S(2)}) copy-start(u32[32]{0:T(128)} %constant.16) | copy-start | bytes 388
  7.2 51.6 %all-gather.3.cloned.1.call-start = ((), (), s32[]{:S(2)}) async-start(), calls=%async_computation.2 | async-start | bytes 3342336 | tf_op jit(solution)/shard_map/all_gather | solution.py:44
  9.6 96.1 %all-gather.5.cloned.1.call-start = ((), (), s32[]{:S(2)}) async-start(), calls=%async_computation.4 | async-start | bytes 3342336 | tf_op jit(solution)/shard_map/all_gather | solution.py:45
  12.1 189.1 %reduce-scatter.5.cloned.1.call-start = ((), (), s32[]{:S(2)}) async-start(), calls=%async_computation.5 | async-start | bytes 6684672 | tf_op jit(solution)/shard_map/reduce_scatter | solution.py:52
  58.8 4.5 %copy-start.1 = (bf16[256,6144]{1,0:T(8,128)(2,1)S(1)}, bf16[256,6144]{1,0:T(8,128)(2,1)}, u32[]{:S(2)}) copy-start(bf16[256,6144]{1,0:T(8,128)(2,1)} %all-gather.3.cloned.1.call-done) | copy-start | bytes 9437188
  58.8 5.2 %copy-start.4 = (bf16[6144,336]{0,1:T(8,128)(2,1)S(1)}, bf16[6144,336]{0,1:T(8,128)(2,1)}, u32[]{:S(2)}) copy-start(bf16[6144,336]{0,1:T(8,128)(2,1)} %param.12) | copy-start | bytes 12386308
  105.8 4.6 %copy-start.3 = (bf16[6144,336]{0,1:T(8,128)(2,1)S(1)}, bf16[6144,336]{0,1:T(8,128)(2,1)}, u32[]{:S(2)}) copy-start(bf16[6144,336]{0,1:T(8,128)(2,1)} %param.11) | copy-start | bytes 12386308
  110.4 2.2 copy-start.5
  117.1 173.2 %reduce-scatter.3.cloned.1.call-start = ((), (), s32[]{:S(2)}) async-start(), calls=%async_computation.3 | async-start | bytes 6684672 | tf_op jit(solution)/shard_map/reduce_scatter | solution.py:51
  124.0 5.5 %copy-start.2 = (bf16[256,6144]{1,0:T(8,128)(2,1)S(1)}, bf16[256,6144]{1,0:T(8,128)(2,1)}, u32[]{:S(2)}) copy-start(bf16[256,6144]{1,0:T(8,128)(2,1)} %all-gather.3.cloned.1.call-done) | copy-start | bytes 9437188
Sparse Core Ops, SparseCore 0:
  10.9 47.8 all-gather.2
  61.7 44.0 all-gather.4
  117.2 84.0 reduce-scatter.4
  205.6 84.6 reduce-scatter.2
where the time goes:
time: 301 us; the launch traced here: 300 us
  waiting for transfers between devices  201 us (67%)
  matrix products  46 us (15%)
  blocking collectives  35.3 us (12%)
  between operations  14.5 us (5%)
    reduce_scatter x1, waiting for transfers between devices, per_device(): lax.psum_scatter(out_rows, 'et', scatter_dimension=0, tiled=True)  85.5 us
    reduce_scatter x1, waiting for transfers between devices, per_device(): lax.psum_scatter(dx_rows, 'et', scatter_dimension=0, tiled=True)  65.3 us
    all_gather x1, waiting for transfers between devices, per_device(): rows_dy = lax.all_gather(slot_dy, 'et', axis=0, tiled=True)  40.4 us
    unnamed x1, blocking collectives  35.3 us
    all_gather x1, waiting for transfers between devices, per_device(): rows_x = lax.all_gather(slot_x, 'et', axis=0, tiled=True)  9.8 us
    dot_general x1, matrix products, per_device(): out_rows = jnp.dot(hidden, w_down, preferred_element_type=jnp.float32)  6.65 us
  transfers between devices with their start and end apart: 4, of which 4 were waited for; matrix products, arithmetic and copies ran while one was open for 10% of the time, Pallas kernels for 0%

commit v1 on v0

v1 whole, which is shorter than its diff:
```python
import jax
import jax.numpy as jnp
from jax import lax
from jax.sharding import PartitionSpec as P

CAP = 16
LANES = 128


def make_per_device(n):
    ring = n // 4
    core_pairs = [(i, i ^ 1) for i in range(n)]
    y_pairs = [(i, i ^ 2) for i in range(n)]
    up_pairs = [(i, (i + 4) % n) for i in range(n)]
    down_pairs = [((i + 4) % n, i) for i in range(n)]

    def permute(x, pairs):
        return lax.ppermute(x, "et", pairs)

    def gather_rows(block):
        here, there = [], []
        held = block
        for k in range(ring):
            if k:
                held = permute(held, up_pairs)
            other = permute(held, y_pairs)
            pair = jnp.concatenate([held, other], axis=0)
            here.append(pair)
            there.append(permute(pair, core_pairs))
        return jnp.concatenate(here + there, axis=0)

    def scatter_rows(own, sent):
        d = own.shape[1]
        total = own + permute(sent, core_pairs).astype(jnp.float32)
        total = total.reshape(ring, 2, CAP, d)
        carry = None
        for k in range(ring - 1, -1, -1):
            got = permute(total[k, 1].astype(jnp.bfloat16), y_pairs)
            term = total[k, 0] + got.astype(jnp.float32)
            if carry is not None:
                term = term + carry.astype(jnp.float32)
            carry = term.astype(jnp.bfloat16)
            if k:
                carry = permute(carry, down_pairs)
        return carry

    def per_device(tokens, out_grad, expert_ids, gate_vals, w_gate, w_up, w_down):
        d = tokens.shape[1]
        landed = expert_ids == 0
        coef = jnp.sum(jnp.where(landed, gate_vals.astype(jnp.float32), 0.0), axis=1).astype(
            jnp.bfloat16
        )
        routed = jnp.any(landed, axis=1)
        slot = jnp.cumsum(routed.astype(jnp.int32)) - 1
        select = (slot[None, :] == jnp.arange(CAP, dtype=jnp.int32)[:, None]) & routed[None, :]
        select_bf = select.astype(jnp.bfloat16)
        wide = jnp.concatenate(
            [tokens, jnp.broadcast_to(coef[:, None], (coef.shape[0], LANES))], axis=1
        )
        slot_x = jnp.dot(select_bf, wide, preferred_element_type=jnp.float32).astype(jnp.bfloat16)
        slot_dy = jnp.dot(select_bf, out_grad, preferred_element_type=jnp.float32).astype(
            jnp.bfloat16
        )
        rows_wide = gather_rows(slot_x)
        rows_dy = gather_rows(slot_dy)
        rows_x = rows_wide[:, :d]
        coef_rows = rows_wide[:, d : d + 1].astype(jnp.float32)
        half = rows_dy.shape[0] // 2

        gate = jnp.dot(rows_x, w_gate, preferred_element_type=jnp.float32)
        up = jnp.dot(rows_x, w_up, preferred_element_type=jnp.float32)
        sig = jax.nn.sigmoid(gate)
        act = gate * sig
        hidden = (coef_rows * act * up).astype(jnp.bfloat16)
        out_rows = jnp.dot(hidden, w_down, preferred_element_type=jnp.float32)
        out_slots = scatter_rows(out_rows[:half], out_rows[half:].astype(jnp.bfloat16))

        scaled = coef_rows * jnp.dot(rows_dy, w_down.T, preferred_element_type=jnp.float32)
        dgate = (scaled * up * sig * (1.0 + gate * (1.0 - sig))).astype(jnp.bfloat16)
        dup = (scaled * act).astype(jnp.bfloat16)
        dx_rows = jnp.dot(dgate, w_gate.T, preferred_element_type=jnp.float32) + jnp.dot(
            dup, w_up.T, preferred_element_type=jnp.float32
        )
        dx_slots = scatter_rows(dx_rows[:half], dx_rows[half:].astype(jnp.bfloat16))

        grad_down = jnp.dot(hidden.T, rows_dy, preferred_element_type=jnp.float32)
        grad_gate = jnp.dot(rows_x.T, dgate, preferred_element_type=jnp.float32)
        grad_up = jnp.dot(rows_x.T, dup, preferred_element_type=jnp.float32)
        mixed = jnp.dot(select_bf.T, out_slots, preferred_element_type=jnp.float32)
        grad_tokens = jnp.dot(select_bf.T, dx_slots, preferred_element_type=jnp.float32)
        return (
            mixed.astype(jnp.bfloat16),
            grad_tokens.astype(jnp.bfloat16),
            grad_gate.astype(jnp.bfloat16),
            grad_up.astype(jnp.bfloat16),
            grad_down.astype(jnp.bfloat16),
        )

    return per_device


def solution(mesh):
    placed = (
        P(("groups", "et"), None),
        P(("groups", "et"), None),
        P(("groups", "et"), None),
        P(("groups", "et"), None),
        P(None, "et"),
        P(None, "et"),
        P("et", None),
    )
    return jax.shard_map(
        make_per_device(mesh.shape["et"]),
        mesh=mesh,
        in_specs=placed,
        out_specs=(
            P(("groups", "et"), None),
            P(("groups", "et"), None),
            P("groups", "et"),
            P("groups", "et"),
            P(("groups", "et"), None),
        ),
        check_vma=False,
    )
```

time: 301 us -> 152 us (0.50)
  waiting for transfers between devices: 201 us -> 78.7 us
  starting transfers between devices: 0.34 us -> 39.8 us
  blocking collectives: 35.3 us -> 0 us
  matrix products: 46 us -> 25.1 us
  between operations: 14.5 us -> 1.07 us
    reduce_scatter x2 -> x0, waiting for transfers between devices: 151 us -> none  [the longest x1 85.5 us: per_device(): lax.psum_scatter(out_rows, 'et', scatter_dimension=0, tiled=True)]
    ppermute x0 -> x38, waiting for transfers between devices: none -> 78.7 us  [permute(): return lax.ppermute(x, 'et', pairs)]
    all_gather x2 -> x0, waiting for transfers between devices: 50.2 us -> none  [the longest x1 40.4 us: per_device(): rows_dy = lax.all_gather(slot_dy, 'et', axis=0, tiled=True)]
    ppermute x0 -> x38, starting transfers between devices: none -> 39.8 us  [permute(): return lax.ppermute(x, 'et', pairs)]
    unnamed x1 -> x0, blocking collectives: 35.3 us -> none
    dot_general x12 -> x11, matrix products: 37 us -> 22.9 us  [the longest x1 3.48 us: per_device(): grad_down = jnp.dot(hidden.T, rows_dy, preferred_element_type=jnp.float32)]
    dot_general x1, matrix products: 6.65 us -> 1.84 us  [per_device(): out_rows = jnp.dot(hidden, w_down, preferred_element_type=jnp.float32)]
  transfers between devices with their start and end apart: 4 -> 38, of which waited for: 4 -> 19; matrix products, arithmetic and copies ran while one was open for 10% -> 13% of each run, Pallas kernels for 0% -> 0%
where the time goes in v1:
time: 152 us; the launch traced here: 151 us
  waiting for transfers between devices  78.7 us (52%)
  starting transfers between devices  39.8 us (26%)
  matrix products  25.1 us (17%)
  other arithmetic  3.61 us (2%)
  local copies, waits for them, and re-layouts  3.18 us (2%)
    ppermute x38, waiting for transfers between devices, permute(): return lax.ppermute(x, 'et', pairs)  78.7 us
    ppermute x38, starting transfers between devices, permute(): return lax.ppermute(x, 'et', pairs)  39.8 us
    dot_general x1, matrix products, per_device(): grad_down = jnp.dot(hidden.T, rows_dy, preferred_element_type=jnp.float32)  3.48 us
    dot_general x1, matrix products, per_device(): grad_gate = jnp.dot(rows_x.T, dgate, preferred_element_type=jnp.float32)  3.25 us
    dot_general x1, matrix products, per_device(): grad_up = jnp.dot(rows_x.T, dup, preferred_element_type=jnp.float32)  3.23 us
  transfers between devices with their start and end apart: 38, of which 19 were waited for; matrix products, arithmetic and copies ran while one was open for 13% of the time, Pallas kernels for 0%

profile of v1, /device:TPU:0, one launch (start us, length us, event | category | flops | bytes accessed | tf_op | source)
XLA Modules:
  0.0 151.4 jit_solution(3619468229491785289)
XLA Ops:
  0.6 0.8 fusion.48
  1.9 0.2 copy-done
  2.1 0.3 constant_dynamic-update-slice_fusion.23
  2.4 3.0 %collective-permute-start.19 = (bf16[16,6144]{1,0:T(8,128)(2,1)S(1)}, bf16[16,6144]{1,0:T(8,128)(2,1)S(1)}, u32[]{:S(2)}, u32[]{:S(2)}) collective-permute-start(bf16[16,6144]{1,0:T(8,128)(2,1)S(1)} %get-tuple-element.19), channel_id=1, source_target_pairs={{0,2},{1,3},{2,0},{3,1},{4,6},{5,7},{6,4},{7,5},{8,10},{9,11},{10,... | collective-permute-start | bytes 589832 | tf_op jit(solution)/shard_map/ppermute | solution.py:18
  5.4 0.7 select_reduce_fusion
  6.2 1.7 %constant_dynamic-update-slice_fusion.11 = (bf16[256,6272]{1,0:T(8,128)(2,1)S(1)}, bf16[16,6272]{1,0:T(8,128)(2,1)S(1)}) fusion(bf16[128,128]{1,0:T(8,128)(2,1)S(1)} %broadcast_in_dim.7, bf16[128,6144]{1,0:T(8,128)(2,1)} %param.7, s32[128]{0:T(128)S(1)} %add_reduce_fusion, pred[128]{0:T(512)(128)(4,1)S(1)} %get-tuple-element.5), kind=kOutput, calls=%fused_computation.86 | convolution fusion | flops 29005824 | bytes 2007680 | tf_op jit(solution)/shard_map/dot_general | solution.py:60
  8.0 2.1 %collective-permute-start.1 = (bf16[16,6272]{1,0:T(8,128)(2,1)S(1)}, bf16[16,6272]{1,0:T(8,128)(2,1)S(1)}, u32[]{:S(2)}, u32[]{:S(2)}) collective-permute-start(bf16[16,6272]{1,0:T(8,128)(2,1)S(1)} %get-tuple-element.21), channel_id=1, source_target_pairs={{0,4},{1,5},{2,6},{3,7},{4,8},{5,9},{6,10},{7,11},{8,12},{9,13},{1... | collective-permute-start | bytes 602120 | tf_op jit(solution)/shard_map/ppermute | solution.py:18
  10.1 1.6 %collective-permute-start.20 = (bf16[16,6144]{1,0:T(8,128)(2,1)S(1)}, bf16[16,6144]{1,0:T(8,128)(2,1)S(1)}, u32[]{:S(2)}, u32[]{:S(2)}) collective-permute-start(bf16[16,6144]{1,0:T(8,128)(2,1)S(1)} %get-tuple-element.19), channel_id=1, source_target_pairs={{0,4},{1,5},{2,6},{3,7},{4,8},{5,9},{6,10},{7,11},{8,12},{9,13},{1... | collective-permute-start | bytes 589832 | tf_op jit(solution)/shard_map/ppermute | solution.py:18
  11.8 9.0 %collective-permute-done.20 = bf16[16,6144]{1,0:T(8,128)(2,1)S(1)} collective-permute-done((bf16[16,6144]{1,0:T(8,128)(2,1)S(1)}, bf16[16,6144]{1,0:T(8,128)(2,1)S(1)}, u32[]{:S(2)}, u32[]{:S(2)}) %collective-permute-start.20) | collective-permute-done | bytes 196640 | tf_op jit(solution)/shard_map/ppermute | solution.py:18
  20.7 1.5 %collective-permute-start.21 = (bf16[16,6144]{1,0:T(8,128)(2,1)S(1)}, bf16[16,6144]{1,0:T(8,128)(2,1)S(1)}, u32[]{:S(2)}, u32[]{:S(2)}) collective-permute-start(bf16[16,6144]{1,0:T(8,128)(2,1)S(1)} %collective-permute-done.20), channel_id=1, source_target_pairs={{0,2},{1,3},{2,0},{3,1},{4,6},{5,7},{6,4},{7,5},{8,10},{9,11},{10,... | collective-permute-start | bytes 589832 | tf_op jit(solution)/shard_map/ppermute | solution.py:18
  22.5 0.6 collective-permute-start.2
  23.1 4.2 %collective-permute-done.21 = bf16[16,6144]{1,0:T(8,128)(2,1)S(1)} collective-permute-done((bf16[16,6144]{1,0:T(8,128)(2,1)S(1)}, bf16[16,6144]{1,0:T(8,128)(2,1)S(1)}, u32[]{:S(2)}, u32[]{:S(2)}) %collective-permute-start.21) | collective-permute-done | bytes 196640 | tf_op jit(solution)/shard_map/ppermute | solution.py:18
  27.3 3.9 %collective-permute-done.22 = bf16[16,6144]{1,0:T(8,128)(2,1)S(1)} collective-permute-done((bf16[16,6144]{1,0:T(8,128)(2,1)S(1)}, bf16[16,6144]{1,0:T(8,128)(2,1)S(1)}, u32[]{:S(2)}, u32[]{:S(2)}) %collective-permute-start.22) | collective-permute-done | bytes 196640 | tf_op jit(solution)/shard_map/ppermute | solution.py:18
  31.2 1.0 collective-permute-start.23
  32.3 2.5 %collective-permute-done.3 = bf16[16,6272]{1,0:T(8,128)(2,1)S(1)} collective-permute-done((bf16[16,6272]{1,0:T(8,128)(2,1)S(1)}, bf16[16,6272]{1,0:T(8,128)(2,1)S(1)}, u32[]{:S(2)}, u32[]{:S(2)}) %collective-permute-start.3) | collective-permute-done | bytes 200736 | tf_op jit(solution)/shard_map/ppermute | solution.py:18
  34.8 3.8 %collective-permute-done.23 = bf16[16,6144]{1,0:T(8,128)(2,1)S(1)} collective-permute-done((bf16[16,6144]{1,0:T(8,128)(2,1)S(1)}, bf16[16,6144]{1,0:T(8,128)(2,1)S(1)}, u32[]{:S(2)}, u32[]{:S(2)}) %collective-permute-start.23) | collective-permute-done | bytes 196640 | tf_op jit(solution)/shard_map/ppermute | solution.py:18
  38.7 3.6 %collective-permute-done.24 = bf16[16,6144]{1,0:T(8,128)(2,1)S(1)} collective-permute-done((bf16[16,6144]{1,0:T(8,128)(2,1)S(1)}, bf16[16,6144]{1,0:T(8,128)(2,1)S(1)}, u32[]{:S(2)}, u32[]{:S(2)}) %collective-permute-start.24) | collective-permute-done | bytes 196640 | tf_op jit(solution)/shard_map/ppermute | solution.py:18
  42.2 2.5 %collective-permute-start.4 = (bf16[16,6272]{1,0:T(8,128)(2,1)S(1)}, bf16[16,6272]{1,0:T(8,128)(2,1)S(1)}, u32[]{:S(2)}, u32[]{:S(2)}) collective-permute-start(bf16[16,6272]{1,0:T(8,128)(2,1)S(1)} %collective-permute-done.3), channel_id=1, source_target_pairs={{0,2},{1,3},{2,0},{3,1},{4,6},{5,7},{6,4},{7,5},{8,10},{9,11},{10,... | collective-permute-start | bytes 602120 | tf_op jit(solution)/shard_map/ppermute | solution.py:18
  44.7 3.7 %collective-permute-done.4 = bf16[16,6272]{1,0:T(8,128)(2,1)S(1)} collective-permute-done((bf16[16,6272]{1,0:T(8,128)(2,1)S(1)}, bf16[16,6272]{1,0:T(8,128)(2,1)S(1)}, u32[]{:S(2)}, u32[]{:S(2)}) %collective-permute-start.4) | collective-permute-done | bytes 200736 | tf_op jit(solution)/shard_map/ppermute | solution.py:18
  48.5 7.4 %collective-permute-done.5 = bf16[16,6272]{1,0:T(8,128)(2,1)S(1)} collective-permute-done((bf16[16,6272]{1,0:T(8,128)(2,1)S(1)}, bf16[16,6272]{1,0:T(8,128)(2,1)S(1)}, u32[]{:S(2)}, u32[]{:S(2)}) %collective-permute-start.5) | collective-permute-done | bytes 200736 | tf_op jit(solution)/shard_map/ppermute | solution.py:18
  55.9 2.0 %collective-permute-start.25 = (bf16[16,6144]{1,0:T(8,128)(2,1)S(1)}, bf16[16,6144]{1,0:T(8,128)(2,1)S(1)}, u32[]{:S(2)}, u32[]{:S(2)}) collective-permute-start(bf16[16,6144]{1,0:T(8,128)(2,1)S(1)} %collective-permute-done.24), channel_id=1, source_target_pairs={{0,2},{1,3},{2,0},{3,1},{4,6},{5,7},{6,4},{7,5},{8,10},{9,11},{10,... | collective-permute-start | bytes 589832 | tf_op jit(solution)/shard_map/ppermute | solution.py:18
  58.0 3.6 %collective-permute-done.25 = bf16[16,6144]{1,0:T(8,128)(2,1)S(1)} collective-permute-done((bf16[16,6144]{1,0:T(8,128)(2,1)S(1)}, bf16[16,6144]{1,0:T(8,128)(2,1)S(1)}, u32[]{:S(2)}, u32[]{:S(2)}) %collective-permute-start.25) | collective-permute-done | bytes 196640 | tf_op jit(solution)/shard_map/ppermute | solution.py:18
  61.7 0.6 collective-permute-start.9
  62.3 2.1 %collective-permute-start.6 = (bf16[16,6272]{1,0:T(8,128)(2,1)S(1)}, bf16[16,6272]{1,0:T(8,128)(2,1)S(1)}, u32[]{:S(2)}, u32[]{:S(2)}) collective-permute-start(bf16[16,6272]{1,0:T(8,128)(2,1)S(1)} %collective-permute-done.5), channel_id=1, source_target_pairs={{0,2},{1,3},{2,0},{3,1},{4,6},{5,7},{6,4},{7,5},{8,10},{9,11},{10,... | collective-permute-start | bytes 602120 | tf_op jit(solution)/shard_map/ppermute | solution.py:18
  64.4 5.1 %collective-permute-done.6 = bf16[16,6272]{1,0:T(8,128)(2,1)S(1)} collective-permute-done((bf16[16,6272]{1,0:T(8,128)(2,1)S(1)}, bf16[16,6272]{1,0:T(8,128)(2,1)S(1)}, u32[]{:S(2)}, u32[]{:S(2)}) %collective-permute-start.6) | collective-permute-done | bytes 200736 | tf_op jit(solution)/shard_map/ppermute | solution.py:18
  69.6 0.6 collective-permute-start.10
  70.4 0.9 collective-permute-done.29
  71.3 0.5 collective-permute-done.10
  72.0 1.3 fusion.4
  73.3 0.9 copy-done.4
  74.2 1.3 fusion.2
  75.4 0.9 copy-done.2
  76.3 1.5 %multiply_convert_fusion = (bf16[256,336]{0,1:T(8,128)(2,1)S(1)}, bf16[256,336]{0,1:T(8,128)(2,1)S(1)}, bf16[256,336]{0,1:T(8,128)(2,1)S(1)}) fusion(f32[256,336]{0,1:T(8,128)S(1)} %fusion.4, f32[256,336]{0,1:T(8,128)S(1)} %fusion.2, f32[256]{0:T(256)S(1)} %convert_reduce_fusion, bf16[256,6144]{1,0:T(8,128)(2,1)S(1)} %constant_dynamic-update-slice_fusion.12, ...), kind=kOutput, calls=%fused_computation.60 | convolution fusion | flops 1058426880 | bytes 8479744 | tf_op jit(solution)/shard_map/dot_general | solution.py:78
  77.9 1.8 %fusion.49 = f32[256,6144]{1,0:T(8,128)S(1)} fusion(bf16[256,336]{0,1:T(8,128)(2,1)S(1)} %get-tuple-element.17, bf16[336,6144]{1,0:T(8,128)(2,1)S(1)} %copy-done.2), kind=kOutput, calls=%fused_computation.114 | convolution fusion | flops 1056964608 | bytes 10592256 | tf_op jit(solution)/shard_map/dot_general | solution.py:75
  79.9 0.2 collective-permute-start.11
  80.1 1.8 %fusion.50 = f32[256,6144]{1,0:T(8,128)S(1)} fusion(bf16[256,336]{0,1:T(8,128)(2,1)S(1)} %get-tuple-element.16, bf16[6144,336]{0,1:T(8,128)(2,1)S(1)} %copy-done.3), kind=kOutput, calls=%fused_computation.115 | convolution fusion | flops 1056964608 | bytes 10592256 | tf_op jit(solution)/shard_map/dot_general | solution.py:81
  81.9 1.8 %convolution_add_fusion = f32[256,6144]{1,0:T(8,128)S(1)} fusion(f32[256,6144]{1,0:T(8,128)S(1)} %fusion.50, bf16[256,336]{0,1:T(8,128)(2,1)S(1)} %get-tuple-element.15, bf16[6144,336]{0,1:T(8,128)(2,1)S(1)} %copy-done.4), kind=kOutput, calls=%fused_computation | convolution fusion | flops 1058537472 | bytes 16883712 | tf_op jit(solution)/shard_map/dot_general | solution.py:81
  84.0 0.4 collective-permute-start.30
  84.4 3.3 %convolution_convert_fusion.1 = bf16[6144,336]{0,1:T(8,128)(2,1)} fusion(bf16[256,336]{0,1:T(8,128)(2,1)S(1)} %get-tuple-element.16, bf16[256,6272]{1,0:T(8,128)(2,1)S(1)} %constant_dynamic-update-slice_fusion), kind=kOutput, calls=%fused_computation.2 | convolution fusion | flops 1059028992 | bytes 7446528 | tf_op jit(solution)/shard_map/dot_general | solution.py:87
  87.6 3.2 %convolution_convert_fusion = bf16[6144,336]{0,1:T(8,128)(2,1)} fusion(bf16[256,336]{0,1:T(8,128)(2,1)S(1)} %get-tuple-element.15, bf16[256,6272]{1,0:T(8,128)(2,1)S(1)} %constant_dynamic-update-slice_fusion), kind=kOutput, calls=%fused_computation.1 | convolution fusion | flops 1059028992 | bytes 7446528 | tf_op jit(solution)/shard_map/dot_general | solution.py:88
  90.9 3.5 %convolution_convert_fusion.2 = bf16[336,6144]{1,0:T(8,128)(2,1)} fusion(bf16[256,336]{0,1:T(8,128)(2,1)S(1)} %get-tuple-element.17, bf16[256,6144]{1,0:T(8,128)(2,1)S(1)} %constant_dynamic-update-slice_fusion.12), kind=kOutput, calls=%fused_computation.3 | convolution fusion | flops 1059028992 | bytes 7446528 | tf_op jit(solution)/shard_map/dot_general | solution.py:86
  94.4 0.4 slice_add_fusion.1
  95.0 1.8 %collective-permute-start.15 = (bf16[16,6144]{1,0:T(8,128)(2,1)S(1)}, bf16[16,6144]{1,0:T(8,128)(2,1)S(1)}, u32[]{:S(2)}, u32[]{:S(2)}) collective-permute-start(bf16[16,6144]{1,0:T(8,128)(2,1)S(1)} %get-tuple-element.12), channel_id=1, source_target_pairs={{0,2},{1,3},{2,0},{3,1},{4,6},{5,7},{6,4},{7,5},{8,10},{9,11},{10,... | collective-permute-start | bytes 589832 | tf_op jit(solution)/shard_map/ppermute | solution.py:18
  96.8 0.3 collective-permute-start.14
  97.1 1.7 %collective-permute-start.13 = (bf16[16,6144]{1,0:T(8,128)(2,1)S(1)}, bf16[16,6144]{1,0:T(8,128)(2,1)S(1)}, u32[]{:S(2)}, u32[]{:S(2)}) collective-permute-start(bf16[16,6144]{1,0:T(8,128)(2,1)S(1)} %get-tuple-element.14), channel_id=1, source_target_pairs={{0,2},{1,3},{2,0},{3,1},{4,6},{5,7},{6,4},{7,5},{8,10},{9,11},{10,... | collective-permute-start | bytes 589832 | tf_op jit(solution)/shard_map/ppermute | solution.py:18
  98.8 0.3 collective-permute-start.12
  99.1 0.4 slice_add_fusion
  99.7 1.8 %collective-permute-start.34 = (bf16[16,6144]{1,0:T(8,128)(2,1)S(1)}, bf16[16,6144]{1,0:T(8,128)(2,1)S(1)}, u32[]{:S(2)}, u32[]{:S(2)}) collective-permute-start(bf16[16,6144]{1,0:T(8,128)(2,1)S(1)} %get-tuple-element.8), channel_id=1, source_target_pairs={{0,2},{1,3},{2,0},{3,1},{4,6},{5,7},{6,4},{7,5},{8,10},{9,11},{10,... | collective-permute-start | bytes 589832 | tf_op jit(solution)/shard_map/ppermute | solution.py:18
  101.6 1.2 collective-permute-done.15
  102.8 1.7 %collective-permute-start.33 = (bf16[16,6144]{1,0:T(8,128)(2,1)S(1)}, bf16[16,6144]{1,0:T(8,128)(2,1)S(1)}, u32[]{:S(2)}, u32[]{:S(2)}) collective-permute-start(bf16[16,6144]{1,0:T(8,128)(2,1)S(1)} %get-tuple-element.9), channel_id=1, source_target_pairs={{0,2},{1,3},{2,0},{3,1},{4,6},{5,7},{6,4},{7,5},{8,10},{9,11},{10,... | collective-permute-start | bytes 589832 | tf_op jit(solution)/shard_map/ppermute | solution.py:18
  104.6 15.1 %collective-permute-done.34 = bf16[16,6144]{1,0:T(8,128)(2,1)S(1)} collective-permute-done((bf16[16,6144]{1,0:T(8,128)(2,1)S(1)}, bf16[16,6144]{1,0:T(8,128)(2,1)S(1)}, u32[]{:S(2)}, u32[]{:S(2)}) %collective-permute-start.34) | collective-permute-done | bytes 196640 | tf_op jit(solution)/shard_map/ppermute | solution.py:18
  119.7 1.8 %collective-permute-start.32 = (bf16[16,6144]{1,0:T(8,128)(2,1)S(1)}, bf16[16,6144]{1,0:T(8,128)(2,1)S(1)}, u32[]{:S(2)}, u32[]{:S(2)}) collective-permute-start(bf16[16,6144]{1,0:T(8,128)(2,1)S(1)} %get-tuple-element.10), channel_id=1, source_target_pairs={{0,2},{1,3},{2,0},{3,1},{4,6},{5,7},{6,4},{7,5},{8,10},{9,11},{10,... | collective-permute-start | bytes 589832 | tf_op jit(solution)/shard_map/ppermute | solution.py:18
  121.5 3.8 %collective-permute-done.16 = bf16[16,6144]{1,0:T(8,128)(2,1)S(1)} collective-permute-done((bf16[16,6144]{1,0:T(8,128)(2,1)S(1)}, bf16[16,6144]{1,0:T(8,128)(2,1)S(1)}, u32[]{:S(2)}, u32[]{:S(2)}) %collective-permute-start.16) | collective-permute-done | bytes 196640 | tf_op jit(solution)/shard_map/ppermute | solution.py:18
  125.3 1.8 %collective-permute-start.35 = (bf16[16,6144]{1,0:T(8,128)(2,1)S(1)}, bf16[16,6144]{1,0:T(8,128)(2,1)S(1)}, u32[]{:S(2)}, u32[]{:S(2)}) collective-permute-start(bf16[16,6144]{1,0:T(8,128)(2,1)S(1)} %fusion.10), channel_id=1, source_target_pairs={{4,0},{5,1},{6,2},{7,3},{8,4},{9,5},{10,6},{11,7},{12,8},{13,9},{1... | collective-permute-start | bytes 589832 | tf_op jit(solution)/shard_map/ppermute | solution.py:18
  127.2 1.8 %collective-permute-start.31 = (bf16[16,6144]{1,0:T(8,128)(2,1)S(1)}, bf16[16,6144]{1,0:T(8,128)(2,1)S(1)}, u32[]{:S(2)}, u32[]{:S(2)}) collective-permute-start(bf16[16,6144]{1,0:T(8,128)(2,1)S(1)} %get-tuple-element.7), channel_id=1, source_target_pairs={{0,2},{1,3},{2,0},{3,1},{4,6},{5,7},{6,4},{7,5},{8,10},{9,11},{10,... | collective-permute-start | bytes 589832 | tf_op jit(solution)/shard_map/ppermute | solution.py:18
  129.0 2.9 %collective-permute-done.35 = bf16[16,6144]{1,0:T(8,128)(2,1)S(1)} collective-permute-done((bf16[16,6144]{1,0:T(8,128)(2,1)S(1)}, bf16[16,6144]{1,0:T(8,128)(2,1)S(1)}, u32[]{:S(2)}, u32[]{:S(2)}) %collective-permute-start.35) | collective-permute-done | bytes 196640 | tf_op jit(solution)/shard_map/ppermute | solution.py:18
  131.9 2.7 %collective-permute-start.17 = (bf16[16,6144]{1,0:T(8,128)(2,1)S(1)}, bf16[16,6144]{1,0:T(8,128)(2,1)S(1)}, u32[]{:S(2)}, u32[]{:S(2)}) collective-permute-start(bf16[16,6144]{1,0:T(8,128)(2,1)S(1)} %fusion.24), channel_id=1, source_target_pairs={{4,0},{5,1},{6,2},{7,3},{8,4},{9,5},{10,6},{11,7},{12,8},{13,9},{1... | collective-permute-start | bytes 589832 | tf_op jit(solution)/shard_map/ppermute | solution.py:18
  134.7 4.7 %collective-permute-done.17 = bf16[16,6144]{1,0:T(8,128)(2,1)S(1)} collective-permute-done((bf16[16,6144]{1,0:T(8,128)(2,1)S(1)}, bf16[16,6144]{1,0:T(8,128)(2,1)S(1)}, u32[]{:S(2)}, u32[]{:S(2)}) %collective-permute-start.17) | collective-permute-done | bytes 196640 | tf_op jit(solution)/shard_map/ppermute | solution.py:18
  139.5 2.8 %collective-permute-start.18 = (bf16[16,6144]{1,0:T(8,128)(2,1)S(1)}, bf16[16,6144]{1,0:T(8,128)(2,1)S(1)}, u32[]{:S(2)}, u32[]{:S(2)}) collective-permute-start(bf16[16,6144]{1,0:T(8,128)(2,1)S(1)} %fusion.27), channel_id=1, source_target_pairs={{4,0},{5,1},{6,2},{7,3},{8,4},{9,5},{10,6},{11,7},{12,8},{13,9},{1... | collective-permute-start | bytes 589832 | tf_op jit(solution)/shard_map/ppermute | solution.py:18
  142.3 1.3 collective-permute-done.36
  143.7 2.8 %collective-permute-start.37 = (bf16[16,6144]{1,0:T(8,128)(2,1)S(1)}, bf16[16,6144]{1,0:T(8,128)(2,1)S(1)}, u32[]{:S(2)}, u32[]{:S(2)}) collective-permute-start(bf16[16,6144]{1,0:T(8,128)(2,1)S(1)} %fusion.16), channel_id=1, source_target_pairs={{4,0},{5,1},{6,2},{7,3},{8,4},{9,5},{10,6},{11,7},{12,8},{13,9},{1... | collective-permute-start | bytes 589832 | tf_op jit(solution)/shard_map/ppermute | solution.py:18
  146.5 1.8 %convolution_convert_fusion.5 = bf16[128,6144]{1,0:T(8,128)(2,1)} fusion(f32[4,2,16,6144]{3,2,1,0:T(8,128)S(1)} %bitcast.101, bf16[16,6144]{1,0:T(8,128)(2,1)S(1)} %collective-permute-done.18, bf16[16,6144]{1,0:T(8,128)(2,1)S(1)} %collective-permute-done.12, s32[128]{0:T(128)S(1)} %add_reduce_fusion, pred[128]{0:T(512)(128)(4,1)S(1)} %get-tuple-element.5), kind=kOutput, calls=%fused_computation.6 | convolution fusion | flops 26447872 | bytes 2360320 | tf_op jit(solution)/shard_map/dot_general | solution.py:89
  148.2 1.4 collective-permute-done.37
  149.7 1.8 %convolution_convert_fusion.4 = bf16[128,6144]{1,0:T(8,128)(2,1)} fusion(f32[4,2,16,6144]{3,2,1,0:T(8,128)S(1)} %bitcast.106, bf16[16,6144]{1,0:T(8,128)(2,1)S(1)} %collective-permute-done.37, bf16[16,6144]{1,0:T(8,128)(2,1)S(1)} %collective-permute-done.31, s32[128]{0:T(128)S(1)} %add_reduce_fusion, pred[128]{0:T(512)(128)(4,1)S(1)} %get-tuple-element.5), kind=kOutput, calls=%fused_computation.5 | convolution fusion | flops 26447872 | bytes 2360320 | tf_op jit(solution)/shard_map/dot_general | solution.py:90
  (87 shorter events, 2.9 us)
Async XLA Ops:
  0.6 1.4 copy-start
  2.4 9.3 %collective-permute-start.19 = (bf16[16,6144]{1,0:T(8,128)(2,1)S(1)}, bf16[16,6144]{1,0:T(8,128)(2,1)S(1)}, u32[]{:S(2)}, u32[]{:S(2)}) collective-permute-start(bf16[16,6144]{1,0:T(8,128)(2,1)S(1)} %get-tuple-element.19), channel_id=1, source_target_pairs={{0,2},{1,3},{2,0},{3,1},{4,6},{5,7},{6,4},{7,5},{8,10},{9,11},{10,... | collective-permute-start | bytes 589832 | tf_op jit(solution)/shard_map/ppermute | solution.py:18
  7.9 14.4 %collective-permute-start = (bf16[16,6272]{1,0:T(8,128)(2,1)S(1)}, bf16[16,6272]{1,0:T(8,128)(2,1)S(1)}, u32[]{:S(2)}, u32[]{:S(2)}) collective-permute-start(bf16[16,6272]{1,0:T(8,128)(2,1)S(1)} %get-tuple-element.21), channel_id=1, source_target_pairs={{0,2},{1,3},{2,0},{3,1},{4,6},{5,7},{6,4},{7,5},{8,10},{9,11},{10,... | collective-permute-start | bytes 602120 | tf_op jit(solution)/shard_map/ppermute | solution.py:18
  8.0 14.4 %collective-permute-start.1 = (bf16[16,6272]{1,0:T(8,128)(2,1)S(1)}, bf16[16,6272]{1,0:T(8,128)(2,1)S(1)}, u32[]{:S(2)}, u32[]{:S(2)}) collective-permute-start(bf16[16,6272]{1,0:T(8,128)(2,1)S(1)} %get-tuple-element.21), channel_id=1, source_target_pairs={{0,4},{1,5},{2,6},{3,7},{4,8},{5,9},{6,10},{7,11},{8,12},{9,13},{1... | collective-permute-start | bytes 602120 | tf_op jit(solution)/shard_map/ppermute | solution.py:18
  10.1 10.7 %collective-permute-start.20 = (bf16[16,6144]{1,0:T(8,128)(2,1)S(1)}, bf16[16,6144]{1,0:T(8,128)(2,1)S(1)}, u32[]{:S(2)}, u32[]{:S(2)}) collective-permute-start(bf16[16,6144]{1,0:T(8,128)(2,1)S(1)} %get-tuple-element.19), channel_id=1, source_target_pairs={{0,4},{1,5},{2,6},{3,7},{4,8},{5,9},{6,10},{7,11},{8,12},{9,13},{1... | collective-permute-start | bytes 589832 | tf_op jit(solution)/shard_map/ppermute | solution.py:18
  11.7 50.0 %collective-permute-start.26 = (bf16[32,6144]{1,0:T(8,128)(2,1)S(1)}, bf16[32,6144]{1,0:T(8,128)(2,1)S(1)}, u32[]{:S(2)}, u32[]{:S(2)}) collective-permute-start(bf16[32,6144]{1,0:T(8,128)(2,1)S(1)} %pad_maximum_fusion.4), channel_id=1, source_target_pairs={{0,1},{1,0},{2,3},{3,2},{4,5},{5,4},{6,7},{7,6},{8,9},{9,8},{10,11... | collective-permute-start | bytes 1179656 | tf_op jit(solution)/shard_map/ppermute | solution.py:18
  20.7 6.5 %collective-permute-start.21 = (bf16[16,6144]{1,0:T(8,128)(2,1)S(1)}, bf16[16,6144]{1,0:T(8,128)(2,1)S(1)}, u32[]{:S(2)}, u32[]{:S(2)}) collective-permute-start(bf16[16,6144]{1,0:T(8,128)(2,1)S(1)} %collective-permute-done.20), channel_id=1, source_target_pairs={{0,2},{1,3},{2,0},{3,1},{4,6},{5,7},{6,4},{7,5},{8,10},{9,11},{10,... | collective-permute-start | bytes 589832 | tf_op jit(solution)/shard_map/ppermute | solution.py:18
  22.3 8.9 %collective-permute-start.22 = (bf16[16,6144]{1,0:T(8,128)(2,1)S(1)}, bf16[16,6144]{1,0:T(8,128)(2,1)S(1)}, u32[]{:S(2)}, u32[]{:S(2)}) collective-permute-start(bf16[16,6144]{1,0:T(8,128)(2,1)S(1)} %collective-permute-done.20), channel_id=1, source_target_pairs={{0,4},{1,5},{2,6},{3,7},{4,8},{5,9},{6,10},{7,11},{8,12},{9,13},{1... | collective-permute-start | bytes 589832 | tf_op jit(solution)/shard_map/ppermute | solution.py:18
  22.4 47.2 %collective-permute-start.7 = (bf16[32,6272]{1,0:T(8,128)(2,1)S(1)}, bf16[32,6272]{1,0:T(8,128)(2,1)S(1)}, u32[]{:S(2)}, u32[]{:S(2)}) collective-permute-start(bf16[32,6272]{1,0:T(8,128)(2,1)S(1)} %pad_maximum_fusion), channel_id=1, source_target_pairs={{0,1},{1,0},{2,3},{3,2},{4,5},{5,4},{6,7},{7,6},{8,9},{9,8},{10,11... | collective-permute-start | bytes 1204232 | tf_op jit(solution)/shard_map/ppermute | solution.py:18
  22.5 8.8 %collective-permute-start.2 = (bf16[16,6272]{1,0:T(8,128)(2,1)S(1)}, bf16[16,6272]{1,0:T(8,128)(2,1)S(1)}, u32[]{:S(2)}, u32[]{:S(2)}) collective-permute-start(bf16[16,6272]{1,0:T(8,128)(2,1)S(1)} %collective-permute-done.1), channel_id=1, source_target_pairs={{0,2},{1,3},{2,0},{3,1},{4,6},{5,7},{6,4},{7,5},{8,10},{9,11},{10,... | collective-permute-start | bytes 602120 | tf_op jit(solution)/shard_map/ppermute | solution.py:18
  27.3 7.5 %collective-permute-start.3 = (bf16[16,6272]{1,0:T(8,128)(2,1)S(1)}, bf16[16,6272]{1,0:T(8,128)(2,1)S(1)}, u32[]{:S(2)}, u32[]{:S(2)}) collective-permute-start(bf16[16,6272]{1,0:T(8,128)(2,1)S(1)} %collective-permute-done.1), channel_id=1, source_target_pairs={{0,4},{1,5},{2,6},{3,7},{4,8},{5,9},{6,10},{7,11},{8,12},{9,13},{1... | collective-permute-start | bytes 602120 | tf_op jit(solution)/shard_map/ppermute | solution.py:18
  31.2 31.1 %collective-permute-start.27 = (bf16[32,6144]{1,0:T(8,128)(2,1)S(1)}, bf16[32,6144]{1,0:T(8,128)(2,1)S(1)}, u32[]{:S(2)}, u32[]{:S(2)}) collective-permute-start(bf16[32,6144]{1,0:T(8,128)(2,1)S(1)} %pad_maximum_fusion.5), channel_id=1, source_target_pairs={{0,1},{1,0},{2,3},{3,2},{4,5},{5,4},{6,7},{7,6},{8,9},{9,8},{10,11... | collective-permute-start | bytes 1179656 | tf_op jit(solution)/shard_map/ppermute | solution.py:18
  31.2 7.4 %collective-permute-start.23 = (bf16[16,6144]{1,0:T(8,128)(2,1)S(1)}, bf16[16,6144]{1,0:T(8,128)(2,1)S(1)}, u32[]{:S(2)}, u32[]{:S(2)}) collective-permute-start(bf16[16,6144]{1,0:T(8,128)(2,1)S(1)} %collective-permute-done.22), channel_id=1, source_target_pairs={{0,2},{1,3},{2,0},{3,1},{4,6},{5,7},{6,4},{7,5},{8,10},{9,11},{10,... | collective-permute-start | bytes 589832 | tf_op jit(solution)/shard_map/ppermute | solution.py:18
  34.8 7.5 %collective-permute-start.24 = (bf16[16,6144]{1,0:T(8,128)(2,1)S(1)}, bf16[16,6144]{1,0:T(8,128)(2,1)S(1)}, u32[]{:S(2)}, u32[]{:S(2)}) collective-permute-start(bf16[16,6144]{1,0:T(8,128)(2,1)S(1)} %collective-permute-done.22), channel_id=1, source_target_pairs={{0,4},{1,5},{2,6},{3,7},{4,8},{5,9},{6,10},{7,11},{8,12},{9,13},{1... | collective-permute-start | bytes 589832 | tf_op jit(solution)/shard_map/ppermute | solution.py:18
  38.6 31.6 %collective-permute-start.8 = (bf16[32,6272]{1,0:T(8,128)(2,1)S(1)}, bf16[32,6272]{1,0:T(8,128)(2,1)S(1)}, u32[]{:S(2)}, u32[]{:S(2)}) collective-permute-start(bf16[32,6272]{1,0:T(8,128)(2,1)S(1)} %pad_maximum_fusion.1), channel_id=1, source_target_pairs={{0,1},{1,0},{2,3},{3,2},{4,5},{5,4},{6,7},{7,6},{8,9},{9,8},{10,11... | collective-permute-start | bytes 1204232 | tf_op jit(solution)/shard_map/ppermute | solution.py:18
  42.2 6.2 %collective-permute-start.4 = (bf16[16,6272]{1,0:T(8,128)(2,1)S(1)}, bf16[16,6272]{1,0:T(8,128)(2,1)S(1)}, u32[]{:S(2)}, u32[]{:S(2)}) collective-permute-start(bf16[16,6272]{1,0:T(8,128)(2,1)S(1)} %collective-permute-done.3), channel_id=1, source_target_pairs={{0,2},{1,3},{2,0},{3,1},{4,6},{5,7},{6,4},{7,5},{8,10},{9,11},{10,... | collective-permute-start | bytes 602120 | tf_op jit(solution)/shard_map/ppermute | solution.py:18
  48.4 7.5 %collective-permute-start.5 = (bf16[16,6272]{1,0:T(8,128)(2,1)S(1)}, bf16[16,6272]{1,0:T(8,128)(2,1)S(1)}, u32[]{:S(2)}, u32[]{:S(2)}) collective-permute-start(bf16[16,6272]{1,0:T(8,128)(2,1)S(1)} %collective-permute-done.3), channel_id=1, source_target_pairs={{0,4},{1,5},{2,6},{3,7},{4,8},{5,9},{6,10},{7,11},{8,12},{9,13},{1... | collective-permute-start | bytes 602120 | tf_op jit(solution)/shard_map/ppermute | solution.py:18
  55.9 5.7 %collective-permute-start.25 = (bf16[16,6144]{1,0:T(8,128)(2,1)S(1)}, bf16[16,6144]{1,0:T(8,128)(2,1)S(1)}, u32[]{:S(2)}, u32[]{:S(2)}) collective-permute-start(bf16[16,6144]{1,0:T(8,128)(2,1)S(1)} %collective-permute-done.24), channel_id=1, source_target_pairs={{0,2},{1,3},{2,0},{3,1},{4,6},{5,7},{6,4},{7,5},{8,10},{9,11},{10,... | collective-permute-start | bytes 589832 | tf_op jit(solution)/shard_map/ppermute | solution.py:18
  61.6 8.7 %collective-permute-start.28 = (bf16[32,6144]{1,0:T(8,128)(2,1)S(1)}, bf16[32,6144]{1,0:T(8,128)(2,1)S(1)}, u32[]{:S(2)}, u32[]{:S(2)}) collective-permute-start(bf16[32,6144]{1,0:T(8,128)(2,1)S(1)} %pad_maximum_fusion.6), channel_id=1, source_target_pairs={{0,1},{1,0},{2,3},{3,2},{4,5},{5,4},{6,7},{7,6},{8,9},{9,8},{10,11... | collective-permute-start | bytes 1179656 | tf_op jit(solution)/shard_map/ppermute | solution.py:18
  61.7 8.7 %collective-permute-start.9 = (bf16[32,6272]{1,0:T(8,128)(2,1)S(1)}, bf16[32,6272]{1,0:T(8,128)(2,1)S(1)}, u32[]{:S(2)}, u32[]{:S(2)}) collective-permute-start(bf16[32,6272]{1,0:T(8,128)(2,1)S(1)} %pad_maximum_fusion.2), channel_id=1, source_target_pairs={{0,1},{1,0},{2,3},{3,2},{4,5},{5,4},{6,7},{7,6},{8,9},{9,8},{10,11... | collective-permute-start | bytes 1204232 | tf_op jit(solution)/shard_map/ppermute | solution.py:18
  62.3 7.3 %collective-permute-start.6 = (bf16[16,6272]{1,0:T(8,128)(2,1)S(1)}, bf16[16,6272]{1,0:T(8,128)(2,1)S(1)}, u32[]{:S(2)}, u32[]{:S(2)}) collective-permute-start(bf16[16,6272]{1,0:T(8,128)(2,1)S(1)} %collective-permute-done.5), channel_id=1, source_target_pairs={{0,2},{1,3},{2,0},{3,1},{4,6},{5,7},{6,4},{7,5},{8,10},{9,11},{10,... | collective-permute-start | bytes 602120 | tf_op jit(solution)/shard_map/ppermute | solution.py:18
  64.4 7.6 %copy-start.3 = (bf16[6144,336]{0,1:T(8,128)(2,1)S(1)}, bf16[6144,336]{0,1:T(8,128)(2,1)}, u32[]{:S(2)}) copy-start(bf16[6144,336]{0,1:T(8,128)(2,1)} %param.11) | copy-start | bytes 12386308
  69.5 1.7 %collective-permute-start.29 = (bf16[32,6144]{1,0:T(8,128)(2,1)S(1)}, bf16[32,6144]{1,0:T(8,128)(2,1)S(1)}, u32[]{:S(2)}, u32[]{:S(2)}) collective-permute-start(bf16[32,6144]{1,0:T(8,128)(2,1)S(1)} %pad_maximum_fusion.7), channel_id=1, source_target_pairs={{0,1},{1,0},{2,3},{3,2},{4,5},{5,4},{6,7},{7,6},{8,9},{9,8},{10,11... | collective-permute-start | bytes 1179656 | tf_op jit(solution)/shard_map/ppermute | solution.py:18
  69.6 2.2 %collective-permute-start.10 = (bf16[32,6272]{1,0:T(8,128)(2,1)S(1)}, bf16[32,6272]{1,0:T(8,128)(2,1)S(1)}, u32[]{:S(2)}, u32[]{:S(2)}) collective-permute-start(bf16[32,6272]{1,0:T(8,128)(2,1)S(1)} %pad_maximum_fusion.3), channel_id=1, source_target_pairs={{0,1},{1,0},{2,3},{3,2},{4,5},{5,4},{6,7},{7,6},{8,9},{9,8},{10,11... | collective-permute-start | bytes 1204232 | tf_op jit(solution)/shard_map/ppermute | solution.py:18
  72.0 2.2 %copy-start.4 = (bf16[6144,336]{0,1:T(8,128)(2,1)S(1)}, bf16[6144,336]{0,1:T(8,128)(2,1)}, u32[]{:S(2)}) copy-start(bf16[6144,336]{0,1:T(8,128)(2,1)} %param.12) | copy-start | bytes 12386308
  74.2 2.2 %copy-start.2 = (bf16[336,6144]{1,0:T(8,128)(2,1)S(1)}, bf16[336,6144]{1,0:T(8,128)(2,1)}, u32[]{:S(2)}) copy-start(bf16[336,6144]{1,0:T(8,128)(2,1)} %param.13) | copy-start | bytes 12386308
  79.9 14.5 %collective-permute-start.11 = (bf16[128,6144]{1,0:T(8,128)(2,1)S(1)}, bf16[128,6144]{1,0:T(8,128)(2,1)S(1)}, u32[]{:S(2)}, u32[]{:S(2)}) collective-permute-start(bf16[128,6144]{1,0:T(8,128)(2,1)S(1)} %slice.196), channel_id=1, source_target_pairs={{0,1},{1,0},{2,3},{3,2},{4,5},{5,4},{6,7},{7,6},{8,9},{9,8},{10,11... | collective-permute-start | bytes 4718600 | tf_op jit(solution)/shard_map/ppermute | solution.py:18
  84.0 15.1 %collective-permute-start.30 = (bf16[128,6144]{1,0:T(8,128)(2,1)S(1)}, bf16[128,6144]{1,0:T(8,128)(2,1)S(1)}, u32[]{:S(2)}, u32[]{:S(2)}) collective-permute-start(bf16[128,6144]{1,0:T(8,128)(2,1)S(1)} %slice.195), channel_id=1, source_target_pairs={{0,1},{1,0},{2,3},{3,2},{4,5},{5,4},{6,7},{7,6},{8,9},{9,8},{10,11... | collective-permute-start | bytes 4718600 | tf_op jit(solution)/shard_map/ppermute | solution.py:18
  95.0 7.8 %collective-permute-start.15 = (bf16[16,6144]{1,0:T(8,128)(2,1)S(1)}, bf16[16,6144]{1,0:T(8,128)(2,1)S(1)}, u32[]{:S(2)}, u32[]{:S(2)}) collective-permute-start(bf16[16,6144]{1,0:T(8,128)(2,1)S(1)} %get-tuple-element.12), channel_id=1, source_target_pairs={{0,2},{1,3},{2,0},{3,1},{4,6},{5,7},{6,4},{7,5},{8,10},{9,11},{10,... | collective-permute-start | bytes 589832 | tf_op jit(solution)/shard_map/ppermute | solution.py:18
  96.8 22.9 %collective-permute-start.14 = (bf16[16,6144]{1,0:T(8,128)(2,1)S(1)}, bf16[16,6144]{1,0:T(8,128)(2,1)S(1)}, u32[]{:S(2)}, u32[]{:S(2)}) collective-permute-start(bf16[16,6144]{1,0:T(8,128)(2,1)S(1)} %get-tuple-element.13), channel_id=1, source_target_pairs={{0,2},{1,3},{2,0},{3,1},{4,6},{5,7},{6,4},{7,5},{8,10},{9,11},{10,... | collective-permute-start | bytes 589832 | tf_op jit(solution)/shard_map/ppermute | solution.py:18
  97.1 37.6 %collective-permute-start.13 = (bf16[16,6144]{1,0:T(8,128)(2,1)S(1)}, bf16[16,6144]{1,0:T(8,128)(2,1)S(1)}, u32[]{:S(2)}, u32[]{:S(2)}) collective-permute-start(bf16[16,6144]{1,0:T(8,128)(2,1)S(1)} %get-tuple-element.14), channel_id=1, source_target_pairs={{0,2},{1,3},{2,0},{3,1},{4,6},{5,7},{6,4},{7,5},{8,10},{9,11},{10,... | collective-permute-start | bytes 589832 | tf_op jit(solution)/shard_map/ppermute | solution.py:18
  98.8 47.6 %collective-permute-start.12 = (bf16[16,6144]{1,0:T(8,128)(2,1)S(1)}, bf16[16,6144]{1,0:T(8,128)(2,1)S(1)}, u32[]{:S(2)}, u32[]{:S(2)}) collective-permute-start(bf16[16,6144]{1,0:T(8,128)(2,1)S(1)} %get-tuple-element.11), channel_id=1, source_target_pairs={{0,2},{1,3},{2,0},{3,1},{4,6},{5,7},{6,4},{7,5},{8,10},{9,11},{10,... | collective-permute-start | bytes 589832 | tf_op jit(solution)/shard_map/ppermute | solution.py:18
  99.7 19.9 %collective-permute-start.34 = (bf16[16,6144]{1,0:T(8,128)(2,1)S(1)}, bf16[16,6144]{1,0:T(8,128)(2,1)S(1)}, u32[]{:S(2)}, u32[]{:S(2)}) collective-permute-start(bf16[16,6144]{1,0:T(8,128)(2,1)S(1)} %get-tuple-element.8), channel_id=1, source_target_pairs={{0,2},{1,3},{2,0},{3,1},{4,6},{5,7},{6,4},{7,5},{8,10},{9,11},{10,... | collective-permute-start | bytes 589832 | tf_op jit(solution)/shard_map/ppermute | solution.py:18
  102.8 24.4 %collective-permute-start.33 = (bf16[16,6144]{1,0:T(8,128)(2,1)S(1)}, bf16[16,6144]{1,0:T(8,128)(2,1)S(1)}, u32[]{:S(2)}, u32[]{:S(2)}) collective-permute-start(bf16[16,6144]{1,0:T(8,128)(2,1)S(1)} %get-tuple-element.9), channel_id=1, source_target_pairs={{0,2},{1,3},{2,0},{3,1},{4,6},{5,7},{6,4},{7,5},{8,10},{9,11},{10,... | collective-permute-start | bytes 589832 | tf_op jit(solution)/shard_map/ppermute | solution.py:18
  119.7 5.7 %collective-permute-start.16 = (bf16[16,6144]{1,0:T(8,128)(2,1)S(1)}, bf16[16,6144]{1,0:T(8,128)(2,1)S(1)}, u32[]{:S(2)}, u32[]{:S(2)}) collective-permute-start(bf16[16,6144]{1,0:T(8,128)(2,1)S(1)} %fusion.21), channel_id=1, source_target_pairs={{4,0},{5,1},{6,2},{7,3},{8,4},{9,5},{10,6},{11,7},{12,8},{13,9},{1... | collective-permute-start | bytes 589832 | tf_op jit(solution)/shard_map/ppermute | solution.py:18
  119.7 22.5 %collective-permute-start.32 = (bf16[16,6144]{1,0:T(8,128)(2,1)S(1)}, bf16[16,6144]{1,0:T(8,128)(2,1)S(1)}, u32[]{:S(2)}, u32[]{:S(2)}) collective-permute-start(bf16[16,6144]{1,0:T(8,128)(2,1)S(1)} %get-tuple-element.10), channel_id=1, source_target_pairs={{0,2},{1,3},{2,0},{3,1},{4,6},{5,7},{6,4},{7,5},{8,10},{9,11},{10,... | collective-permute-start | bytes 589832 | tf_op jit(solution)/shard_map/ppermute | solution.py:18
  125.3 6.5 %collective-permute-start.35 = (bf16[16,6144]{1,0:T(8,128)(2,1)S(1)}, bf16[16,6144]{1,0:T(8,128)(2,1)S(1)}, u32[]{:S(2)}, u32[]{:S(2)}) collective-permute-start(bf16[16,6144]{1,0:T(8,128)(2,1)S(1)} %fusion.10), channel_id=1, source_target_pairs={{4,0},{5,1},{6,2},{7,3},{8,4},{9,5},{10,6},{11,7},{12,8},{13,9},{1... | collective-permute-start | bytes 589832 | tf_op jit(solution)/shard_map/ppermute | solution.py:18
  127.2 21.0 %collective-permute-start.31 = (bf16[16,6144]{1,0:T(8,128)(2,1)S(1)}, bf16[16,6144]{1,0:T(8,128)(2,1)S(1)}, u32[]{:S(2)}, u32[]{:S(2)}) collective-permute-start(bf16[16,6144]{1,0:T(8,128)(2,1)S(1)} %get-tuple-element.7), channel_id=1, source_target_pairs={{0,2},{1,3},{2,0},{3,1},{4,6},{5,7},{6,4},{7,5},{8,10},{9,11},{10,... | collective-permute-start | bytes 589832 | tf_op jit(solution)/shard_map/ppermute | solution.py:18
  131.9 7.5 %collective-permute-start.17 = (bf16[16,6144]{1,0:T(8,128)(2,1)S(1)}, bf16[16,6144]{1,0:T(8,128)(2,1)S(1)}, u32[]{:S(2)}, u32[]{:S(2)}) collective-permute-start(bf16[16,6144]{1,0:T(8,128)(2,1)S(1)} %fusion.24), channel_id=1, source_target_pairs={{4,0},{5,1},{6,2},{7,3},{8,4},{9,5},{10,6},{11,7},{12,8},{13,9},{1... | collective-permute-start | bytes 589832 | tf_op jit(solution)/shard_map/ppermute | solution.py:18
  134.6 16.8 %copy-start.1 = (bf16[128,6144]{1,0:T(8,128)(2,1)S(1)}, bf16[128,6144]{1,0:T(8,128)(2,1)}, u32[]{:S(2)}) copy-start(bf16[128,6144]{1,0:T(8,128)(2,1)} %param.8) | copy-start | bytes 4718596
  134.7 8.9 %collective-permute-start.36 = (bf16[16,6144]{1,0:T(8,128)(2,1)S(1)}, bf16[16,6144]{1,0:T(8,128)(2,1)S(1)}, u32[]{:S(2)}, u32[]{:S(2)}) collective-permute-start(bf16[16,6144]{1,0:T(8,128)(2,1)S(1)} %fusion.13), channel_id=1, source_target_pairs={{4,0},{5,1},{6,2},{7,3},{8,4},{9,5},{10,6},{11,7},{12,8},{13,9},{1... | collective-permute-start | bytes 589832 | tf_op jit(solution)/shard_map/ppermute | solution.py:18
  139.5 7.0 %collective-permute-start.18 = (bf16[16,6144]{1,0:T(8,128)(2,1)S(1)}, bf16[16,6144]{1,0:T(8,128)(2,1)S(1)}, u32[]{:S(2)}, u32[]{:S(2)}) collective-permute-start(bf16[16,6144]{1,0:T(8,128)(2,1)S(1)} %fusion.27), channel_id=1, source_target_pairs={{4,0},{5,1},{6,2},{7,3},{8,4},{9,5},{10,6},{11,7},{12,8},{13,9},{1... | collective-permute-start | bytes 589832 | tf_op jit(solution)/shard_map/ppermute | solution.py:18
  143.7 6.0 %collective-permute-start.37 = (bf16[16,6144]{1,0:T(8,128)(2,1)S(1)}, bf16[16,6144]{1,0:T(8,128)(2,1)S(1)}, u32[]{:S(2)}, u32[]{:S(2)}) collective-permute-start(bf16[16,6144]{1,0:T(8,128)(2,1)S(1)} %fusion.16), channel_id=1, source_target_pairs={{4,0},{5,1},{6,2},{7,3},{8,4},{9,5},{10,6},{11,7},{12,8},{13,9},{1... | collective-permute-start | bytes 589832 | tf_op jit(solution)/shard_map/ppermute | solution.py:18

commit v2 on v1

v2 whole, which is shorter than its diff:
```python
import jax
import jax.numpy as jnp
from jax import lax
from jax.sharding import PartitionSpec as P

CAP = 16
LANES = 128


def ring_of(n):
    chips = n // 2
    order = list(range(0, chips, 2)) + list(range(chips - 1, 0, -2))
    right = []
    for at, chip in enumerate(order):
        nxt = order[(at + 1) % chips]
        right += [(2 * chip + core, 2 * nxt + core) for core in (0, 1)]
    return right, [(b, a) for a, b in right]


def make_per_device(n):
    steps = n // 4
    core_pairs = [(i, i ^ 1) for i in range(n)]
    right_pairs, left_pairs = ring_of(n)

    def permute(x, pairs):
        return lax.ppermute(x, "et", pairs)

    def gather_rows(x, dy):
        held_xr = held_xl = x
        held_dr = held_dl = dy
        got_x, got_d = [x], [dy]
        split = 1
        for k in range(1, steps + 1):
            if k == steps - 1:
                split = len(got_x)
                early_x = permute(jnp.concatenate(got_x, axis=0), core_pairs)
                early_d = permute(jnp.concatenate(got_d, axis=0), core_pairs)
            if k == steps:
                held_xr, early_x = lax.optimization_barrier((held_xr, early_x))
                held_dl, early_d = lax.optimization_barrier((held_dl, early_d))
                got_x.append(permute(held_xr, right_pairs))
                got_d.append(permute(held_dl, left_pairs))
            else:
                held_xr = permute(held_xr, right_pairs)
                held_xl = permute(held_xl, left_pairs)
                held_dr = permute(held_dr, right_pairs)
                held_dl = permute(held_dl, left_pairs)
                got_x += [held_xr, held_xl]
                got_d += [held_dr, held_dl]
        late_x = permute(jnp.concatenate(got_x[split:], axis=0), core_pairs)
        late_d = permute(jnp.concatenate(got_d[split:], axis=0), core_pairs)
        return (
            jnp.concatenate(got_x + [early_x, late_x], axis=0),
            jnp.concatenate(got_d + [early_d, late_d], axis=0),
        )

    def pair_sum(own, sent):
        total = own + permute(sent, core_pairs).astype(jnp.float32)
        return total.reshape(2 * steps, CAP, own.shape[1])

    def blocks_at(total, carry, k, far_left):
        blocks = {}
        for way in ("l", "r"):
            if k == steps:
                if (way == "l") != far_left:
                    continue
                block = total[2 * steps - 1]
            else:
                block = total[2 * k - 1 if way == "l" else 2 * k]
            if way in carry:
                block = block + carry[way].astype(jnp.float32)
            blocks[way] = block.astype(jnp.bfloat16)
        return blocks

    def send(blocks):
        return {w: permute(b, left_pairs if w == "l" else right_pairs) for w, b in blocks.items()}

    def final(total, carry):
        done = total[0] + carry["l"].astype(jnp.float32) + carry["r"].astype(jnp.float32)
        return done.astype(jnp.bfloat16)

    def after(value, *marks):
        return lax.optimization_barrier((value,) + marks)[0]

    def per_device(tokens, out_grad, expert_ids, gate_vals, w_gate, w_up, w_down):
        d = tokens.shape[1]
        landed = expert_ids == 0
        coef = jnp.sum(jnp.where(landed, gate_vals.astype(jnp.float32), 0.0), axis=1).astype(
            jnp.bfloat16
        )
        routed = jnp.any(landed, axis=1)
        slot = jnp.cumsum(routed.astype(jnp.int32)) - 1
        select = (slot[None, :] == jnp.arange(CAP, dtype=jnp.int32)[:, None]) & routed[None, :]
        select_bf = select.astype(jnp.bfloat16)
        wide = jnp.concatenate(
            [tokens, jnp.broadcast_to(coef[:, None], (coef.shape[0], LANES))], axis=1
        )
        slot_x = jnp.dot(select_bf, wide, preferred_element_type=jnp.float32).astype(jnp.bfloat16)
        slot_dy = jnp.dot(select_bf, out_grad, preferred_element_type=jnp.float32).astype(
            jnp.bfloat16
        )
        rows_wide, rows_dy = gather_rows(slot_x, slot_dy)
        rows_x = rows_wide[:, :d]
        coef_rows = rows_wide[:, d : d + 1].astype(jnp.float32)
        half = rows_dy.shape[0] // 2

        gate = jnp.dot(rows_x, w_gate, preferred_element_type=jnp.float32)
        up = jnp.dot(rows_x, w_up, preferred_element_type=jnp.float32)
        sig = jax.nn.sigmoid(gate)
        act = gate * sig
        hidden = (coef_rows * act * up).astype(jnp.bfloat16)
        out_rows = jnp.dot(hidden, w_down, preferred_element_type=jnp.float32)
        out_total = pair_sum(out_rows[:half], out_rows[half:].astype(jnp.bfloat16))

        scaled = coef_rows * jnp.dot(rows_dy, w_down.T, preferred_element_type=jnp.float32)
        dgate = (scaled * up * sig * (1.0 + gate * (1.0 - sig))).astype(jnp.bfloat16)
        dup = (scaled * act).astype(jnp.bfloat16)
        dgate, out_total = lax.optimization_barrier((dgate, out_total))
        out_blocks = blocks_at(out_total, {}, steps, True)
        out_carry = send(out_blocks)
        dx_rows = jnp.dot(dgate, w_gate.T, preferred_element_type=jnp.float32) + jnp.dot(
            dup, w_up.T, preferred_element_type=jnp.float32
        )
        dx_total = pair_sum(dx_rows[:half], dx_rows[half:].astype(jnp.bfloat16))
        dx_carry = send(blocks_at(dx_total, {}, steps, False))

        grads = []
        work = [(rows_x, dgate), (rows_x, dup), (hidden, rows_dy)]
        for k in range(steps - 1, 0, -1):
            out_blocks = blocks_at(out_total, out_carry, k, True)
            out_carry = send(out_blocks)
            if work:
                lhs, rhs = work.pop(0)
                marks = list(out_blocks.values())
                if len(grads) == 2:
                    lhs = after(lhs, *marks)
                else:
                    rhs = after(rhs, *marks)
                grads.append(jnp.dot(lhs.T, rhs, preferred_element_type=jnp.float32))
            dx_carry = send(blocks_at(dx_total, dx_carry, k, False))
        for lhs, rhs in work:
            grads.append(jnp.dot(lhs.T, rhs, preferred_element_type=jnp.float32))
        grad_gate, grad_up, grad_down = grads
        out_slots = final(out_total, out_carry)
        dx_slots = final(dx_total, dx_carry)
        mixed = jnp.dot(select_bf.T, out_slots, preferred_element_type=jnp.float32)
        grad_tokens = jnp.dot(select_bf.T, dx_slots, preferred_element_type=jnp.float32)
        return (
            mixed.astype(jnp.bfloat16),
            grad_tokens.astype(jnp.bfloat16),
            grad_gate.astype(jnp.bfloat16),
            grad_up.astype(jnp.bfloat16),
            grad_down.astype(jnp.bfloat16),
        )

    return per_device


def solution(mesh):
    placed = (
        P(("groups", "et"), None),
        P(("groups", "et"), None),
        P(("groups", "et"), None),
        P(("groups", "et"), None),
        P(None, "et"),
        P(None, "et"),
        P("et", None),
    )
    return jax.shard_map(
        make_per_device(mesh.shape["et"]),
        mesh=mesh,
        in_specs=placed,
        out_specs=(
            P(("groups", "et"), None),
            P(("groups", "et"), None),
            P("groups", "et"),
            P("groups", "et"),
            P(("groups", "et"), None),
        ),
        check_vma=False,
    )
```

time: 152 us -> 109 us (0.72)
  waiting for transfers between devices: 78.7 us -> 47.5 us
  starting transfers between devices: 39.8 us -> 29.1 us
    ppermute x38 -> x34, waiting for transfers between devices: 78.7 us -> 47.5 us  [permute(): return lax.ppermute(x, 'et', pairs)]
    ppermute x38 -> x34, starting transfers between devices: 39.8 us -> 29.1 us  [permute(): return lax.ppermute(x, 'et', pairs)]
  transfers between devices with their start and end apart: 38 -> 34, of which waited for: 19 -> 23; matrix products, arithmetic and copies ran while one was open for 13% -> 18% of each run, Pallas kernels for 0% -> 0%
where the time goes in v2:
time: 109 us
  waiting for transfers between devices  47.5 us (44%)
  starting transfers between devices  29.1 us (27%)
  matrix products  24.8 us (23%)
  other arithmetic  3.33 us (3%)
  local copies, waits for them, and re-layouts  3.27 us (3%)
    ppermute x34, waiting for transfers between devices, permute(): return lax.ppermute(x, 'et', pairs)  47.5 us
    ppermute x34, starting transfers between devices, permute(): return lax.ppermute(x, 'et', pairs)  29.1 us
    dot_general x3, matrix products, per_device(): grads.append(jnp.dot(lhs.T, rhs, preferred_element_type=jnp.float32))  9.71 us
    unnamed x24, local copies, waits for them, and re-layouts  2.49 us
  transfers between devices with their start and end apart: 34, of which 23 were waited for; matrix products, arithmetic and copies ran while one was open for 18% of the time, Pallas kernels for 0%

profile of v2, /device:TPU:0, one launch (start us, length us, event | category | flops | bytes accessed | tf_op | source)
XLA Modules:
  0.0 108.9 jit_solution(2435752554460720420)
XLA Ops:
  0.6 0.8 fusion.41
  2.1 0.3 constant_dynamic-update-slice_fusion.19
  2.4 3.1 %collective-permute-start.9 = (bf16[16,6144]{1,0:T(8,128)(2,1)S(1)}, bf16[16,6144]{1,0:T(8,128)(2,1)S(1)}, u32[]{:S(2)}, u32[]{:S(2)}) collective-permute-start(bf16[16,6144]{1,0:T(8,128)(2,1)S(1)} %get-tuple-element.60), channel_id=1, source_target_pairs={{0,4},{1,5},{4,8},{5,9},{8,12},{9,13},{12,14},{13,15},{14,10},{15,... | collective-permute-start | bytes 589832 | tf_op jit(solution)/shard_map/ppermute | solution.py:26
  5.5 0.7 select_reduce_fusion
  6.3 1.7 %constant_dynamic-update-slice_fusion.4 = (bf16[80,6272]{1,0:T(8,128)(2,1)S(1)}, bf16[256,6272]{1,0:T(8,128)(2,1)S(1)}, bf16[16,6272]{1,0:T(8,128)(2,1)S(1)}) fusion(bf16[128,128]{1,0:T(8,128)(2,1)S(1)} %broadcast_in_dim.7, bf16[128,6144]{1,0:T(8,128)(2,1)} %param.7, s32[128]{0:T(128)S(1)} %add_reduce_fusion, pred[128]{0:T(512)(128)(4,1)S(1)} %get-tuple-element.25), kind=kOutput, calls=%fused_computation.63 | convolution fusion | flops 29005824 | bytes 2208384 | tf_op jit(solution)/shard_map/dot_general | solution.py:98
  8.0 2.1 %collective-permute-start = (bf16[16,6272]{1,0:T(8,128)(2,1)S(1)}, bf16[16,6272]{1,0:T(8,128)(2,1)S(1)}, u32[]{:S(2)}, u32[]{:S(2)}) collective-permute-start(bf16[16,6272]{1,0:T(8,128)(2,1)S(1)} %get-tuple-element.61), channel_id=1, source_target_pairs={{0,4},{1,5},{4,8},{5,9},{8,12},{9,13},{12,14},{13,15},{14,10},{15,... | collective-permute-start | bytes 602120 | tf_op jit(solution)/shard_map/ppermute | solution.py:26
  10.1 0.3 collective-permute-done.9
  10.3 1.9 %collective-permute-start.11 = (bf16[16,6144]{1,0:T(8,128)(2,1)S(1)}, bf16[16,6144]{1,0:T(8,128)(2,1)S(1)}, u32[]{:S(2)}, u32[]{:S(2)}) collective-permute-start(bf16[16,6144]{1,0:T(8,128)(2,1)S(1)} %collective-permute-done.9), channel_id=1, source_target_pairs={{0,4},{1,5},{4,8},{5,9},{8,12},{9,13},{12,14},{13,15},{14,10},{15,... | collective-permute-start | bytes 589832 | tf_op jit(solution)/shard_map/ppermute | solution.py:26
  12.4 3.5 %collective-permute-done = bf16[16,6272]{1,0:T(8,128)(2,1)S(1)} collective-permute-done((bf16[16,6272]{1,0:T(8,128)(2,1)S(1)}, bf16[16,6272]{1,0:T(8,128)(2,1)S(1)}, u32[]{:S(2)}, u32[]{:S(2)}) %collective-permute-start) | collective-permute-done | bytes 200736 | tf_op jit(solution)/shard_map/ppermute | solution.py:26
  16.0 2.0 %collective-permute-start.2 = (bf16[16,6272]{1,0:T(8,128)(2,1)S(1)}, bf16[16,6272]{1,0:T(8,128)(2,1)S(1)}, u32[]{:S(2)}, u32[]{:S(2)}) collective-permute-start(bf16[16,6272]{1,0:T(8,128)(2,1)S(1)} %collective-permute-done), channel_id=1, source_target_pairs={{0,4},{1,5},{4,8},{5,9},{8,12},{9,13},{12,14},{13,15},{14,10},{15,... | collective-permute-start | bytes 602120 | tf_op jit(solution)/shard_map/ppermute | solution.py:26
  18.1 2.1 %collective-permute-done.11 = bf16[16,6144]{1,0:T(8,128)(2,1)S(1)} collective-permute-done((bf16[16,6144]{1,0:T(8,128)(2,1)S(1)}, bf16[16,6144]{1,0:T(8,128)(2,1)S(1)}, u32[]{:S(2)}, u32[]{:S(2)}) %collective-permute-start.11) | collective-permute-done | bytes 196640 | tf_op jit(solution)/shard_map/ppermute | solution.py:26
  20.2 2.0 %collective-permute-done.12 = bf16[16,6144]{1,0:T(8,128)(2,1)S(1)} collective-permute-done((bf16[16,6144]{1,0:T(8,128)(2,1)S(1)}, bf16[16,6144]{1,0:T(8,128)(2,1)S(1)}, u32[]{:S(2)}, u32[]{:S(2)}) %collective-permute-start.12) | collective-permute-done | bytes 196640 | tf_op jit(solution)/shard_map/ppermute | solution.py:26
  22.3 1.6 %collective-permute-start.13 = (bf16[16,6144]{1,0:T(8,128)(2,1)S(1)}, bf16[16,6144]{1,0:T(8,128)(2,1)S(1)}, u32[]{:S(2)}, u32[]{:S(2)}) collective-permute-start(bf16[16,6144]{1,0:T(8,128)(2,1)S(1)} %collective-permute-done.11), channel_id=1, source_target_pairs={{0,4},{1,5},{4,8},{5,9},{8,12},{9,13},{12,14},{13,15},{14,10},{15,... | collective-permute-start | bytes 589832 | tf_op jit(solution)/shard_map/ppermute | solution.py:26
  23.9 0.4 collective-permute-start.14
  24.7 1.6 %collective-permute-start.4 = (bf16[16,6272]{1,0:T(8,128)(2,1)S(1)}, bf16[16,6272]{1,0:T(8,128)(2,1)S(1)}, u32[]{:S(2)}, u32[]{:S(2)}) collective-permute-start(bf16[16,6272]{1,0:T(8,128)(2,1)S(1)} %collective-permute-done.2), channel_id=1, source_target_pairs={{0,4},{1,5},{4,8},{5,9},{8,12},{9,13},{12,14},{13,15},{14,10},{15,... | collective-permute-start | bytes 602120 | tf_op jit(solution)/shard_map/ppermute | solution.py:26
  26.4 3.7 %collective-permute-done.13 = bf16[16,6144]{1,0:T(8,128)(2,1)S(1)} collective-permute-done((bf16[16,6144]{1,0:T(8,128)(2,1)S(1)}, bf16[16,6144]{1,0:T(8,128)(2,1)S(1)}, u32[]{:S(2)}, u32[]{:S(2)}) %collective-permute-start.13) | collective-permute-done | bytes 196640 | tf_op jit(solution)/shard_map/ppermute | solution.py:26
  30.2 0.7 collective-permute-done.14
  30.9 3.0 %collective-permute-done.4 = bf16[16,6272]{1,0:T(8,128)(2,1)S(1)} collective-permute-done((bf16[16,6272]{1,0:T(8,128)(2,1)S(1)}, bf16[16,6272]{1,0:T(8,128)(2,1)S(1)}, u32[]{:S(2)}, u32[]{:S(2)}) %collective-permute-start.4) | collective-permute-done | bytes 200736 | tf_op jit(solution)/shard_map/ppermute | solution.py:26
  33.9 0.3 collective-permute-start.16
  34.2 1.9 %collective-permute-done.5 = bf16[16,6272]{1,0:T(8,128)(2,1)S(1)} collective-permute-done((bf16[16,6272]{1,0:T(8,128)(2,1)S(1)}, bf16[16,6272]{1,0:T(8,128)(2,1)S(1)}, u32[]{:S(2)}, u32[]{:S(2)}) %collective-permute-start.5) | collective-permute-done | bytes 200736 | tf_op jit(solution)/shard_map/ppermute | solution.py:26
  36.2 1.6 %collective-permute-start.7 = (bf16[16,6272]{1,0:T(8,128)(2,1)S(1)}, bf16[16,6272]{1,0:T(8,128)(2,1)S(1)}, u32[]{:S(2)}, u32[]{:S(2)}) collective-permute-start(bf16[16,6272]{1,0:T(8,128)(2,1)S(1)} %collective-permute-done.4), channel_id=1, source_target_pairs={{0,4},{1,5},{4,8},{5,9},{8,12},{9,13},{12,14},{13,15},{14,10},{15,... | collective-permute-start | bytes 602120 | tf_op jit(solution)/shard_map/ppermute | solution.py:26
  37.8 2.6 %collective-permute-done.16 = bf16[16,6144]{1,0:T(8,128)(2,1)S(1)} collective-permute-done((bf16[16,6144]{1,0:T(8,128)(2,1)S(1)}, bf16[16,6144]{1,0:T(8,128)(2,1)S(1)}, u32[]{:S(2)}, u32[]{:S(2)}) %collective-permute-start.16) | collective-permute-done | bytes 196640 | tf_op jit(solution)/shard_map/ppermute | solution.py:26
  40.7 1.3 %collective-permute-done.7 = bf16[16,6272]{1,0:T(8,128)(2,1)S(1)} collective-permute-done((bf16[16,6272]{1,0:T(8,128)(2,1)S(1)}, bf16[16,6272]{1,0:T(8,128)(2,1)S(1)}, u32[]{:S(2)}, u32[]{:S(2)}) %collective-permute-start.7) | collective-permute-done | bytes 200736 | tf_op jit(solution)/shard_map/ppermute | solution.py:26
  42.3 0.3 collective-permute-done.17
  42.6 1.5 %collective-permute-done.8 = bf16[48,6272]{1,0:T(8,128)(2,1)S(1)} collective-permute-done((bf16[48,6272]{1,0:T(8,128)(2,1)S(1)}, bf16[48,6272]{1,0:T(8,128)(2,1)S(1)}, u32[]{:S(2)}, u32[]{:S(2)}) %collective-permute-start.8) | collective-permute-done | bytes 602144 | tf_op jit(solution)/shard_map/ppermute | solution.py:26
  44.3 1.3 %fusion.2 = f32[256,336]{0,1:T(8,128)S(1)} fusion(bf16[6144,336]{0,1:T(8,128)(2,1)S(1)} %copy-done.3, bf16[256,6272]{1,0:T(8,128)(2,1)S(1)} %constant_dynamic-update-slice_fusion.5), kind=kOutput, calls=%fused_computation.14 | convolution fusion | flops 1056964608 | bytes 7618560 | tf_op jit(solution)/shard_map/dot_general | solution.py:107
  45.6 0.9 copy-done.4
  46.5 1.3 %fusion.4 = f32[256,336]{0,1:T(8,128)S(1)} fusion(bf16[6144,336]{0,1:T(8,128)(2,1)S(1)} %copy-done.4, bf16[256,6272]{1,0:T(8,128)(2,1)S(1)} %constant_dynamic-update-slice_fusion.5), kind=kOutput, calls=%fused_computation.16 | convolution fusion | flops 1056964608 | bytes 7618560 | tf_op jit(solution)/shard_map/dot_general | solution.py:108
  47.7 0.9 copy-done.2
  48.6 1.5 %multiply_convert_fusion = (bf16[256,336]{0,1:T(8,128)(2,1)S(1)}, bf16[256,336]{0,1:T(8,128)(2,1)S(1)}, bf16[256,336]{0,1:T(8,128)(2,1)S(1)}) fusion(f32[256,336]{0,1:T(8,128)S(1)} %fusion.2, f32[256,336]{0,1:T(8,128)S(1)} %fusion.4, f32[256]{0:T(256)S(1)} %convert_reduce_fusion, bf16[256,6144]{1,0:T(8,128)(2,1)S(1)} %constant_dynamic-update-slice_fusion.20, ...), kind=kOutput, calls=%fused_computation.50 | convolution fusion | flops 1058426880 | bytes 8479744 | tf_op jit(solution)/shard_map/dot_general | solution.py:115
  50.2 1.8 %fusion.43 = f32[256,6144]{1,0:T(8,128)S(1)} fusion(bf16[256,336]{0,1:T(8,128)(2,1)S(1)} %get-tuple-element.22, bf16[336,6144]{1,0:T(8,128)(2,1)S(1)} %copy-done.2), kind=kOutput, calls=%fused_computation.106 | convolution fusion | flops 1056964608 | bytes 10592256 | tf_op jit(solution)/shard_map/dot_general | solution.py:112
  52.2 0.2 collective-permute-start.18
  52.4 3.3 %collective-permute-done.18 = bf16[128,6144]{1,0:T(8,128)(2,1)S(1)} collective-permute-done((bf16[128,6144]{1,0:T(8,128)(2,1)S(1)}, bf16[128,6144]{1,0:T(8,128)(2,1)S(1)}, u32[]{:S(2)}, u32[]{:S(2)}) %collective-permute-start.18) | collective-permute-done | bytes 1572896 | tf_op jit(solution)/shard_map/ppermute | solution.py:26
  55.7 0.3 slice_add_fusion.1
  56.2 0.4 collective-permute-start.19
  56.6 1.7 %collective-permute-start.23 = (bf16[16,6144]{1,0:T(8,128)(2,1)S(1)}, bf16[16,6144]{1,0:T(8,128)(2,1)S(1)}, u32[]{:S(2)}, u32[]{:S(2)}) collective-permute-start(bf16[16,6144]{1,0:T(8,128)(2,1)S(1)} %get-tuple-element.36), channel_id=1, source_target_pairs={{0,4},{1,5},{4,8},{5,9},{8,12},{9,13},{12,14},{13,15},{14,10},{15,... | collective-permute-start | bytes 589832 | tf_op jit(solution)/shard_map/ppermute | solution.py:26
  58.3 1.8 %fusion.44 = f32[256,6144]{1,0:T(8,128)S(1)} fusion(bf16[256,336]{0,1:T(8,128)(2,1)S(1)} %get-tuple-element.20, bf16[6144,336]{0,1:T(8,128)(2,1)S(1)} %copy-done.3), kind=kOutput, calls=%fused_computation.107 | convolution fusion | flops 1056964608 | bytes 10592256 | tf_op jit(solution)/shard_map/dot_general | solution.py:121
  60.1 3.1 %collective-permute-done.19 = bf16[16,6144]{1,0:T(8,128)(2,1)S(1)} collective-permute-done((bf16[16,6144]{1,0:T(8,128)(2,1)S(1)}, bf16[16,6144]{1,0:T(8,128)(2,1)S(1)}, u32[]{:S(2)}, u32[]{:S(2)}) %collective-permute-start.19) | collective-permute-done | bytes 196640 | tf_op jit(solution)/shard_map/ppermute | solution.py:26
  63.2 0.6 collective-permute-start.20
  63.8 1.8 %convolution_add_fusion = f32[256,6144]{1,0:T(8,128)S(1)} fusion(f32[256,6144]{1,0:T(8,128)S(1)} %fusion.44, bf16[256,336]{0,1:T(8,128)(2,1)S(1)} %get-tuple-element.21, bf16[6144,336]{0,1:T(8,128)(2,1)S(1)} %copy-done.4), kind=kOutput, calls=%fused_computation | convolution fusion | flops 1058537472 | bytes 16883712 | tf_op jit(solution)/shard_map/dot_general | solution.py:121
  65.9 3.7 %collective-permute-done.20 = bf16[16,6144]{1,0:T(8,128)(2,1)S(1)} collective-permute-done((bf16[16,6144]{1,0:T(8,128)(2,1)S(1)}, bf16[16,6144]{1,0:T(8,128)(2,1)S(1)}, u32[]{:S(2)}, u32[]{:S(2)}) %collective-permute-start.20) | collective-permute-done | bytes 196640 | tf_op jit(solution)/shard_map/ppermute | solution.py:26
  69.7 0.4 collective-permute-start.21
  70.1 3.3 %convolution_convert_fusion.1 = bf16[6144,336]{0,1:T(8,128)(2,1)} fusion(bf16[256,336]{0,1:T(8,128)(2,1)S(1)} %get-tuple-element.20, bf16[256,6272]{1,0:T(8,128)(2,1)S(1)} %constant_dynamic-update-slice_fusion.5), kind=kOutput, calls=%fused_computation.2 | convolution fusion | flops 1059028992 | bytes 7446528 | tf_op jit(solution)/shard_map/dot_general | solution.py:139
  73.3 2.1 %collective-permute-done.21 = bf16[16,6144]{1,0:T(8,128)(2,1)S(1)} collective-permute-done((bf16[16,6144]{1,0:T(8,128)(2,1)S(1)}, bf16[16,6144]{1,0:T(8,128)(2,1)S(1)}, u32[]{:S(2)}, u32[]{:S(2)}) %collective-permute-start.21) | collective-permute-done | bytes 196640 | tf_op jit(solution)/shard_map/ppermute | solution.py:26
  75.5 1.6 %collective-permute-start.24 = (bf16[16,6144]{1,0:T(8,128)(2,1)S(1)}, bf16[16,6144]{1,0:T(8,128)(2,1)S(1)}, u32[]{:S(2)}, u32[]{:S(2)}) collective-permute-start(bf16[16,6144]{1,0:T(8,128)(2,1)S(1)} %get-tuple-element.32), channel_id=1, source_target_pairs={{0,4},{1,5},{4,8},{5,9},{8,12},{9,13},{12,14},{13,15},{14,10},{15,... | collective-permute-start | bytes 589832 | tf_op jit(solution)/shard_map/ppermute | solution.py:26
  77.1 0.5 collective-permute-start.22
  77.5 0.5 fusion.40
  78.1 0.4 collective-permute-start.27
  78.5 1.7 %collective-permute-start.30 = (bf16[16,6144]{1,0:T(8,128)(2,1)S(1)}, bf16[16,6144]{1,0:T(8,128)(2,1)S(1)}, u32[]{:S(2)}, u32[]{:S(2)}) collective-permute-start(bf16[16,6144]{1,0:T(8,128)(2,1)S(1)} %get-tuple-element.34), channel_id=1, source_target_pairs={{0,4},{1,5},{4,8},{5,9},{8,12},{9,13},{12,14},{13,15},{14,10},{15,... | collective-permute-start | bytes 589832 | tf_op jit(solution)/shard_map/ppermute | solution.py:26
  80.1 3.2 %convolution_convert_fusion = bf16[6144,336]{0,1:T(8,128)(2,1)} fusion(bf16[256,336]{0,1:T(8,128)(2,1)S(1)} %get-tuple-element.21, bf16[256,6272]{1,0:T(8,128)(2,1)S(1)} %constant_dynamic-update-slice_fusion.5), kind=kOutput, calls=%fused_computation.1 | convolution fusion | flops 1059028992 | bytes 7446528 | tf_op jit(solution)/shard_map/dot_general | solution.py:139
  83.4 2.9 %collective-permute-done.27 = bf16[16,6144]{1,0:T(8,128)(2,1)S(1)} collective-permute-done((bf16[16,6144]{1,0:T(8,128)(2,1)S(1)}, bf16[16,6144]{1,0:T(8,128)(2,1)S(1)}, u32[]{:S(2)}, u32[]{:S(2)}) %collective-permute-start.27) | collective-permute-done | bytes 196640 | tf_op jit(solution)/shard_map/ppermute | solution.py:26
  86.4 2.0 %collective-permute-start.31 = (bf16[16,6144]{1,0:T(8,128)(2,1)S(1)}, bf16[16,6144]{1,0:T(8,128)(2,1)S(1)}, u32[]{:S(2)}, u32[]{:S(2)}) collective-permute-start(bf16[16,6144]{1,0:T(8,128)(2,1)S(1)} %get-tuple-element.30), channel_id=1, source_target_pairs={{0,4},{1,5},{4,8},{5,9},{8,12},{9,13},{12,14},{13,15},{14,10},{15,... | collective-permute-start | bytes 589832 | tf_op jit(solution)/shard_map/ppermute | solution.py:26
  88.4 1.6 %collective-permute-start.25 = (bf16[16,6144]{1,0:T(8,128)(2,1)S(1)}, bf16[16,6144]{1,0:T(8,128)(2,1)S(1)}, u32[]{:S(2)}, u32[]{:S(2)}) collective-permute-start(bf16[16,6144]{1,0:T(8,128)(2,1)S(1)} %fusion.17), channel_id=1, source_target_pairs={{0,4},{1,5},{4,8},{5,9},{8,12},{9,13},{12,14},{13,15},{14,10},{15,... | collective-permute-start | bytes 589832 | tf_op jit(solution)/shard_map/ppermute | solution.py:26
  90.1 2.0 %collective-permute-done.28 = bf16[16,6144]{1,0:T(8,128)(2,1)S(1)} collective-permute-done((bf16[16,6144]{1,0:T(8,128)(2,1)S(1)}, bf16[16,6144]{1,0:T(8,128)(2,1)S(1)}, u32[]{:S(2)}, u32[]{:S(2)}) %collective-permute-start.28) | collective-permute-done | bytes 196640 | tf_op jit(solution)/shard_map/ppermute | solution.py:26
  92.0 2.0 %collective-permute-done.31 = bf16[16,6144]{1,0:T(8,128)(2,1)S(1)} collective-permute-done((bf16[16,6144]{1,0:T(8,128)(2,1)S(1)}, bf16[16,6144]{1,0:T(8,128)(2,1)S(1)}, u32[]{:S(2)}, u32[]{:S(2)}) %collective-permute-start.31) | collective-permute-done | bytes 196640 | tf_op jit(solution)/shard_map/ppermute | solution.py:26
  94.1 1.5 %collective-permute-start.32 = (bf16[16,6144]{1,0:T(8,128)(2,1)S(1)}, bf16[16,6144]{1,0:T(8,128)(2,1)S(1)}, u32[]{:S(2)}, u32[]{:S(2)}) collective-permute-start(bf16[16,6144]{1,0:T(8,128)(2,1)S(1)} %get-tuple-element.28), channel_id=1, source_target_pairs={{0,4},{1,5},{4,8},{5,9},{8,12},{9,13},{12,14},{13,15},{14,10},{15,... | collective-permute-start | bytes 589832 | tf_op jit(solution)/shard_map/ppermute | solution.py:26
  95.6 3.2 %convolution_convert_fusion.2 = bf16[336,6144]{1,0:T(8,128)(2,1)} fusion(bf16[256,336]{0,1:T(8,128)(2,1)S(1)} %get-tuple-element.22, bf16[256,6144]{1,0:T(8,128)(2,1)S(1)} %constant_dynamic-update-slice_fusion.20), kind=kOutput, calls=%fused_computation.3 | convolution fusion | flops 1059028992 | bytes 7446528 | tf_op jit(solution)/shard_map/dot_general | solution.py:139
  98.9 0.6 collective-permute-start.29
  99.4 2.0 %collective-permute-done.32 = bf16[16,6144]{1,0:T(8,128)(2,1)S(1)} collective-permute-done((bf16[16,6144]{1,0:T(8,128)(2,1)S(1)}, bf16[16,6144]{1,0:T(8,128)(2,1)S(1)}, u32[]{:S(2)}, u32[]{:S(2)}) %collective-permute-start.32) | collective-permute-done | bytes 196640 | tf_op jit(solution)/shard_map/ppermute | solution.py:26
  101.4 0.6 collective-permute-start.33
  102.0 1.8 %convolution_convert_fusion.5 = bf16[128,6144]{1,0:T(8,128)(2,1)} fusion(bf16[16,6144]{1,0:T(8,128)(2,1)S(1)} %collective-permute-done.25, bf16[16,6144]{1,0:T(8,128)(2,1)S(1)} %collective-permute-done.22, f32[8,16,6144]{2,1,0:T(8,128)S(1)} %bitcast.54, s32[128]{0:T(128)S(1)} %add_reduce_fusion, pred[128]{0:T(512)(128)(4,1)S(1)} %get-tuple-element.25), kind=kOutput, calls=%fused_computation.6 | convolution fusion | flops 26447872 | bytes 2360320 | tf_op jit(solution)/shard_map/dot_general | solution.py:146
  103.8 0.8 collective-permute-done.29
  104.5 2.6 %collective-permute-done.33 = bf16[16,6144]{1,0:T(8,128)(2,1)S(1)} collective-permute-done((bf16[16,6144]{1,0:T(8,128)(2,1)S(1)}, bf16[16,6144]{1,0:T(8,128)(2,1)S(1)}, u32[]{:S(2)}, u32[]{:S(2)}) %collective-permute-start.33) | collective-permute-done | bytes 196640 | tf_op jit(solution)/shard_map/ppermute | solution.py:26
  107.2 1.8 %convolution_convert_fusion.4 = bf16[128,6144]{1,0:T(8,128)(2,1)} fusion(f32[128,6144]{1,0:T(8,128)S(1)} %get-tuple-element.24, bf16[16,6144]{1,0:T(8,128)(2,1)S(1)} %collective-permute-done.33, bf16[16,6144]{1,0:T(8,128)(2,1)S(1)} %collective-permute-done.29, s32[128]{0:T(128)S(1)} %add_reduce_fusion, pred[128]{0:T(512)(128)(4,1)S(1)} %get-tuple-element.25), kind=kOutput, calls=%fused_computation.5 | convolution fusion | flops 26447872 | bytes 2360320 | tf_op jit(solution)/shard_map/dot_general | solution.py:147
  (69 shorter events, 3.4 us)
Async XLA Ops:
  0.6 1.4 %copy-start = (bf16[128,6144]{1,0:T(8,128)(2,1)S(1)}, bf16[128,6144]{1,0:T(8,128)(2,1)}, u32[]{:S(2)}) copy-start(bf16[128,6144]{1,0:T(8,128)(2,1)} %param.8) | copy-start | bytes 4718596
  2.4 8.0 %collective-permute-start.9 = (bf16[16,6144]{1,0:T(8,128)(2,1)S(1)}, bf16[16,6144]{1,0:T(8,128)(2,1)S(1)}, u32[]{:S(2)}, u32[]{:S(2)}) collective-permute-start(bf16[16,6144]{1,0:T(8,128)(2,1)S(1)} %get-tuple-element.60), channel_id=1, source_target_pairs={{0,4},{1,5},{4,8},{5,9},{8,12},{9,13},{12,14},{13,15},{14,10},{15,... | collective-permute-start | bytes 589832 | tf_op jit(solution)/shard_map/ppermute | solution.py:26
  5.5 6.7 %collective-permute-start.10 = (bf16[16,6144]{1,0:T(8,128)(2,1)S(1)}, bf16[16,6144]{1,0:T(8,128)(2,1)S(1)}, u32[]{:S(2)}, u32[]{:S(2)}) collective-permute-start(bf16[16,6144]{1,0:T(8,128)(2,1)S(1)} %get-tuple-element.60), channel_id=1, source_target_pairs={{4,0},{5,1},{8,4},{9,5},{12,8},{13,9},{14,12},{15,13},{10,14},{11,... | collective-permute-start | bytes 589832 | tf_op jit(solution)/shard_map/ppermute | solution.py:26
  8.0 8.0 %collective-permute-start = (bf16[16,6272]{1,0:T(8,128)(2,1)S(1)}, bf16[16,6272]{1,0:T(8,128)(2,1)S(1)}, u32[]{:S(2)}, u32[]{:S(2)}) collective-permute-start(bf16[16,6272]{1,0:T(8,128)(2,1)S(1)} %get-tuple-element.61), channel_id=1, source_target_pairs={{0,4},{1,5},{4,8},{5,9},{8,12},{9,13},{12,14},{13,15},{14,10},{15,... | collective-permute-start | bytes 602120 | tf_op jit(solution)/shard_map/ppermute | solution.py:26
  10.1 7.9 %collective-permute-start.1 = (bf16[16,6272]{1,0:T(8,128)(2,1)S(1)}, bf16[16,6272]{1,0:T(8,128)(2,1)S(1)}, u32[]{:S(2)}, u32[]{:S(2)}) collective-permute-start(bf16[16,6272]{1,0:T(8,128)(2,1)S(1)} %get-tuple-element.61), channel_id=1, source_target_pairs={{4,0},{5,1},{8,4},{9,5},{12,8},{13,9},{14,12},{15,13},{10,14},{11,... | collective-permute-start | bytes 602120 | tf_op jit(solution)/shard_map/ppermute | solution.py:26
  10.3 9.8 %collective-permute-start.11 = (bf16[16,6144]{1,0:T(8,128)(2,1)S(1)}, bf16[16,6144]{1,0:T(8,128)(2,1)S(1)}, u32[]{:S(2)}, u32[]{:S(2)}) collective-permute-start(bf16[16,6144]{1,0:T(8,128)(2,1)S(1)} %collective-permute-done.9), channel_id=1, source_target_pairs={{0,4},{1,5},{4,8},{5,9},{8,12},{9,13},{12,14},{13,15},{14,10},{15,... | collective-permute-start | bytes 589832 | tf_op jit(solution)/shard_map/ppermute | solution.py:26
  12.2 10.0 %collective-permute-start.12 = (bf16[16,6144]{1,0:T(8,128)(2,1)S(1)}, bf16[16,6144]{1,0:T(8,128)(2,1)S(1)}, u32[]{:S(2)}, u32[]{:S(2)}) collective-permute-start(bf16[16,6144]{1,0:T(8,128)(2,1)S(1)} %collective-permute-done.10), channel_id=1, source_target_pairs={{4,0},{5,1},{8,4},{9,5},{12,8},{13,9},{14,12},{15,13},{10,14},{11,... | collective-permute-start | bytes 589832 | tf_op jit(solution)/shard_map/ppermute | solution.py:26
  16.0 8.4 %collective-permute-start.2 = (bf16[16,6272]{1,0:T(8,128)(2,1)S(1)}, bf16[16,6272]{1,0:T(8,128)(2,1)S(1)}, u32[]{:S(2)}, u32[]{:S(2)}) collective-permute-start(bf16[16,6272]{1,0:T(8,128)(2,1)S(1)} %collective-permute-done), channel_id=1, source_target_pairs={{0,4},{1,5},{4,8},{5,9},{8,12},{9,13},{12,14},{13,15},{14,10},{15,... | collective-permute-start | bytes 602120 | tf_op jit(solution)/shard_map/ppermute | solution.py:26
  18.0 6.6 %collective-permute-start.3 = (bf16[16,6272]{1,0:T(8,128)(2,1)S(1)}, bf16[16,6272]{1,0:T(8,128)(2,1)S(1)}, u32[]{:S(2)}, u32[]{:S(2)}) collective-permute-start(bf16[16,6272]{1,0:T(8,128)(2,1)S(1)} %collective-permute-done.1), channel_id=1, source_target_pairs={{4,0},{5,1},{8,4},{9,5},{12,8},{13,9},{14,12},{15,13},{10,14},{11,... | collective-permute-start | bytes 602120 | tf_op jit(solution)/shard_map/ppermute | solution.py:26
  22.2 11.7 %collective-permute-start.15 = (bf16[80,6144]{1,0:T(8,128)(2,1)S(1)}, bf16[80,6144]{1,0:T(8,128)(2,1)S(1)}, u32[]{:S(2)}, u32[]{:S(2)}) collective-permute-start(bf16[80,6144]{1,0:T(8,128)(2,1)S(1)} %get-tuple-element.50), channel_id=1, source_target_pairs={{0,1},{1,0},{2,3},{3,2},{4,5},{5,4},{6,7},{7,6},{8,9},{9,8},{10,11... | collective-permute-start | bytes 2949128 | tf_op jit(solution)/shard_map/ppermute | solution.py:26
  22.3 7.8 %collective-permute-start.13 = (bf16[16,6144]{1,0:T(8,128)(2,1)S(1)}, bf16[16,6144]{1,0:T(8,128)(2,1)S(1)}, u32[]{:S(2)}, u32[]{:S(2)}) collective-permute-start(bf16[16,6144]{1,0:T(8,128)(2,1)S(1)} %collective-permute-done.11), channel_id=1, source_target_pairs={{0,4},{1,5},{4,8},{5,9},{8,12},{9,13},{12,14},{13,15},{14,10},{15,... | collective-permute-start | bytes 589832 | tf_op jit(solution)/shard_map/ppermute | solution.py:26
  23.9 7.0 %collective-permute-start.14 = (bf16[16,6144]{1,0:T(8,128)(2,1)S(1)}, bf16[16,6144]{1,0:T(8,128)(2,1)S(1)}, u32[]{:S(2)}, u32[]{:S(2)}) collective-permute-start(bf16[16,6144]{1,0:T(8,128)(2,1)S(1)} %collective-permute-done.12), channel_id=1, source_target_pairs={{4,0},{5,1},{8,4},{9,5},{12,8},{13,9},{14,12},{15,13},{10,14},{11,... | collective-permute-start | bytes 589832 | tf_op jit(solution)/shard_map/ppermute | solution.py:26
  24.7 11.5 %collective-permute-start.6 = (bf16[80,6272]{1,0:T(8,128)(2,1)S(1)}, bf16[80,6272]{1,0:T(8,128)(2,1)S(1)}, u32[]{:S(2)}, u32[]{:S(2)}) collective-permute-start(bf16[80,6272]{1,0:T(8,128)(2,1)S(1)} %get-tuple-element.40), channel_id=1, source_target_pairs={{0,1},{1,0},{2,3},{3,2},{4,5},{5,4},{6,7},{7,6},{8,9},{9,8},{10,11... | collective-permute-start | bytes 3010568 | tf_op jit(solution)/shard_map/ppermute | solution.py:26
  24.7 9.2 %collective-permute-start.4 = (bf16[16,6272]{1,0:T(8,128)(2,1)S(1)}, bf16[16,6272]{1,0:T(8,128)(2,1)S(1)}, u32[]{:S(2)}, u32[]{:S(2)}) collective-permute-start(bf16[16,6272]{1,0:T(8,128)(2,1)S(1)} %collective-permute-done.2), channel_id=1, source_target_pairs={{0,4},{1,5},{4,8},{5,9},{8,12},{9,13},{12,14},{13,15},{14,10},{15,... | collective-permute-start | bytes 602120 | tf_op jit(solution)/shard_map/ppermute | solution.py:26
  30.1 6.1 %collective-permute-start.5 = (bf16[16,6272]{1,0:T(8,128)(2,1)S(1)}, bf16[16,6272]{1,0:T(8,128)(2,1)S(1)}, u32[]{:S(2)}, u32[]{:S(2)}) collective-permute-start(bf16[16,6272]{1,0:T(8,128)(2,1)S(1)} %collective-permute-done.3), channel_id=1, source_target_pairs={{4,0},{5,1},{8,4},{9,5},{12,8},{13,9},{14,12},{15,13},{10,14},{11,... | collective-permute-start | bytes 602120 | tf_op jit(solution)/shard_map/ppermute | solution.py:26
  33.9 6.5 %collective-permute-start.16 = (bf16[16,6144]{1,0:T(8,128)(2,1)S(1)}, bf16[16,6144]{1,0:T(8,128)(2,1)S(1)}, u32[]{:S(2)}, u32[]{:S(2)}) collective-permute-start(bf16[16,6144]{1,0:T(8,128)(2,1)S(1)} %collective-permute-done.14), channel_id=1, source_target_pairs={{4,0},{5,1},{8,4},{9,5},{12,8},{13,9},{14,12},{15,13},{10,14},{11,... | collective-permute-start | bytes 589832 | tf_op jit(solution)/shard_map/ppermute | solution.py:26
  36.2 5.8 %collective-permute-start.7 = (bf16[16,6272]{1,0:T(8,128)(2,1)S(1)}, bf16[16,6272]{1,0:T(8,128)(2,1)S(1)}, u32[]{:S(2)}, u32[]{:S(2)}) collective-permute-start(bf16[16,6272]{1,0:T(8,128)(2,1)S(1)} %collective-permute-done.4), channel_id=1, source_target_pairs={{0,4},{1,5},{4,8},{5,9},{8,12},{9,13},{12,14},{13,15},{14,10},{15,... | collective-permute-start | bytes 602120 | tf_op jit(solution)/shard_map/ppermute | solution.py:26
  40.5 2.1 %collective-permute-start.17 = (bf16[48,6144]{1,0:T(8,128)(2,1)S(1)}, bf16[48,6144]{1,0:T(8,128)(2,1)S(1)}, u32[]{:S(2)}, u32[]{:S(2)}) collective-permute-start(bf16[48,6144]{1,0:T(8,128)(2,1)S(1)} %pad_maximum_fusion.1), channel_id=1, source_target_pairs={{0,1},{1,0},{2,3},{3,2},{4,5},{5,4},{6,7},{7,6},{8,9},{9,8},{10,11... | collective-permute-start | bytes 1769480 | tf_op jit(solution)/shard_map/ppermute | solution.py:26
  40.7 3.6 %copy-start.3 = (bf16[6144,336]{0,1:T(8,128)(2,1)S(1)}, bf16[6144,336]{0,1:T(8,128)(2,1)}, u32[]{:S(2)}) copy-start(bf16[6144,336]{0,1:T(8,128)(2,1)} %param.11) | copy-start | bytes 12386308
  42.0 2.1 %collective-permute-start.8 = (bf16[48,6272]{1,0:T(8,128)(2,1)S(1)}, bf16[48,6272]{1,0:T(8,128)(2,1)S(1)}, u32[]{:S(2)}, u32[]{:S(2)}) collective-permute-start(bf16[48,6272]{1,0:T(8,128)(2,1)S(1)} %pad_maximum_fusion), channel_id=1, source_target_pairs={{0,1},{1,0},{2,3},{3,2},{4,5},{5,4},{6,7},{7,6},{8,9},{9,8},{10,11... | collective-permute-start | bytes 1806344 | tf_op jit(solution)/shard_map/ppermute | solution.py:26
  44.3 2.2 %copy-start.4 = (bf16[6144,336]{0,1:T(8,128)(2,1)S(1)}, bf16[6144,336]{0,1:T(8,128)(2,1)}, u32[]{:S(2)}) copy-start(bf16[6144,336]{0,1:T(8,128)(2,1)} %param.12) | copy-start | bytes 12386308
  46.5 2.2 %copy-start.2 = (bf16[336,6144]{1,0:T(8,128)(2,1)S(1)}, bf16[336,6144]{1,0:T(8,128)(2,1)}, u32[]{:S(2)}) copy-start(bf16[336,6144]{1,0:T(8,128)(2,1)} %param.13) | copy-start | bytes 12386308
  52.2 3.5 %collective-permute-start.18 = (bf16[128,6144]{1,0:T(8,128)(2,1)S(1)}, bf16[128,6144]{1,0:T(8,128)(2,1)S(1)}, u32[]{:S(2)}, u32[]{:S(2)}) collective-permute-start(bf16[128,6144]{1,0:T(8,128)(2,1)S(1)} %slice.162), channel_id=1, source_target_pairs={{0,1},{1,0},{2,3},{3,2},{4,5},{5,4},{6,7},{7,6},{8,9},{9,8},{10,11... | collective-permute-start | bytes 4718600 | tf_op jit(solution)/shard_map/ppermute | solution.py:26
  56.2 7.0 %collective-permute-start.19 = (bf16[16,6144]{1,0:T(8,128)(2,1)S(1)}, bf16[16,6144]{1,0:T(8,128)(2,1)S(1)}, u32[]{:S(2)}, u32[]{:S(2)}) collective-permute-start(bf16[16,6144]{1,0:T(8,128)(2,1)S(1)} %get-tuple-element.35), channel_id=1, source_target_pairs={{4,0},{5,1},{8,4},{9,5},{12,8},{13,9},{14,12},{15,13},{10,14},{11,... | collective-permute-start | bytes 589832 | tf_op jit(solution)/shard_map/ppermute | solution.py:26
  56.6 16.7 %collective-permute-start.23 = (bf16[16,6144]{1,0:T(8,128)(2,1)S(1)}, bf16[16,6144]{1,0:T(8,128)(2,1)S(1)}, u32[]{:S(2)}, u32[]{:S(2)}) collective-permute-start(bf16[16,6144]{1,0:T(8,128)(2,1)S(1)} %get-tuple-element.36), channel_id=1, source_target_pairs={{0,4},{1,5},{4,8},{5,9},{8,12},{9,13},{12,14},{13,15},{14,10},{15,... | collective-permute-start | bytes 589832 | tf_op jit(solution)/shard_map/ppermute | solution.py:26
  63.2 6.4 %collective-permute-start.20 = (bf16[16,6144]{1,0:T(8,128)(2,1)S(1)}, bf16[16,6144]{1,0:T(8,128)(2,1)S(1)}, u32[]{:S(2)}, u32[]{:S(2)}) collective-permute-start(bf16[16,6144]{1,0:T(8,128)(2,1)S(1)} %fusion.18), channel_id=1, source_target_pairs={{4,0},{5,1},{8,4},{9,5},{12,8},{13,9},{14,12},{15,13},{10,14},{11,... | collective-permute-start | bytes 589832 | tf_op jit(solution)/shard_map/ppermute | solution.py:26
  65.9 11.7 %collective-permute-start.26 = (bf16[128,6144]{1,0:T(8,128)(2,1)S(1)}, bf16[128,6144]{1,0:T(8,128)(2,1)S(1)}, u32[]{:S(2)}, u32[]{:S(2)}) collective-permute-start(bf16[128,6144]{1,0:T(8,128)(2,1)S(1)} %slice.161), channel_id=1, source_target_pairs={{0,1},{1,0},{2,3},{3,2},{4,5},{5,4},{6,7},{7,6},{8,9},{9,8},{10,11... | collective-permute-start | bytes 4718600 | tf_op jit(solution)/shard_map/ppermute | solution.py:26
  69.7 5.7 %collective-permute-start.21 = (bf16[16,6144]{1,0:T(8,128)(2,1)S(1)}, bf16[16,6144]{1,0:T(8,128)(2,1)S(1)}, u32[]{:S(2)}, u32[]{:S(2)}) collective-permute-start(bf16[16,6144]{1,0:T(8,128)(2,1)S(1)} %fusion.19), channel_id=1, source_target_pairs={{4,0},{5,1},{8,4},{9,5},{12,8},{13,9},{14,12},{15,13},{10,14},{11,... | collective-permute-start | bytes 589832 | tf_op jit(solution)/shard_map/ppermute | solution.py:26
  75.5 12.9 %collective-permute-start.24 = (bf16[16,6144]{1,0:T(8,128)(2,1)S(1)}, bf16[16,6144]{1,0:T(8,128)(2,1)S(1)}, u32[]{:S(2)}, u32[]{:S(2)}) collective-permute-start(bf16[16,6144]{1,0:T(8,128)(2,1)S(1)} %get-tuple-element.32), channel_id=1, source_target_pairs={{0,4},{1,5},{4,8},{5,9},{8,12},{9,13},{12,14},{13,15},{14,10},{15,... | collective-permute-start | bytes 589832 | tf_op jit(solution)/shard_map/ppermute | solution.py:26
  77.1 24.9 %collective-permute-start.22 = (bf16[16,6144]{1,0:T(8,128)(2,1)S(1)}, bf16[16,6144]{1,0:T(8,128)(2,1)S(1)}, u32[]{:S(2)}, u32[]{:S(2)}) collective-permute-start(bf16[16,6144]{1,0:T(8,128)(2,1)S(1)} %get-tuple-element.31), channel_id=1, source_target_pairs={{4,0},{5,1},{8,4},{9,5},{12,8},{13,9},{14,12},{15,13},{10,14},{11,... | collective-permute-start | bytes 589832 | tf_op jit(solution)/shard_map/ppermute | solution.py:26
  78.1 8.2 %collective-permute-start.27 = (bf16[16,6144]{1,0:T(8,128)(2,1)S(1)}, bf16[16,6144]{1,0:T(8,128)(2,1)S(1)}, u32[]{:S(2)}, u32[]{:S(2)}) collective-permute-start(bf16[16,6144]{1,0:T(8,128)(2,1)S(1)} %get-tuple-element.33), channel_id=1, source_target_pairs={{4,0},{5,1},{8,4},{9,5},{12,8},{13,9},{14,12},{15,13},{10,14},{11,... | collective-permute-start | bytes 589832 | tf_op jit(solution)/shard_map/ppermute | solution.py:26
  78.5 7.8 %collective-permute-start.30 = (bf16[16,6144]{1,0:T(8,128)(2,1)S(1)}, bf16[16,6144]{1,0:T(8,128)(2,1)S(1)}, u32[]{:S(2)}, u32[]{:S(2)}) collective-permute-start(bf16[16,6144]{1,0:T(8,128)(2,1)S(1)} %get-tuple-element.34), channel_id=1, source_target_pairs={{0,4},{1,5},{4,8},{5,9},{8,12},{9,13},{12,14},{13,15},{14,10},{15,... | collective-permute-start | bytes 589832 | tf_op jit(solution)/shard_map/ppermute | solution.py:26
  86.3 5.7 %collective-permute-start.28 = (bf16[16,6144]{1,0:T(8,128)(2,1)S(1)}, bf16[16,6144]{1,0:T(8,128)(2,1)S(1)}, u32[]{:S(2)}, u32[]{:S(2)}) collective-permute-start(bf16[16,6144]{1,0:T(8,128)(2,1)S(1)} %get-tuple-element.29), channel_id=1, source_target_pairs={{4,0},{5,1},{8,4},{9,5},{12,8},{13,9},{14,12},{15,13},{10,14},{11,... | collective-permute-start | bytes 589832 | tf_op jit(solution)/shard_map/ppermute | solution.py:26
  86.4 7.6 %collective-permute-start.31 = (bf16[16,6144]{1,0:T(8,128)(2,1)S(1)}, bf16[16,6144]{1,0:T(8,128)(2,1)S(1)}, u32[]{:S(2)}, u32[]{:S(2)}) collective-permute-start(bf16[16,6144]{1,0:T(8,128)(2,1)S(1)} %get-tuple-element.30), channel_id=1, source_target_pairs={{0,4},{1,5},{4,8},{5,9},{8,12},{9,13},{12,14},{13,15},{14,10},{15,... | collective-permute-start | bytes 589832 | tf_op jit(solution)/shard_map/ppermute | solution.py:26
  88.4 13.6 %collective-permute-start.25 = (bf16[16,6144]{1,0:T(8,128)(2,1)S(1)}, bf16[16,6144]{1,0:T(8,128)(2,1)S(1)}, u32[]{:S(2)}, u32[]{:S(2)}) collective-permute-start(bf16[16,6144]{1,0:T(8,128)(2,1)S(1)} %fusion.17), channel_id=1, source_target_pairs={{0,4},{1,5},{4,8},{5,9},{8,12},{9,13},{12,14},{13,15},{14,10},{15,... | collective-permute-start | bytes 589832 | tf_op jit(solution)/shard_map/ppermute | solution.py:26
  94.1 7.3 %collective-permute-start.32 = (bf16[16,6144]{1,0:T(8,128)(2,1)S(1)}, bf16[16,6144]{1,0:T(8,128)(2,1)S(1)}, u32[]{:S(2)}, u32[]{:S(2)}) collective-permute-start(bf16[16,6144]{1,0:T(8,128)(2,1)S(1)} %get-tuple-element.28), channel_id=1, source_target_pairs={{0,4},{1,5},{4,8},{5,9},{8,12},{9,13},{12,14},{13,15},{14,10},{15,... | collective-permute-start | bytes 589832 | tf_op jit(solution)/shard_map/ppermute | solution.py:26
  95.6 13.3 %copy-start.1 = (bf16[128,6144]{1,0:T(8,128)(2,1)S(1)}, bf16[128,6144]{1,0:T(8,128)(2,1)}, u32[]{:S(2)}) copy-start(bf16[128,6144]{1,0:T(8,128)(2,1)} %param.8) | copy-start | bytes 4718596
  98.9 5.7 %collective-permute-start.29 = (bf16[16,6144]{1,0:T(8,128)(2,1)S(1)}, bf16[16,6144]{1,0:T(8,128)(2,1)S(1)}, u32[]{:S(2)}, u32[]{:S(2)}) collective-permute-start(bf16[16,6144]{1,0:T(8,128)(2,1)S(1)} %get-tuple-element.27), channel_id=1, source_target_pairs={{4,0},{5,1},{8,4},{9,5},{12,8},{13,9},{14,12},{15,13},{10,14},{11,... | collective-permute-start | bytes 589832 | tf_op jit(solution)/shard_map/ppermute | solution.py:26
  101.4 5.7 %collective-permute-start.33 = (bf16[16,6144]{1,0:T(8,128)(2,1)S(1)}, bf16[16,6144]{1,0:T(8,128)(2,1)S(1)}, u32[]{:S(2)}, u32[]{:S(2)}) collective-permute-start(bf16[16,6144]{1,0:T(8,128)(2,1)S(1)} %fusion.11), channel_id=1, source_target_pairs={{0,4},{1,5},{4,8},{5,9},{8,12},{9,13},{12,14},{13,15},{14,10},{15,... | collective-permute-start | bytes 589832 | tf_op jit(solution)/shard_map/ppermute | solution.py:26

commit v3 on v2

--- a/solution.py
+++ b/solution.py
@@ -29,58 +29,58 @@
         held_xr = held_xl = x
         held_dr = held_dl = dy
         got_x, got_d = [x], [dy]
-        split = 1
-        for k in range(1, steps + 1):
-            if k == steps - 1:
-                split = len(got_x)
-                early_x = permute(jnp.concatenate(got_x, axis=0), core_pairs)
-                early_d = permute(jnp.concatenate(got_d, axis=0), core_pairs)
-            if k == steps:
-                held_xr, early_x = lax.optimization_barrier((held_xr, early_x))
-                held_dl, early_d = lax.optimization_barrier((held_dl, early_d))
-                got_x.append(permute(held_xr, right_pairs))
-                got_d.append(permute(held_dl, left_pairs))
-            else:
-                held_xr = permute(held_xr, right_pairs)
-                held_xl = permute(held_xl, left_pairs)
-                held_dr = permute(held_dr, right_pairs)
-                held_dl = permute(held_dl, left_pairs)
-                got_x += [held_xr, held_xl]
-                got_d += [held_dr, held_dl]
-        late_x = permute(jnp.concatenate(got_x[split:], axis=0), core_pairs)
-        late_d = permute(jnp.concatenate(got_d[split:], axis=0), core_pairs)
+        for k in range(1, steps):
+            held_xr = permute(held_xr, right_pairs)
+            held_dl = permute(held_dl, left_pairs)
+            held_dr = permute(held_dr, right_pairs)
+            held_xl = permute(held_xl, left_pairs)
+            got_x += [held_xr, held_xl]
+            got_d += [held_dr, held_dl]
+        far_x = permute(held_xr, right_pairs)
+        far_d = permute(held_dl, left_pairs)
+        early_x = permute(jnp.concatenate(got_x, axis=0), core_pairs)
+        early_d = permute(jnp.concatenate(got_d, axis=0), core_pairs)
+        late_x = permute(far_x, core_pairs)
+        late_d = permute(far_d, core_pairs)
         return (
-            jnp.concatenate(got_x + [early_x, late_x], axis=0),
-            jnp.concatenate(got_d + [early_d, late_d], axis=0),
+            jnp.concatenate(got_x + [far_x, early_x, late_x], axis=0),
+            jnp.concatenate(got_d + [far_d, early_d, late_d], axis=0),
         )
 
+    cut = max(2 * steps - 3, 1) * CAP
+
     def pair_sum(own, sent):
-        total = own + permute(sent, core_pairs).astype(jnp.float32)
-        return total.reshape(2 * steps, CAP, own.shape[1])
+        far = own[cut:] + permute(sent[cut:], core_pairs).astype(jnp.float32)
+        near = own[:cut] + permute(sent[:cut], core_pairs).astype(jnp.float32)
+        return near, far
 
-    def blocks_at(total, carry, k, far_left):
+    def block_of(total, at):
+        at = at * CAP
+        return total[0][at : at + CAP] if at < cut else total[1][at - cut : at - cut + CAP]
+
+    def wave(total, carry, at, far_way):
         blocks = {}
         for way in ("l", "r"):
-            if k == steps:
-                if (way == "l") != far_left:
-                    continue
-                block = total[2 * steps - 1]
-            else:
-                block = total[2 * k - 1 if way == "l" else 2 * k]
+            k = steps - at + (way == far_way)
+            if k < 1:
+                continue
+            block = block_of(total, 2 * k - (way == "l" or k == steps))
             if way in carry:
                 block = block + carry[way].astype(jnp.float32)
             blocks[way] = block.astype(jnp.bfloat16)
-        return blocks
+        return lax.optimization_barrier(blocks)
 
     def send(blocks):
         return {w: permute(b, left_pairs if w == "l" else right_pairs) for w, b in blocks.items()}
 
     def final(total, carry):
-        done = total[0] + carry["l"].astype(jnp.float32) + carry["r"].astype(jnp.float32)
+        done = block_of(total, 0) + carry["l"].astype(jnp.float32) + carry["r"].astype(jnp.float32)
         return done.astype(jnp.bfloat16)
 
-    def after(value, *marks):
-        return lax.optimization_barrier((value,) + marks)[0]
+    def tie(value, blocks):
+        ways = list(blocks)
+        tied = lax.optimization_barrier((value, *[blocks[w] for w in ways]))
+        return tied[0], dict(zip(ways, tied[1:]))
 
     def per_device(tokens, out_grad, expert_ids, gate_vals, w_gate, w_up, w_down):
         d = tokens.shape[1]
@@ -110,34 +110,38 @@
         act = gate * sig
         hidden = (coef_rows * act * up).astype(jnp.bfloat16)
         out_rows = jnp.dot(hidden, w_down, preferred_element_type=jnp.float32)
-        out_total = pair_sum(out_rows[:half], out_rows[half:].astype(jnp.bfloat16))
+        out_sent = out_rows[half:].astype(jnp.bfloat16)
+        rows_dy, out_sent = lax.optimization_barrier((rows_dy, out_sent))
+        out_total = pair_sum(out_rows[:half], out_sent)
 
-        scaled = coef_rows * jnp.dot(rows_dy, w_down.T, preferred_element_type=jnp.float32)
+        dhid = jnp.dot(rows_dy, w_down.T, preferred_element_type=jnp.float32)
+        scaled = coef_rows * dhid
         dgate = (scaled * up * sig * (1.0 + gate * (1.0 - sig))).astype(jnp.bfloat16)
         dup = (scaled * act).astype(jnp.bfloat16)
-        dgate, out_total = lax.optimization_barrier((dgate, out_total))
-        out_blocks = blocks_at(out_total, {}, steps, True)
-        out_carry = send(out_blocks)
+        dgate, blocks = tie(dgate, wave(out_total, {}, 1, "l"))
+        out_carry = send(blocks)
         dx_rows = jnp.dot(dgate, w_gate.T, preferred_element_type=jnp.float32) + jnp.dot(
             dup, w_up.T, preferred_element_type=jnp.float32
         )
-        dx_total = pair_sum(dx_rows[:half], dx_rows[half:].astype(jnp.bfloat16))
-        dx_carry = send(blocks_at(dx_total, {}, steps, False))
+        dx_sent = dx_rows[half:].astype(jnp.bfloat16)
+        dx_sent, out_carry = tie(dx_sent, out_carry)
+        dx_total = pair_sum(dx_rows[:half], dx_sent)
+        dx_carry = {}
 
         grads = []
         work = [(rows_x, dgate), (rows_x, dup), (hidden, rows_dy)]
-        for k in range(steps - 1, 0, -1):
-            out_blocks = blocks_at(out_total, out_carry, k, True)
-            out_carry = send(out_blocks)
+        for at in range(2, steps + 2):
+            if at <= steps:
+                out_carry.update(send(wave(out_total, out_carry, at, "l")))
+            blocks = wave(dx_total, dx_carry, at - 1, "r")
+            if at == 2:
+                far, out_carry = tie(dx_total[1], out_carry)
+                dx_total = (dx_total[0], far)
             if work:
                 lhs, rhs = work.pop(0)
-                marks = list(out_blocks.values())
-                if len(grads) == 2:
-                    lhs = after(lhs, *marks)
-                else:
-                    rhs = after(rhs, *marks)
+                rhs, blocks = tie(rhs, blocks)
                 grads.append(jnp.dot(lhs.T, rhs, preferred_element_type=jnp.float32))
-            dx_carry = send(blocks_at(dx_total, dx_carry, k, False))
+            dx_carry.update(send(blocks))
         for lhs, rhs in work:
             grads.append(jnp.dot(lhs.T, rhs, preferred_element_type=jnp.float32))
         grad_gate, grad_up, grad_down = grads

time: 109 us -> 104 us (0.954)
  waiting for transfers between devices: 47.5 us -> 40 us
  starting transfers between devices: 29.1 us -> 31.4 us
    ppermute x34 -> x36, waiting for transfers between devices: 47.5 us -> 40 us  [permute(): return lax.ppermute(x, 'et', pairs)]
    ppermute x34 -> x36, starting transfers between devices: 29.1 us -> 31.4 us  [permute(): return lax.ppermute(x, 'et', pairs)]
  transfers between devices with their start and end apart: 34 -> 36, of which waited for: 23 -> 21; matrix products, arithmetic and copies ran while one was open for 18% -> 20% of each run, Pallas kernels for 0% -> 0%
where the time goes in v3:
time: 104 us
  waiting for transfers between devices  40 us (38%)
  starting transfers between devices  31.4 us (30%)
  matrix products  24.6 us (24%)
  local copies, waits for them, and re-layouts  4.17 us (4%)
  other arithmetic  2.88 us (3%)
    ppermute x36, waiting for transfers between devices, permute(): return lax.ppermute(x, 'et', pairs)  40 us
    ppermute x36, starting transfers between devices, permute(): return lax.ppermute(x, 'et', pairs)  31.4 us
    dot_general x3, matrix products, per_device(): grads.append(jnp.dot(lhs.T, rhs, preferred_element_type=jnp.float32))  9.71 us
    unnamed x24, local copies, waits for them, and re-layouts  3.24 us
  transfers between devices with their start and end apart: 36, of which 21 were waited for; matrix products, arithmetic and copies ran while one was open for 20% of the time, Pallas kernels for 0%

profile of v3, /device:TPU:0, one launch (start us, length us, event | category | flops | bytes accessed | tf_op | source)
XLA Modules:
  0.0 104.0 jit_solution(1989174729900044257)
XLA Ops:
  0.6 0.8 fusion.41
  1.9 0.2 copy-done
  2.1 0.3 constant_dynamic-update-slice_fusion.23
  2.4 3.0 %collective-permute-start.10 = (bf16[16,6144]{1,0:T(8,128)(2,1)S(1)}, bf16[16,6144]{1,0:T(8,128)(2,1)S(1)}, u32[]{:S(2)}, u32[]{:S(2)}) collective-permute-start(bf16[16,6144]{1,0:T(8,128)(2,1)S(1)} %get-tuple-element.116), channel_id=1, source_target_pairs={{4,0},{5,1},{8,4},{9,5},{12,8},{13,9},{14,12},{15,13},{10,14},{11,... | collective-permute-start | bytes 589832 | tf_op jit(solution)/shard_map/ppermute | solution.py:26
  5.5 0.7 select_reduce_fusion
  6.3 1.7 %constant_dynamic-update-slice_fusion.6 = (bf16[112,6272]{1,0:T(8,128)(2,1)S(1)}, bf16[256,6272]{1,0:T(8,128)(2,1)S(1)}, bf16[16,6272]{1,0:T(8,128)(2,1)S(1)}) fusion(bf16[128,128]{1,0:T(8,128)(2,1)S(1)} %broadcast_in_dim.7, bf16[128,6144]{1,0:T(8,128)(2,1)} %param.7, s32[128]{0:T(128)S(1)} %add_reduce_fusion, pred[128]{0:T(512)(128)(4,1)S(1)} %get-tuple-element.73), kind=kOutput, calls=%fused_computation.61 | convolution fusion | flops 29005824 | bytes 2208384 | tf_op jit(solution)/shard_map/dot_general | solution.py:98
  8.0 2.0 %collective-permute-start.1 = (bf16[16,6272]{1,0:T(8,128)(2,1)S(1)}, bf16[16,6272]{1,0:T(8,128)(2,1)S(1)}, u32[]{:S(2)}, u32[]{:S(2)}) collective-permute-start(bf16[16,6272]{1,0:T(8,128)(2,1)S(1)} %get-tuple-element.113), channel_id=1, source_target_pairs={{4,0},{5,1},{8,4},{9,5},{12,8},{13,9},{14,12},{15,13},{10,14},{11,... | collective-permute-start | bytes 602120 | tf_op jit(solution)/shard_map/ppermute | solution.py:26
  10.1 0.3 collective-permute-done.10
  10.4 1.7 %collective-permute-start.12 = (bf16[16,6144]{1,0:T(8,128)(2,1)S(1)}, bf16[16,6144]{1,0:T(8,128)(2,1)S(1)}, u32[]{:S(2)}, u32[]{:S(2)}) collective-permute-start(bf16[16,6144]{1,0:T(8,128)(2,1)S(1)} %collective-permute-done.10), channel_id=1, source_target_pairs={{4,0},{5,1},{8,4},{9,5},{12,8},{13,9},{14,12},{15,13},{10,14},{11,... | collective-permute-start | bytes 589832 | tf_op jit(solution)/shard_map/ppermute | solution.py:26
  12.1 0.3 collective-permute-start.11
  12.5 3.5 %collective-permute-done.1 = bf16[16,6272]{1,0:T(8,128)(2,1)S(1)} collective-permute-done((bf16[16,6272]{1,0:T(8,128)(2,1)S(1)}, bf16[16,6272]{1,0:T(8,128)(2,1)S(1)}, u32[]{:S(2)}, u32[]{:S(2)}) %collective-permute-start.1) | collective-permute-done | bytes 200736 | tf_op jit(solution)/shard_map/ppermute | solution.py:26
  16.0 1.9 %collective-permute-start.3 = (bf16[16,6272]{1,0:T(8,128)(2,1)S(1)}, bf16[16,6272]{1,0:T(8,128)(2,1)S(1)}, u32[]{:S(2)}, u32[]{:S(2)}) collective-permute-start(bf16[16,6272]{1,0:T(8,128)(2,1)S(1)} %collective-permute-done.1), channel_id=1, source_target_pairs={{4,0},{5,1},{8,4},{9,5},{12,8},{13,9},{14,12},{15,13},{10,14},{11,... | collective-permute-start | bytes 602120 | tf_op jit(solution)/shard_map/ppermute | solution.py:26
  18.1 2.1 %collective-permute-done.12 = bf16[16,6144]{1,0:T(8,128)(2,1)S(1)} collective-permute-done((bf16[16,6144]{1,0:T(8,128)(2,1)S(1)}, bf16[16,6144]{1,0:T(8,128)(2,1)S(1)}, u32[]{:S(2)}, u32[]{:S(2)}) %collective-permute-start.12) | collective-permute-done | bytes 196640 | tf_op jit(solution)/shard_map/ppermute | solution.py:26
  20.2 1.9 %collective-permute-start.14 = (bf16[16,6144]{1,0:T(8,128)(2,1)S(1)}, bf16[16,6144]{1,0:T(8,128)(2,1)S(1)}, u32[]{:S(2)}, u32[]{:S(2)}) collective-permute-start(bf16[16,6144]{1,0:T(8,128)(2,1)S(1)} %collective-permute-done.12), channel_id=1, source_target_pairs={{4,0},{5,1},{8,4},{9,5},{12,8},{13,9},{14,12},{15,13},{10,14},{11,... | collective-permute-start | bytes 589832 | tf_op jit(solution)/shard_map/ppermute | solution.py:26
  22.3 2.2 %collective-permute-done.3 = bf16[16,6272]{1,0:T(8,128)(2,1)S(1)} collective-permute-done((bf16[16,6272]{1,0:T(8,128)(2,1)S(1)}, bf16[16,6272]{1,0:T(8,128)(2,1)S(1)}, u32[]{:S(2)}, u32[]{:S(2)}) %collective-permute-start.3) | collective-permute-done | bytes 200736 | tf_op jit(solution)/shard_map/ppermute | solution.py:26
  24.5 1.9 %collective-permute-start.5 = (bf16[16,6272]{1,0:T(8,128)(2,1)S(1)}, bf16[16,6272]{1,0:T(8,128)(2,1)S(1)}, u32[]{:S(2)}, u32[]{:S(2)}) collective-permute-start(bf16[16,6272]{1,0:T(8,128)(2,1)S(1)} %collective-permute-done.3), channel_id=1, source_target_pairs={{4,0},{5,1},{8,4},{9,5},{12,8},{13,9},{14,12},{15,13},{10,14},{11,... | collective-permute-start | bytes 602120 | tf_op jit(solution)/shard_map/ppermute | solution.py:26
  26.6 4.0 %collective-permute-done.13 = bf16[16,6144]{1,0:T(8,128)(2,1)S(1)} collective-permute-done((bf16[16,6144]{1,0:T(8,128)(2,1)S(1)}, bf16[16,6144]{1,0:T(8,128)(2,1)S(1)}, u32[]{:S(2)}, u32[]{:S(2)}) %collective-permute-start.13) | collective-permute-done | bytes 196640 | tf_op jit(solution)/shard_map/ppermute | solution.py:26
  30.8 1.6 %collective-permute-start.15 = (bf16[16,6144]{1,0:T(8,128)(2,1)S(1)}, bf16[16,6144]{1,0:T(8,128)(2,1)S(1)}, u32[]{:S(2)}, u32[]{:S(2)}) collective-permute-start(bf16[16,6144]{1,0:T(8,128)(2,1)S(1)} %collective-permute-done.14), channel_id=1, source_target_pairs={{4,0},{5,1},{8,4},{9,5},{12,8},{13,9},{14,12},{15,13},{10,14},{11,... | collective-permute-start | bytes 589832 | tf_op jit(solution)/shard_map/ppermute | solution.py:26
  32.4 0.6 collective-permute-done.4
  33.3 0.5 collective-permute-start.6
  33.7 4.4 %collective-permute-done.15 = bf16[16,6144]{1,0:T(8,128)(2,1)S(1)} collective-permute-done((bf16[16,6144]{1,0:T(8,128)(2,1)S(1)}, bf16[16,6144]{1,0:T(8,128)(2,1)S(1)}, u32[]{:S(2)}, u32[]{:S(2)}) %collective-permute-start.15) | collective-permute-done | bytes 196640 | tf_op jit(solution)/shard_map/ppermute | solution.py:26
  38.1 2.5 %collective-permute-done.6 = bf16[16,6272]{1,0:T(8,128)(2,1)S(1)} collective-permute-done((bf16[16,6272]{1,0:T(8,128)(2,1)S(1)}, bf16[16,6272]{1,0:T(8,128)(2,1)S(1)}, u32[]{:S(2)}, u32[]{:S(2)}) %collective-permute-start.6) | collective-permute-done | bytes 200736 | tf_op jit(solution)/shard_map/ppermute | solution.py:26
  41.0 1.0 %collective-permute-done.8 = bf16[16,6272]{1,0:T(8,128)(2,1)S(1)} collective-permute-done((bf16[16,6272]{1,0:T(8,128)(2,1)S(1)}, bf16[16,6272]{1,0:T(8,128)(2,1)S(1)}, u32[]{:S(2)}, u32[]{:S(2)}) %collective-permute-start.8) | collective-permute-done | bytes 200736 | tf_op jit(solution)/shard_map/ppermute | solution.py:26
  42.2 0.6 copy-done.3
  42.8 1.3 %fusion.4 = f32[256,336]{0,1:T(8,128)S(1)} fusion(bf16[6144,336]{0,1:T(8,128)(2,1)S(1)} %copy-done.3, bf16[256,6272]{1,0:T(8,128)(2,1)S(1)} %constant_dynamic-update-slice_fusion.7), kind=kOutput, calls=%fused_computation.14 | convolution fusion | flops 1056964608 | bytes 7618560 | tf_op jit(solution)/shard_map/dot_general | solution.py:107
  44.1 0.9 copy-done.4
  45.0 1.3 %multiply_convert_fusion.2 = (bf16[256,336]{0,1:T(8,128)(2,1)S(1)}, f32[256,336]{0,1:T(8,128)S(1)}) fusion(f32[256]{0:T(256)S(1)} %convert_reduce_fusion, f32[256,336]{0,1:T(8,128)S(1)} %fusion.4, bf16[6144,336]{0,1:T(8,128)(2,1)S(1)} %copy-done.4, bf16[256,6272]{1,0:T(8,128)(2,1)S(1)} %constant_dynamic-update-slice_fusion.7), kind=kOutput, calls=%fused_computation.51 | convolution fusion | flops 1057566720 | bytes 8135680 | tf_op jit(solution)/shard_map/dot_general | solution.py:108
  46.3 0.9 copy-done.2
  47.2 1.8 %fusion.44 = f32[256,6144]{1,0:T(8,128)S(1)} fusion(bf16[256,336]{0,1:T(8,128)(2,1)S(1)} %get-tuple-element.114, bf16[336,6144]{1,0:T(8,128)(2,1)S(1)} %copy-done.2), kind=kOutput, calls=%fused_computation.109 | convolution fusion | flops 1056964608 | bytes 10592256 | tf_op jit(solution)/shard_map/dot_general | solution.py:112
  49.2 0.6 collective-permute-start.19
  50.0 1.3 %multiply_convert_fusion = (bf16[256,336]{0,1:T(8,128)(2,1)S(1)}, bf16[256,336]{0,1:T(8,128)(2,1)S(1)}) fusion(f32[256,336]{0,1:T(8,128)S(1)} %fusion.4, f32[256,336]{0,1:T(8,128)S(1)} %get-tuple-element.115, bf16[256,6144]{1,0:T(8,128)(2,1)S(1)} %constant_dynamic-update-slice_fusion.24, bf16[336,6144]{1,0:T(8,128)(2,1)S(1)} %copy-done.2, ...), kind=kOutput, calls=%fused_computation.49 | convolution fusion | flops 1058168832 | bytes 8307712 | tf_op jit(solution)/shard_map/dot_general | solution.py:117
  51.6 1.6 %collective-permute-start.20 = (bf16[16,6144]{1,0:T(8,128)(2,1)S(1)}, bf16[16,6144]{1,0:T(8,128)(2,1)S(1)}, u32[]{:S(2)}, u32[]{:S(2)}) collective-permute-start(bf16[16,6144]{1,0:T(8,128)(2,1)S(1)} %get-tuple-element.42), channel_id=1, source_target_pairs={{4,0},{5,1},{8,4},{9,5},{12,8},{13,9},{14,12},{15,13},{10,14},{11,... | collective-permute-start | bytes 589832 | tf_op jit(solution)/shard_map/ppermute | solution.py:26
  53.3 0.4 collective-permute-start.21
  53.7 1.8 %fusion.45 = f32[256,6144]{1,0:T(8,128)S(1)} fusion(bf16[256,336]{0,1:T(8,128)(2,1)S(1)} %get-tuple-element.66, bf16[6144,336]{0,1:T(8,128)(2,1)S(1)} %copy-done.3), kind=kOutput, calls=%fused_computation.110 | convolution fusion | flops 1056964608 | bytes 10592256 | tf_op jit(solution)/shard_map/dot_general | solution.py:123
  55.6 1.8 %convolution_add_fusion = f32[256,6144]{1,0:T(8,128)S(1)} fusion(f32[256,6144]{1,0:T(8,128)S(1)} %fusion.45, bf16[256,336]{0,1:T(8,128)(2,1)S(1)} %get-tuple-element.67, bf16[6144,336]{0,1:T(8,128)(2,1)S(1)} %copy-done.4), kind=kOutput, calls=%fused_computation | convolution fusion | flops 1058537472 | bytes 16883712 | tf_op jit(solution)/shard_map/dot_general | solution.py:123
  57.6 1.3 %collective-permute-done.20 = bf16[16,6144]{1,0:T(8,128)(2,1)S(1)} collective-permute-done((bf16[16,6144]{1,0:T(8,128)(2,1)S(1)}, bf16[16,6144]{1,0:T(8,128)(2,1)S(1)}, u32[]{:S(2)}, u32[]{:S(2)}) %collective-permute-start.20) | collective-permute-done | bytes 196640 | tf_op jit(solution)/shard_map/ppermute | solution.py:26
  58.9 1.3 %collective-permute-done.21 = bf16[16,6144]{1,0:T(8,128)(2,1)S(1)} collective-permute-done((bf16[16,6144]{1,0:T(8,128)(2,1)S(1)}, bf16[16,6144]{1,0:T(8,128)(2,1)S(1)}, u32[]{:S(2)}, u32[]{:S(2)}) %collective-permute-start.21) | collective-permute-done | bytes 196640 | tf_op jit(solution)/shard_map/ppermute | solution.py:26
  60.3 0.5 collective-permute-start.28
  61.1 1.6 %collective-permute-start.23 = (bf16[16,6144]{1,0:T(8,128)(2,1)S(1)}, bf16[16,6144]{1,0:T(8,128)(2,1)S(1)}, u32[]{:S(2)}, u32[]{:S(2)}) collective-permute-start(bf16[16,6144]{1,0:T(8,128)(2,1)S(1)} %fusion.17), channel_id=1, source_target_pairs={{4,0},{5,1},{8,4},{9,5},{12,8},{13,9},{14,12},{15,13},{10,14},{11,... | collective-permute-start | bytes 589832 | tf_op jit(solution)/shard_map/ppermute | solution.py:26
  62.8 0.4 collective-permute-start.24
  63.4 4.7 %collective-permute-done.23 = bf16[16,6144]{1,0:T(8,128)(2,1)S(1)} collective-permute-done((bf16[16,6144]{1,0:T(8,128)(2,1)S(1)}, bf16[16,6144]{1,0:T(8,128)(2,1)S(1)}, u32[]{:S(2)}, u32[]{:S(2)}) %collective-permute-start.23) | collective-permute-done | bytes 196640 | tf_op jit(solution)/shard_map/ppermute | solution.py:26
  68.1 1.3 %collective-permute-done.24 = bf16[16,6144]{1,0:T(8,128)(2,1)S(1)} collective-permute-done((bf16[16,6144]{1,0:T(8,128)(2,1)S(1)}, bf16[16,6144]{1,0:T(8,128)(2,1)S(1)}, u32[]{:S(2)}, u32[]{:S(2)}) %collective-permute-start.24) | collective-permute-done | bytes 196640 | tf_op jit(solution)/shard_map/ppermute | solution.py:26
  69.4 1.7 %collective-permute-start.25 = (bf16[16,6144]{1,0:T(8,128)(2,1)S(1)}, bf16[16,6144]{1,0:T(8,128)(2,1)S(1)}, u32[]{:S(2)}, u32[]{:S(2)}) collective-permute-start(bf16[16,6144]{1,0:T(8,128)(2,1)S(1)} %get-tuple-element.51), channel_id=1, source_target_pairs={{4,0},{5,1},{8,4},{9,5},{12,8},{13,9},{14,12},{15,13},{10,14},{11,... | collective-permute-start | bytes 589832 | tf_op jit(solution)/shard_map/ppermute | solution.py:26
  71.1 0.4 collective-permute-start.27
  71.5 1.6 %collective-permute-start.29 = (bf16[16,6144]{1,0:T(8,128)(2,1)S(1)}, bf16[16,6144]{1,0:T(8,128)(2,1)S(1)}, u32[]{:S(2)}, u32[]{:S(2)}) collective-permute-start(bf16[16,6144]{1,0:T(8,128)(2,1)S(1)} %get-tuple-element.55), channel_id=1, source_target_pairs={{4,0},{5,1},{8,4},{9,5},{12,8},{13,9},{14,12},{15,13},{10,14},{11,... | collective-permute-start | bytes 589832 | tf_op jit(solution)/shard_map/ppermute | solution.py:26
  73.1 0.4 collective-permute-start.30
  73.6 3.3 %convolution_convert_fusion.1 = bf16[6144,336]{0,1:T(8,128)(2,1)} fusion(bf16[256,336]{0,1:T(8,128)(2,1)S(1)} %get-tuple-element.66, bf16[256,6272]{1,0:T(8,128)(2,1)S(1)} %constant_dynamic-update-slice_fusion.7), kind=kOutput, calls=%fused_computation.2 | convolution fusion | flops 1059028992 | bytes 7446528 | tf_op jit(solution)/shard_map/dot_general | solution.py:143
  76.8 0.5 collective-permute-done.25
  77.4 1.6 %collective-permute-start.26 = (bf16[16,6144]{1,0:T(8,128)(2,1)S(1)}, bf16[16,6144]{1,0:T(8,128)(2,1)S(1)}, u32[]{:S(2)}, u32[]{:S(2)}) collective-permute-start(bf16[16,6144]{1,0:T(8,128)(2,1)S(1)} %fusion.19), channel_id=1, source_target_pairs={{4,0},{5,1},{8,4},{9,5},{12,8},{13,9},{14,12},{15,13},{10,14},{11,... | collective-permute-start | bytes 589832 | tf_op jit(solution)/shard_map/ppermute | solution.py:26
  79.0 1.7 %collective-permute-done.30 = bf16[16,6144]{1,0:T(8,128)(2,1)S(1)} collective-permute-done((bf16[16,6144]{1,0:T(8,128)(2,1)S(1)}, bf16[16,6144]{1,0:T(8,128)(2,1)S(1)}, u32[]{:S(2)}, u32[]{:S(2)}) %collective-permute-start.30) | collective-permute-done | bytes 196640 | tf_op jit(solution)/shard_map/ppermute | solution.py:26
  81.0 0.6 collective-permute-done.29
  81.6 1.6 %collective-permute-start.31 = (bf16[16,6144]{1,0:T(8,128)(2,1)S(1)}, bf16[16,6144]{1,0:T(8,128)(2,1)S(1)}, u32[]{:S(2)}, u32[]{:S(2)}) collective-permute-start(bf16[16,6144]{1,0:T(8,128)(2,1)S(1)} %fusion.11), channel_id=1, source_target_pairs={{4,0},{5,1},{8,4},{9,5},{12,8},{13,9},{14,12},{15,13},{10,14},{11,... | collective-permute-start | bytes 589832 | tf_op jit(solution)/shard_map/ppermute | solution.py:26
  83.2 0.4 collective-permute-start.32
  83.7 3.2 %convolution_convert_fusion = bf16[6144,336]{0,1:T(8,128)(2,1)} fusion(bf16[256,336]{0,1:T(8,128)(2,1)S(1)} %get-tuple-element.67, bf16[256,6272]{1,0:T(8,128)(2,1)S(1)} %constant_dynamic-update-slice_fusion.7), kind=kOutput, calls=%fused_computation.1 | convolution fusion | flops 1059028992 | bytes 7446528 | tf_op jit(solution)/shard_map/dot_general | solution.py:143
  86.9 0.9 collective-permute-done.31
  87.9 1.3 %collective-permute-done.32 = bf16[16,6144]{1,0:T(8,128)(2,1)S(1)} collective-permute-done((bf16[16,6144]{1,0:T(8,128)(2,1)S(1)}, bf16[16,6144]{1,0:T(8,128)(2,1)S(1)}, u32[]{:S(2)}, u32[]{:S(2)}) %collective-permute-start.32) | collective-permute-done | bytes 196640 | tf_op jit(solution)/shard_map/ppermute | solution.py:26
  89.3 0.5 collective-permute-start.34
  89.8 1.8 %convolution_convert_fusion.5 = bf16[128,6144]{1,0:T(8,128)(2,1)} fusion(f32[80,6144]{1,0:T(8,128)S(1)} %slice_add_fusion.1, bf16[16,6144]{1,0:T(8,128)(2,1)S(1)} %collective-permute-done.27, bf16[16,6144]{1,0:T(8,128)(2,1)S(1)} %collective-permute-done.26, s32[128]{0:T(128)S(1)} %add_reduce_fusion, pred[128]{0:T(512)(128)(4,1)S(1)} %get-tuple-element.73), kind=kOutput, calls=%fused_computation.6 | convolution fusion | flops 26447872 | bytes 2360320 | tf_op jit(solution)/shard_map/dot_general | solution.py:150
  91.5 1.6 %collective-permute-start.33 = (bf16[16,6144]{1,0:T(8,128)(2,1)S(1)}, bf16[16,6144]{1,0:T(8,128)(2,1)S(1)}, u32[]{:S(2)}, u32[]{:S(2)}) collective-permute-start(bf16[16,6144]{1,0:T(8,128)(2,1)S(1)} %get-tuple-element.64), channel_id=1, source_target_pairs={{4,0},{5,1},{8,4},{9,5},{12,8},{13,9},{14,12},{15,13},{10,14},{11,... | collective-permute-start | bytes 589832 | tf_op jit(solution)/shard_map/ppermute | solution.py:26
  93.1 3.4 %collective-permute-done.34 = bf16[16,6144]{1,0:T(8,128)(2,1)S(1)} collective-permute-done((bf16[16,6144]{1,0:T(8,128)(2,1)S(1)}, bf16[16,6144]{1,0:T(8,128)(2,1)S(1)}, u32[]{:S(2)}, u32[]{:S(2)}) %collective-permute-start.34) | collective-permute-done | bytes 196640 | tf_op jit(solution)/shard_map/ppermute | solution.py:26
  96.6 0.5 collective-permute-start.35
  97.1 3.2 %convolution_convert_fusion.2 = bf16[336,6144]{1,0:T(8,128)(2,1)} fusion(bf16[256,336]{0,1:T(8,128)(2,1)S(1)} %get-tuple-element.114, bf16[256,6144]{1,0:T(8,128)(2,1)S(1)} %constant_dynamic-update-slice_fusion.24), kind=kOutput, calls=%fused_computation.3 | convolution fusion | flops 1059028992 | bytes 7446528 | tf_op jit(solution)/shard_map/dot_general | solution.py:143
  100.3 2.0 %collective-permute-done.35 = bf16[16,6144]{1,0:T(8,128)(2,1)S(1)} collective-permute-done((bf16[16,6144]{1,0:T(8,128)(2,1)S(1)}, bf16[16,6144]{1,0:T(8,128)(2,1)S(1)}, u32[]{:S(2)}, u32[]{:S(2)}) %collective-permute-start.35) | collective-permute-done | bytes 196640 | tf_op jit(solution)/shard_map/ppermute | solution.py:26
  102.3 1.8 %convolution_convert_fusion.4 = bf16[128,6144]{1,0:T(8,128)(2,1)} fusion(f32[80,6144]{1,0:T(8,128)S(1)} %slice_add_fusion, bf16[16,6144]{1,0:T(8,128)(2,1)S(1)} %collective-permute-done.35, bf16[16,6144]{1,0:T(8,128)(2,1)S(1)} %collective-permute-done.33, s32[128]{0:T(128)S(1)} %add_reduce_fusion, pred[128]{0:T(512)(128)(4,1)S(1)} %get-tuple-element.73), kind=kOutput, calls=%fused_computation.5 | convolution fusion | flops 26447872 | bytes 2360320 | tf_op jit(solution)/shard_map/dot_general | solution.py:151
  (77 shorter events, 4.1 us)
Async XLA Ops:
  0.6 1.4 %copy-start = (bf16[128,6144]{1,0:T(8,128)(2,1)S(1)}, bf16[128,6144]{1,0:T(8,128)(2,1)}, u32[]{:S(2)}) copy-start(bf16[128,6144]{1,0:T(8,128)(2,1)} %param.8) | copy-start | bytes 4718596
  2.4 8.0 %collective-permute-start.10 = (bf16[16,6144]{1,0:T(8,128)(2,1)S(1)}, bf16[16,6144]{1,0:T(8,128)(2,1)S(1)}, u32[]{:S(2)}, u32[]{:S(2)}) collective-permute-start(bf16[16,6144]{1,0:T(8,128)(2,1)S(1)} %get-tuple-element.116), channel_id=1, source_target_pairs={{4,0},{5,1},{8,4},{9,5},{12,8},{13,9},{14,12},{15,13},{10,14},{11,... | collective-permute-start | bytes 589832 | tf_op jit(solution)/shard_map/ppermute | solution.py:26
  5.4 6.7 %collective-permute-start.9 = (bf16[16,6144]{1,0:T(8,128)(2,1)S(1)}, bf16[16,6144]{1,0:T(8,128)(2,1)S(1)}, u32[]{:S(2)}, u32[]{:S(2)}) collective-permute-start(bf16[16,6144]{1,0:T(8,128)(2,1)S(1)} %get-tuple-element.116), channel_id=1, source_target_pairs={{0,4},{1,5},{4,8},{5,9},{8,12},{9,13},{12,14},{13,15},{14,10},{15,... | collective-permute-start | bytes 589832 | tf_op jit(solution)/shard_map/ppermute | solution.py:26
  8.0 8.0 %collective-permute-start.1 = (bf16[16,6272]{1,0:T(8,128)(2,1)S(1)}, bf16[16,6272]{1,0:T(8,128)(2,1)S(1)}, u32[]{:S(2)}, u32[]{:S(2)}) collective-permute-start(bf16[16,6272]{1,0:T(8,128)(2,1)S(1)} %get-tuple-element.113), channel_id=1, source_target_pairs={{4,0},{5,1},{8,4},{9,5},{12,8},{13,9},{14,12},{15,13},{10,14},{11,... | collective-permute-start | bytes 602120 | tf_op jit(solution)/shard_map/ppermute | solution.py:26
  10.0 7.9 %collective-permute-start = (bf16[16,6272]{1,0:T(8,128)(2,1)S(1)}, bf16[16,6272]{1,0:T(8,128)(2,1)S(1)}, u32[]{:S(2)}, u32[]{:S(2)}) collective-permute-start(bf16[16,6272]{1,0:T(8,128)(2,1)S(1)} %get-tuple-element.113), channel_id=1, source_target_pairs={{0,4},{1,5},{4,8},{5,9},{8,12},{9,13},{12,14},{13,15},{14,10},{15,... | collective-permute-start | bytes 602120 | tf_op jit(solution)/shard_map/ppermute | solution.py:26
  10.4 9.8 %collective-permute-start.12 = (bf16[16,6144]{1,0:T(8,128)(2,1)S(1)}, bf16[16,6144]{1,0:T(8,128)(2,1)S(1)}, u32[]{:S(2)}, u32[]{:S(2)}) collective-permute-start(bf16[16,6144]{1,0:T(8,128)(2,1)S(1)} %collective-permute-done.10), channel_id=1, source_target_pairs={{4,0},{5,1},{8,4},{9,5},{12,8},{13,9},{14,12},{15,13},{10,14},{11,... | collective-permute-start | bytes 589832 | tf_op jit(solution)/shard_map/ppermute | solution.py:26
  12.1 10.0 %collective-permute-start.11 = (bf16[16,6144]{1,0:T(8,128)(2,1)S(1)}, bf16[16,6144]{1,0:T(8,128)(2,1)S(1)}, u32[]{:S(2)}, u32[]{:S(2)}) collective-permute-start(bf16[16,6144]{1,0:T(8,128)(2,1)S(1)} %collective-permute-done.9), channel_id=1, source_target_pairs={{0,4},{1,5},{4,8},{5,9},{8,12},{9,13},{12,14},{13,15},{14,10},{15,... | collective-permute-start | bytes 589832 | tf_op jit(solution)/shard_map/ppermute | solution.py:26
  16.0 8.5 %collective-permute-start.3 = (bf16[16,6272]{1,0:T(8,128)(2,1)S(1)}, bf16[16,6272]{1,0:T(8,128)(2,1)S(1)}, u32[]{:S(2)}, u32[]{:S(2)}) collective-permute-start(bf16[16,6272]{1,0:T(8,128)(2,1)S(1)} %collective-permute-done.1), channel_id=1, source_target_pairs={{4,0},{5,1},{8,4},{9,5},{12,8},{13,9},{14,12},{15,13},{10,14},{11,... | collective-permute-start | bytes 602120 | tf_op jit(solution)/shard_map/ppermute | solution.py:26
  17.9 8.5 %collective-permute-start.2 = (bf16[16,6272]{1,0:T(8,128)(2,1)S(1)}, bf16[16,6272]{1,0:T(8,128)(2,1)S(1)}, u32[]{:S(2)}, u32[]{:S(2)}) collective-permute-start(bf16[16,6272]{1,0:T(8,128)(2,1)S(1)} %collective-permute-done), channel_id=1, source_target_pairs={{0,4},{1,5},{4,8},{5,9},{8,12},{9,13},{12,14},{13,15},{14,10},{15,... | collective-permute-start | bytes 602120 | tf_op jit(solution)/shard_map/ppermute | solution.py:26
  20.2 10.5 %collective-permute-start.14 = (bf16[16,6144]{1,0:T(8,128)(2,1)S(1)}, bf16[16,6144]{1,0:T(8,128)(2,1)S(1)}, u32[]{:S(2)}, u32[]{:S(2)}) collective-permute-start(bf16[16,6144]{1,0:T(8,128)(2,1)S(1)} %collective-permute-done.12), channel_id=1, source_target_pairs={{4,0},{5,1},{8,4},{9,5},{12,8},{13,9},{14,12},{15,13},{10,14},{11,... | collective-permute-start | bytes 589832 | tf_op jit(solution)/shard_map/ppermute | solution.py:26
  22.1 8.5 %collective-permute-start.13 = (bf16[16,6144]{1,0:T(8,128)(2,1)S(1)}, bf16[16,6144]{1,0:T(8,128)(2,1)S(1)}, u32[]{:S(2)}, u32[]{:S(2)}) collective-permute-start(bf16[16,6144]{1,0:T(8,128)(2,1)S(1)} %collective-permute-done.11), channel_id=1, source_target_pairs={{0,4},{1,5},{4,8},{5,9},{8,12},{9,13},{12,14},{13,15},{14,10},{15,... | collective-permute-start | bytes 589832 | tf_op jit(solution)/shard_map/ppermute | solution.py:26
  24.5 8.6 %collective-permute-start.5 = (bf16[16,6272]{1,0:T(8,128)(2,1)S(1)}, bf16[16,6272]{1,0:T(8,128)(2,1)S(1)}, u32[]{:S(2)}, u32[]{:S(2)}) collective-permute-start(bf16[16,6272]{1,0:T(8,128)(2,1)S(1)} %collective-permute-done.3), channel_id=1, source_target_pairs={{4,0},{5,1},{8,4},{9,5},{12,8},{13,9},{14,12},{15,13},{10,14},{11,... | collective-permute-start | bytes 602120 | tf_op jit(solution)/shard_map/ppermute | solution.py:26
  26.4 6.6 %collective-permute-start.4 = (bf16[16,6272]{1,0:T(8,128)(2,1)S(1)}, bf16[16,6272]{1,0:T(8,128)(2,1)S(1)}, u32[]{:S(2)}, u32[]{:S(2)}) collective-permute-start(bf16[16,6272]{1,0:T(8,128)(2,1)S(1)} %collective-permute-done.2), channel_id=1, source_target_pairs={{0,4},{1,5},{4,8},{5,9},{8,12},{9,13},{12,14},{13,15},{14,10},{15,... | collective-permute-start | bytes 602120 | tf_op jit(solution)/shard_map/ppermute | solution.py:26
  30.7 9.9 %collective-permute-start.16 = (bf16[112,6144]{1,0:T(8,128)(2,1)S(1)}, bf16[112,6144]{1,0:T(8,128)(2,1)S(1)}, u32[]{:S(2)}, u32[]{:S(2)}) collective-permute-start(bf16[112,6144]{1,0:T(8,128)(2,1)S(1)} %get-tuple-element.99), channel_id=1, source_target_pairs={{0,1},{1,0},{2,3},{3,2},{4,5},{5,4},{6,7},{7,6},{8,9},{9,8},{10,11... | collective-permute-start | bytes 4128776 | tf_op jit(solution)/shard_map/ppermute | solution.py:26
  30.8 7.3 %collective-permute-start.15 = (bf16[16,6144]{1,0:T(8,128)(2,1)S(1)}, bf16[16,6144]{1,0:T(8,128)(2,1)S(1)}, u32[]{:S(2)}, u32[]{:S(2)}) collective-permute-start(bf16[16,6144]{1,0:T(8,128)(2,1)S(1)} %collective-permute-done.14), channel_id=1, source_target_pairs={{4,0},{5,1},{8,4},{9,5},{12,8},{13,9},{14,12},{15,13},{10,14},{11,... | collective-permute-start | bytes 589832 | tf_op jit(solution)/shard_map/ppermute | solution.py:26
  33.2 7.7 %collective-permute-start.7 = (bf16[112,6272]{1,0:T(8,128)(2,1)S(1)}, bf16[112,6272]{1,0:T(8,128)(2,1)S(1)}, u32[]{:S(2)}, u32[]{:S(2)}) collective-permute-start(bf16[112,6272]{1,0:T(8,128)(2,1)S(1)} %get-tuple-element.85), channel_id=1, source_target_pairs={{0,1},{1,0},{2,3},{3,2},{4,5},{5,4},{6,7},{7,6},{8,9},{9,8},{10,11... | collective-permute-start | bytes 4214792 | tf_op jit(solution)/shard_map/ppermute | solution.py:26
  33.3 7.4 %collective-permute-start.6 = (bf16[16,6272]{1,0:T(8,128)(2,1)S(1)}, bf16[16,6272]{1,0:T(8,128)(2,1)S(1)}, u32[]{:S(2)}, u32[]{:S(2)}) collective-permute-start(bf16[16,6272]{1,0:T(8,128)(2,1)S(1)} %collective-permute-done.4), channel_id=1, source_target_pairs={{0,4},{1,5},{4,8},{5,9},{8,12},{9,13},{12,14},{13,15},{14,10},{15,... | collective-permute-start | bytes 602120 | tf_op jit(solution)/shard_map/ppermute | solution.py:26
  38.1 2.7 %collective-permute-start.17 = (bf16[16,6144]{1,0:T(8,128)(2,1)S(1)}, bf16[16,6144]{1,0:T(8,128)(2,1)S(1)}, u32[]{:S(2)}, u32[]{:S(2)}) collective-permute-start(bf16[16,6144]{1,0:T(8,128)(2,1)S(1)} %collective-permute-done.15), channel_id=1, source_target_pairs={{0,1},{1,0},{2,3},{3,2},{4,5},{5,4},{6,7},{7,6},{8,9},{9,8},{10,11... | collective-permute-start | bytes 589832 | tf_op jit(solution)/shard_map/ppermute | solution.py:26
  40.6 1.4 %collective-permute-start.8 = (bf16[16,6272]{1,0:T(8,128)(2,1)S(1)}, bf16[16,6272]{1,0:T(8,128)(2,1)S(1)}, u32[]{:S(2)}, u32[]{:S(2)}) collective-permute-start(bf16[16,6272]{1,0:T(8,128)(2,1)S(1)} %collective-permute-done.6), channel_id=1, source_target_pairs={{0,1},{1,0},{2,3},{3,2},{4,5},{5,4},{6,7},{7,6},{8,9},{9,8},{10,11... | collective-permute-start | bytes 602120 | tf_op jit(solution)/shard_map/ppermute | solution.py:26
  40.7 2.2 %copy-start.3 = (bf16[6144,336]{0,1:T(8,128)(2,1)S(1)}, bf16[6144,336]{0,1:T(8,128)(2,1)}, u32[]{:S(2)}) copy-start(bf16[6144,336]{0,1:T(8,128)(2,1)} %param.11) | copy-start | bytes 12386308
  42.8 2.2 %copy-start.4 = (bf16[6144,336]{0,1:T(8,128)(2,1)S(1)}, bf16[6144,336]{0,1:T(8,128)(2,1)}, u32[]{:S(2)}) copy-start(bf16[6144,336]{0,1:T(8,128)(2,1)} %param.12) | copy-start | bytes 12386308
  45.0 2.2 %copy-start.2 = (bf16[336,6144]{1,0:T(8,128)(2,1)S(1)}, bf16[336,6144]{1,0:T(8,128)(2,1)}, u32[]{:S(2)}) copy-start(bf16[336,6144]{1,0:T(8,128)(2,1)} %param.13) | copy-start | bytes 12386308
  49.2 2.2 %collective-permute-start.19 = (bf16[48,6144]{1,0:T(8,128)(2,1)S(1)}, bf16[48,6144]{1,0:T(8,128)(2,1)S(1)}, u32[]{:S(2)}, u32[]{:S(2)}) collective-permute-start(bf16[48,6144]{1,0:T(8,128)(2,1)S(1)} %slice.105), channel_id=1, source_target_pairs={{0,1},{1,0},{2,3},{3,2},{4,5},{5,4},{6,7},{7,6},{8,9},{9,8},{10,11... | collective-permute-start | bytes 1769480 | tf_op jit(solution)/shard_map/ppermute | solution.py:26
  49.9 11.0 %collective-permute-start.18 = (bf16[80,6144]{1,0:T(8,128)(2,1)S(1)}, bf16[80,6144]{1,0:T(8,128)(2,1)S(1)}, u32[]{:S(2)}, u32[]{:S(2)}) collective-permute-start(bf16[80,6144]{1,0:T(8,128)(2,1)S(1)} %slice.100), channel_id=1, source_target_pairs={{0,1},{1,0},{2,3},{3,2},{4,5},{5,4},{6,7},{7,6},{8,9},{9,8},{10,11... | collective-permute-start | bytes 2949128 | tf_op jit(solution)/shard_map/ppermute | solution.py:26
  51.6 7.2 %collective-permute-start.20 = (bf16[16,6144]{1,0:T(8,128)(2,1)S(1)}, bf16[16,6144]{1,0:T(8,128)(2,1)S(1)}, u32[]{:S(2)}, u32[]{:S(2)}) collective-permute-start(bf16[16,6144]{1,0:T(8,128)(2,1)S(1)} %get-tuple-element.42), channel_id=1, source_target_pairs={{4,0},{5,1},{8,4},{9,5},{12,8},{13,9},{14,12},{15,13},{10,14},{11,... | collective-permute-start | bytes 589832 | tf_op jit(solution)/shard_map/ppermute | solution.py:26
  53.3 6.9 %collective-permute-start.21 = (bf16[16,6144]{1,0:T(8,128)(2,1)S(1)}, bf16[16,6144]{1,0:T(8,128)(2,1)S(1)}, u32[]{:S(2)}, u32[]{:S(2)}) collective-permute-start(bf16[16,6144]{1,0:T(8,128)(2,1)S(1)} %get-tuple-element.43), channel_id=1, source_target_pairs={{0,4},{1,5},{4,8},{5,9},{8,12},{9,13},{12,14},{13,15},{14,10},{15,... | collective-permute-start | bytes 589832 | tf_op jit(solution)/shard_map/ppermute | solution.py:26
  60.3 2.9 %collective-permute-start.22 = (bf16[48,6144]{1,0:T(8,128)(2,1)S(1)}, bf16[48,6144]{1,0:T(8,128)(2,1)S(1)}, u32[]{:S(2)}, u32[]{:S(2)}) collective-permute-start(bf16[48,6144]{1,0:T(8,128)(2,1)S(1)} %slice.110), channel_id=1, source_target_pairs={{0,1},{1,0},{2,3},{3,2},{4,5},{5,4},{6,7},{7,6},{8,9},{9,8},{10,11... | collective-permute-start | bytes 1769480 | tf_op jit(solution)/shard_map/ppermute | solution.py:26
  60.3 20.4 %collective-permute-start.28 = (bf16[80,6144]{1,0:T(8,128)(2,1)S(1)}, bf16[80,6144]{1,0:T(8,128)(2,1)S(1)}, u32[]{:S(2)}, u32[]{:S(2)}) collective-permute-start(bf16[80,6144]{1,0:T(8,128)(2,1)S(1)} %slice.115), channel_id=1, source_target_pairs={{0,1},{1,0},{2,3},{3,2},{4,5},{5,4},{6,7},{7,6},{8,9},{9,8},{10,11... | collective-permute-start | bytes 2949128 | tf_op jit(solution)/shard_map/ppermute | solution.py:26
  61.1 6.9 %collective-permute-start.23 = (bf16[16,6144]{1,0:T(8,128)(2,1)S(1)}, bf16[16,6144]{1,0:T(8,128)(2,1)S(1)}, u32[]{:S(2)}, u32[]{:S(2)}) collective-permute-start(bf16[16,6144]{1,0:T(8,128)(2,1)S(1)} %fusion.17), channel_id=1, source_target_pairs={{4,0},{5,1},{8,4},{9,5},{12,8},{13,9},{14,12},{15,13},{10,14},{11,... | collective-permute-start | bytes 589832 | tf_op jit(solution)/shard_map/ppermute | solution.py:26
  62.8 6.6 %collective-permute-start.24 = (bf16[16,6144]{1,0:T(8,128)(2,1)S(1)}, bf16[16,6144]{1,0:T(8,128)(2,1)S(1)}, u32[]{:S(2)}, u32[]{:S(2)}) collective-permute-start(bf16[16,6144]{1,0:T(8,128)(2,1)S(1)} %fusion.16), channel_id=1, source_target_pairs={{0,4},{1,5},{4,8},{5,9},{8,12},{9,13},{12,14},{13,15},{14,10},{15,... | collective-permute-start | bytes 589832 | tf_op jit(solution)/shard_map/ppermute | solution.py:26
  69.4 7.9 %collective-permute-start.25 = (bf16[16,6144]{1,0:T(8,128)(2,1)S(1)}, bf16[16,6144]{1,0:T(8,128)(2,1)S(1)}, u32[]{:S(2)}, u32[]{:S(2)}) collective-permute-start(bf16[16,6144]{1,0:T(8,128)(2,1)S(1)} %get-tuple-element.51), channel_id=1, source_target_pairs={{4,0},{5,1},{8,4},{9,5},{12,8},{13,9},{14,12},{15,13},{10,14},{11,... | collective-permute-start | bytes 589832 | tf_op jit(solution)/shard_map/ppermute | solution.py:26
  71.1 18.7 %collective-permute-start.27 = (bf16[16,6144]{1,0:T(8,128)(2,1)S(1)}, bf16[16,6144]{1,0:T(8,128)(2,1)S(1)}, u32[]{:S(2)}, u32[]{:S(2)}) collective-permute-start(bf16[16,6144]{1,0:T(8,128)(2,1)S(1)} %get-tuple-element.52), channel_id=1, source_target_pairs={{0,4},{1,5},{4,8},{5,9},{8,12},{9,13},{12,14},{13,15},{14,10},{15,... | collective-permute-start | bytes 589832 | tf_op jit(solution)/shard_map/ppermute | solution.py:26
  71.5 10.0 %collective-permute-start.29 = (bf16[16,6144]{1,0:T(8,128)(2,1)S(1)}, bf16[16,6144]{1,0:T(8,128)(2,1)S(1)}, u32[]{:S(2)}, u32[]{:S(2)}) collective-permute-start(bf16[16,6144]{1,0:T(8,128)(2,1)S(1)} %get-tuple-element.55), channel_id=1, source_target_pairs={{4,0},{5,1},{8,4},{9,5},{12,8},{13,9},{14,12},{15,13},{10,14},{11,... | collective-permute-start | bytes 589832 | tf_op jit(solution)/shard_map/ppermute | solution.py:26
  73.1 7.6 %collective-permute-start.30 = (bf16[16,6144]{1,0:T(8,128)(2,1)S(1)}, bf16[16,6144]{1,0:T(8,128)(2,1)S(1)}, u32[]{:S(2)}, u32[]{:S(2)}) collective-permute-start(bf16[16,6144]{1,0:T(8,128)(2,1)S(1)} %get-tuple-element.57), channel_id=1, source_target_pairs={{0,4},{1,5},{4,8},{5,9},{8,12},{9,13},{12,14},{13,15},{14,10},{15,... | collective-permute-start | bytes 589832 | tf_op jit(solution)/shard_map/ppermute | solution.py:26
  77.4 12.4 %collective-permute-start.26 = (bf16[16,6144]{1,0:T(8,128)(2,1)S(1)}, bf16[16,6144]{1,0:T(8,128)(2,1)S(1)}, u32[]{:S(2)}, u32[]{:S(2)}) collective-permute-start(bf16[16,6144]{1,0:T(8,128)(2,1)S(1)} %fusion.19), channel_id=1, source_target_pairs={{4,0},{5,1},{8,4},{9,5},{12,8},{13,9},{14,12},{15,13},{10,14},{11,... | collective-permute-start | bytes 589832 | tf_op jit(solution)/shard_map/ppermute | solution.py:26
  81.6 6.2 %collective-permute-start.31 = (bf16[16,6144]{1,0:T(8,128)(2,1)S(1)}, bf16[16,6144]{1,0:T(8,128)(2,1)S(1)}, u32[]{:S(2)}, u32[]{:S(2)}) collective-permute-start(bf16[16,6144]{1,0:T(8,128)(2,1)S(1)} %fusion.11), channel_id=1, source_target_pairs={{4,0},{5,1},{8,4},{9,5},{12,8},{13,9},{14,12},{15,13},{10,14},{11,... | collective-permute-start | bytes 589832 | tf_op jit(solution)/shard_map/ppermute | solution.py:26
  83.2 6.0 %collective-permute-start.32 = (bf16[16,6144]{1,0:T(8,128)(2,1)S(1)}, bf16[16,6144]{1,0:T(8,128)(2,1)S(1)}, u32[]{:S(2)}, u32[]{:S(2)}) collective-permute-start(bf16[16,6144]{1,0:T(8,128)(2,1)S(1)} %add_convert_fusion), channel_id=1, source_target_pairs={{0,4},{1,5},{4,8},{5,9},{8,12},{9,13},{12,14},{13,15},{14,10},{15,... | collective-permute-start | bytes 589832 | tf_op jit(solution)/shard_map/ppermute | solution.py:26
  89.3 7.2 %collective-permute-start.34 = (bf16[16,6144]{1,0:T(8,128)(2,1)S(1)}, bf16[16,6144]{1,0:T(8,128)(2,1)S(1)}, u32[]{:S(2)}, u32[]{:S(2)}) collective-permute-start(bf16[16,6144]{1,0:T(8,128)(2,1)S(1)} %get-tuple-element.65), channel_id=1, source_target_pairs={{0,4},{1,5},{4,8},{5,9},{8,12},{9,13},{12,14},{13,15},{14,10},{15,... | collective-permute-start | bytes 589832 | tf_op jit(solution)/shard_map/ppermute | solution.py:26
  91.5 8.8 %collective-permute-start.33 = (bf16[16,6144]{1,0:T(8,128)(2,1)S(1)}, bf16[16,6144]{1,0:T(8,128)(2,1)S(1)}, u32[]{:S(2)}, u32[]{:S(2)}) collective-permute-start(bf16[16,6144]{1,0:T(8,128)(2,1)S(1)} %get-tuple-element.64), channel_id=1, source_target_pairs={{4,0},{5,1},{8,4},{9,5},{12,8},{13,9},{14,12},{15,13},{10,14},{11,... | collective-permute-start | bytes 589832 | tf_op jit(solution)/shard_map/ppermute | solution.py:26
  96.6 5.7 %collective-permute-start.35 = (bf16[16,6144]{1,0:T(8,128)(2,1)S(1)}, bf16[16,6144]{1,0:T(8,128)(2,1)S(1)}, u32[]{:S(2)}, u32[]{:S(2)}) collective-permute-start(bf16[16,6144]{1,0:T(8,128)(2,1)S(1)} %fusion.9), channel_id=1, source_target_pairs={{0,4},{1,5},{4,8},{5,9},{8,12},{9,13},{12,14},{13,15},{14,10},{15,... | collective-permute-start | bytes 589832 | tf_op jit(solution)/shard_map/ppermute | solution.py:26
  97.1 7.0 %copy-start.1 = (bf16[128,6144]{1,0:T(8,128)(2,1)S(1)}, bf16[128,6144]{1,0:T(8,128)(2,1)}, u32[]{:S(2)}) copy-start(bf16[128,6144]{1,0:T(8,128)(2,1)} %param.8) | copy-start | bytes 4718596

commit v4 on v3

--- a/solution.py
+++ b/solution.py
@@ -1,10 +1,151 @@
 import jax
 import jax.numpy as jnp
 from jax import lax
+from jax.experimental import pallas as pl
+from jax.experimental.pallas import tpu as pltpu
 from jax.sharding import PartitionSpec as P
 
 CAP = 16
 LANES = 128
+ANY = pl.BlockSpec(memory_space=pl.ANY)
+CONTRACT_ROWS = (((0,), (0,)), ((), ()))
+MARK = jax.ShapeDtypeStruct((8, LANES), jnp.float32)
+
+
+def whole(shape):
+    return pl.BlockSpec(shape, lambda j: (0,) * len(shape))
+
+
+def columns(rows, width):
+    return pl.BlockSpec((rows, width), lambda j: (0, j))
+
+
+def parts_of(d, most):
+    width = LANES
+    for w in range(LANES, most + 1, LANES):
+        if d % w == 0:
+            width = w
+    return d // width, width
+
+
+def params(megabytes):
+    return pltpu.CompilerParams(vmem_limit_bytes=megabytes << 20)
+
+
+def select_kernel(x_ref, dy_ref, ids_ref, vals_ref, wide_ref, slot_dy_ref, select_ref):
+    j = pl.program_id(0)
+    t = x_ref.shape[0]
+    width = x_ref.shape[1]
+
+    @pl.when(j == 0)
+    def _():
+        landed = ids_ref[...] == 0
+        coef = jnp.sum(
+            jnp.where(landed, vals_ref[...].astype(jnp.float32), 0.0), axis=0, keepdims=True
+        )
+        coef = coef.astype(jnp.bfloat16).astype(jnp.float32)
+        routed = jnp.max(jnp.where(landed, 1.0, 0.0), axis=0, keepdims=True)
+        upto = lax.broadcasted_iota(jnp.int32, (t, t), 0) <= lax.broadcasted_iota(
+            jnp.int32, (t, t), 1
+        )
+        seen = jnp.dot(
+            jnp.broadcast_to(routed, (CAP, t)).astype(jnp.bfloat16),
+            jnp.where(upto, 1.0, 0.0).astype(jnp.bfloat16),
+            preferred_element_type=jnp.float32,
+        )
+        slot = lax.broadcasted_iota(jnp.int32, (CAP, t), 0).astype(jnp.float32) + 1.0
+        select = jnp.where((seen == slot) & (routed > 0.0), 1.0, 0.0)
+        select_ref[...] = select.astype(jnp.bfloat16)
+        slot_coef = jnp.sum(select * coef, axis=1, keepdims=True)
+        wide_ref[:, wide_ref.shape[1] - LANES :] = jnp.broadcast_to(
+            slot_coef, (CAP, LANES)
+        ).astype(jnp.bfloat16)
+
+    select = select_ref[...]
+    at = pl.multiple_of(j * width, LANES)
+    wide_ref[:, pl.ds(at, width)] = jnp.dot(
+        select, x_ref[...], preferred_element_type=jnp.float32
+    ).astype(jnp.bfloat16)
+    slot_dy_ref[...] = jnp.dot(
+        select, dy_ref[...], preferred_element_type=jnp.float32
+    ).astype(jnp.bfloat16)
+
+
+def select_rows(tokens, out_grad, expert_ids, gate_vals):
+    t, d = tokens.shape
+    top = expert_ids.shape[1]
+    parts, width = parts_of(d, 2048)
+    return pl.pallas_call(
+        select_kernel,
+        grid=(parts,),
+        in_specs=[columns(t, width), columns(t, width), whole((top, t)), whole((top, t))],
+        out_specs=[whole((CAP, d + LANES)), columns(CAP, width), whole((CAP, t))],
+        out_shape=[
+            jax.ShapeDtypeStruct((CAP, d + LANES), jnp.bfloat16),
+            jax.ShapeDtypeStruct((CAP, d), jnp.bfloat16),
+            jax.ShapeDtypeStruct((CAP, t), jnp.bfloat16),
+        ],
+        compiler_params=params(56),
+        cost_estimate=pl.CostEstimate(
+            flops=4 * CAP * t * d, bytes_accessed=4 * t * d, transcendentals=0
+        ),
+    )(tokens, out_grad, expert_ids.T, gate_vals.T)
+
+
+def spread_kernel(marks, own_ref, left_ref, right_ref, select_ref, *refs):
+    total = (
+        own_ref[...] + left_ref[...].astype(jnp.float32) + right_ref[...].astype(jnp.float32)
+    )
+    refs[marks][...] = lax.dot_general(
+        select_ref[...],
+        total.astype(jnp.bfloat16),
+        CONTRACT_ROWS,
+        preferred_element_type=jnp.float32,
+    ).astype(jnp.bfloat16)
+
+
+def spread_rows(near, carry, select, marks):
+    d = near.shape[1]
+    t = select.shape[1]
+    parts, width = parts_of(d, 2048)
+    return pl.pallas_call(
+        lambda *refs: spread_kernel(len(marks), *refs),
+        grid=(parts,),
+        in_specs=[columns(CAP, width)] * 3 + [whole((CAP, t))] + [ANY] * len(marks),
+        out_specs=columns(t, width),
+        out_shape=jax.ShapeDtypeStruct((t, d), jnp.bfloat16),
+        compiler_params=params(16),
+        cost_estimate=pl.CostEstimate(
+            flops=2 * CAP * t * d, bytes_accessed=2 * t * d, transcendentals=0
+        ),
+    )(near, carry["l"], carry["r"], select, *marks)
+
+
+def grads_kernel(sides, marks, rows_ref, *refs):
+    outs = refs[sides + marks :]
+    rows = rows_ref[...]
+    for i in range(sides):
+        outs[i][...] = lax.dot_general(
+            refs[i][...], rows, CONTRACT_ROWS, preferred_element_type=jnp.float32
+        ).astype(jnp.bfloat16)
+    outs[sides][...] = jnp.zeros(outs[sides].shape, jnp.float32)
+
+
+def weight_grads(rows, sides, d, marks):
+    r, f = sides[0].shape
+    parts, width = parts_of(d, 1024)
+    n = len(sides)
+    return pl.pallas_call(
+        lambda *refs: grads_kernel(n, len(marks), *refs),
+        grid=(parts,),
+        in_specs=[columns(r, width)] + [whole((r, f))] * n + [ANY] * len(marks),
+        out_specs=[columns(f, width)] * n + [whole(MARK.shape)],
+        out_shape=[jax.ShapeDtypeStruct((f, d), jnp.bfloat16)] * n + [MARK],
+        compiler_params=params(24),
+        cost_estimate=pl.CostEstimate(
+            flops=2 * n * r * f * d, bytes_accessed=2 * d * (r + n * f), transcendentals=0
+        ),
+    )(rows, *sides, *marks)
 
 
 def ring_of(n):
@@ -73,10 +214,6 @@
     def send(blocks):
         return {w: permute(b, left_pairs if w == "l" else right_pairs) for w, b in blocks.items()}
 
-    def final(total, carry):
-        done = block_of(total, 0) + carry["l"].astype(jnp.float32) + carry["r"].astype(jnp.float32)
-        return done.astype(jnp.bfloat16)
-
     def tie(value, blocks):
         ways = list(blocks)
         tied = lax.optimization_barrier((value, *[blocks[w] for w in ways]))
@@ -84,21 +221,7 @@
 
     def per_device(tokens, out_grad, expert_ids, gate_vals, w_gate, w_up, w_down):
         d = tokens.shape[1]
-        landed = expert_ids == 0
-        coef = jnp.sum(jnp.where(landed, gate_vals.astype(jnp.float32), 0.0), axis=1).astype(
-            jnp.bfloat16
-        )
-        routed = jnp.any(landed, axis=1)
-        slot = jnp.cumsum(routed.astype(jnp.int32)) - 1
-        select = (slot[None, :] == jnp.arange(CAP, dtype=jnp.int32)[:, None]) & routed[None, :]
-        select_bf = select.astype(jnp.bfloat16)
-        wide = jnp.concatenate(
-            [tokens, jnp.broadcast_to(coef[:, None], (coef.shape[0], LANES))], axis=1
-        )
-        slot_x = jnp.dot(select_bf, wide, preferred_element_type=jnp.float32).astype(jnp.bfloat16)
-        slot_dy = jnp.dot(select_bf, out_grad, preferred_element_type=jnp.float32).astype(
-            jnp.bfloat16
-        )
+        slot_x, slot_dy, select = select_rows(tokens, out_grad, expert_ids, gate_vals)
         rows_wide, rows_dy = gather_rows(slot_x, slot_dy)
         rows_x = rows_wide[:, :d]
         coef_rows = rows_wide[:, d : d + 1].astype(jnp.float32)
@@ -128,34 +251,27 @@
         dx_total = pair_sum(dx_rows[:half], dx_sent)
         dx_carry = {}
 
-        grads = []
-        work = [(rows_x, dgate), (rows_x, dup), (hidden, rows_dy)]
         for at in range(2, steps + 2):
+            out_blocks = {}
             if at <= steps:
-                out_carry.update(send(wave(out_total, out_carry, at, "l")))
-            blocks = wave(dx_total, dx_carry, at - 1, "r")
+                out_blocks = wave(out_total, out_carry, at, "l")
+                out_carry.update(send(out_blocks))
+            dx_blocks = wave(dx_total, dx_carry, at - 1, "r")
+            dx_carry.update(send(dx_blocks))
             if at == 2:
-                far, out_carry = tie(dx_total[1], out_carry)
-                dx_total = (dx_total[0], far)
-            if work:
-                lhs, rhs = work.pop(0)
-                rhs, blocks = tie(rhs, blocks)
-                grads.append(jnp.dot(lhs.T, rhs, preferred_element_type=jnp.float32))
-            dx_carry.update(send(blocks))
-        for lhs, rhs in work:
-            grads.append(jnp.dot(lhs.T, rhs, preferred_element_type=jnp.float32))
-        grad_gate, grad_up, grad_down = grads
-        out_slots = final(out_total, out_carry)
-        dx_slots = final(dx_total, dx_carry)
-        mixed = jnp.dot(select_bf.T, out_slots, preferred_element_type=jnp.float32)
-        grad_tokens = jnp.dot(select_bf.T, dx_slots, preferred_element_type=jnp.float32)
-        return (
-            mixed.astype(jnp.bfloat16),
-            grad_tokens.astype(jnp.bfloat16),
-            grad_gate.astype(jnp.bfloat16),
-            grad_up.astype(jnp.bfloat16),
-            grad_down.astype(jnp.bfloat16),
-        )
+                marks = [*out_blocks.values(), *dx_blocks.values()]
+                grad_gate, grad_up, mark = weight_grads(rows_wide, [dgate, dup], d, marks)
+                mark, out_carry = tie(mark, out_carry)
+            if at == min(3, steps + 1):
+                marks = [*out_blocks.values(), *dx_blocks.values(), mark]
+                grad_down, mark = weight_grads(rows_dy, [hidden], d, marks)
+                if at < steps:
+                    mark, out_carry = tie(mark, out_carry)
+                else:
+                    mark, dx_carry = tie(mark, dx_carry)
+        mixed = spread_rows(out_total[0], out_carry, select, [mark])
+        grad_tokens = spread_rows(dx_total[0], dx_carry, select, [])
+        return (mixed, grad_tokens, grad_gate.T, grad_up.T, grad_down)
 
     return per_device
 

time: 104 us -> 99.1 us (0.953)
  Pallas kernels: 0 us -> 17.7 us
  matrix products: 24.6 us -> 10.9 us
  waiting for transfers between devices: 40 us -> 32 us
  other arithmetic: 2.88 us -> 1.09 us
    pallas_call x0 -> x5, Pallas kernels: none -> 17.7 us  [the longest x2 9.3 us: weight_grads(): pl.pallas_call(lambda *refs: grads_kernel(n, len(marks), *refs), grid=(pa...]
    dot_general x7 -> x0, matrix products: 15.3 us -> none  [the longest x3 9.71 us: per_device(): grads.append(jnp.dot(lhs.T, rhs, preferred_element_type=jnp.float32))]
    ppermute x36, waiting for transfers between devices: 40 us -> 32 us  [permute(): return lax.ppermute(x, 'et', pairs)]
  transfers between devices with their start and end apart: 36 -> 36, of which waited for: 21 -> 17; matrix products, arithmetic and copies ran while one was open for 20% -> 10% of each run, Pallas kernels for 0% -> 12%
where the time goes in v4:
time: 99.1 us; the launch traced here: 98.7 us
  waiting for transfers between devices  32 us (32%)
  starting transfers between devices  31.4 us (32%)
  Pallas kernels  17.7 us (18%)
  matrix products  10.9 us (11%)
  local copies, waits for them, and re-layouts  4.66 us (5%)
  other arithmetic  1.09 us (1%)
  between operations  1.02 us (1%)
    ppermute x36, waiting for transfers between devices, permute(): return lax.ppermute(x, 'et', pairs)  32 us
    ppermute x36, starting transfers between devices, permute(): return lax.ppermute(x, 'et', pairs)  31.4 us
    pallas_call x2, Pallas kernels, weight_grads(): pl.pallas_call(lambda *refs: grads_kernel(n, len(marks), *refs), grid=(pa...  9.3 us
    pallas_call x2, Pallas kernels, spread_rows(): pl.pallas_call(lambda *refs: spread_kernel(len(marks), *refs), grid=(part...  4.57 us
    unnamed x24, local copies, waits for them, and re-layouts  3.93 us
    pallas_call x1, Pallas kernels, select_rows(): pl.pallas_call(select_kernel, grid=(parts,), in_specs=[columns(t, width),...  3.83 us
  transfers between devices with their start and end apart: 36, of which 17 were waited for; matrix products, arithmetic and copies ran while one was open for 10% of the time, Pallas kernels for 12%

profile of v4, /device:TPU:0, one launch (start us, length us, event | category | flops | bytes accessed | tf_op | source)
XLA Modules:
  0.0 98.7 jit_solution(9229060189332523833)
XLA Ops:
  0.6 3.8 %shard_map.110 = (bf16[16,6272]{1,0:T(8,128)(2,1)}, bf16[16,6144]{1,0:T(8,128)(2,1)}, bf16[16,128]{1,0:T(8,128)(2,1)}) custom-call(bf16[128,6144]{1,0:T(8,128)(2,1)} %x_ref.1, bf16[128,6144]{1,0:T(8,128)(2,1)} %dy_ref.1, s32[4,128]{1,0:T(4,128)} %bitcast.14, bf16[4,128]{1,0:T(4,128)(2,1)} %bitcast.15), custom_call_target="tpu_custom_call" | custom-call | flops 50331648 | bytes 3145728 | tf_op jit(solution)/shard_map/pallas_call | solution.py:78
  4.5 3.0 %collective-permute-start.10 = (bf16[16,6144]{1,0:T(8,128)(2,1)}, bf16[16,6144]{1,0:T(8,128)(2,1)S(1)}, u32[]{:S(2)}, u32[]{:S(2)}) collective-permute-start(bf16[16,6144]{1,0:T(8,128)(2,1)} %get-tuple-element.40), channel_id=1, source_target_pairs={{4,0},{5,1},{8,4},{9,5},{12,8},{13,9},{14,12},{15,13},{10,14},{11,... | collective-permute-start | bytes 589832 | tf_op jit(solution)/shard_map/ppermute | solution.py:167
  7.6 1.9 %collective-permute-start.1 = (bf16[16,6272]{1,0:T(8,128)(2,1)}, bf16[16,6272]{1,0:T(8,128)(2,1)S(1)}, u32[]{:S(2)}, u32[]{:S(2)}) collective-permute-start(bf16[16,6272]{1,0:T(8,128)(2,1)} %get-tuple-element.39), channel_id=1, source_target_pairs={{4,0},{5,1},{8,4},{9,5},{12,8},{13,9},{14,12},{15,13},{10,14},{11,... | collective-permute-start | bytes 602120 | tf_op jit(solution)/shard_map/ppermute | solution.py:167
  9.6 1.0 %constant_dynamic-update-slice_fusion.6 = (bf16[112,6272]{1,0:T(8,128)(2,1)S(1)}, bf16[256,6272]{1,0:T(8,128)(2,1)S(1)}) fusion(bf16[16,6272]{1,0:T(8,128)(2,1)} %get-tuple-element.39), kind=kLoop, calls=%fused_computation.44 | loop fusion | bytes 602112
  10.6 1.0 constant_dynamic-update-slice_fusion.23
  11.6 1.9 %collective-permute-done.10 = bf16[16,6144]{1,0:T(8,128)(2,1)S(1)} collective-permute-done((bf16[16,6144]{1,0:T(8,128)(2,1)}, bf16[16,6144]{1,0:T(8,128)(2,1)S(1)}, u32[]{:S(2)}, u32[]{:S(2)}) %collective-permute-start.10) | collective-permute-done | bytes 196640 | tf_op jit(solution)/shard_map/ppermute | solution.py:167
  13.5 2.0 %collective-permute-start.12 = (bf16[16,6144]{1,0:T(8,128)(2,1)S(1)}, bf16[16,6144]{1,0:T(8,128)(2,1)S(1)}, u32[]{:S(2)}, u32[]{:S(2)}) collective-permute-start(bf16[16,6144]{1,0:T(8,128)(2,1)S(1)} %collective-permute-done.10), channel_id=1, source_target_pairs={{4,0},{5,1},{8,4},{9,5},{12,8},{13,9},{14,12},{15,13},{10,14},{11,... | collective-permute-start | bytes 589832 | tf_op jit(solution)/shard_map/ppermute | solution.py:167
  15.6 2.1 %collective-permute-done.1 = bf16[16,6272]{1,0:T(8,128)(2,1)S(1)} collective-permute-done((bf16[16,6272]{1,0:T(8,128)(2,1)}, bf16[16,6272]{1,0:T(8,128)(2,1)S(1)}, u32[]{:S(2)}, u32[]{:S(2)}) %collective-permute-start.1) | collective-permute-done | bytes 200736 | tf_op jit(solution)/shard_map/ppermute | solution.py:167
  17.8 2.0 %collective-permute-start.3 = (bf16[16,6272]{1,0:T(8,128)(2,1)S(1)}, bf16[16,6272]{1,0:T(8,128)(2,1)S(1)}, u32[]{:S(2)}, u32[]{:S(2)}) collective-permute-start(bf16[16,6272]{1,0:T(8,128)(2,1)S(1)} %collective-permute-done.1), channel_id=1, source_target_pairs={{4,0},{5,1},{8,4},{9,5},{12,8},{13,9},{14,12},{15,13},{10,14},{11,... | collective-permute-start | bytes 602120 | tf_op jit(solution)/shard_map/ppermute | solution.py:167
  19.9 2.0 %collective-permute-done.12 = bf16[16,6144]{1,0:T(8,128)(2,1)S(1)} collective-permute-done((bf16[16,6144]{1,0:T(8,128)(2,1)S(1)}, bf16[16,6144]{1,0:T(8,128)(2,1)S(1)}, u32[]{:S(2)}, u32[]{:S(2)}) %collective-permute-start.12) | collective-permute-done | bytes 196640 | tf_op jit(solution)/shard_map/ppermute | solution.py:167
  22.0 2.0 %collective-permute-start.14 = (bf16[16,6144]{1,0:T(8,128)(2,1)S(1)}, bf16[16,6144]{1,0:T(8,128)(2,1)S(1)}, u32[]{:S(2)}, u32[]{:S(2)}) collective-permute-start(bf16[16,6144]{1,0:T(8,128)(2,1)S(1)} %collective-permute-done.12), channel_id=1, source_target_pairs={{4,0},{5,1},{8,4},{9,5},{12,8},{13,9},{14,12},{15,13},{10,14},{11,... | collective-permute-start | bytes 589832 | tf_op jit(solution)/shard_map/ppermute | solution.py:167
  24.2 2.1 %collective-permute-done.3 = bf16[16,6272]{1,0:T(8,128)(2,1)S(1)} collective-permute-done((bf16[16,6272]{1,0:T(8,128)(2,1)S(1)}, bf16[16,6272]{1,0:T(8,128)(2,1)S(1)}, u32[]{:S(2)}, u32[]{:S(2)}) %collective-permute-start.3) | collective-permute-done | bytes 200736 | tf_op jit(solution)/shard_map/ppermute | solution.py:167
  26.3 2.0 %collective-permute-start.5 = (bf16[16,6272]{1,0:T(8,128)(2,1)S(1)}, bf16[16,6272]{1,0:T(8,128)(2,1)S(1)}, u32[]{:S(2)}, u32[]{:S(2)}) collective-permute-start(bf16[16,6272]{1,0:T(8,128)(2,1)S(1)} %collective-permute-done.3), channel_id=1, source_target_pairs={{4,0},{5,1},{8,4},{9,5},{12,8},{13,9},{14,12},{15,13},{10,14},{11,... | collective-permute-start | bytes 602120 | tf_op jit(solution)/shard_map/ppermute | solution.py:167
  28.5 4.1 %collective-permute-done.13 = bf16[16,6144]{1,0:T(8,128)(2,1)S(1)} collective-permute-done((bf16[16,6144]{1,0:T(8,128)(2,1)S(1)}, bf16[16,6144]{1,0:T(8,128)(2,1)S(1)}, u32[]{:S(2)}, u32[]{:S(2)}) %collective-permute-start.13) | collective-permute-done | bytes 196640 | tf_op jit(solution)/shard_map/ppermute | solution.py:167
  32.7 1.6 %collective-permute-start.15 = (bf16[16,6144]{1,0:T(8,128)(2,1)S(1)}, bf16[16,6144]{1,0:T(8,128)(2,1)S(1)}, u32[]{:S(2)}, u32[]{:S(2)}) collective-permute-start(bf16[16,6144]{1,0:T(8,128)(2,1)S(1)} %collective-permute-done.14), channel_id=1, source_target_pairs={{4,0},{5,1},{8,4},{9,5},{12,8},{13,9},{14,12},{15,13},{10,14},{11,... | collective-permute-start | bytes 589832 | tf_op jit(solution)/shard_map/ppermute | solution.py:167
  34.3 1.1 %collective-permute-done.4 = bf16[16,6272]{1,0:T(8,128)(2,1)S(1)} collective-permute-done((bf16[16,6272]{1,0:T(8,128)(2,1)S(1)}, bf16[16,6272]{1,0:T(8,128)(2,1)S(1)}, u32[]{:S(2)}, u32[]{:S(2)}) %collective-permute-start.4) | collective-permute-done | bytes 200736 | tf_op jit(solution)/shard_map/ppermute | solution.py:167
  35.5 0.5 collective-permute-start.6
  36.0 4.0 %collective-permute-done.15 = bf16[16,6144]{1,0:T(8,128)(2,1)S(1)} collective-permute-done((bf16[16,6144]{1,0:T(8,128)(2,1)S(1)}, bf16[16,6144]{1,0:T(8,128)(2,1)S(1)}, u32[]{:S(2)}, u32[]{:S(2)}) %collective-permute-start.15) | collective-permute-done | bytes 196640 | tf_op jit(solution)/shard_map/ppermute | solution.py:167
  40.0 2.9 %collective-permute-done.6 = bf16[16,6272]{1,0:T(8,128)(2,1)S(1)} collective-permute-done((bf16[16,6272]{1,0:T(8,128)(2,1)S(1)}, bf16[16,6272]{1,0:T(8,128)(2,1)S(1)}, u32[]{:S(2)}, u32[]{:S(2)}) %collective-permute-start.6) | collective-permute-done | bytes 200736 | tf_op jit(solution)/shard_map/ppermute | solution.py:167
  43.1 0.2 constant_dynamic-update-slice_fusion.8
  43.3 1.0 %collective-permute-done.8 = bf16[16,6272]{1,0:T(8,128)(2,1)S(1)} collective-permute-done((bf16[16,6272]{1,0:T(8,128)(2,1)S(1)}, bf16[16,6272]{1,0:T(8,128)(2,1)S(1)}, u32[]{:S(2)}, u32[]{:S(2)}) %collective-permute-start.8) | collective-permute-done | bytes 200736 | tf_op jit(solution)/shard_map/ppermute | solution.py:167
  44.5 0.6 copy-done.2
  45.1 1.8 %fusion.2 = f32[256,336]{1,0:T(8,128)S(1)} fusion(bf16[6144,336]{0,1:T(8,128)(2,1)S(1)} %copy-done.2, bf16[256,6272]{1,0:T(8,128)(2,1)S(1)} %constant_dynamic-update-slice_fusion.7.refs_0_), kind=kOutput, calls=%fused_computation.5 | convolution fusion | flops 1056964608 | bytes 7618560 | tf_op jit(solution)/shard_map/dot_general | solution.py:230
  46.9 0.4 copy-done.3
  47.3 1.8 %multiply_convert_fusion.2 = (bf16[256,336]{1,0:T(8,128)(2,1)S(1)}, f32[256,336]{1,0:T(8,128)S(1)}) fusion(f32[256]{0:T(256)S(1)} %convert_reduce_fusion, f32[256,336]{1,0:T(8,128)S(1)} %fusion.2, bf16[6144,336]{0,1:T(8,128)(2,1)S(1)} %copy-done.3, bf16[256,6272]{1,0:T(8,128)(2,1)S(1)} %constant_dynamic-update-slice_fusion.7.refs_0_), kind=kOutput, calls=%fused_computation.34 | convolution fusion | flops 1057566720 | bytes 8184832 | tf_op jit(solution)/shard_map/dot_general | solution.py:231
  49.1 0.4 copy-done.1
  49.4 1.8 %fusion.19 = f32[256,6144]{1,0:T(8,128)S(1)} fusion(bf16[256,336]{1,0:T(8,128)(2,1)S(1)} %get-tuple-element.115.refs_1_, bf16[336,6144]{1,0:T(8,128)(2,1)S(1)} %copy-done.1), kind=kOutput, calls=%fused_computation.76 | convolution fusion | flops 1056964608 | bytes 10592256 | tf_op jit(solution)/shard_map/dot_general | solution.py:235
  51.2 0.2 slice.180
  51.6 0.6 collective-permute-start.19
  52.2 1.9 %multiply_convert_fusion = (bf16[256,336]{1,0:T(8,128)(2,1)S(1)}, bf16[256,336]{1,0:T(8,128)(2,1)S(1)}) fusion(f32[256,336]{1,0:T(8,128)S(1)} %fusion.2, f32[256,336]{1,0:T(8,128)S(1)} %get-tuple-element.116, bf16[256,6144]{1,0:T(8,128)(2,1)S(1)} %constant_dynamic-update-slice_fusion.24.refs_0_, bf16[336,6144]{1,0:T(8,128)(2,1)S(1)} %copy-done.1, ...), kind=kOutput, calls=%fused_computation.32 | convolution fusion | flops 1058168832 | bytes 8307712 | tf_op jit(solution)/shard_map/dot_general | solution.py:240
  54.1 0.2 fusion.16
  54.3 1.6 %collective-permute-start.20 = (bf16[16,6144]{1,0:T(8,128)(2,1)S(1)}, bf16[16,6144]{1,0:T(8,128)(2,1)S(1)}, u32[]{:S(2)}, u32[]{:S(2)}) collective-permute-start(bf16[16,6144]{1,0:T(8,128)(2,1)S(1)} %get-tuple-element.46), channel_id=1, source_target_pairs={{4,0},{5,1},{8,4},{9,5},{12,8},{13,9},{14,12},{15,13},{10,14},{11,... | collective-permute-start | bytes 589832 | tf_op jit(solution)/shard_map/ppermute | solution.py:167
  55.9 0.5 collective-permute-start.21
  56.4 1.8 %fusion.20 = f32[256,6144]{1,0:T(8,128)S(1)} fusion(bf16[256,336]{1,0:T(8,128)(2,1)S(1)} %get-tuple-element.45.refs_1_, bf16[6144,336]{0,1:T(8,128)(2,1)S(1)} %copy-done.2), kind=kOutput, calls=%fused_computation.77 | convolution fusion | flops 1056964608 | bytes 10592256 | tf_op jit(solution)/shard_map/dot_general | solution.py:246
  58.2 1.8 %convolution_add_fusion = f32[256,6144]{1,0:T(8,128)S(1)} fusion(f32[256,6144]{1,0:T(8,128)S(1)} %fusion.20, bf16[256,336]{1,0:T(8,128)(2,1)S(1)} %get-tuple-element.81.refs_2_, bf16[6144,336]{0,1:T(8,128)(2,1)S(1)} %copy-done.3), kind=kOutput, calls=%fused_computation | convolution fusion | flops 1058537472 | bytes 16883712 | tf_op jit(solution)/shard_map/dot_general | solution.py:246
  60.0 0.2 slice.179
  60.2 1.4 %collective-permute-done.20 = bf16[16,6144]{1,0:T(8,128)(2,1)S(1)} collective-permute-done((bf16[16,6144]{1,0:T(8,128)(2,1)S(1)}, bf16[16,6144]{1,0:T(8,128)(2,1)S(1)}, u32[]{:S(2)}, u32[]{:S(2)}) %collective-permute-start.20) | collective-permute-done | bytes 196640 | tf_op jit(solution)/shard_map/ppermute | solution.py:167
  61.6 1.3 %collective-permute-done.21 = bf16[16,6144]{1,0:T(8,128)(2,1)S(1)} collective-permute-done((bf16[16,6144]{1,0:T(8,128)(2,1)S(1)}, bf16[16,6144]{1,0:T(8,128)(2,1)S(1)}, u32[]{:S(2)}, u32[]{:S(2)}) %collective-permute-start.21) | collective-permute-done | bytes 196640 | tf_op jit(solution)/shard_map/ppermute | solution.py:167
  63.1 0.5 collective-permute-start.25
  63.6 0.2 slice_add_fusion.1.refs_0_
  63.8 1.6 %collective-permute-start.23 = (bf16[16,6144]{1,0:T(8,128)(2,1)S(1)}, bf16[16,6144]{1,0:T(8,128)(2,1)S(1)}, u32[]{:S(2)}, u32[]{:S(2)}) collective-permute-start(bf16[16,6144]{1,0:T(8,128)(2,1)S(1)} %fusion.11.refs_3_), channel_id=1, source_target_pairs={{4,0},{5,1},{8,4},{9,5},{12,8},{13,9},{14,12},{15,13},{10,14},{11,... | collective-permute-start | bytes 589832 | tf_op jit(solution)/shard_map/ppermute | solution.py:167
  65.5 0.4 collective-permute-start.24
  65.9 0.1 fusion.15
  66.1 1.6 %collective-permute-start.26 = (bf16[16,6144]{1,0:T(8,128)(2,1)S(1)}, bf16[16,6144]{1,0:T(8,128)(2,1)S(1)}, u32[]{:S(2)}, u32[]{:S(2)}) collective-permute-start(bf16[16,6144]{1,0:T(8,128)(2,1)S(1)} %get-tuple-element.53.refs_5_), channel_id=1, source_target_pairs={{4,0},{5,1},{8,4},{9,5},{12,8},{13,9},{14,12},{15,13},{10,14},{11,... | collective-permute-start | bytes 589832 | tf_op jit(solution)/shard_map/ppermute | solution.py:167
  67.7 0.4 collective-permute-start.27
  68.2 5.1 %shard_map.111 = (bf16[336,6144]{1,0:T(8,128)(2,1)}, bf16[336,6144]{1,0:T(8,128)(2,1)}, f32[8,128]{1,0:T(8,128)S(1)}) custom-call(bf16[256,6272]{1,0:T(8,128)(2,1)S(1)} %constant_dynamic-update-slice_fusion.7.refs_0_, bf16[256,336]{1,0:T(8,128)(2,1)S(1)} %get-tuple-element.45.refs_1_, bf16[256,336]{1,0:T(8,128)(2,1)S(1)} %get-tuple-element.81.refs_2_, ...), custom_call_target="tpu_custom_call" | custom-call | flops 2113929216 | bytes 11403264 | tf_op jit(solution)/shard_map/pallas_call | solution.py:138
  73.4 1.6 %collective-permute-start.28 = (bf16[16,6144]{1,0:T(8,128)(2,1)S(1)}, bf16[16,6144]{1,0:T(8,128)(2,1)S(1)}, u32[]{:S(2)}, u32[]{:S(2)}) collective-permute-start(bf16[16,6144]{1,0:T(8,128)(2,1)S(1)} %get-tuple-element.58.refs_2_), channel_id=1, source_target_pairs={{4,0},{5,1},{8,4},{9,5},{12,8},{13,9},{14,12},{15,13},{10,14},{11,... | collective-permute-start | bytes 589832 | tf_op jit(solution)/shard_map/ppermute | solution.py:167
  75.0 0.4 collective-permute-start.29
  75.5 0.8 collective-permute-done.27
  76.3 0.2 slice_add_fusion.refs_0_
  76.6 1.6 %collective-permute-start.31 = (bf16[16,6144]{1,0:T(8,128)(2,1)S(1)}, bf16[16,6144]{1,0:T(8,128)(2,1)S(1)}, u32[]{:S(2)}, u32[]{:S(2)}) collective-permute-start(bf16[16,6144]{1,0:T(8,128)(2,1)S(1)} %fusion.8.refs_4_), channel_id=1, source_target_pairs={{4,0},{5,1},{8,4},{9,5},{12,8},{13,9},{14,12},{15,13},{10,14},{11,... | collective-permute-start | bytes 589832 | tf_op jit(solution)/shard_map/ppermute | solution.py:167
  78.2 0.4 collective-permute-start.32
  78.7 4.2 %shard_map.112 = (bf16[336,6144]{1,0:T(8,128)(2,1)}, f32[8,128]{1,0:T(8,128)S(1)}) custom-call(bf16[256,6144]{1,0:T(8,128)(2,1)S(1)} %constant_dynamic-update-slice_fusion.24.refs_0_, bf16[256,336]{1,0:T(8,128)(2,1)S(1)} %get-tuple-element.115.refs_1_, bf16[16,6144]{1,0:T(8,128)(2,1)S(1)} %get-tuple-element.58.refs_2_, ...), custom_call_target="tpu_custom_call" | custom-call | flops 1056964608 | bytes 7274496 | tf_op jit(solution)/shard_map/pallas_call | solution.py:138
  82.9 0.6 collective-permute-done.31
  83.4 1.5 %collective-permute-done.32 = bf16[16,6144]{1,0:T(8,128)(2,1)S(1)} collective-permute-done((bf16[16,6144]{1,0:T(8,128)(2,1)S(1)}, bf16[16,6144]{1,0:T(8,128)(2,1)S(1)}, u32[]{:S(2)}, u32[]{:S(2)}) %collective-permute-start.32) | collective-permute-done | bytes 196640 | tf_op jit(solution)/shard_map/ppermute | solution.py:167
  85.0 0.5 collective-permute-start.34
  85.5 1.6 %collective-permute-start.30 = (bf16[16,6144]{1,0:T(8,128)(2,1)S(1)}, bf16[16,6144]{1,0:T(8,128)(2,1)S(1)}, u32[]{:S(2)}, u32[]{:S(2)}) collective-permute-start(bf16[16,6144]{1,0:T(8,128)(2,1)S(1)} %fusion.13), channel_id=1, source_target_pairs={{4,0},{5,1},{8,4},{9,5},{12,8},{13,9},{14,12},{15,13},{10,14},{11,... | collective-permute-start | bytes 589832 | tf_op jit(solution)/shard_map/ppermute | solution.py:167
  87.1 1.4 %collective-permute-start.33 = (bf16[16,6144]{1,0:T(8,128)(2,1)S(1)}, bf16[16,6144]{1,0:T(8,128)(2,1)S(1)}, u32[]{:S(2)}, u32[]{:S(2)}) collective-permute-start(bf16[16,6144]{1,0:T(8,128)(2,1)S(1)} %get-tuple-element.68), channel_id=1, source_target_pairs={{4,0},{5,1},{8,4},{9,5},{12,8},{13,9},{14,12},{15,13},{10,14},{11,... | collective-permute-start | bytes 589832 | tf_op jit(solution)/shard_map/ppermute | solution.py:167
  88.5 2.1 %collective-permute-done.34 = bf16[16,6144]{1,0:T(8,128)(2,1)S(1)} collective-permute-done((bf16[16,6144]{1,0:T(8,128)(2,1)S(1)}, bf16[16,6144]{1,0:T(8,128)(2,1)S(1)}, u32[]{:S(2)}, u32[]{:S(2)}) %collective-permute-start.34) | collective-permute-done | bytes 196640 | tf_op jit(solution)/shard_map/ppermute | solution.py:167
  90.7 0.5 collective-permute-start.35
  91.2 1.8 %collective-permute-done.30.refs_1_ = bf16[16,6144]{1,0:T(8,128)(2,1)S(1)} collective-permute-done((bf16[16,6144]{1,0:T(8,128)(2,1)S(1)}, bf16[16,6144]{1,0:T(8,128)(2,1)S(1)}, u32[]{:S(2)}, u32[]{:S(2)}) %collective-permute-start.30) | collective-permute-done | bytes 196640 | tf_op jit(solution)/shard_map/ppermute | solution.py:167
  93.0 2.3 %shard_map.113 = bf16[128,6144]{1,0:T(8,128)(2,1)} custom-call(f32[80,6144]{1,0:T(8,128)S(1)} %slice_add_fusion.1.refs_0_, bf16[16,6144]{1,0:T(8,128)(2,1)S(1)} %collective-permute-done.30.refs_1_, bf16[16,6144]{1,0:T(8,128)(2,1)S(1)} %collective-permute-done.29.refs_2_, bf16[16,128]{1,0:T(8,128)(2,1)S(1)} %copy-done, f32[8,128]{1,0:T(8,128)S(1)} %get-tuple-element.67.refs_4_), custom_call_target="tpu_custom_call" | custom-call | flops 25165824 | bytes 1572864 | tf_op jit(solution)/shard_map/pallas_call | solution.py:111
  95.3 1.1 %collective-permute-done.35.refs_2_ = bf16[16,6144]{1,0:T(8,128)(2,1)S(1)} collective-permute-done((bf16[16,6144]{1,0:T(8,128)(2,1)S(1)}, bf16[16,6144]{1,0:T(8,128)(2,1)S(1)}, u32[]{:S(2)}, u32[]{:S(2)}) %collective-permute-start.35) | collective-permute-done | bytes 196640 | tf_op jit(solution)/shard_map/ppermute | solution.py:167
  96.5 2.3 %shard_map.114 = bf16[128,6144]{1,0:T(8,128)(2,1)} custom-call(f32[80,6144]{1,0:T(8,128)S(1)} %slice_add_fusion.refs_0_, bf16[16,6144]{1,0:T(8,128)(2,1)S(1)} %collective-permute-done.33.refs_1_, bf16[16,6144]{1,0:T(8,128)(2,1)S(1)} %collective-permute-done.35.refs_2_, bf16[16,128]{1,0:T(8,128)(2,1)S(1)} %copy-done), custom_call_target="tpu_custom_call" | custom-call | flops 25165824 | bytes 1572864 | tf_op jit(solution)/shard_map/pallas_call | solution.py:111
  (68 shorter events, 2.4 us)
Async XLA Ops:
  4.5 9.0 %collective-permute-start.10 = (bf16[16,6144]{1,0:T(8,128)(2,1)}, bf16[16,6144]{1,0:T(8,128)(2,1)S(1)}, u32[]{:S(2)}, u32[]{:S(2)}) collective-permute-start(bf16[16,6144]{1,0:T(8,128)(2,1)} %get-tuple-element.40), channel_id=1, source_target_pairs={{4,0},{5,1},{8,4},{9,5},{12,8},{13,9},{14,12},{15,13},{10,14},{11,... | collective-permute-start | bytes 589832 | tf_op jit(solution)/shard_map/ppermute | solution.py:167
  7.5 8.0 %collective-permute-start.9 = (bf16[16,6144]{1,0:T(8,128)(2,1)}, bf16[16,6144]{1,0:T(8,128)(2,1)S(1)}, u32[]{:S(2)}, u32[]{:S(2)}) collective-permute-start(bf16[16,6144]{1,0:T(8,128)(2,1)} %get-tuple-element.40), channel_id=1, source_target_pairs={{0,4},{1,5},{4,8},{5,9},{8,12},{9,13},{12,14},{13,15},{14,10},{15,... | collective-permute-start | bytes 589832 | tf_op jit(solution)/shard_map/ppermute | solution.py:167
  7.6 10.2 %collective-permute-start.1 = (bf16[16,6272]{1,0:T(8,128)(2,1)}, bf16[16,6272]{1,0:T(8,128)(2,1)S(1)}, u32[]{:S(2)}, u32[]{:S(2)}) collective-permute-start(bf16[16,6272]{1,0:T(8,128)(2,1)} %get-tuple-element.39), channel_id=1, source_target_pairs={{4,0},{5,1},{8,4},{9,5},{12,8},{13,9},{14,12},{15,13},{10,14},{11,... | collective-permute-start | bytes 602120 | tf_op jit(solution)/shard_map/ppermute | solution.py:167
  9.5 10.3 %collective-permute-start = (bf16[16,6272]{1,0:T(8,128)(2,1)}, bf16[16,6272]{1,0:T(8,128)(2,1)S(1)}, u32[]{:S(2)}, u32[]{:S(2)}) collective-permute-start(bf16[16,6272]{1,0:T(8,128)(2,1)} %get-tuple-element.39), channel_id=1, source_target_pairs={{0,4},{1,5},{4,8},{5,9},{8,12},{9,13},{12,14},{13,15},{14,10},{15,... | collective-permute-start | bytes 602120 | tf_op jit(solution)/shard_map/ppermute | solution.py:167
  13.5 8.5 %collective-permute-start.12 = (bf16[16,6144]{1,0:T(8,128)(2,1)S(1)}, bf16[16,6144]{1,0:T(8,128)(2,1)S(1)}, u32[]{:S(2)}, u32[]{:S(2)}) collective-permute-start(bf16[16,6144]{1,0:T(8,128)(2,1)S(1)} %collective-permute-done.10), channel_id=1, source_target_pairs={{4,0},{5,1},{8,4},{9,5},{12,8},{13,9},{14,12},{15,13},{10,14},{11,... | collective-permute-start | bytes 589832 | tf_op jit(solution)/shard_map/ppermute | solution.py:167
  15.5 8.5 %collective-permute-start.11 = (bf16[16,6144]{1,0:T(8,128)(2,1)S(1)}, bf16[16,6144]{1,0:T(8,128)(2,1)S(1)}, u32[]{:S(2)}, u32[]{:S(2)}) collective-permute-start(bf16[16,6144]{1,0:T(8,128)(2,1)S(1)} %collective-permute-done.9), channel_id=1, source_target_pairs={{0,4},{1,5},{4,8},{5,9},{8,12},{9,13},{12,14},{13,15},{14,10},{15,... | collective-permute-start | bytes 589832 | tf_op jit(solution)/shard_map/ppermute | solution.py:167
  17.8 8.5 %collective-permute-start.3 = (bf16[16,6272]{1,0:T(8,128)(2,1)S(1)}, bf16[16,6272]{1,0:T(8,128)(2,1)S(1)}, u32[]{:S(2)}, u32[]{:S(2)}) collective-permute-start(bf16[16,6272]{1,0:T(8,128)(2,1)S(1)} %collective-permute-done.1), channel_id=1, source_target_pairs={{4,0},{5,1},{8,4},{9,5},{12,8},{13,9},{14,12},{15,13},{10,14},{11,... | collective-permute-start | bytes 602120 | tf_op jit(solution)/shard_map/ppermute | solution.py:167
  19.8 8.5 %collective-permute-start.2 = (bf16[16,6272]{1,0:T(8,128)(2,1)S(1)}, bf16[16,6272]{1,0:T(8,128)(2,1)S(1)}, u32[]{:S(2)}, u32[]{:S(2)}) collective-permute-start(bf16[16,6272]{1,0:T(8,128)(2,1)S(1)} %collective-permute-done), channel_id=1, source_target_pairs={{0,4},{1,5},{4,8},{5,9},{8,12},{9,13},{12,14},{13,15},{14,10},{15,... | collective-permute-start | bytes 602120 | tf_op jit(solution)/shard_map/ppermute | solution.py:167
  22.0 10.6 %collective-permute-start.14 = (bf16[16,6144]{1,0:T(8,128)(2,1)S(1)}, bf16[16,6144]{1,0:T(8,128)(2,1)S(1)}, u32[]{:S(2)}, u32[]{:S(2)}) collective-permute-start(bf16[16,6144]{1,0:T(8,128)(2,1)S(1)} %collective-permute-done.12), channel_id=1, source_target_pairs={{4,0},{5,1},{8,4},{9,5},{12,8},{13,9},{14,12},{15,13},{10,14},{11,... | collective-permute-start | bytes 589832 | tf_op jit(solution)/shard_map/ppermute | solution.py:167
  24.0 8.5 %collective-permute-start.13 = (bf16[16,6144]{1,0:T(8,128)(2,1)S(1)}, bf16[16,6144]{1,0:T(8,128)(2,1)S(1)}, u32[]{:S(2)}, u32[]{:S(2)}) collective-permute-start(bf16[16,6144]{1,0:T(8,128)(2,1)S(1)} %collective-permute-done.11), channel_id=1, source_target_pairs={{0,4},{1,5},{4,8},{5,9},{8,12},{9,13},{12,14},{13,15},{14,10},{15,... | collective-permute-start | bytes 589832 | tf_op jit(solution)/shard_map/ppermute | solution.py:167
  26.3 9.1 %collective-permute-start.5 = (bf16[16,6272]{1,0:T(8,128)(2,1)S(1)}, bf16[16,6272]{1,0:T(8,128)(2,1)S(1)}, u32[]{:S(2)}, u32[]{:S(2)}) collective-permute-start(bf16[16,6272]{1,0:T(8,128)(2,1)S(1)} %collective-permute-done.3), channel_id=1, source_target_pairs={{4,0},{5,1},{8,4},{9,5},{12,8},{13,9},{14,12},{15,13},{10,14},{11,... | collective-permute-start | bytes 602120 | tf_op jit(solution)/shard_map/ppermute | solution.py:167
  28.3 7.0 %collective-permute-start.4 = (bf16[16,6272]{1,0:T(8,128)(2,1)S(1)}, bf16[16,6272]{1,0:T(8,128)(2,1)S(1)}, u32[]{:S(2)}, u32[]{:S(2)}) collective-permute-start(bf16[16,6272]{1,0:T(8,128)(2,1)S(1)} %collective-permute-done.2), channel_id=1, source_target_pairs={{0,4},{1,5},{4,8},{5,9},{8,12},{9,13},{12,14},{13,15},{14,10},{15,... | collective-permute-start | bytes 602120 | tf_op jit(solution)/shard_map/ppermute | solution.py:167
  32.6 10.4 %collective-permute-start.16 = (bf16[112,6144]{1,0:T(8,128)(2,1)S(1)}, bf16[112,6144]{1,0:T(8,128)(2,1)S(1)}, u32[]{:S(2)}, u32[]{:S(2)}) collective-permute-start(bf16[112,6144]{1,0:T(8,128)(2,1)S(1)} %get-tuple-element.101), channel_id=1, source_target_pairs={{0,1},{1,0},{2,3},{3,2},{4,5},{5,4},{6,7},{7,6},{8,9},{9,8},{10,11... | collective-permute-start | bytes 4128776 | tf_op jit(solution)/shard_map/ppermute | solution.py:167
  32.7 7.3 %collective-permute-start.15 = (bf16[16,6144]{1,0:T(8,128)(2,1)S(1)}, bf16[16,6144]{1,0:T(8,128)(2,1)S(1)}, u32[]{:S(2)}, u32[]{:S(2)}) collective-permute-start(bf16[16,6144]{1,0:T(8,128)(2,1)S(1)} %collective-permute-done.14), channel_id=1, source_target_pairs={{4,0},{5,1},{8,4},{9,5},{12,8},{13,9},{14,12},{15,13},{10,14},{11,... | collective-permute-start | bytes 589832 | tf_op jit(solution)/shard_map/ppermute | solution.py:167
  35.4 7.7 %collective-permute-start.7 = (bf16[112,6272]{1,0:T(8,128)(2,1)S(1)}, bf16[112,6272]{1,0:T(8,128)(2,1)S(1)}, u32[]{:S(2)}, u32[]{:S(2)}) collective-permute-start(bf16[112,6272]{1,0:T(8,128)(2,1)S(1)} %get-tuple-element.87), channel_id=1, source_target_pairs={{0,1},{1,0},{2,3},{3,2},{4,5},{5,4},{6,7},{7,6},{8,9},{9,8},{10,11... | collective-permute-start | bytes 4214792 | tf_op jit(solution)/shard_map/ppermute | solution.py:167
  35.5 7.4 %collective-permute-start.6 = (bf16[16,6272]{1,0:T(8,128)(2,1)S(1)}, bf16[16,6272]{1,0:T(8,128)(2,1)S(1)}, u32[]{:S(2)}, u32[]{:S(2)}) collective-permute-start(bf16[16,6272]{1,0:T(8,128)(2,1)S(1)} %collective-permute-done.4), channel_id=1, source_target_pairs={{0,4},{1,5},{4,8},{5,9},{8,12},{9,13},{12,14},{13,15},{14,10},{15,... | collective-permute-start | bytes 602120 | tf_op jit(solution)/shard_map/ppermute | solution.py:167
  40.0 3.1 %collective-permute-start.17 = (bf16[16,6144]{1,0:T(8,128)(2,1)S(1)}, bf16[16,6144]{1,0:T(8,128)(2,1)S(1)}, u32[]{:S(2)}, u32[]{:S(2)}) collective-permute-start(bf16[16,6144]{1,0:T(8,128)(2,1)S(1)} %collective-permute-done.15), channel_id=1, source_target_pairs={{0,1},{1,0},{2,3},{3,2},{4,5},{5,4},{6,7},{7,6},{8,9},{9,8},{10,11... | collective-permute-start | bytes 589832 | tf_op jit(solution)/shard_map/ppermute | solution.py:167
  42.9 1.4 %collective-permute-start.8 = (bf16[16,6272]{1,0:T(8,128)(2,1)S(1)}, bf16[16,6272]{1,0:T(8,128)(2,1)S(1)}, u32[]{:S(2)}, u32[]{:S(2)}) collective-permute-start(bf16[16,6272]{1,0:T(8,128)(2,1)S(1)} %collective-permute-done.6), channel_id=1, source_target_pairs={{0,1},{1,0},{2,3},{3,2},{4,5},{5,4},{6,7},{7,6},{8,9},{9,8},{10,11... | collective-permute-start | bytes 602120 | tf_op jit(solution)/shard_map/ppermute | solution.py:167
  42.9 2.2 %copy-start.2 = (bf16[6144,336]{0,1:T(8,128)(2,1)S(1)}, bf16[6144,336]{0,1:T(8,128)(2,1)}, u32[]{:S(2)}) copy-start(bf16[6144,336]{0,1:T(8,128)(2,1)} %param.11) | copy-start | bytes 12386308
  45.1 2.2 %copy-start.3 = (bf16[6144,336]{0,1:T(8,128)(2,1)S(1)}, bf16[6144,336]{0,1:T(8,128)(2,1)}, u32[]{:S(2)}) copy-start(bf16[6144,336]{0,1:T(8,128)(2,1)} %param.12) | copy-start | bytes 12386308
  47.3 2.2 %copy-start.1 = (bf16[336,6144]{1,0:T(8,128)(2,1)S(1)}, bf16[336,6144]{1,0:T(8,128)(2,1)}, u32[]{:S(2)}) copy-start(bf16[336,6144]{1,0:T(8,128)(2,1)} %param.13) | copy-start | bytes 12386308
  51.6 2.5 %collective-permute-start.19 = (bf16[48,6144]{1,0:T(8,128)(2,1)S(1)}, bf16[48,6144]{1,0:T(8,128)(2,1)S(1)}, u32[]{:S(2)}, u32[]{:S(2)}) collective-permute-start(bf16[48,6144]{1,0:T(8,128)(2,1)S(1)} %slice.98), channel_id=1, source_target_pairs={{0,1},{1,0},{2,3},{3,2},{4,5},{5,4},{6,7},{7,6},{8,9},{9,8},{10,11... | collective-permute-start | bytes 1769480 | tf_op jit(solution)/shard_map/ppermute | solution.py:167
  52.1 11.5 %collective-permute-start.18 = (bf16[80,6144]{1,0:T(8,128)(2,1)S(1)}, bf16[80,6144]{1,0:T(8,128)(2,1)S(1)}, u32[]{:S(2)}, u32[]{:S(2)}) collective-permute-start(bf16[80,6144]{1,0:T(8,128)(2,1)S(1)} %slice.94), channel_id=1, source_target_pairs={{0,1},{1,0},{2,3},{3,2},{4,5},{5,4},{6,7},{7,6},{8,9},{9,8},{10,11... | collective-permute-start | bytes 2949128 | tf_op jit(solution)/shard_map/ppermute | solution.py:167
  54.3 7.3 %collective-permute-start.20 = (bf16[16,6144]{1,0:T(8,128)(2,1)S(1)}, bf16[16,6144]{1,0:T(8,128)(2,1)S(1)}, u32[]{:S(2)}, u32[]{:S(2)}) collective-permute-start(bf16[16,6144]{1,0:T(8,128)(2,1)S(1)} %get-tuple-element.46), channel_id=1, source_target_pairs={{4,0},{5,1},{8,4},{9,5},{12,8},{13,9},{14,12},{15,13},{10,14},{11,... | collective-permute-start | bytes 589832 | tf_op jit(solution)/shard_map/ppermute | solution.py:167
  55.9 7.0 %collective-permute-start.21 = (bf16[16,6144]{1,0:T(8,128)(2,1)S(1)}, bf16[16,6144]{1,0:T(8,128)(2,1)S(1)}, u32[]{:S(2)}, u32[]{:S(2)}) collective-permute-start(bf16[16,6144]{1,0:T(8,128)(2,1)S(1)} %get-tuple-element.47), channel_id=1, source_target_pairs={{0,4},{1,5},{4,8},{5,9},{8,12},{9,13},{12,14},{13,15},{14,10},{15,... | collective-permute-start | bytes 589832 | tf_op jit(solution)/shard_map/ppermute | solution.py:167
  63.0 2.9 %collective-permute-start.22 = (bf16[48,6144]{1,0:T(8,128)(2,1)S(1)}, bf16[48,6144]{1,0:T(8,128)(2,1)S(1)}, u32[]{:S(2)}, u32[]{:S(2)}) collective-permute-start(bf16[48,6144]{1,0:T(8,128)(2,1)S(1)} %slice.105), channel_id=1, source_target_pairs={{0,1},{1,0},{2,3},{3,2},{4,5},{5,4},{6,7},{7,6},{8,9},{9,8},{10,11... | collective-permute-start | bytes 1769480 | tf_op jit(solution)/shard_map/ppermute | solution.py:167
  63.1 13.3 %collective-permute-start.25 = (bf16[80,6144]{1,0:T(8,128)(2,1)S(1)}, bf16[80,6144]{1,0:T(8,128)(2,1)S(1)}, u32[]{:S(2)}, u32[]{:S(2)}) collective-permute-start(bf16[80,6144]{1,0:T(8,128)(2,1)S(1)} %slice.110), channel_id=1, source_target_pairs={{0,1},{1,0},{2,3},{3,2},{4,5},{5,4},{6,7},{7,6},{8,9},{9,8},{10,11... | collective-permute-start | bytes 2949128 | tf_op jit(solution)/shard_map/ppermute | solution.py:167
  63.8 9.5 %collective-permute-start.23 = (bf16[16,6144]{1,0:T(8,128)(2,1)S(1)}, bf16[16,6144]{1,0:T(8,128)(2,1)S(1)}, u32[]{:S(2)}, u32[]{:S(2)}) collective-permute-start(bf16[16,6144]{1,0:T(8,128)(2,1)S(1)} %fusion.11.refs_3_), channel_id=1, source_target_pairs={{4,0},{5,1},{8,4},{9,5},{12,8},{13,9},{14,12},{15,13},{10,14},{11,... | collective-permute-start | bytes 589832 | tf_op jit(solution)/shard_map/ppermute | solution.py:167
  65.5 7.8 %collective-permute-start.24 = (bf16[16,6144]{1,0:T(8,128)(2,1)S(1)}, bf16[16,6144]{1,0:T(8,128)(2,1)S(1)}, u32[]{:S(2)}, u32[]{:S(2)}) collective-permute-start(bf16[16,6144]{1,0:T(8,128)(2,1)S(1)} %fusion.10.refs_4_), channel_id=1, source_target_pairs={{0,4},{1,5},{4,8},{5,9},{8,12},{9,13},{12,14},{13,15},{14,10},{15,... | collective-permute-start | bytes 589832 | tf_op jit(solution)/shard_map/ppermute | solution.py:167
  66.1 10.4 %collective-permute-start.26 = (bf16[16,6144]{1,0:T(8,128)(2,1)S(1)}, bf16[16,6144]{1,0:T(8,128)(2,1)S(1)}, u32[]{:S(2)}, u32[]{:S(2)}) collective-permute-start(bf16[16,6144]{1,0:T(8,128)(2,1)S(1)} %get-tuple-element.53.refs_5_), channel_id=1, source_target_pairs={{4,0},{5,1},{8,4},{9,5},{12,8},{13,9},{14,12},{15,13},{10,14},{11,... | collective-permute-start | bytes 589832 | tf_op jit(solution)/shard_map/ppermute | solution.py:167
  67.7 8.6 %collective-permute-start.27 = (bf16[16,6144]{1,0:T(8,128)(2,1)S(1)}, bf16[16,6144]{1,0:T(8,128)(2,1)S(1)}, u32[]{:S(2)}, u32[]{:S(2)}) collective-permute-start(bf16[16,6144]{1,0:T(8,128)(2,1)S(1)} %get-tuple-element.54.refs_6_), channel_id=1, source_target_pairs={{0,4},{1,5},{4,8},{5,9},{8,12},{9,13},{12,14},{13,15},{14,10},{15,... | collective-permute-start | bytes 589832 | tf_op jit(solution)/shard_map/ppermute | solution.py:167
  73.4 9.5 %collective-permute-start.28 = (bf16[16,6144]{1,0:T(8,128)(2,1)S(1)}, bf16[16,6144]{1,0:T(8,128)(2,1)S(1)}, u32[]{:S(2)}, u32[]{:S(2)}) collective-permute-start(bf16[16,6144]{1,0:T(8,128)(2,1)S(1)} %get-tuple-element.58.refs_2_), channel_id=1, source_target_pairs={{4,0},{5,1},{8,4},{9,5},{12,8},{13,9},{14,12},{15,13},{10,14},{11,... | collective-permute-start | bytes 589832 | tf_op jit(solution)/shard_map/ppermute | solution.py:167
  75.0 7.8 %collective-permute-start.29 = (bf16[16,6144]{1,0:T(8,128)(2,1)S(1)}, bf16[16,6144]{1,0:T(8,128)(2,1)S(1)}, u32[]{:S(2)}, u32[]{:S(2)}) collective-permute-start(bf16[16,6144]{1,0:T(8,128)(2,1)S(1)} %get-tuple-element.59.refs_3_), channel_id=1, source_target_pairs={{0,4},{1,5},{4,8},{5,9},{8,12},{9,13},{12,14},{13,15},{14,10},{15,... | collective-permute-start | bytes 589832 | tf_op jit(solution)/shard_map/ppermute | solution.py:167
  76.6 16.5 %copy-start = (bf16[16,128]{1,0:T(8,128)(2,1)S(1)}, bf16[16,128]{1,0:T(8,128)(2,1)}, u32[]{:S(2)}) copy-start(bf16[16,128]{1,0:T(8,128)(2,1)} %get-tuple-element.66.refs_3_) | copy-start | bytes 12292
  76.6 6.8 %collective-permute-start.31 = (bf16[16,6144]{1,0:T(8,128)(2,1)S(1)}, bf16[16,6144]{1,0:T(8,128)(2,1)S(1)}, u32[]{:S(2)}, u32[]{:S(2)}) collective-permute-start(bf16[16,6144]{1,0:T(8,128)(2,1)S(1)} %fusion.8.refs_4_), channel_id=1, source_target_pairs={{4,0},{5,1},{8,4},{9,5},{12,8},{13,9},{14,12},{15,13},{10,14},{11,... | collective-permute-start | bytes 589832 | tf_op jit(solution)/shard_map/ppermute | solution.py:167
  78.2 6.7 %collective-permute-start.32 = (bf16[16,6144]{1,0:T(8,128)(2,1)S(1)}, bf16[16,6144]{1,0:T(8,128)(2,1)S(1)}, u32[]{:S(2)}, u32[]{:S(2)}) collective-permute-start(bf16[16,6144]{1,0:T(8,128)(2,1)S(1)} %fusion.7.refs_5_), channel_id=1, source_target_pairs={{0,4},{1,5},{4,8},{5,9},{8,12},{9,13},{12,14},{13,15},{14,10},{15,... | collective-permute-start | bytes 589832 | tf_op jit(solution)/shard_map/ppermute | solution.py:167
  85.0 5.7 %collective-permute-start.34 = (bf16[16,6144]{1,0:T(8,128)(2,1)S(1)}, bf16[16,6144]{1,0:T(8,128)(2,1)S(1)}, u32[]{:S(2)}, u32[]{:S(2)}) collective-permute-start(bf16[16,6144]{1,0:T(8,128)(2,1)S(1)} %get-tuple-element.69), channel_id=1, source_target_pairs={{0,4},{1,5},{4,8},{5,9},{8,12},{9,13},{12,14},{13,15},{14,10},{15,... | collective-permute-start | bytes 589832 | tf_op jit(solution)/shard_map/ppermute | solution.py:167
  85.5 7.5 %collective-permute-start.30 = (bf16[16,6144]{1,0:T(8,128)(2,1)S(1)}, bf16[16,6144]{1,0:T(8,128)(2,1)S(1)}, u32[]{:S(2)}, u32[]{:S(2)}) collective-permute-start(bf16[16,6144]{1,0:T(8,128)(2,1)S(1)} %fusion.13), channel_id=1, source_target_pairs={{4,0},{5,1},{8,4},{9,5},{12,8},{13,9},{14,12},{15,13},{10,14},{11,... | collective-permute-start | bytes 589832 | tf_op jit(solution)/shard_map/ppermute | solution.py:167
  87.1 8.2 %collective-permute-start.33 = (bf16[16,6144]{1,0:T(8,128)(2,1)S(1)}, bf16[16,6144]{1,0:T(8,128)(2,1)S(1)}, u32[]{:S(2)}, u32[]{:S(2)}) collective-permute-start(bf16[16,6144]{1,0:T(8,128)(2,1)S(1)} %get-tuple-element.68), channel_id=1, source_target_pairs={{4,0},{5,1},{8,4},{9,5},{12,8},{13,9},{14,12},{15,13},{10,14},{11,... | collective-permute-start | bytes 589832 | tf_op jit(solution)/shard_map/ppermute | solution.py:167
  90.7 5.7 %collective-permute-start.35 = (bf16[16,6144]{1,0:T(8,128)(2,1)S(1)}, bf16[16,6144]{1,0:T(8,128)(2,1)S(1)}, u32[]{:S(2)}, u32[]{:S(2)}) collective-permute-start(bf16[16,6144]{1,0:T(8,128)(2,1)S(1)} %fusion.4), channel_id=1, source_target_pairs={{0,4},{1,5},{4,8},{5,9},{8,12},{9,13},{12,14},{13,15},{14,10},{15,... | collective-permute-start | bytes 589832 | tf_op jit(solution)/shard_map/ppermute | solution.py:167

commit v5 on v3

--- a/solution.py
+++ b/solution.py
@@ -1,10 +1,58 @@
 import jax
 import jax.numpy as jnp
 from jax import lax
+from jax.experimental import pallas as pl
+from jax.experimental.pallas import tpu as pltpu
 from jax.sharding import PartitionSpec as P
 
 CAP = 16
 LANES = 128
+ANY = pl.BlockSpec(memory_space=pl.ANY)
+MARK = jax.ShapeDtypeStruct((8, LANES), jnp.float32)
+
+
+def whole(shape):
+    return pl.BlockSpec(shape, lambda j: (0,) * len(shape))
+
+
+def columns(rows, width):
+    return pl.BlockSpec((rows, width), lambda j: (0, j))
+
+
+def parts_of(d, most):
+    width = LANES
+    for w in range(LANES, most + 1, LANES):
+        if d % w == 0:
+            width = w
+    return d // width, width
+
+
+def params(megabytes):
+    return pltpu.CompilerParams(vmem_limit_bytes=megabytes << 20)
+
+
+def grad_kernel(marks, side_ref, rows_ref, *refs):
+    out_ref, mark_ref = refs[marks:]
+    out_ref[...] = jnp.dot(
+        side_ref[...], rows_ref[...], preferred_element_type=jnp.float32
+    ).astype(jnp.bfloat16)
+    mark_ref[...] = jnp.zeros(mark_ref.shape, jnp.float32)
+
+
+def weight_grad(side, rows, d, marks):
+    r, f = side.shape
+    parts, width = parts_of(d, 1024)
+    return pl.pallas_call(
+        lambda *refs: grad_kernel(len(marks), *refs),
+        grid=(parts,),
+        in_specs=[whole((f, r)), columns(r, width)] + [ANY] * len(marks),
+        out_specs=[columns(f, width), whole(MARK.shape)],
+        out_shape=[jax.ShapeDtypeStruct((f, d), jnp.bfloat16), MARK],
+        compiler_params=params(12),
+        cost_estimate=pl.CostEstimate(
+            flops=2 * r * f * d, bytes_accessed=2 * d * (r + f), transcendentals=0
+        ),
+    )(side.T, rows, *marks)
 
 
 def ring_of(n):
@@ -26,26 +74,24 @@
         return lax.ppermute(x, "et", pairs)
 
     def gather_rows(x, dy):
-        held_xr = held_xl = x
+        held_xr, held_xl = permute(x, right_pairs), permute(x, left_pairs)
         held_dr = held_dl = dy
-        got_x, got_d = [x], [dy]
+        got_x, got_d = [x, held_xr, held_xl], [dy]
         for k in range(1, steps):
-            held_xr = permute(held_xr, right_pairs)
+            if k > 1:
+                held_xr = permute(held_xr, right_pairs)
+                held_xl = permute(held_xl, left_pairs)
+                got_x += [held_xr, held_xl]
             held_dl = permute(held_dl, left_pairs)
             held_dr = permute(held_dr, right_pairs)
-            held_xl = permute(held_xl, left_pairs)
-            got_x += [held_xr, held_xl]
             got_d += [held_dr, held_dl]
         far_x = permute(held_xr, right_pairs)
         far_d = permute(held_dl, left_pairs)
         early_x = permute(jnp.concatenate(got_x, axis=0), core_pairs)
         early_d = permute(jnp.concatenate(got_d, axis=0), core_pairs)
         late_x = permute(far_x, core_pairs)
-        late_d = permute(far_d, core_pairs)
-        return (
-            jnp.concatenate(got_x + [far_x, early_x, late_x], axis=0),
-            jnp.concatenate(got_d + [far_d, early_d, late_d], axis=0),
-        )
+        rows_x = jnp.concatenate(got_x + [far_x, early_x, late_x], axis=0)
+        return rows_x, got_d, early_d, far_d
 
     cut = max(2 * steps - 3, 1) * CAP
 
@@ -73,8 +119,8 @@
     def send(blocks):
         return {w: permute(b, left_pairs if w == "l" else right_pairs) for w, b in blocks.items()}
 
-    def final(total, carry):
-        done = block_of(total, 0) + carry["l"].astype(jnp.float32) + carry["r"].astype(jnp.float32)
+    def final(near, carry):
+        done = near[:CAP] + carry["l"].astype(jnp.float32) + carry["r"].astype(jnp.float32)
         return done.astype(jnp.bfloat16)
 
     def tie(value, blocks):
@@ -91,18 +137,18 @@
         routed = jnp.any(landed, axis=1)
         slot = jnp.cumsum(routed.astype(jnp.int32)) - 1
         select = (slot[None, :] == jnp.arange(CAP, dtype=jnp.int32)[:, None]) & routed[None, :]
-        select_bf = select.astype(jnp.bfloat16)
-        wide = jnp.concatenate(
-            [tokens, jnp.broadcast_to(coef[:, None], (coef.shape[0], LANES))], axis=1
-        )
-        slot_x = jnp.dot(select_bf, wide, preferred_element_type=jnp.float32).astype(jnp.bfloat16)
-        slot_dy = jnp.dot(select_bf, out_grad, preferred_element_type=jnp.float32).astype(
-            jnp.bfloat16
-        )
-        rows_wide, rows_dy = gather_rows(slot_x, slot_dy)
+        select = select.astype(jnp.bfloat16)
+        slot_x, slot_dy, slot_coef = (
+            jnp.dot(select, a, preferred_element_type=jnp.float32).astype(jnp.bfloat16)
+            for a in (tokens, out_grad, coef[:, None])
+        )
+        slot_coef = jnp.broadcast_to(slot_coef, (CAP, LANES))
+        rows_wide, got_d, early_d, far_d = gather_rows(
+            jnp.concatenate([slot_x, slot_coef], axis=1), slot_dy
+        )
         rows_x = rows_wide[:, :d]
         coef_rows = rows_wide[:, d : d + 1].astype(jnp.float32)
-        half = rows_dy.shape[0] // 2
+        half = rows_wide.shape[0] // 2
 
         gate = jnp.dot(rows_x, w_gate, preferred_element_type=jnp.float32)
         up = jnp.dot(rows_x, w_up, preferred_element_type=jnp.float32)
@@ -111,8 +157,9 @@
         hidden = (coef_rows * act * up).astype(jnp.bfloat16)
         out_rows = jnp.dot(hidden, w_down, preferred_element_type=jnp.float32)
         out_sent = out_rows[half:].astype(jnp.bfloat16)
-        rows_dy, out_sent = lax.optimization_barrier((rows_dy, out_sent))
+        out_rows, far_d = lax.optimization_barrier((out_rows, far_d))
         out_total = pair_sum(out_rows[:half], out_sent)
+        rows_dy = jnp.concatenate(got_d + [far_d, early_d, permute(far_d, core_pairs)], axis=0)
 
         dhid = jnp.dot(rows_dy, w_down.T, preferred_element_type=jnp.float32)
         scaled = coef_rows * dhid
@@ -128,34 +175,31 @@
         dx_total = pair_sum(dx_rows[:half], dx_sent)
         dx_carry = {}
 
-        grads = []
-        work = [(rows_x, dgate), (rows_x, dup), (hidden, rows_dy)]
+        grads, marks = [], []
+        work = [(dgate, rows_wide), (dup, rows_wide), (hidden, rows_dy)]
         for at in range(2, steps + 2):
             if at <= steps:
                 out_carry.update(send(wave(out_total, out_carry, at, "l")))
-            blocks = wave(dx_total, dx_carry, at - 1, "r")
-            if at == 2:
-                far, out_carry = tie(dx_total[1], out_carry)
-                dx_total = (dx_total[0], far)
+            dx_blocks = wave(dx_total, dx_carry, at - 1, "r")
             if work:
-                lhs, rhs = work.pop(0)
-                rhs, blocks = tie(rhs, blocks)
-                grads.append(jnp.dot(lhs.T, rhs, preferred_element_type=jnp.float32))
-            dx_carry.update(send(blocks))
-        for lhs, rhs in work:
-            grads.append(jnp.dot(lhs.T, rhs, preferred_element_type=jnp.float32))
+                side, rows = work.pop(0)
+                side, dx_blocks = tie(side, dx_blocks)
+                grad, mark = weight_grad(side, rows, d, marks)
+                grads.append(grad)
+                if work and at <= steps:
+                    mark, out_carry = tie(mark, out_carry)
+                marks = [mark]
+            dx_carry.update(send(dx_blocks))
+        for side, rows in work:
+            grads.append(weight_grad(side, rows, d, marks)[0])
         grad_gate, grad_up, grad_down = grads
-        out_slots = final(out_total, out_carry)
-        dx_slots = final(dx_total, dx_carry)
-        mixed = jnp.dot(select_bf.T, out_slots, preferred_element_type=jnp.float32)
-        grad_tokens = jnp.dot(select_bf.T, dx_slots, preferred_element_type=jnp.float32)
-        return (
-            mixed.astype(jnp.bfloat16),
-            grad_tokens.astype(jnp.bfloat16),
-            grad_gate.astype(jnp.bfloat16),
-            grad_up.astype(jnp.bfloat16),
-            grad_down.astype(jnp.bfloat16),
-        )
+        mixed, grad_tokens = (
+            jnp.dot(select.T, final(total[0], carry), preferred_element_type=jnp.float32).astype(
+                jnp.bfloat16
+            )
+            for total, carry in ((out_total, out_carry), (dx_total, dx_carry))
+        )
+        return (mixed, grad_tokens, grad_gate.T, grad_up.T, grad_down)
 
     return per_device
 

time: 104 us -> 96.4 us (0.927)
  Pallas kernels: 0 us -> 12.5 us
  matrix products: 24.6 us -> 15 us
  waiting for transfers between devices: 40 us -> 30.5 us
    pallas_call x0 -> x3, Pallas kernels: none -> 12.5 us  [weight_grad(): pl.pallas_call(lambda *refs: grad_kernel(len(marks), *refs), grid=(parts,...]
    dot_general x7 -> x5, matrix products: 15.3 us -> 5.68 us  [the longest x2 3.53 us: per_device(): jnp.dot(select.T, final(total[0], carry), preferred_element_type=jnp.floa...]
    ppermute x36, waiting for transfers between devices: 40 us -> 30.5 us  [permute(): return lax.ppermute(x, 'et', pairs)]
  transfers between devices with their start and end apart: 36 -> 36, of which waited for: 21 -> 16; matrix products, arithmetic and copies ran while one was open for 20% -> 16% of each run, Pallas kernels for 0% -> 13%
where the time goes in v5:
time: 96.4 us; the launch traced here: 96.2 us
  starting transfers between devices  31.5 us (33%)
  waiting for transfers between devices  30.5 us (32%)
  matrix products  15 us (16%)
  Pallas kernels  12.5 us (13%)
  local copies, waits for them, and re-layouts  3.34 us (3%)
  other arithmetic  2.25 us (2%)
  between operations  1.02 us (1%)
    ppermute x36, starting transfers between devices, permute(): return lax.ppermute(x, 'et', pairs)  31.5 us
    ppermute x36, waiting for transfers between devices, permute(): return lax.ppermute(x, 'et', pairs)  30.5 us
    pallas_call x3, Pallas kernels, weight_grad(): pl.pallas_call(lambda *refs: grad_kernel(len(marks), *refs), grid=(parts,...  12.5 us
    dot_general x2, matrix products, per_device(): jnp.dot(select.T, final(total[0], carry), preferred_element_type=jnp.floa...  3.53 us
    unnamed x24, local copies, waits for them, and re-layouts  2.61 us
    dot_general x3, matrix products, per_device(): jnp.dot(select, a, preferred_element_type=jnp.float32).astype(jnp.bfloat16)  2.15 us
  transfers between devices with their start and end apart: 36, of which 16 were waited for; matrix products, arithmetic and copies ran while one was open for 16% of the time, Pallas kernels for 13%

profile of v5, /device:TPU:0, one launch (start us, length us, event | category | flops | bytes accessed | tf_op | source)
XLA Modules:
  0.0 96.2 jit_solution(13019612709308864509)
XLA Ops:
  0.6 0.8 select_reduce_fusion
  1.6 0.2 reduce-window.8
  1.9 0.2 copy-done
  2.1 0.3 constant_dynamic-update-slice_fusion.23
  2.4 3.1 %collective-permute-start.14 = (bf16[16,6144]{1,0:T(8,128)(2,1)S(1)}, bf16[16,6144]{1,0:T(8,128)(2,1)S(1)}, u32[]{:S(2)}, u32[]{:S(2)}) collective-permute-start(bf16[16,6144]{1,0:T(8,128)(2,1)S(1)} %get-tuple-element.134), channel_id=1, source_target_pairs={{0,4},{1,5},{4,8},{5,9},{8,12},{9,13},{12,14},{13,15},{14,10},{15,... | collective-permute-start | bytes 589832 | tf_op jit(solution)/shard_map/ppermute | solution.py:74
  5.6 1.7 %convolution_convert_fusion.3 = bf16[16,6144]{1,0:T(8,128)(2,1)S(1)} fusion(bf16[128,6144]{1,0:T(8,128)(2,1)} %param.7, s32[128]{0:T(128)S(1)} %add_reduce_fusion, pred[128]{0:T(512)(128)(4,1)S(1)} %reduce_or.9), kind=kOutput, calls=%fused_computation.4 | convolution fusion | flops 25268224 | bytes 1770112 | tf_op jit(solution)/shard_map/dot_general | solution.py:142
  7.5 2.1 %collective-permute-start = (bf16[16,6272]{1,0:T(8,128)(2,1)S(1)}, bf16[16,6272]{1,0:T(8,128)(2,1)S(1)}, u32[]{:S(2)}, u32[]{:S(2)}) collective-permute-start(bf16[16,6272]{1,0:T(8,128)(2,1)S(1)} %get-tuple-element.115), channel_id=1, source_target_pairs={{0,4},{1,5},{4,8},{5,9},{8,12},{9,13},{12,14},{13,15},{14,10},{15,... | collective-permute-start | bytes 602120 | tf_op jit(solution)/shard_map/ppermute | solution.py:74
  9.5 1.4 %collective-permute-done.14 = bf16[16,6144]{1,0:T(8,128)(2,1)S(1)} collective-permute-done((bf16[16,6144]{1,0:T(8,128)(2,1)S(1)}, bf16[16,6144]{1,0:T(8,128)(2,1)S(1)}, u32[]{:S(2)}, u32[]{:S(2)}) %collective-permute-start.14) | collective-permute-done | bytes 196640 | tf_op jit(solution)/shard_map/ppermute | solution.py:74
  10.9 1.9 %collective-permute-start.15 = (bf16[16,6144]{1,0:T(8,128)(2,1)S(1)}, bf16[16,6144]{1,0:T(8,128)(2,1)S(1)}, u32[]{:S(2)}, u32[]{:S(2)}) collective-permute-start(bf16[16,6144]{1,0:T(8,128)(2,1)S(1)} %collective-permute-done.14), channel_id=1, source_target_pairs={{0,4},{1,5},{4,8},{5,9},{8,12},{9,13},{12,14},{13,15},{14,10},{15,... | collective-permute-start | bytes 589832 | tf_op jit(solution)/shard_map/ppermute | solution.py:74
  12.8 0.2 collective-permute-start.10
  13.0 2.4 %collective-permute-done = bf16[16,6272]{1,0:T(8,128)(2,1)S(1)} collective-permute-done((bf16[16,6272]{1,0:T(8,128)(2,1)S(1)}, bf16[16,6272]{1,0:T(8,128)(2,1)S(1)}, u32[]{:S(2)}, u32[]{:S(2)}) %collective-permute-start) | collective-permute-done | bytes 200736 | tf_op jit(solution)/shard_map/ppermute | solution.py:74
  15.4 2.0 %collective-permute-start.2 = (bf16[16,6272]{1,0:T(8,128)(2,1)S(1)}, bf16[16,6272]{1,0:T(8,128)(2,1)S(1)}, u32[]{:S(2)}, u32[]{:S(2)}) collective-permute-start(bf16[16,6272]{1,0:T(8,128)(2,1)S(1)} %collective-permute-done), channel_id=1, source_target_pairs={{0,4},{1,5},{4,8},{5,9},{8,12},{9,13},{12,14},{13,15},{14,10},{15,... | collective-permute-start | bytes 602120 | tf_op jit(solution)/shard_map/ppermute | solution.py:74
  17.5 2.1 %collective-permute-done.15 = bf16[16,6144]{1,0:T(8,128)(2,1)S(1)} collective-permute-done((bf16[16,6144]{1,0:T(8,128)(2,1)S(1)}, bf16[16,6144]{1,0:T(8,128)(2,1)S(1)}, u32[]{:S(2)}, u32[]{:S(2)}) %collective-permute-start.15) | collective-permute-done | bytes 196640 | tf_op jit(solution)/shard_map/ppermute | solution.py:74
  19.6 2.0 %collective-permute-start.16 = (bf16[16,6144]{1,0:T(8,128)(2,1)S(1)}, bf16[16,6144]{1,0:T(8,128)(2,1)S(1)}, u32[]{:S(2)}, u32[]{:S(2)}) collective-permute-start(bf16[16,6144]{1,0:T(8,128)(2,1)S(1)} %collective-permute-done.15), channel_id=1, source_target_pairs={{0,4},{1,5},{4,8},{5,9},{8,12},{9,13},{12,14},{13,15},{14,10},{15,... | collective-permute-start | bytes 589832 | tf_op jit(solution)/shard_map/ppermute | solution.py:74
  21.7 2.2 %collective-permute-done.2 = bf16[16,6272]{1,0:T(8,128)(2,1)S(1)} collective-permute-done((bf16[16,6272]{1,0:T(8,128)(2,1)S(1)}, bf16[16,6272]{1,0:T(8,128)(2,1)S(1)}, u32[]{:S(2)}, u32[]{:S(2)}) %collective-permute-start.2) | collective-permute-done | bytes 200736 | tf_op jit(solution)/shard_map/ppermute | solution.py:74
  23.9 2.0 %collective-permute-start.4 = (bf16[16,6272]{1,0:T(8,128)(2,1)S(1)}, bf16[16,6272]{1,0:T(8,128)(2,1)S(1)}, u32[]{:S(2)}, u32[]{:S(2)}) collective-permute-start(bf16[16,6272]{1,0:T(8,128)(2,1)S(1)} %collective-permute-done.2), channel_id=1, source_target_pairs={{0,4},{1,5},{4,8},{5,9},{8,12},{9,13},{12,14},{13,15},{14,10},{15,... | collective-permute-start | bytes 602120 | tf_op jit(solution)/shard_map/ppermute | solution.py:74
  26.1 2.1 %collective-permute-done.16 = bf16[16,6144]{1,0:T(8,128)(2,1)S(1)} collective-permute-done((bf16[16,6144]{1,0:T(8,128)(2,1)S(1)}, bf16[16,6144]{1,0:T(8,128)(2,1)S(1)}, u32[]{:S(2)}, u32[]{:S(2)}) %collective-permute-start.16) | collective-permute-done | bytes 196640 | tf_op jit(solution)/shard_map/ppermute | solution.py:74
  28.2 3.5 %collective-permute-done.4 = bf16[16,6272]{1,0:T(8,128)(2,1)S(1)} collective-permute-done((bf16[16,6272]{1,0:T(8,128)(2,1)S(1)}, bf16[16,6272]{1,0:T(8,128)(2,1)S(1)}, u32[]{:S(2)}, u32[]{:S(2)}) %collective-permute-start.4) | collective-permute-done | bytes 200736 | tf_op jit(solution)/shard_map/ppermute | solution.py:74
  31.7 1.5 %collective-permute-done.5 = bf16[16,6272]{1,0:T(8,128)(2,1)S(1)} collective-permute-done((bf16[16,6272]{1,0:T(8,128)(2,1)S(1)}, bf16[16,6272]{1,0:T(8,128)(2,1)S(1)}, u32[]{:S(2)}, u32[]{:S(2)}) %collective-permute-start.5) | collective-permute-done | bytes 200736 | tf_op jit(solution)/shard_map/ppermute | solution.py:74
  33.3 1.6 %collective-permute-start.6 = (bf16[16,6272]{1,0:T(8,128)(2,1)S(1)}, bf16[16,6272]{1,0:T(8,128)(2,1)S(1)}, u32[]{:S(2)}, u32[]{:S(2)}) collective-permute-start(bf16[16,6272]{1,0:T(8,128)(2,1)S(1)} %collective-permute-done.4), channel_id=1, source_target_pairs={{0,4},{1,5},{4,8},{5,9},{8,12},{9,13},{12,14},{13,15},{14,10},{15,... | collective-permute-start | bytes 602120 | tf_op jit(solution)/shard_map/ppermute | solution.py:74
  34.9 0.2 collective-permute-start.17
  35.2 0.4 collective-permute-start.12
  35.6 5.0 %collective-permute-done.6 = bf16[16,6272]{1,0:T(8,128)(2,1)S(1)} collective-permute-done((bf16[16,6272]{1,0:T(8,128)(2,1)S(1)}, bf16[16,6272]{1,0:T(8,128)(2,1)S(1)}, u32[]{:S(2)}, u32[]{:S(2)}) %collective-permute-start.6) | collective-permute-done | bytes 200736 | tf_op jit(solution)/shard_map/ppermute | solution.py:74
  40.7 0.2 constant_dynamic-update-slice_fusion.8
  40.9 1.2 %collective-permute-done.8 = bf16[16,6272]{1,0:T(8,128)(2,1)S(1)} collective-permute-done((bf16[16,6272]{1,0:T(8,128)(2,1)S(1)}, bf16[16,6272]{1,0:T(8,128)(2,1)S(1)}, u32[]{:S(2)}, u32[]{:S(2)}) %collective-permute-start.8) | collective-permute-done | bytes 200736 | tf_op jit(solution)/shard_map/ppermute | solution.py:74
  42.3 1.3 %fusion.2 = f32[256,336]{0,1:T(8,128)S(1)} fusion(bf16[6144,336]{0,1:T(8,128)(2,1)S(1)} %copy-done.2, bf16[256,6272]{1,0:T(8,128)(2,1)S(1)} %constant_dynamic-update-slice_fusion.7.refs_1_), kind=kOutput, calls=%fused_computation.8 | convolution fusion | flops 1056964608 | bytes 7618560 | tf_op jit(solution)/shard_map/dot_general | solution.py:153
  43.5 0.9 copy-done.4
  44.4 1.3 %multiply_convert_fusion.2 = (bf16[256,336]{0,1:T(8,128)(2,1)S(1)}, f32[256,336]{0,1:T(8,128)S(1)}) fusion(f32[256]{0:T(256)S(1)} %convert_reduce_fusion, f32[256,336]{0,1:T(8,128)S(1)} %fusion.2, bf16[6144,336]{0,1:T(8,128)(2,1)S(1)} %copy-done.4, bf16[256,6272]{1,0:T(8,128)(2,1)S(1)} %constant_dynamic-update-slice_fusion.7.refs_1_), kind=kOutput, calls=%fused_computation.45 | convolution fusion | flops 1057566720 | bytes 8135680 | tf_op jit(solution)/shard_map/dot_general | solution.py:154
  45.7 0.9 copy-done.3
  46.6 1.8 %fusion.42 = (bf16[256,6144]{1,0:T(8,128)(2,1)S(1)}, f32[256,6144]{1,0:T(8,128)S(1)}) fusion(bf16[256,336]{0,1:T(8,128)(2,1)S(1)} %get-tuple-element.82, bf16[336,6144]{1,0:T(8,128)(2,1)S(1)} %copy-done.3), kind=kOutput, calls=%fused_computation.105 | convolution fusion | flops 1058537472 | bytes 13737984 | tf_op jit(solution)/shard_map/dot_general | solution.py:158
  48.6 0.2 collective-permute-start.18
  48.8 0.4 collective-permute-start.19
  49.4 0.7 collective-permute-done.18
  50.1 1.3 %multiply_convert_fusion = (bf16[256,336]{0,1:T(8,128)(2,1)S(1)}, bf16[256,336]{0,1:T(8,128)(2,1)S(1)}) fusion(f32[256,336]{0,1:T(8,128)S(1)} %fusion.2, f32[256,336]{0,1:T(8,128)S(1)} %get-tuple-element.131, bf16[256,6144]{1,0:T(8,128)(2,1)S(1)} %constant_dynamic-update-slice_fusion.24.refs_1_, bf16[336,6144]{1,0:T(8,128)(2,1)S(1)} %copy-done.3, ...), kind=kOutput, calls=%fused_computation.43 | convolution fusion | flops 1058168832 | bytes 8307712 | tf_op jit(solution)/shard_map/dot_general | solution.py:164
  51.6 0.3 collective-permute-start.20
  51.9 1.7 %collective-permute-start.21 = (bf16[16,6144]{1,0:T(8,128)(2,1)S(1)}, bf16[16,6144]{1,0:T(8,128)(2,1)S(1)}, u32[]{:S(2)}, u32[]{:S(2)}) collective-permute-start(bf16[16,6144]{1,0:T(8,128)(2,1)S(1)} %get-tuple-element.51), channel_id=1, source_target_pairs={{0,4},{1,5},{4,8},{5,9},{8,12},{9,13},{12,14},{13,15},{14,10},{15,... | collective-permute-start | bytes 589832 | tf_op jit(solution)/shard_map/ppermute | solution.py:74
  53.7 1.8 %fusion.43 = f32[256,6144]{1,0:T(8,128)S(1)} fusion(bf16[256,336]{0,1:T(8,128)(2,1)S(1)} %get-tuple-element.60, bf16[6144,336]{0,1:T(8,128)(2,1)S(1)} %copy-done.2), kind=kOutput, calls=%fused_computation.106 | convolution fusion | flops 1056964608 | bytes 10592256 | tf_op jit(solution)/shard_map/dot_general | solution.py:170
  55.5 1.8 %convolution_add_fusion = f32[256,6144]{1,0:T(8,128)S(1)} fusion(f32[256,6144]{1,0:T(8,128)S(1)} %fusion.43, bf16[256,336]{0,1:T(8,128)(2,1)S(1)} %get-tuple-element.59, bf16[6144,336]{0,1:T(8,128)(2,1)S(1)} %copy-done.4), kind=kOutput, calls=%fused_computation | convolution fusion | flops 1058537472 | bytes 16883712 | tf_op jit(solution)/shard_map/dot_general | solution.py:170
  57.3 0.2 slice.198
  57.5 1.1 %collective-permute-done.20 = bf16[16,6144]{1,0:T(8,128)(2,1)S(1)} collective-permute-done((bf16[16,6144]{1,0:T(8,128)(2,1)S(1)}, bf16[16,6144]{1,0:T(8,128)(2,1)S(1)}, u32[]{:S(2)}, u32[]{:S(2)}) %collective-permute-start.20) | collective-permute-done | bytes 196640 | tf_op jit(solution)/shard_map/ppermute | solution.py:74
  58.6 0.2 collective-permute-done.21
  59.0 0.5 collective-permute-start.22
  59.8 1.5 %collective-permute-start.26 = (bf16[16,6144]{1,0:T(8,128)(2,1)S(1)}, bf16[16,6144]{1,0:T(8,128)(2,1)S(1)}, u32[]{:S(2)}, u32[]{:S(2)}) collective-permute-start(bf16[16,6144]{1,0:T(8,128)(2,1)S(1)} %fusion.13), channel_id=1, source_target_pairs={{4,0},{5,1},{8,4},{9,5},{12,8},{13,9},{14,12},{15,13},{10,14},{11,... | collective-permute-start | bytes 589832 | tf_op jit(solution)/shard_map/ppermute | solution.py:74
  61.3 0.6 collective-permute-start.27
  62.0 1.5 %collective-permute-start.24 = (bf16[16,6144]{1,0:T(8,128)(2,1)S(1)}, bf16[16,6144]{1,0:T(8,128)(2,1)S(1)}, u32[]{:S(2)}, u32[]{:S(2)}) collective-permute-start(bf16[16,6144]{1,0:T(8,128)(2,1)S(1)} %get-tuple-element.55), channel_id=1, source_target_pairs={{4,0},{5,1},{8,4},{9,5},{12,8},{13,9},{14,12},{15,13},{10,14},{11,... | collective-permute-start | bytes 589832 | tf_op jit(solution)/shard_map/ppermute | solution.py:74
  63.5 0.6 collective-permute-start.25
  64.1 4.2 %shard_map.110 = (bf16[336,6144]{1,0:T(8,128)(2,1)}, f32[8,128]{1,0:T(8,128)S(1)}) custom-call(bf16[336,256]{1,0:T(8,128)(2,1)S(1)} %bitcast.26, bf16[256,6272]{1,0:T(8,128)(2,1)S(1)} %constant_dynamic-update-slice_fusion.7.refs_1_), custom_call_target="tpu_custom_call" | custom-call | flops 1056964608 | bytes 7274496 | tf_op jit(solution)/shard_map/pallas_call | solution.py:45
  68.3 0.8 collective-permute-done.27
  69.1 1.6 %collective-permute-start.28 = (bf16[16,6144]{1,0:T(8,128)(2,1)S(1)}, bf16[16,6144]{1,0:T(8,128)(2,1)S(1)}, u32[]{:S(2)}, u32[]{:S(2)}) collective-permute-start(bf16[16,6144]{1,0:T(8,128)(2,1)S(1)} %get-tuple-element.70), channel_id=1, source_target_pairs={{4,0},{5,1},{8,4},{9,5},{12,8},{13,9},{14,12},{15,13},{10,14},{11,... | collective-permute-start | bytes 589832 | tf_op jit(solution)/shard_map/ppermute | solution.py:74
  70.8 0.4 collective-permute-start.29
  71.2 1.8 %collective-permute-done.25 = bf16[16,6144]{1,0:T(8,128)(2,1)S(1)} collective-permute-done((bf16[16,6144]{1,0:T(8,128)(2,1)S(1)}, bf16[16,6144]{1,0:T(8,128)(2,1)S(1)}, u32[]{:S(2)}, u32[]{:S(2)}) %collective-permute-start.25) | collective-permute-done | bytes 196640 | tf_op jit(solution)/shard_map/ppermute | solution.py:74
  73.0 0.2 slice_add_fusion
  73.3 1.6 %collective-permute-start.31 = (bf16[16,6144]{1,0:T(8,128)(2,1)S(1)}, bf16[16,6144]{1,0:T(8,128)(2,1)S(1)}, u32[]{:S(2)}, u32[]{:S(2)}) collective-permute-start(bf16[16,6144]{1,0:T(8,128)(2,1)S(1)} %fusion.15), channel_id=1, source_target_pairs={{4,0},{5,1},{8,4},{9,5},{12,8},{13,9},{14,12},{15,13},{10,14},{11,... | collective-permute-start | bytes 589832 | tf_op jit(solution)/shard_map/ppermute | solution.py:74
  74.9 0.4 collective-permute-start.32
  75.3 4.2 %shard_map.111 = (bf16[336,6144]{1,0:T(8,128)(2,1)}, f32[8,128]{1,0:T(8,128)S(1)}) custom-call(bf16[336,256]{1,0:T(8,128)(2,1)S(1)} %bitcast.28, bf16[256,6272]{1,0:T(8,128)(2,1)S(1)} %constant_dynamic-update-slice_fusion.7.refs_1_, f32[8,128]{1,0:T(8,128)S(1)} %get-tuple-element.66.refs_2_), custom_call_target="tpu_custom_call" | custom-call | flops 1056964608 | bytes 7274496 | tf_op jit(solution)/shard_map/pallas_call | solution.py:45
  79.5 1.1 %collective-permute-done.32 = bf16[16,6144]{1,0:T(8,128)(2,1)S(1)} collective-permute-done((bf16[16,6144]{1,0:T(8,128)(2,1)S(1)}, bf16[16,6144]{1,0:T(8,128)(2,1)S(1)}, u32[]{:S(2)}, u32[]{:S(2)}) %collective-permute-start.32) | collective-permute-done | bytes 196640 | tf_op jit(solution)/shard_map/ppermute | solution.py:74
  80.7 0.5 collective-permute-start.34
  81.3 1.6 %collective-permute-start.30 = (bf16[16,6144]{1,0:T(8,128)(2,1)S(1)}, bf16[16,6144]{1,0:T(8,128)(2,1)S(1)}, u32[]{:S(2)}, u32[]{:S(2)}) collective-permute-start(bf16[16,6144]{1,0:T(8,128)(2,1)S(1)} %fusion.16), channel_id=1, source_target_pairs={{4,0},{5,1},{8,4},{9,5},{12,8},{13,9},{14,12},{15,13},{10,14},{11,... | collective-permute-start | bytes 589832 | tf_op jit(solution)/shard_map/ppermute | solution.py:74
  82.9 1.6 %collective-permute-start.33 = (bf16[16,6144]{1,0:T(8,128)(2,1)S(1)}, bf16[16,6144]{1,0:T(8,128)(2,1)S(1)}, u32[]{:S(2)}, u32[]{:S(2)}) collective-permute-start(bf16[16,6144]{1,0:T(8,128)(2,1)S(1)} %get-tuple-element.78), channel_id=1, source_target_pairs={{4,0},{5,1},{8,4},{9,5},{12,8},{13,9},{14,12},{15,13},{10,14},{11,... | collective-permute-start | bytes 589832 | tf_op jit(solution)/shard_map/ppermute | solution.py:74
  84.5 4.1 %shard_map.112 = (bf16[336,6144]{1,0:T(8,128)(2,1)}, f32[8,128]{1,0:T(8,128)}) custom-call(bf16[336,256]{1,0:T(8,128)(2,1)S(1)} %bitcast.27, bf16[256,6144]{1,0:T(8,128)(2,1)S(1)} %constant_dynamic-update-slice_fusion.24.refs_1_, f32[8,128]{1,0:T(8,128)S(1)} %get-tuple-element.83.refs_2_), custom_call_target="tpu_custom_call" | custom-call | flops 1056964608 | bytes 7274496 | tf_op jit(solution)/shard_map/pallas_call | solution.py:45
  88.7 0.5 collective-permute-start.35
  89.2 1.8 %convolution_convert_fusion.1 = bf16[128,6144]{1,0:T(8,128)(2,1)} fusion(f32[80,6144]{1,0:T(8,128)S(1)} %convert_add_fusion, bf16[16,6144]{1,0:T(8,128)(2,1)S(1)} %collective-permute-done.29, bf16[16,6144]{1,0:T(8,128)(2,1)S(1)} %collective-permute-done.30, s32[128]{0:T(128)S(1)} %add_reduce_fusion, pred[128]{0:T(512)(128)(4,1)S(1)} %reduce_or.9), kind=kOutput, calls=%fused_computation.2 | convolution fusion | flops 26447872 | bytes 2360320 | tf_op jit(solution)/shard_map/dot_general | solution.py:197
  90.9 3.5 %collective-permute-done.35 = bf16[16,6144]{1,0:T(8,128)(2,1)S(1)} collective-permute-done((bf16[16,6144]{1,0:T(8,128)(2,1)S(1)}, bf16[16,6144]{1,0:T(8,128)(2,1)S(1)}, u32[]{:S(2)}, u32[]{:S(2)}) %collective-permute-start.35) | collective-permute-done | bytes 196640 | tf_op jit(solution)/shard_map/ppermute | solution.py:74
  94.4 1.8 %convolution_convert_fusion = bf16[128,6144]{1,0:T(8,128)(2,1)} fusion(f32[80,6144]{1,0:T(8,128)S(1)} %slice_add_fusion, bf16[16,6144]{1,0:T(8,128)(2,1)S(1)} %collective-permute-done.35, bf16[16,6144]{1,0:T(8,128)(2,1)S(1)} %collective-permute-done.33, s32[128]{0:T(128)S(1)} %add_reduce_fusion, pred[128]{0:T(512)(128)(4,1)S(1)} %reduce_or.9), kind=kOutput, calls=%fused_computation.1 | convolution fusion | flops 26447872 | bytes 2360320 | tf_op jit(solution)/shard_map/dot_general | solution.py:197
  (78 shorter events, 2.6 us)
Async XLA Ops:
  0.6 1.4 %copy-start = (bf16[128,6144]{1,0:T(8,128)(2,1)S(1)}, bf16[128,6144]{1,0:T(8,128)(2,1)}, u32[]{:S(2)}) copy-start(bf16[128,6144]{1,0:T(8,128)(2,1)} %param.8) | copy-start | bytes 4718596
  2.4 8.5 %collective-permute-start.14 = (bf16[16,6144]{1,0:T(8,128)(2,1)S(1)}, bf16[16,6144]{1,0:T(8,128)(2,1)S(1)}, u32[]{:S(2)}, u32[]{:S(2)}) collective-permute-start(bf16[16,6144]{1,0:T(8,128)(2,1)S(1)} %get-tuple-element.134), channel_id=1, source_target_pairs={{0,4},{1,5},{4,8},{5,9},{8,12},{9,13},{12,14},{13,15},{14,10},{15,... | collective-permute-start | bytes 589832 | tf_op jit(solution)/shard_map/ppermute | solution.py:74
  5.5 7.3 %collective-permute-start.9 = (bf16[16,6144]{1,0:T(8,128)(2,1)S(1)}, bf16[16,6144]{1,0:T(8,128)(2,1)S(1)}, u32[]{:S(2)}, u32[]{:S(2)}) collective-permute-start(bf16[16,6144]{1,0:T(8,128)(2,1)S(1)} %get-tuple-element.134), channel_id=1, source_target_pairs={{4,0},{5,1},{8,4},{9,5},{12,8},{13,9},{14,12},{15,13},{10,14},{11,... | collective-permute-start | bytes 589832 | tf_op jit(solution)/shard_map/ppermute | solution.py:74
  7.5 8.0 %collective-permute-start = (bf16[16,6272]{1,0:T(8,128)(2,1)S(1)}, bf16[16,6272]{1,0:T(8,128)(2,1)S(1)}, u32[]{:S(2)}, u32[]{:S(2)}) collective-permute-start(bf16[16,6272]{1,0:T(8,128)(2,1)S(1)} %get-tuple-element.115), channel_id=1, source_target_pairs={{0,4},{1,5},{4,8},{5,9},{8,12},{9,13},{12,14},{13,15},{14,10},{15,... | collective-permute-start | bytes 602120 | tf_op jit(solution)/shard_map/ppermute | solution.py:74
  9.5 7.9 %collective-permute-start.1 = (bf16[16,6272]{1,0:T(8,128)(2,1)S(1)}, bf16[16,6272]{1,0:T(8,128)(2,1)S(1)}, u32[]{:S(2)}, u32[]{:S(2)}) collective-permute-start(bf16[16,6272]{1,0:T(8,128)(2,1)S(1)} %get-tuple-element.115), channel_id=1, source_target_pairs={{4,0},{5,1},{8,4},{9,5},{12,8},{13,9},{14,12},{15,13},{10,14},{11,... | collective-permute-start | bytes 602120 | tf_op jit(solution)/shard_map/ppermute | solution.py:74
  10.9 8.7 %collective-permute-start.15 = (bf16[16,6144]{1,0:T(8,128)(2,1)S(1)}, bf16[16,6144]{1,0:T(8,128)(2,1)S(1)}, u32[]{:S(2)}, u32[]{:S(2)}) collective-permute-start(bf16[16,6144]{1,0:T(8,128)(2,1)S(1)} %collective-permute-done.14), channel_id=1, source_target_pairs={{0,4},{1,5},{4,8},{5,9},{8,12},{9,13},{12,14},{13,15},{14,10},{15,... | collective-permute-start | bytes 589832 | tf_op jit(solution)/shard_map/ppermute | solution.py:74
  12.8 8.9 %collective-permute-start.10 = (bf16[16,6144]{1,0:T(8,128)(2,1)S(1)}, bf16[16,6144]{1,0:T(8,128)(2,1)S(1)}, u32[]{:S(2)}, u32[]{:S(2)}) collective-permute-start(bf16[16,6144]{1,0:T(8,128)(2,1)S(1)} %collective-permute-done.9), channel_id=1, source_target_pairs={{4,0},{5,1},{8,4},{9,5},{12,8},{13,9},{14,12},{15,13},{10,14},{11,... | collective-permute-start | bytes 589832 | tf_op jit(solution)/shard_map/ppermute | solution.py:74
  15.4 8.5 %collective-permute-start.2 = (bf16[16,6272]{1,0:T(8,128)(2,1)S(1)}, bf16[16,6272]{1,0:T(8,128)(2,1)S(1)}, u32[]{:S(2)}, u32[]{:S(2)}) collective-permute-start(bf16[16,6272]{1,0:T(8,128)(2,1)S(1)} %collective-permute-done), channel_id=1, source_target_pairs={{0,4},{1,5},{4,8},{5,9},{8,12},{9,13},{12,14},{13,15},{14,10},{15,... | collective-permute-start | bytes 602120 | tf_op jit(solution)/shard_map/ppermute | solution.py:74
  17.5 8.5 %collective-permute-start.3 = (bf16[16,6272]{1,0:T(8,128)(2,1)S(1)}, bf16[16,6272]{1,0:T(8,128)(2,1)S(1)}, u32[]{:S(2)}, u32[]{:S(2)}) collective-permute-start(bf16[16,6272]{1,0:T(8,128)(2,1)S(1)} %collective-permute-done.1), channel_id=1, source_target_pairs={{4,0},{5,1},{8,4},{9,5},{12,8},{13,9},{14,12},{15,13},{10,14},{11,... | collective-permute-start | bytes 602120 | tf_op jit(solution)/shard_map/ppermute | solution.py:74
  19.6 8.5 %collective-permute-start.16 = (bf16[16,6144]{1,0:T(8,128)(2,1)S(1)}, bf16[16,6144]{1,0:T(8,128)(2,1)S(1)}, u32[]{:S(2)}, u32[]{:S(2)}) collective-permute-start(bf16[16,6144]{1,0:T(8,128)(2,1)S(1)} %collective-permute-done.15), channel_id=1, source_target_pairs={{0,4},{1,5},{4,8},{5,9},{8,12},{9,13},{12,14},{13,15},{14,10},{15,... | collective-permute-start | bytes 589832 | tf_op jit(solution)/shard_map/ppermute | solution.py:74
  21.7 13.2 %collective-permute-start.11 = (bf16[16,6144]{1,0:T(8,128)(2,1)S(1)}, bf16[16,6144]{1,0:T(8,128)(2,1)S(1)}, u32[]{:S(2)}, u32[]{:S(2)}) collective-permute-start(bf16[16,6144]{1,0:T(8,128)(2,1)S(1)} %collective-permute-done.10), channel_id=1, source_target_pairs={{4,0},{5,1},{8,4},{9,5},{12,8},{13,9},{14,12},{15,13},{10,14},{11,... | collective-permute-start | bytes 589832 | tf_op jit(solution)/shard_map/ppermute | solution.py:74
  23.9 7.7 %collective-permute-start.4 = (bf16[16,6272]{1,0:T(8,128)(2,1)S(1)}, bf16[16,6272]{1,0:T(8,128)(2,1)S(1)}, u32[]{:S(2)}, u32[]{:S(2)}) collective-permute-start(bf16[16,6272]{1,0:T(8,128)(2,1)S(1)} %collective-permute-done.2), channel_id=1, source_target_pairs={{0,4},{1,5},{4,8},{5,9},{8,12},{9,13},{12,14},{13,15},{14,10},{15,... | collective-permute-start | bytes 602120 | tf_op jit(solution)/shard_map/ppermute | solution.py:74
  26.0 7.2 %collective-permute-start.5 = (bf16[16,6272]{1,0:T(8,128)(2,1)S(1)}, bf16[16,6272]{1,0:T(8,128)(2,1)S(1)}, u32[]{:S(2)}, u32[]{:S(2)}) collective-permute-start(bf16[16,6272]{1,0:T(8,128)(2,1)S(1)} %collective-permute-done.3), channel_id=1, source_target_pairs={{4,0},{5,1},{8,4},{9,5},{12,8},{13,9},{14,12},{15,13},{10,14},{11,... | collective-permute-start | bytes 602120 | tf_op jit(solution)/shard_map/ppermute | solution.py:74
  26.1 16.2 %copy-start.2 = (bf16[6144,336]{0,1:T(8,128)(2,1)S(1)}, bf16[6144,336]{0,1:T(8,128)(2,1)}, u32[]{:S(2)}) copy-start(bf16[6144,336]{0,1:T(8,128)(2,1)} %param.11) | copy-start | bytes 12386308
  33.2 7.5 %collective-permute-start.7 = (bf16[112,6272]{1,0:T(8,128)(2,1)S(1)}, bf16[112,6272]{1,0:T(8,128)(2,1)S(1)}, u32[]{:S(2)}, u32[]{:S(2)}) collective-permute-start(bf16[112,6272]{1,0:T(8,128)(2,1)S(1)} %get-tuple-element.101), channel_id=1, source_target_pairs={{0,1},{1,0},{2,3},{3,2},{4,5},{5,4},{6,7},{7,6},{8,9},{9,8},{10,11... | collective-permute-start | bytes 4214792 | tf_op jit(solution)/shard_map/ppermute | solution.py:74
  33.3 7.4 %collective-permute-start.6 = (bf16[16,6272]{1,0:T(8,128)(2,1)S(1)}, bf16[16,6272]{1,0:T(8,128)(2,1)S(1)}, u32[]{:S(2)}, u32[]{:S(2)}) collective-permute-start(bf16[16,6272]{1,0:T(8,128)(2,1)S(1)} %collective-permute-done.4), channel_id=1, source_target_pairs={{0,4},{1,5},{4,8},{5,9},{8,12},{9,13},{12,14},{13,15},{14,10},{15,... | collective-permute-start | bytes 602120 | tf_op jit(solution)/shard_map/ppermute | solution.py:74
  34.9 14.4 %collective-permute-start.17 = (bf16[112,6144]{1,0:T(8,128)(2,1)S(1)}, bf16[112,6144]{1,0:T(8,128)(2,1)S(1)}, u32[]{:S(2)}, u32[]{:S(2)}) collective-permute-start(bf16[112,6144]{1,0:T(8,128)(2,1)S(1)} %get-tuple-element.116), channel_id=1, source_target_pairs={{0,1},{1,0},{2,3},{3,2},{4,5},{5,4},{6,7},{7,6},{8,9},{9,8},{10,11... | collective-permute-start | bytes 4128776 | tf_op jit(solution)/shard_map/ppermute | solution.py:74
  35.2 13.4 %collective-permute-start.12 = (bf16[16,6144]{1,0:T(8,128)(2,1)S(1)}, bf16[16,6144]{1,0:T(8,128)(2,1)S(1)}, u32[]{:S(2)}, u32[]{:S(2)}) collective-permute-start(bf16[16,6144]{1,0:T(8,128)(2,1)S(1)} %collective-permute-done.11), channel_id=1, source_target_pairs={{4,0},{5,1},{8,4},{9,5},{12,8},{13,9},{14,12},{15,13},{10,14},{11,... | collective-permute-start | bytes 589832 | tf_op jit(solution)/shard_map/ppermute | solution.py:74
  40.7 1.4 %collective-permute-start.8 = (bf16[16,6272]{1,0:T(8,128)(2,1)S(1)}, bf16[16,6272]{1,0:T(8,128)(2,1)S(1)}, u32[]{:S(2)}, u32[]{:S(2)}) collective-permute-start(bf16[16,6272]{1,0:T(8,128)(2,1)S(1)} %collective-permute-done.6), channel_id=1, source_target_pairs={{0,1},{1,0},{2,3},{3,2},{4,5},{5,4},{6,7},{7,6},{8,9},{9,8},{10,11... | collective-permute-start | bytes 602120 | tf_op jit(solution)/shard_map/ppermute | solution.py:74
  42.3 2.2 %copy-start.4 = (bf16[6144,336]{0,1:T(8,128)(2,1)S(1)}, bf16[6144,336]{0,1:T(8,128)(2,1)}, u32[]{:S(2)}) copy-start(bf16[6144,336]{0,1:T(8,128)(2,1)} %param.12) | copy-start | bytes 12386308
  44.4 2.2 %copy-start.3 = (bf16[336,6144]{1,0:T(8,128)(2,1)S(1)}, bf16[336,6144]{1,0:T(8,128)(2,1)}, u32[]{:S(2)}) copy-start(bf16[336,6144]{1,0:T(8,128)(2,1)} %param.13) | copy-start | bytes 12386308
  48.6 1.5 %collective-permute-start.18 = (bf16[16,6144]{1,0:T(8,128)(2,1)S(1)}, bf16[16,6144]{1,0:T(8,128)(2,1)S(1)}, u32[]{:S(2)}, u32[]{:S(2)}) collective-permute-start(bf16[16,6144]{1,0:T(8,128)(2,1)S(1)} %collective-permute-done.12), channel_id=1, source_target_pairs={{0,1},{1,0},{2,3},{3,2},{4,5},{5,4},{6,7},{7,6},{8,9},{9,8},{10,11... | collective-permute-start | bytes 589832 | tf_op jit(solution)/shard_map/ppermute | solution.py:74
  48.8 2.6 %collective-permute-start.19 = (bf16[48,6144]{1,0:T(8,128)(2,1)S(1)}, bf16[48,6144]{1,0:T(8,128)(2,1)S(1)}, u32[]{:S(2)}, u32[]{:S(2)}) collective-permute-start(bf16[48,6144]{1,0:T(8,128)(2,1)S(1)} %slice.128), channel_id=1, source_target_pairs={{0,1},{1,0},{2,3},{3,2},{4,5},{5,4},{6,7},{7,6},{8,9},{9,8},{10,11... | collective-permute-start | bytes 1769480 | tf_op jit(solution)/shard_map/ppermute | solution.py:74
  49.1 10.4 %collective-permute-start.13 = (bf16[80,6144]{1,0:T(8,128)(2,1)S(1)}, bf16[80,6144]{1,0:T(8,128)(2,1)S(1)}, u32[]{:S(2)}, u32[]{:S(2)}) collective-permute-start(bf16[80,6144]{1,0:T(8,128)(2,1)S(1)} %slice.125), channel_id=1, source_target_pairs={{0,1},{1,0},{2,3},{3,2},{4,5},{5,4},{6,7},{7,6},{8,9},{9,8},{10,11... | collective-permute-start | bytes 2949128 | tf_op jit(solution)/shard_map/ppermute | solution.py:74
  51.6 7.0 %collective-permute-start.20 = (bf16[16,6144]{1,0:T(8,128)(2,1)S(1)}, bf16[16,6144]{1,0:T(8,128)(2,1)S(1)}, u32[]{:S(2)}, u32[]{:S(2)}) collective-permute-start(bf16[16,6144]{1,0:T(8,128)(2,1)S(1)} %get-tuple-element.50), channel_id=1, source_target_pairs={{4,0},{5,1},{8,4},{9,5},{12,8},{13,9},{14,12},{15,13},{10,14},{11,... | collective-permute-start | bytes 589832 | tf_op jit(solution)/shard_map/ppermute | solution.py:74
  51.9 6.9 %collective-permute-start.21 = (bf16[16,6144]{1,0:T(8,128)(2,1)S(1)}, bf16[16,6144]{1,0:T(8,128)(2,1)S(1)}, u32[]{:S(2)}, u32[]{:S(2)}) collective-permute-start(bf16[16,6144]{1,0:T(8,128)(2,1)S(1)} %get-tuple-element.51), channel_id=1, source_target_pairs={{0,4},{1,5},{4,8},{5,9},{8,12},{9,13},{12,14},{13,15},{14,10},{15,... | collective-permute-start | bytes 589832 | tf_op jit(solution)/shard_map/ppermute | solution.py:74
  58.9 2.9 %collective-permute-start.23 = (bf16[48,6144]{1,0:T(8,128)(2,1)S(1)}, bf16[48,6144]{1,0:T(8,128)(2,1)S(1)}, u32[]{:S(2)}, u32[]{:S(2)}) collective-permute-start(bf16[48,6144]{1,0:T(8,128)(2,1)S(1)} %slice.111), channel_id=1, source_target_pairs={{0,1},{1,0},{2,3},{3,2},{4,5},{5,4},{6,7},{7,6},{8,9},{9,8},{10,11... | collective-permute-start | bytes 1769480 | tf_op jit(solution)/shard_map/ppermute | solution.py:74
  59.0 14.0 %collective-permute-start.22 = (bf16[80,6144]{1,0:T(8,128)(2,1)S(1)}, bf16[80,6144]{1,0:T(8,128)(2,1)S(1)}, u32[]{:S(2)}, u32[]{:S(2)}) collective-permute-start(bf16[80,6144]{1,0:T(8,128)(2,1)S(1)} %slice.108), channel_id=1, source_target_pairs={{0,1},{1,0},{2,3},{3,2},{4,5},{5,4},{6,7},{7,6},{8,9},{9,8},{10,11... | collective-permute-start | bytes 2949128 | tf_op jit(solution)/shard_map/ppermute | solution.py:74
  59.8 8.5 %collective-permute-start.26 = (bf16[16,6144]{1,0:T(8,128)(2,1)S(1)}, bf16[16,6144]{1,0:T(8,128)(2,1)S(1)}, u32[]{:S(2)}, u32[]{:S(2)}) collective-permute-start(bf16[16,6144]{1,0:T(8,128)(2,1)S(1)} %fusion.13), channel_id=1, source_target_pairs={{4,0},{5,1},{8,4},{9,5},{12,8},{13,9},{14,12},{15,13},{10,14},{11,... | collective-permute-start | bytes 589832 | tf_op jit(solution)/shard_map/ppermute | solution.py:74
  61.3 7.8 %collective-permute-start.27 = (bf16[16,6144]{1,0:T(8,128)(2,1)S(1)}, bf16[16,6144]{1,0:T(8,128)(2,1)S(1)}, u32[]{:S(2)}, u32[]{:S(2)}) collective-permute-start(bf16[16,6144]{1,0:T(8,128)(2,1)S(1)} %fusion.12), channel_id=1, source_target_pairs={{0,4},{1,5},{4,8},{5,9},{8,12},{9,13},{12,14},{13,15},{14,10},{15,... | collective-permute-start | bytes 589832 | tf_op jit(solution)/shard_map/ppermute | solution.py:74
  62.0 11.2 %collective-permute-start.24 = (bf16[16,6144]{1,0:T(8,128)(2,1)S(1)}, bf16[16,6144]{1,0:T(8,128)(2,1)S(1)}, u32[]{:S(2)}, u32[]{:S(2)}) collective-permute-start(bf16[16,6144]{1,0:T(8,128)(2,1)S(1)} %get-tuple-element.55), channel_id=1, source_target_pairs={{4,0},{5,1},{8,4},{9,5},{12,8},{13,9},{14,12},{15,13},{10,14},{11,... | collective-permute-start | bytes 589832 | tf_op jit(solution)/shard_map/ppermute | solution.py:74
  63.5 9.4 %collective-permute-start.25 = (bf16[16,6144]{1,0:T(8,128)(2,1)S(1)}, bf16[16,6144]{1,0:T(8,128)(2,1)S(1)}, u32[]{:S(2)}, u32[]{:S(2)}) collective-permute-start(bf16[16,6144]{1,0:T(8,128)(2,1)S(1)} %get-tuple-element.56), channel_id=1, source_target_pairs={{0,4},{1,5},{4,8},{5,9},{8,12},{9,13},{12,14},{13,15},{14,10},{15,... | collective-permute-start | bytes 589832 | tf_op jit(solution)/shard_map/ppermute | solution.py:74
  69.1 10.4 %collective-permute-start.28 = (bf16[16,6144]{1,0:T(8,128)(2,1)S(1)}, bf16[16,6144]{1,0:T(8,128)(2,1)S(1)}, u32[]{:S(2)}, u32[]{:S(2)}) collective-permute-start(bf16[16,6144]{1,0:T(8,128)(2,1)S(1)} %get-tuple-element.70), channel_id=1, source_target_pairs={{4,0},{5,1},{8,4},{9,5},{12,8},{13,9},{14,12},{15,13},{10,14},{11,... | collective-permute-start | bytes 589832 | tf_op jit(solution)/shard_map/ppermute | solution.py:74
  70.8 8.8 %collective-permute-start.29 = (bf16[16,6144]{1,0:T(8,128)(2,1)S(1)}, bf16[16,6144]{1,0:T(8,128)(2,1)S(1)}, u32[]{:S(2)}, u32[]{:S(2)}) collective-permute-start(bf16[16,6144]{1,0:T(8,128)(2,1)S(1)} %get-tuple-element.71), channel_id=1, source_target_pairs={{0,4},{1,5},{4,8},{5,9},{8,12},{9,13},{12,14},{13,15},{14,10},{15,... | collective-permute-start | bytes 589832 | tf_op jit(solution)/shard_map/ppermute | solution.py:74
  73.3 6.3 %collective-permute-start.31 = (bf16[16,6144]{1,0:T(8,128)(2,1)S(1)}, bf16[16,6144]{1,0:T(8,128)(2,1)S(1)}, u32[]{:S(2)}, u32[]{:S(2)}) collective-permute-start(bf16[16,6144]{1,0:T(8,128)(2,1)S(1)} %fusion.15), channel_id=1, source_target_pairs={{4,0},{5,1},{8,4},{9,5},{12,8},{13,9},{14,12},{15,13},{10,14},{11,... | collective-permute-start | bytes 589832 | tf_op jit(solution)/shard_map/ppermute | solution.py:74
  74.9 5.8 %collective-permute-start.32 = (bf16[16,6144]{1,0:T(8,128)(2,1)S(1)}, bf16[16,6144]{1,0:T(8,128)(2,1)S(1)}, u32[]{:S(2)}, u32[]{:S(2)}) collective-permute-start(bf16[16,6144]{1,0:T(8,128)(2,1)S(1)} %fusion.14), channel_id=1, source_target_pairs={{0,4},{1,5},{4,8},{5,9},{8,12},{9,13},{12,14},{13,15},{14,10},{15,... | collective-permute-start | bytes 589832 | tf_op jit(solution)/shard_map/ppermute | solution.py:74
  80.7 7.9 %collective-permute-start.34 = (bf16[16,6144]{1,0:T(8,128)(2,1)S(1)}, bf16[16,6144]{1,0:T(8,128)(2,1)S(1)}, u32[]{:S(2)}, u32[]{:S(2)}) collective-permute-start(bf16[16,6144]{1,0:T(8,128)(2,1)S(1)} %get-tuple-element.79), channel_id=1, source_target_pairs={{0,4},{1,5},{4,8},{5,9},{8,12},{9,13},{12,14},{13,15},{14,10},{15,... | collective-permute-start | bytes 589832 | tf_op jit(solution)/shard_map/ppermute | solution.py:74
  81.3 7.9 %collective-permute-start.30 = (bf16[16,6144]{1,0:T(8,128)(2,1)S(1)}, bf16[16,6144]{1,0:T(8,128)(2,1)S(1)}, u32[]{:S(2)}, u32[]{:S(2)}) collective-permute-start(bf16[16,6144]{1,0:T(8,128)(2,1)S(1)} %fusion.16), channel_id=1, source_target_pairs={{4,0},{5,1},{8,4},{9,5},{12,8},{13,9},{14,12},{15,13},{10,14},{11,... | collective-permute-start | bytes 589832 | tf_op jit(solution)/shard_map/ppermute | solution.py:74
  82.9 8.0 %collective-permute-start.33 = (bf16[16,6144]{1,0:T(8,128)(2,1)S(1)}, bf16[16,6144]{1,0:T(8,128)(2,1)S(1)}, u32[]{:S(2)}, u32[]{:S(2)}) collective-permute-start(bf16[16,6144]{1,0:T(8,128)(2,1)S(1)} %get-tuple-element.78), channel_id=1, source_target_pairs={{4,0},{5,1},{8,4},{9,5},{12,8},{13,9},{14,12},{15,13},{10,14},{11,... | collective-permute-start | bytes 589832 | tf_op jit(solution)/shard_map/ppermute | solution.py:74
  84.5 11.7 %copy-start.1 = (bf16[128,6144]{1,0:T(8,128)(2,1)S(1)}, bf16[128,6144]{1,0:T(8,128)(2,1)}, u32[]{:S(2)}) copy-start(bf16[128,6144]{1,0:T(8,128)(2,1)} %param.8) | copy-start | bytes 4718596
  88.7 5.7 %collective-permute-start.35 = (bf16[16,6144]{1,0:T(8,128)(2,1)S(1)}, bf16[16,6144]{1,0:T(8,128)(2,1)S(1)}, u32[]{:S(2)}, u32[]{:S(2)}) collective-permute-start(bf16[16,6144]{1,0:T(8,128)(2,1)S(1)} %fusion.5), channel_id=1, source_target_pairs={{0,4},{1,5},{4,8},{5,9},{8,12},{9,13},{12,14},{13,15},{14,10},{15,... | collective-permute-start | bytes 589832 | tf_op jit(solution)/shard_map/ppermute | solution.py:74

commit v6 on v5

--- a/solution.py
+++ b/solution.py
@@ -11,14 +11,6 @@
 MARK = jax.ShapeDtypeStruct((8, LANES), jnp.float32)
 
 
-def whole(shape):
-    return pl.BlockSpec(shape, lambda j: (0,) * len(shape))
-
-
-def columns(rows, width):
-    return pl.BlockSpec((rows, width), lambda j: (0, j))
-
-
 def parts_of(d, most):
     width = LANES
     for w in range(LANES, most + 1, LANES):
@@ -31,24 +23,46 @@
     return pltpu.CompilerParams(vmem_limit_bytes=megabytes << 20)
 
 
-def grad_kernel(marks, side_ref, rows_ref, *refs):
-    out_ref, mark_ref = refs[marks:]
-    out_ref[...] = jnp.dot(
-        side_ref[...], rows_ref[...], preferred_element_type=jnp.float32
-    ).astype(jnp.bfloat16)
+def grad_kernel(parts, width, marks, side_ref, rows_ref, *refs):
+    out_ref, mark_ref, rows_buf, out_buf, load_sem, store_sem = refs[marks:]
+    spans = [pl.ds(j * width, width) for j in range(parts)]
+    loads = [
+        pltpu.make_async_copy(rows_ref.at[:, at], rows_buf.at[:, at], load_sem.at[j])
+        for j, at in enumerate(spans)
+    ]
+    stores = [
+        pltpu.make_async_copy(out_buf.at[:, at], out_ref.at[:, at], store_sem.at[j])
+        for j, at in enumerate(spans)
+    ]
+    for load in loads:
+        load.start()
     mark_ref[...] = jnp.zeros(mark_ref.shape, jnp.float32)
+    side = side_ref[...]
+    for j, at in enumerate(spans):
+        loads[j].wait()
+        out_buf[:, at] = jnp.dot(
+            side, rows_buf[:, at], preferred_element_type=jnp.float32
+        ).astype(jnp.bfloat16)
+        stores[j].start()
+    for store in stores:
+        store.wait()
 
 
 def weight_grad(side, rows, d, marks):
     r, f = side.shape
     parts, width = parts_of(d, 1024)
     return pl.pallas_call(
-        lambda *refs: grad_kernel(len(marks), *refs),
-        grid=(parts,),
-        in_specs=[whole((f, r)), columns(r, width)] + [ANY] * len(marks),
-        out_specs=[columns(f, width), whole(MARK.shape)],
+        lambda *refs: grad_kernel(parts, width, len(marks), *refs),
+        in_specs=[pl.BlockSpec(memory_space=pltpu.VMEM), ANY] + [ANY] * len(marks),
+        out_specs=[ANY, pl.BlockSpec(memory_space=pltpu.VMEM)],
         out_shape=[jax.ShapeDtypeStruct((f, d), jnp.bfloat16), MARK],
-        compiler_params=params(12),
+        scratch_shapes=[
+            pltpu.VMEM((r, d), jnp.bfloat16),
+            pltpu.VMEM((f, d), jnp.bfloat16),
+            pltpu.SemaphoreType.DMA((parts,)),
+            pltpu.SemaphoreType.DMA((parts,)),
+        ],
+        compiler_params=params(20),
         cost_estimate=pl.CostEstimate(
             flops=2 * r * f * d, bytes_accessed=2 * d * (r + f), transcendentals=0
         ),
@@ -73,25 +87,30 @@
     def permute(x, pairs):
         return lax.ppermute(x, "et", pairs)
 
+    def far_block(held_r, held_l):
+        at = held_r.shape[1] // 2 // LANES * LANES
+        return jnp.concatenate(
+            [permute(held_r[:, :at], right_pairs), permute(held_l[:, at:], left_pairs)], axis=1
+        )
+
     def gather_rows(x, dy):
-        held_xr, held_xl = permute(x, right_pairs), permute(x, left_pairs)
+        held_xr = held_xl = x
         held_dr = held_dl = dy
-        got_x, got_d = [x, held_xr, held_xl], [dy]
+        got_x, got_d = [x], [dy]
         for k in range(1, steps):
-            if k > 1:
-                held_xr = permute(held_xr, right_pairs)
-                held_xl = permute(held_xl, left_pairs)
-                got_x += [held_xr, held_xl]
+            held_xr = permute(held_xr, right_pairs)
+            held_xl = permute(held_xl, left_pairs)
+            held_dr = permute(held_dr, right_pairs)
             held_dl = permute(held_dl, left_pairs)
-            held_dr = permute(held_dr, right_pairs)
+            got_x += [held_xr, held_xl]
             got_d += [held_dr, held_dl]
-        far_x = permute(held_xr, right_pairs)
-        far_d = permute(held_dl, left_pairs)
+        got_d.append(far_block(held_dr, held_dl))
+        far_x = far_block(held_xr, held_xl)
         early_x = permute(jnp.concatenate(got_x, axis=0), core_pairs)
-        early_d = permute(jnp.concatenate(got_d, axis=0), core_pairs)
         late_x = permute(far_x, core_pairs)
         rows_x = jnp.concatenate(got_x + [far_x, early_x, late_x], axis=0)
-        return rows_x, got_d, early_d, far_d
+        chip_d = jnp.concatenate(got_d, axis=0)
+        return rows_x, jnp.concatenate([chip_d, permute(chip_d, core_pairs)], axis=0)
 
     cut = max(2 * steps - 3, 1) * CAP
 
@@ -143,7 +162,7 @@
             for a in (tokens, out_grad, coef[:, None])
         )
         slot_coef = jnp.broadcast_to(slot_coef, (CAP, LANES))
-        rows_wide, got_d, early_d, far_d = gather_rows(
+        rows_wide, rows_dy = gather_rows(
             jnp.concatenate([slot_x, slot_coef], axis=1), slot_dy
         )
         rows_x = rows_wide[:, :d]
@@ -157,9 +176,8 @@
         hidden = (coef_rows * act * up).astype(jnp.bfloat16)
         out_rows = jnp.dot(hidden, w_down, preferred_element_type=jnp.float32)
         out_sent = out_rows[half:].astype(jnp.bfloat16)
-        out_rows, far_d = lax.optimization_barrier((out_rows, far_d))
+        rows_dy, out_sent = lax.optimization_barrier((rows_dy, out_sent))
         out_total = pair_sum(out_rows[:half], out_sent)
-        rows_dy = jnp.concatenate(got_d + [far_d, early_d, permute(far_d, core_pairs)], axis=0)
 
         dhid = jnp.dot(rows_dy, w_down.T, preferred_element_type=jnp.float32)
         scaled = coef_rows * dhid
@@ -181,7 +199,7 @@
             if at <= steps:
                 out_carry.update(send(wave(out_total, out_carry, at, "l")))
             dx_blocks = wave(dx_total, dx_carry, at - 1, "r")
-            if work:
+            if work and at in (2, 3, steps + 1):
                 side, rows = work.pop(0)
                 side, dx_blocks = tie(side, dx_blocks)
                 grad, mark = weight_grad(side, rows, d, marks)

time: 96.4 us -> 96.5 us (level)
  starting transfers between devices: 31.5 us -> 34 us
  Pallas kernels: 12.5 us -> 10.4 us
    ppermute x36 -> x37, starting transfers between devices: 31.5 us -> 34 us  [permute(): return lax.ppermute(x, 'et', pairs)]
    pallas_call x3, Pallas kernels: 12.5 us -> 10.4 us  [weight_grad(): pl.pallas_call(lambda *refs: grad_kernel(parts, width, len(marks), *refs)...]
    ppermute x36 -> x37, waiting for transfers between devices: 30.5 us -> 29.6 us  [permute(): return lax.ppermute(x, 'et', pairs)]
    unnamed x24 -> x26, local copies, waits for them, and re-layouts: 2.61 us -> 2.54 us
  transfers between devices with their start and end apart: 36 -> 37, of which waited for: 16 -> 21; matrix products, arithmetic and copies ran while one was open for 16% -> 16% of each run, Pallas kernels for 13% -> 11%
where the time goes in v6:
time: 96.5 us; the launch traced here: 96.2 us
  starting transfers between devices  34 us (35%)
  waiting for transfers between devices  29.6 us (31%)
  matrix products  15 us (16%)
  Pallas kernels  10.4 us (11%)
  local copies, waits for them, and re-layouts  3.59 us (4%)
  other arithmetic  2.47 us (3%)
  between operations  1.09 us (1%)
    ppermute x37, starting transfers between devices, permute(): return lax.ppermute(x, 'et', pairs)  34 us
    ppermute x37, waiting for transfers between devices, permute(): return lax.ppermute(x, 'et', pairs)  29.6 us
    pallas_call x3, Pallas kernels, weight_grad(): pl.pallas_call(lambda *refs: grad_kernel(parts, width, len(marks), *refs)...  10.4 us
    dot_general x2, matrix products, per_device(): jnp.dot(select.T, final(total[0], carry), preferred_element_type=jnp.floa...  3.53 us
    unnamed x26, local copies, waits for them, and re-layouts  2.54 us
    dot_general x3, matrix products, per_device(): jnp.dot(select, a, preferred_element_type=jnp.float32).astype(jnp.bfloat16)  2.15 us
  transfers between devices with their start and end apart: 37, of which 21 were waited for; matrix products, arithmetic and copies ran while one was open for 16% of the time, Pallas kernels for 11%

profile of v6, /device:TPU:0, one launch (start us, length us, event | category | flops | bytes accessed | tf_op | source)
XLA Modules:
  0.0 96.2 jit_solution(17040108369664874317)
XLA Ops:
  0.6 0.8 select_reduce_fusion
  2.1 0.3 constant_dynamic-update-slice_fusion.23
  2.4 3.0 %collective-permute-start.11 = (bf16[16,6144]{1,0:T(8,128)(2,1)S(1)}, bf16[16,6144]{1,0:T(8,128)(2,1)S(1)}, u32[]{:S(2)}, u32[]{:S(2)}) collective-permute-start(bf16[16,6144]{1,0:T(8,128)(2,1)S(1)} %get-tuple-element.130), channel_id=1, source_target_pairs={{4,0},{5,1},{8,4},{9,5},{12,8},{13,9},{14,12},{15,13},{10,14},{11,... | collective-permute-start | bytes 589832 | tf_op jit(solution)/shard_map/ppermute | solution.py:88
  5.7 1.7 %convolution_convert_fusion.3 = bf16[16,6144]{1,0:T(8,128)(2,1)S(1)} fusion(bf16[128,6144]{1,0:T(8,128)(2,1)} %param.7, s32[128]{0:T(128)S(1)} %add_reduce_fusion, pred[128]{0:T(512)(128)(4,1)S(1)} %reduce_or.9), kind=kOutput, calls=%fused_computation.4 | convolution fusion | flops 25268224 | bytes 1770112 | tf_op jit(solution)/shard_map/dot_general | solution.py:161
  7.5 2.0 %collective-permute-start = (bf16[16,6272]{1,0:T(8,128)(2,1)S(1)}, bf16[16,6272]{1,0:T(8,128)(2,1)S(1)}, u32[]{:S(2)}, u32[]{:S(2)}) collective-permute-start(bf16[16,6272]{1,0:T(8,128)(2,1)S(1)} %get-tuple-element.113), channel_id=1, source_target_pairs={{0,4},{1,5},{4,8},{5,9},{8,12},{9,13},{12,14},{13,15},{14,10},{15,... | collective-permute-start | bytes 602120 | tf_op jit(solution)/shard_map/ppermute | solution.py:88
  9.6 0.8 collective-permute-done.11
  10.4 2.2 %collective-permute-start.13 = (bf16[16,6144]{1,0:T(8,128)(2,1)S(1)}, bf16[16,6144]{1,0:T(8,128)(2,1)S(1)}, u32[]{:S(2)}, u32[]{:S(2)}) collective-permute-start(bf16[16,6144]{1,0:T(8,128)(2,1)S(1)} %collective-permute-done.11), channel_id=1, source_target_pairs={{4,0},{5,1},{8,4},{9,5},{12,8},{13,9},{14,12},{15,13},{10,14},{11,... | collective-permute-start | bytes 589832 | tf_op jit(solution)/shard_map/ppermute | solution.py:88
  12.6 0.7 collective-permute-done.10
  13.3 4.2 %collective-permute-done = bf16[16,6272]{1,0:T(8,128)(2,1)S(1)} collective-permute-done((bf16[16,6272]{1,0:T(8,128)(2,1)S(1)}, bf16[16,6272]{1,0:T(8,128)(2,1)S(1)}, u32[]{:S(2)}, u32[]{:S(2)}) %collective-permute-start) | collective-permute-done | bytes 200736 | tf_op jit(solution)/shard_map/ppermute | solution.py:88
  17.5 2.0 %collective-permute-start.3 = (bf16[16,6272]{1,0:T(8,128)(2,1)S(1)}, bf16[16,6272]{1,0:T(8,128)(2,1)S(1)}, u32[]{:S(2)}, u32[]{:S(2)}) collective-permute-start(bf16[16,6272]{1,0:T(8,128)(2,1)S(1)} %collective-permute-done.1), channel_id=1, source_target_pairs={{4,0},{5,1},{8,4},{9,5},{12,8},{13,9},{14,12},{15,13},{10,14},{11,... | collective-permute-start | bytes 602120 | tf_op jit(solution)/shard_map/ppermute | solution.py:88
  19.6 1.5 %collective-permute-done.13 = bf16[16,6144]{1,0:T(8,128)(2,1)S(1)} collective-permute-done((bf16[16,6144]{1,0:T(8,128)(2,1)S(1)}, bf16[16,6144]{1,0:T(8,128)(2,1)S(1)}, u32[]{:S(2)}, u32[]{:S(2)}) %collective-permute-start.13) | collective-permute-done | bytes 196640 | tf_op jit(solution)/shard_map/ppermute | solution.py:88
  21.2 0.6 collective-permute-start.15
  21.8 1.4 %collective-permute-start.14 = (bf16[16,6144]{1,0:T(8,128)(2,1)S(1)}, bf16[16,6144]{1,0:T(8,128)(2,1)S(1)}, u32[]{:S(2)}, u32[]{:S(2)}) collective-permute-start(bf16[16,6144]{1,0:T(8,128)(2,1)S(1)} %collective-permute-done.12), channel_id=1, source_target_pairs={{0,4},{1,5},{4,8},{5,9},{8,12},{9,13},{12,14},{13,15},{14,10},{15,... | collective-permute-start | bytes 589832 | tf_op jit(solution)/shard_map/ppermute | solution.py:88
  23.3 2.8 %collective-permute-done.2 = bf16[16,6272]{1,0:T(8,128)(2,1)S(1)} collective-permute-done((bf16[16,6272]{1,0:T(8,128)(2,1)S(1)}, bf16[16,6272]{1,0:T(8,128)(2,1)S(1)}, u32[]{:S(2)}, u32[]{:S(2)}) %collective-permute-start.2) | collective-permute-done | bytes 200736 | tf_op jit(solution)/shard_map/ppermute | solution.py:88
  26.1 2.0 %collective-permute-start.5 = (bf16[16,6272]{1,0:T(8,128)(2,1)S(1)}, bf16[16,6272]{1,0:T(8,128)(2,1)S(1)}, u32[]{:S(2)}, u32[]{:S(2)}) collective-permute-start(bf16[16,6272]{1,0:T(8,128)(2,1)S(1)} %collective-permute-done.3), channel_id=1, source_target_pairs={{4,0},{5,1},{8,4},{9,5},{12,8},{13,9},{14,12},{15,13},{10,14},{11,... | collective-permute-start | bytes 602120 | tf_op jit(solution)/shard_map/ppermute | solution.py:88
  28.2 1.5 %collective-permute-done.15 = bf16[16,6144]{1,0:T(8,128)(2,1)S(1)} collective-permute-done((bf16[16,6144]{1,0:T(8,128)(2,1)S(1)}, bf16[16,6144]{1,0:T(8,128)(2,1)S(1)}, u32[]{:S(2)}, u32[]{:S(2)}) %collective-permute-start.15) | collective-permute-done | bytes 196640 | tf_op jit(solution)/shard_map/ppermute | solution.py:88
  29.7 0.9 collective-permute-start.17
  30.6 1.2 %collective-permute-start.16 = (bf16[16,3072]{1,0:T(8,128)(2,1)S(1)}, bf16[16,3072]{1,0:T(8,128)(2,1)S(1)}, u32[]{:S(2)}, u32[]{:S(2)}) collective-permute-start(bf16[16,3072]{1,0:T(8,128)(2,1)S(1)} %slice.145), channel_id=1, source_target_pairs={{0,4},{1,5},{4,8},{5,9},{8,12},{9,13},{12,14},{13,15},{14,10},{15,... | collective-permute-start | bytes 294920 | tf_op jit(solution)/shard_map/ppermute | solution.py:88
  31.9 2.3 %collective-permute-done.4 = bf16[16,6272]{1,0:T(8,128)(2,1)S(1)} collective-permute-done((bf16[16,6272]{1,0:T(8,128)(2,1)S(1)}, bf16[16,6272]{1,0:T(8,128)(2,1)S(1)}, u32[]{:S(2)}, u32[]{:S(2)}) %collective-permute-start.4) | collective-permute-done | bytes 200736 | tf_op jit(solution)/shard_map/ppermute | solution.py:88
  34.2 0.5 collective-permute-start.6
  34.7 1.7 %collective-permute-start.7 = (bf16[16,3200]{1,0:T(8,128)(2,1)S(1)}, bf16[16,3200]{1,0:T(8,128)(2,1)S(1)}, u32[]{:S(2)}, u32[]{:S(2)}) collective-permute-start(bf16[16,3200]{1,0:T(8,128)(2,1)S(1)} %slice.141), channel_id=1, source_target_pairs={{4,0},{5,1},{8,4},{9,5},{12,8},{13,9},{14,12},{15,13},{10,14},{11,... | collective-permute-start | bytes 307208 | tf_op jit(solution)/shard_map/ppermute | solution.py:88
  36.5 0.5 collective-permute-start.18
  37.1 1.8 %collective-permute-done.6 = bf16[16,3072]{1,0:T(8,128)(2,1)S(1)} collective-permute-done((bf16[16,3072]{1,0:T(8,128)(2,1)S(1)}, bf16[16,3072]{1,0:T(8,128)(2,1)S(1)}, u32[]{:S(2)}, u32[]{:S(2)}) %collective-permute-start.6) | collective-permute-done | bytes 98336 | tf_op jit(solution)/shard_map/ppermute | solution.py:88
  38.9 0.5 collective-permute-done.7
  39.8 2.4 %collective-permute-done.9 = bf16[16,6272]{1,0:T(8,128)(2,1)S(1)} collective-permute-done((bf16[16,6272]{1,0:T(8,128)(2,1)S(1)}, bf16[16,6272]{1,0:T(8,128)(2,1)S(1)}, u32[]{:S(2)}, u32[]{:S(2)}) %collective-permute-start.9) | collective-permute-done | bytes 200736 | tf_op jit(solution)/shard_map/ppermute | solution.py:88
  42.3 1.3 %fusion.2 = f32[256,336]{0,1:T(8,128)S(1)} fusion(bf16[6144,336]{0,1:T(8,128)(2,1)S(1)} %copy-done.3, bf16[256,6272]{1,0:T(8,128)(2,1)S(1)} %constant_dynamic-update-slice_fusion.7.refs_1_), kind=kOutput, calls=%fused_computation.9 | convolution fusion | flops 1056964608 | bytes 7618560 | tf_op jit(solution)/shard_map/dot_general | solution.py:172
  43.6 0.9 copy-done.4
  44.5 1.3 %multiply_convert_fusion.2 = (bf16[256,336]{0,1:T(8,128)(2,1)S(1)}, f32[256,336]{0,1:T(8,128)S(1)}) fusion(f32[256]{0:T(256)S(1)} %convert_reduce_fusion, f32[256,336]{0,1:T(8,128)S(1)} %fusion.2, bf16[6144,336]{0,1:T(8,128)(2,1)S(1)} %copy-done.4, bf16[256,6272]{1,0:T(8,128)(2,1)S(1)} %constant_dynamic-update-slice_fusion.7.refs_1_), kind=kOutput, calls=%fused_computation.46 | convolution fusion | flops 1057566720 | bytes 8135680 | tf_op jit(solution)/shard_map/dot_general | solution.py:173
  45.8 0.9 copy-done.2
  46.7 1.8 %fusion.42 = f32[256,6144]{1,0:T(8,128)S(1)} fusion(bf16[256,336]{0,1:T(8,128)(2,1)S(1)} %get-tuple-element.80, bf16[336,6144]{1,0:T(8,128)(2,1)S(1)} %copy-done.2), kind=kOutput, calls=%fused_computation.109 | convolution fusion | flops 1056964608 | bytes 10592256 | tf_op jit(solution)/shard_map/dot_general | solution.py:177
  48.5 0.2 slice.222
  48.9 0.2 collective-permute-start.20
  49.2 0.4 collective-permute-start.19
  49.6 1.3 %multiply_convert_fusion = (bf16[256,336]{0,1:T(8,128)(2,1)S(1)}, bf16[256,336]{0,1:T(8,128)(2,1)S(1)}) fusion(f32[256,336]{0,1:T(8,128)S(1)} %fusion.2, f32[256,336]{0,1:T(8,128)S(1)} %get-tuple-element.129, bf16[256,6144]{1,0:T(8,128)(2,1)S(1)} %constant_dynamic-update-slice_fusion.24.refs_1_, bf16[336,6144]{1,0:T(8,128)(2,1)S(1)} %copy-done.2, ...), kind=kOutput, calls=%fused_computation.44 | convolution fusion | flops 1058168832 | bytes 8307712 | tf_op jit(solution)/shard_map/dot_general | solution.py:182
  51.2 1.6 %collective-permute-start.21 = (bf16[16,6144]{1,0:T(8,128)(2,1)S(1)}, bf16[16,6144]{1,0:T(8,128)(2,1)S(1)}, u32[]{:S(2)}, u32[]{:S(2)}) collective-permute-start(bf16[16,6144]{1,0:T(8,128)(2,1)S(1)} %get-tuple-element.49), channel_id=1, source_target_pairs={{4,0},{5,1},{8,4},{9,5},{12,8},{13,9},{14,12},{15,13},{10,14},{11,... | collective-permute-start | bytes 589832 | tf_op jit(solution)/shard_map/ppermute | solution.py:88
  52.8 0.5 collective-permute-start.22
  53.2 1.8 %fusion.43 = f32[256,6144]{1,0:T(8,128)S(1)} fusion(bf16[256,336]{0,1:T(8,128)(2,1)S(1)} %get-tuple-element.59, bf16[6144,336]{0,1:T(8,128)(2,1)S(1)} %copy-done.3), kind=kOutput, calls=%fused_computation.110 | convolution fusion | flops 1056964608 | bytes 10592256 | tf_op jit(solution)/shard_map/dot_general | solution.py:188
  55.1 1.8 %convolution_add_fusion = f32[256,6144]{1,0:T(8,128)S(1)} fusion(f32[256,6144]{1,0:T(8,128)S(1)} %fusion.43, bf16[256,336]{0,1:T(8,128)(2,1)S(1)} %get-tuple-element.58, bf16[6144,336]{0,1:T(8,128)(2,1)S(1)} %copy-done.4), kind=kOutput, calls=%fused_computation | convolution fusion | flops 1058537472 | bytes 16883712 | tf_op jit(solution)/shard_map/dot_general | solution.py:188
  57.1 1.1 %collective-permute-done.21 = bf16[16,6144]{1,0:T(8,128)(2,1)S(1)} collective-permute-done((bf16[16,6144]{1,0:T(8,128)(2,1)S(1)}, bf16[16,6144]{1,0:T(8,128)(2,1)S(1)}, u32[]{:S(2)}, u32[]{:S(2)}) %collective-permute-start.21) | collective-permute-done | bytes 196640 | tf_op jit(solution)/shard_map/ppermute | solution.py:88
  58.2 1.3 %collective-permute-done.22 = bf16[16,6144]{1,0:T(8,128)(2,1)S(1)} collective-permute-done((bf16[16,6144]{1,0:T(8,128)(2,1)S(1)}, bf16[16,6144]{1,0:T(8,128)(2,1)S(1)}, u32[]{:S(2)}, u32[]{:S(2)}) %collective-permute-start.22) | collective-permute-done | bytes 196640 | tf_op jit(solution)/shard_map/ppermute | solution.py:88
  59.6 0.5 collective-permute-start.23
  60.4 1.6 %collective-permute-start.27 = (bf16[16,6144]{1,0:T(8,128)(2,1)S(1)}, bf16[16,6144]{1,0:T(8,128)(2,1)S(1)}, u32[]{:S(2)}, u32[]{:S(2)}) collective-permute-start(bf16[16,6144]{1,0:T(8,128)(2,1)S(1)} %fusion.13), channel_id=1, source_target_pairs={{4,0},{5,1},{8,4},{9,5},{12,8},{13,9},{14,12},{15,13},{10,14},{11,... | collective-permute-start | bytes 589832 | tf_op jit(solution)/shard_map/ppermute | solution.py:88
  62.1 0.4 collective-permute-start.28
  62.7 1.6 %collective-permute-start.25 = (bf16[16,6144]{1,0:T(8,128)(2,1)S(1)}, bf16[16,6144]{1,0:T(8,128)(2,1)S(1)}, u32[]{:S(2)}, u32[]{:S(2)}) collective-permute-start(bf16[16,6144]{1,0:T(8,128)(2,1)S(1)} %get-tuple-element.54), channel_id=1, source_target_pairs={{4,0},{5,1},{8,4},{9,5},{12,8},{13,9},{14,12},{15,13},{10,14},{11,... | collective-permute-start | bytes 589832 | tf_op jit(solution)/shard_map/ppermute | solution.py:88
  64.3 0.4 collective-permute-start.26
  64.8 3.3 %shard_map.110 = (bf16[336,6144]{1,0:T(8,128)(2,1)}, f32[8,128]{1,0:T(8,128)S(1)}) custom-call(bf16[336,256]{1,0:T(8,128)(2,1)S(1)} %bitcast.27, bf16[256,6272]{1,0:T(8,128)(2,1)S(1)} %constant_dynamic-update-slice_fusion.7.refs_1_), custom_call_target="tpu_custom_call" | custom-call | flops 1056964608 | bytes 7274496 | tf_op jit(solution)/shard_map/pallas_call | solution.py:54
  68.2 1.6 %collective-permute-done.28 = bf16[16,6144]{1,0:T(8,128)(2,1)S(1)} collective-permute-done((bf16[16,6144]{1,0:T(8,128)(2,1)S(1)}, bf16[16,6144]{1,0:T(8,128)(2,1)S(1)}, u32[]{:S(2)}, u32[]{:S(2)}) %collective-permute-start.28) | collective-permute-done | bytes 196640 | tf_op jit(solution)/shard_map/ppermute | solution.py:88
  69.9 1.6 %collective-permute-start.29 = (bf16[16,6144]{1,0:T(8,128)(2,1)S(1)}, bf16[16,6144]{1,0:T(8,128)(2,1)S(1)}, u32[]{:S(2)}, u32[]{:S(2)}) collective-permute-start(bf16[16,6144]{1,0:T(8,128)(2,1)S(1)} %get-tuple-element.69), channel_id=1, source_target_pairs={{4,0},{5,1},{8,4},{9,5},{12,8},{13,9},{14,12},{15,13},{10,14},{11,... | collective-permute-start | bytes 589832 | tf_op jit(solution)/shard_map/ppermute | solution.py:88
  71.6 0.4 collective-permute-start.30
  72.0 2.1 %collective-permute-done.26 = bf16[16,6144]{1,0:T(8,128)(2,1)S(1)} collective-permute-done((bf16[16,6144]{1,0:T(8,128)(2,1)S(1)}, bf16[16,6144]{1,0:T(8,128)(2,1)S(1)}, u32[]{:S(2)}, u32[]{:S(2)}) %collective-permute-start.26) | collective-permute-done | bytes 196640 | tf_op jit(solution)/shard_map/ppermute | solution.py:88
  74.1 0.2 slice_add_fusion
  74.4 1.6 %collective-permute-start.32 = (bf16[16,6144]{1,0:T(8,128)(2,1)S(1)}, bf16[16,6144]{1,0:T(8,128)(2,1)S(1)}, u32[]{:S(2)}, u32[]{:S(2)}) collective-permute-start(bf16[16,6144]{1,0:T(8,128)(2,1)S(1)} %fusion.15), channel_id=1, source_target_pairs={{4,0},{5,1},{8,4},{9,5},{12,8},{13,9},{14,12},{15,13},{10,14},{11,... | collective-permute-start | bytes 589832 | tf_op jit(solution)/shard_map/ppermute | solution.py:88
  76.0 0.4 collective-permute-start.33
  76.5 3.3 %shard_map.111 = (bf16[336,6144]{1,0:T(8,128)(2,1)}, f32[8,128]{1,0:T(8,128)S(1)}) custom-call(bf16[336,256]{1,0:T(8,128)(2,1)S(1)} %bitcast.28, bf16[256,6272]{1,0:T(8,128)(2,1)S(1)} %constant_dynamic-update-slice_fusion.7.refs_1_, f32[8,128]{1,0:T(8,128)S(1)} %get-tuple-element.65.refs_2_), custom_call_target="tpu_custom_call" | custom-call | flops 1056964608 | bytes 7274496 | tf_op jit(solution)/shard_map/pallas_call | solution.py:54
  79.8 0.3 collective-permute-done.32
  80.1 1.6 %collective-permute-done.33 = bf16[16,6144]{1,0:T(8,128)(2,1)S(1)} collective-permute-done((bf16[16,6144]{1,0:T(8,128)(2,1)S(1)}, bf16[16,6144]{1,0:T(8,128)(2,1)S(1)}, u32[]{:S(2)}, u32[]{:S(2)}) %collective-permute-start.33) | collective-permute-done | bytes 196640 | tf_op jit(solution)/shard_map/ppermute | solution.py:88
  81.8 0.5 collective-permute-start.35
  82.3 1.6 %collective-permute-start.31 = (bf16[16,6144]{1,0:T(8,128)(2,1)S(1)}, bf16[16,6144]{1,0:T(8,128)(2,1)S(1)}, u32[]{:S(2)}, u32[]{:S(2)}) collective-permute-start(bf16[16,6144]{1,0:T(8,128)(2,1)S(1)} %fusion.16), channel_id=1, source_target_pairs={{4,0},{5,1},{8,4},{9,5},{12,8},{13,9},{14,12},{15,13},{10,14},{11,... | collective-permute-start | bytes 589832 | tf_op jit(solution)/shard_map/ppermute | solution.py:88
  84.0 1.2 %collective-permute-start.34 = (bf16[16,6144]{1,0:T(8,128)(2,1)S(1)}, bf16[16,6144]{1,0:T(8,128)(2,1)S(1)}, u32[]{:S(2)}, u32[]{:S(2)}) collective-permute-start(bf16[16,6144]{1,0:T(8,128)(2,1)S(1)} %get-tuple-element.75), channel_id=1, source_target_pairs={{4,0},{5,1},{8,4},{9,5},{12,8},{13,9},{14,12},{15,13},{10,14},{11,... | collective-permute-start | bytes 589832 | tf_op jit(solution)/shard_map/ppermute | solution.py:88
  85.1 2.8 %collective-permute-done.35 = bf16[16,6144]{1,0:T(8,128)(2,1)S(1)} collective-permute-done((bf16[16,6144]{1,0:T(8,128)(2,1)S(1)}, bf16[16,6144]{1,0:T(8,128)(2,1)S(1)}, u32[]{:S(2)}, u32[]{:S(2)}) %collective-permute-start.35) | collective-permute-done | bytes 196640 | tf_op jit(solution)/shard_map/ppermute | solution.py:88
  87.9 0.7 collective-permute-start.36
  88.8 1.8 %convolution_convert_fusion.1 = bf16[128,6144]{1,0:T(8,128)(2,1)} fusion(f32[80,6144]{1,0:T(8,128)S(1)} %slice_add_fusion.1, bf16[16,6144]{1,0:T(8,128)(2,1)S(1)} %collective-permute-done.30, bf16[16,6144]{1,0:T(8,128)(2,1)S(1)} %collective-permute-done.31, s32[128]{0:T(128)S(1)} %add_reduce_fusion, pred[128]{0:T(512)(128)(4,1)S(1)} %reduce_or.9), kind=kOutput, calls=%fused_computation.2 | convolution fusion | flops 26447872 | bytes 2360320 | tf_op jit(solution)/shard_map/dot_general | solution.py:215
  90.5 3.9 %shard_map.112 = (bf16[336,6144]{1,0:T(8,128)(2,1)}, f32[8,128]{1,0:T(8,128)}) custom-call(bf16[336,256]{1,0:T(8,128)(2,1)S(1)} %bitcast.26, bf16[256,6144]{1,0:T(8,128)(2,1)S(1)} %constant_dynamic-update-slice_fusion.24.refs_1_, f32[8,128]{1,0:T(8,128)S(1)} %get-tuple-element.81.refs_2_), custom_call_target="tpu_custom_call" | custom-call | flops 1056964608 | bytes 7274496 | tf_op jit(solution)/shard_map/pallas_call | solution.py:54
  94.4 1.8 %convolution_convert_fusion = bf16[128,6144]{1,0:T(8,128)(2,1)} fusion(f32[80,6144]{1,0:T(8,128)S(1)} %slice_add_fusion, bf16[16,6144]{1,0:T(8,128)(2,1)S(1)} %collective-permute-done.36, bf16[16,6144]{1,0:T(8,128)(2,1)S(1)} %collective-permute-done.34, s32[128]{0:T(128)S(1)} %add_reduce_fusion, pred[128]{0:T(512)(128)(4,1)S(1)} %reduce_or.9), kind=kOutput, calls=%fused_computation.1 | convolution fusion | flops 26447872 | bytes 2360320 | tf_op jit(solution)/shard_map/dot_general | solution.py:215
  (88 shorter events, 4.1 us)
Async XLA Ops:
  0.6 1.4 %copy-start = (bf16[128,6144]{1,0:T(8,128)(2,1)S(1)}, bf16[128,6144]{1,0:T(8,128)(2,1)}, u32[]{:S(2)}) copy-start(bf16[128,6144]{1,0:T(8,128)(2,1)} %param.8) | copy-start | bytes 4718596
  2.4 8.0 %collective-permute-start.11 = (bf16[16,6144]{1,0:T(8,128)(2,1)S(1)}, bf16[16,6144]{1,0:T(8,128)(2,1)S(1)}, u32[]{:S(2)}, u32[]{:S(2)}) collective-permute-start(bf16[16,6144]{1,0:T(8,128)(2,1)S(1)} %get-tuple-element.130), channel_id=1, source_target_pairs={{4,0},{5,1},{8,4},{9,5},{12,8},{13,9},{14,12},{15,13},{10,14},{11,... | collective-permute-start | bytes 589832 | tf_op jit(solution)/shard_map/ppermute | solution.py:88
  5.4 7.8 %collective-permute-start.10 = (bf16[16,6144]{1,0:T(8,128)(2,1)S(1)}, bf16[16,6144]{1,0:T(8,128)(2,1)S(1)}, u32[]{:S(2)}, u32[]{:S(2)}) collective-permute-start(bf16[16,6144]{1,0:T(8,128)(2,1)S(1)} %get-tuple-element.130), channel_id=1, source_target_pairs={{0,4},{1,5},{4,8},{5,9},{8,12},{9,13},{12,14},{13,15},{14,10},{15,... | collective-permute-start | bytes 589832 | tf_op jit(solution)/shard_map/ppermute | solution.py:88
  7.5 10.0 %collective-permute-start = (bf16[16,6272]{1,0:T(8,128)(2,1)S(1)}, bf16[16,6272]{1,0:T(8,128)(2,1)S(1)}, u32[]{:S(2)}, u32[]{:S(2)}) collective-permute-start(bf16[16,6272]{1,0:T(8,128)(2,1)S(1)} %get-tuple-element.113), channel_id=1, source_target_pairs={{0,4},{1,5},{4,8},{5,9},{8,12},{9,13},{12,14},{13,15},{14,10},{15,... | collective-permute-start | bytes 602120 | tf_op jit(solution)/shard_map/ppermute | solution.py:88
  9.5 8.0 %collective-permute-start.1 = (bf16[16,6272]{1,0:T(8,128)(2,1)S(1)}, bf16[16,6272]{1,0:T(8,128)(2,1)S(1)}, u32[]{:S(2)}, u32[]{:S(2)}) collective-permute-start(bf16[16,6272]{1,0:T(8,128)(2,1)S(1)} %get-tuple-element.113), channel_id=1, source_target_pairs={{4,0},{5,1},{8,4},{9,5},{12,8},{13,9},{14,12},{15,13},{10,14},{11,... | collective-permute-start | bytes 602120 | tf_op jit(solution)/shard_map/ppermute | solution.py:88
  10.4 10.8 %collective-permute-start.13 = (bf16[16,6144]{1,0:T(8,128)(2,1)S(1)}, bf16[16,6144]{1,0:T(8,128)(2,1)S(1)}, u32[]{:S(2)}, u32[]{:S(2)}) collective-permute-start(bf16[16,6144]{1,0:T(8,128)(2,1)S(1)} %collective-permute-done.11), channel_id=1, source_target_pairs={{4,0},{5,1},{8,4},{9,5},{12,8},{13,9},{14,12},{15,13},{10,14},{11,... | collective-permute-start | bytes 589832 | tf_op jit(solution)/shard_map/ppermute | solution.py:88
  13.2 8.5 %collective-permute-start.12 = (bf16[16,6144]{1,0:T(8,128)(2,1)S(1)}, bf16[16,6144]{1,0:T(8,128)(2,1)S(1)}, u32[]{:S(2)}, u32[]{:S(2)}) collective-permute-start(bf16[16,6144]{1,0:T(8,128)(2,1)S(1)} %collective-permute-done.10), channel_id=1, source_target_pairs={{0,4},{1,5},{4,8},{5,9},{8,12},{9,13},{12,14},{13,15},{14,10},{15,... | collective-permute-start | bytes 589832 | tf_op jit(solution)/shard_map/ppermute | solution.py:88
  17.5 8.5 %collective-permute-start.2 = (bf16[16,6272]{1,0:T(8,128)(2,1)S(1)}, bf16[16,6272]{1,0:T(8,128)(2,1)S(1)}, u32[]{:S(2)}, u32[]{:S(2)}) collective-permute-start(bf16[16,6272]{1,0:T(8,128)(2,1)S(1)} %collective-permute-done), channel_id=1, source_target_pairs={{0,4},{1,5},{4,8},{5,9},{8,12},{9,13},{12,14},{13,15},{14,10},{15,... | collective-permute-start | bytes 602120 | tf_op jit(solution)/shard_map/ppermute | solution.py:88
  17.5 8.5 %collective-permute-start.3 = (bf16[16,6272]{1,0:T(8,128)(2,1)S(1)}, bf16[16,6272]{1,0:T(8,128)(2,1)S(1)}, u32[]{:S(2)}, u32[]{:S(2)}) collective-permute-start(bf16[16,6272]{1,0:T(8,128)(2,1)S(1)} %collective-permute-done.1), channel_id=1, source_target_pairs={{4,0},{5,1},{8,4},{9,5},{12,8},{13,9},{14,12},{15,13},{10,14},{11,... | collective-permute-start | bytes 602120 | tf_op jit(solution)/shard_map/ppermute | solution.py:88
  21.2 8.5 %collective-permute-start.15 = (bf16[16,6144]{1,0:T(8,128)(2,1)S(1)}, bf16[16,6144]{1,0:T(8,128)(2,1)S(1)}, u32[]{:S(2)}, u32[]{:S(2)}) collective-permute-start(bf16[16,6144]{1,0:T(8,128)(2,1)S(1)} %collective-permute-done.13), channel_id=1, source_target_pairs={{4,0},{5,1},{8,4},{9,5},{12,8},{13,9},{14,12},{15,13},{10,14},{11,... | collective-permute-start | bytes 589832 | tf_op jit(solution)/shard_map/ppermute | solution.py:88
  21.8 8.8 %collective-permute-start.14 = (bf16[16,6144]{1,0:T(8,128)(2,1)S(1)}, bf16[16,6144]{1,0:T(8,128)(2,1)S(1)}, u32[]{:S(2)}, u32[]{:S(2)}) collective-permute-start(bf16[16,6144]{1,0:T(8,128)(2,1)S(1)} %collective-permute-done.12), channel_id=1, source_target_pairs={{0,4},{1,5},{4,8},{5,9},{8,12},{9,13},{12,14},{13,15},{14,10},{15,... | collective-permute-start | bytes 589832 | tf_op jit(solution)/shard_map/ppermute | solution.py:88
  26.1 8.1 %collective-permute-start.4 = (bf16[16,6272]{1,0:T(8,128)(2,1)S(1)}, bf16[16,6272]{1,0:T(8,128)(2,1)S(1)}, u32[]{:S(2)}, u32[]{:S(2)}) collective-permute-start(bf16[16,6272]{1,0:T(8,128)(2,1)S(1)} %collective-permute-done.2), channel_id=1, source_target_pairs={{0,4},{1,5},{4,8},{5,9},{8,12},{9,13},{12,14},{13,15},{14,10},{15,... | collective-permute-start | bytes 602120 | tf_op jit(solution)/shard_map/ppermute | solution.py:88
  26.1 8.6 %collective-permute-start.5 = (bf16[16,6272]{1,0:T(8,128)(2,1)S(1)}, bf16[16,6272]{1,0:T(8,128)(2,1)S(1)}, u32[]{:S(2)}, u32[]{:S(2)}) collective-permute-start(bf16[16,6272]{1,0:T(8,128)(2,1)S(1)} %collective-permute-done.3), channel_id=1, source_target_pairs={{4,0},{5,1},{8,4},{9,5},{12,8},{13,9},{14,12},{15,13},{10,14},{11,... | collective-permute-start | bytes 602120 | tf_op jit(solution)/shard_map/ppermute | solution.py:88
  29.7 6.8 %collective-permute-start.17 = (bf16[16,3072]{1,0:T(8,128)(2,1)S(1)}, bf16[16,3072]{1,0:T(8,128)(2,1)S(1)}, u32[]{:S(2)}, u32[]{:S(2)}) collective-permute-start(bf16[16,3072]{1,0:T(8,128)(2,1)S(1)} %slice.146), channel_id=1, source_target_pairs={{4,0},{5,1},{8,4},{9,5},{12,8},{13,9},{14,12},{15,13},{10,14},{11,... | collective-permute-start | bytes 294920 | tf_op jit(solution)/shard_map/ppermute | solution.py:88
  30.6 5.9 %collective-permute-start.16 = (bf16[16,3072]{1,0:T(8,128)(2,1)S(1)}, bf16[16,3072]{1,0:T(8,128)(2,1)S(1)}, u32[]{:S(2)}, u32[]{:S(2)}) collective-permute-start(bf16[16,3072]{1,0:T(8,128)(2,1)S(1)} %slice.145), channel_id=1, source_target_pairs={{0,4},{1,5},{4,8},{5,9},{8,12},{9,13},{12,14},{13,15},{14,10},{15,... | collective-permute-start | bytes 294920 | tf_op jit(solution)/shard_map/ppermute | solution.py:88
  34.2 8.1 %copy-start.3 = (bf16[6144,336]{0,1:T(8,128)(2,1)S(1)}, bf16[6144,336]{0,1:T(8,128)(2,1)}, u32[]{:S(2)}) copy-start(bf16[6144,336]{0,1:T(8,128)(2,1)} %param.11) | copy-start | bytes 12386308
  34.2 4.7 %collective-permute-start.6 = (bf16[16,3072]{1,0:T(8,128)(2,1)S(1)}, bf16[16,3072]{1,0:T(8,128)(2,1)S(1)}, u32[]{:S(2)}, u32[]{:S(2)}) collective-permute-start(bf16[16,3072]{1,0:T(8,128)(2,1)S(1)} %slice.140), channel_id=1, source_target_pairs={{0,4},{1,5},{4,8},{5,9},{8,12},{9,13},{12,14},{13,15},{14,10},{15,... | collective-permute-start | bytes 294920 | tf_op jit(solution)/shard_map/ppermute | solution.py:88
  34.7 4.7 %collective-permute-start.7 = (bf16[16,3200]{1,0:T(8,128)(2,1)S(1)}, bf16[16,3200]{1,0:T(8,128)(2,1)S(1)}, u32[]{:S(2)}, u32[]{:S(2)}) collective-permute-start(bf16[16,3200]{1,0:T(8,128)(2,1)S(1)} %slice.141), channel_id=1, source_target_pairs={{4,0},{5,1},{8,4},{9,5},{12,8},{13,9},{14,12},{15,13},{10,14},{11,... | collective-permute-start | bytes 307208 | tf_op jit(solution)/shard_map/ppermute | solution.py:88
  36.4 3.2 %collective-permute-start.8 = (bf16[112,6272]{1,0:T(8,128)(2,1)S(1)}, bf16[112,6272]{1,0:T(8,128)(2,1)S(1)}, u32[]{:S(2)}, u32[]{:S(2)}) collective-permute-start(bf16[112,6272]{1,0:T(8,128)(2,1)S(1)} %get-tuple-element.99), channel_id=1, source_target_pairs={{0,1},{1,0},{2,3},{3,2},{4,5},{5,4},{6,7},{7,6},{8,9},{9,8},{10,11... | collective-permute-start | bytes 4214792 | tf_op jit(solution)/shard_map/ppermute | solution.py:88
  36.5 12.2 %collective-permute-start.18 = (bf16[128,6144]{1,0:T(8,128)(2,1)S(1)}, bf16[128,6144]{1,0:T(8,128)(2,1)S(1)}, u32[]{:S(2)}, u32[]{:S(2)}) collective-permute-start(bf16[128,6144]{1,0:T(8,128)(2,1)S(1)} %maximum_dynamic-update-slice_fusion), channel_id=1, source_target_pairs={{0,1},{1,0},{2,3},{3,2},{4,5},{5,4},{6,7},{7,6},{8,9},{9,8},{10,11... | collective-permute-start | bytes 4718600 | tf_op jit(solution)/shard_map/ppermute | solution.py:88
  39.4 2.8 %collective-permute-start.9 = (bf16[16,6272]{1,0:T(8,128)(2,1)S(1)}, bf16[16,6272]{1,0:T(8,128)(2,1)S(1)}, u32[]{:S(2)}, u32[]{:S(2)}) collective-permute-start(bf16[16,6272]{1,0:T(8,128)(2,1)S(1)} %pad_maximum_fusion), channel_id=1, source_target_pairs={{0,1},{1,0},{2,3},{3,2},{4,5},{5,4},{6,7},{7,6},{8,9},{9,8},{10,11... | collective-permute-start | bytes 602120 | tf_op jit(solution)/shard_map/ppermute | solution.py:88
  42.3 2.2 %copy-start.4 = (bf16[6144,336]{0,1:T(8,128)(2,1)S(1)}, bf16[6144,336]{0,1:T(8,128)(2,1)}, u32[]{:S(2)}) copy-start(bf16[6144,336]{0,1:T(8,128)(2,1)} %param.12) | copy-start | bytes 12386308
  44.5 2.2 %copy-start.2 = (bf16[336,6144]{1,0:T(8,128)(2,1)S(1)}, bf16[336,6144]{1,0:T(8,128)(2,1)}, u32[]{:S(2)}) copy-start(bf16[336,6144]{1,0:T(8,128)(2,1)} %param.13) | copy-start | bytes 12386308
  48.9 2.1 %collective-permute-start.20 = (bf16[48,6144]{1,0:T(8,128)(2,1)S(1)}, bf16[48,6144]{1,0:T(8,128)(2,1)S(1)}, u32[]{:S(2)}, u32[]{:S(2)}) collective-permute-start(bf16[48,6144]{1,0:T(8,128)(2,1)S(1)} %slice.120), channel_id=1, source_target_pairs={{0,1},{1,0},{2,3},{3,2},{4,5},{5,4},{6,7},{7,6},{8,9},{9,8},{10,11... | collective-permute-start | bytes 1769480 | tf_op jit(solution)/shard_map/ppermute | solution.py:88
  49.2 11.0 %collective-permute-start.19 = (bf16[80,6144]{1,0:T(8,128)(2,1)S(1)}, bf16[80,6144]{1,0:T(8,128)(2,1)S(1)}, u32[]{:S(2)}, u32[]{:S(2)}) collective-permute-start(bf16[80,6144]{1,0:T(8,128)(2,1)S(1)} %slice.116), channel_id=1, source_target_pairs={{0,1},{1,0},{2,3},{3,2},{4,5},{5,4},{6,7},{7,6},{8,9},{9,8},{10,11... | collective-permute-start | bytes 2949128 | tf_op jit(solution)/shard_map/ppermute | solution.py:88
  51.2 7.0 %collective-permute-start.21 = (bf16[16,6144]{1,0:T(8,128)(2,1)S(1)}, bf16[16,6144]{1,0:T(8,128)(2,1)S(1)}, u32[]{:S(2)}, u32[]{:S(2)}) collective-permute-start(bf16[16,6144]{1,0:T(8,128)(2,1)S(1)} %get-tuple-element.49), channel_id=1, source_target_pairs={{4,0},{5,1},{8,4},{9,5},{12,8},{13,9},{14,12},{15,13},{10,14},{11,... | collective-permute-start | bytes 589832 | tf_op jit(solution)/shard_map/ppermute | solution.py:88
  52.8 6.7 %collective-permute-start.22 = (bf16[16,6144]{1,0:T(8,128)(2,1)S(1)}, bf16[16,6144]{1,0:T(8,128)(2,1)S(1)}, u32[]{:S(2)}, u32[]{:S(2)}) collective-permute-start(bf16[16,6144]{1,0:T(8,128)(2,1)S(1)} %get-tuple-element.50), channel_id=1, source_target_pairs={{0,4},{1,5},{4,8},{5,9},{8,12},{9,13},{12,14},{13,15},{14,10},{15,... | collective-permute-start | bytes 589832 | tf_op jit(solution)/shard_map/ppermute | solution.py:88
  59.6 2.9 %collective-permute-start.24 = (bf16[48,6144]{1,0:T(8,128)(2,1)S(1)}, bf16[48,6144]{1,0:T(8,128)(2,1)S(1)}, u32[]{:S(2)}, u32[]{:S(2)}) collective-permute-start(bf16[48,6144]{1,0:T(8,128)(2,1)S(1)} %slice.128), channel_id=1, source_target_pairs={{0,1},{1,0},{2,3},{3,2},{4,5},{5,4},{6,7},{7,6},{8,9},{9,8},{10,11... | collective-permute-start | bytes 1769480 | tf_op jit(solution)/shard_map/ppermute | solution.py:88
  59.6 14.5 %collective-permute-start.23 = (bf16[80,6144]{1,0:T(8,128)(2,1)S(1)}, bf16[80,6144]{1,0:T(8,128)(2,1)S(1)}, u32[]{:S(2)}, u32[]{:S(2)}) collective-permute-start(bf16[80,6144]{1,0:T(8,128)(2,1)S(1)} %slice.125), channel_id=1, source_target_pairs={{0,1},{1,0},{2,3},{3,2},{4,5},{5,4},{6,7},{7,6},{8,9},{9,8},{10,11... | collective-permute-start | bytes 2949128 | tf_op jit(solution)/shard_map/ppermute | solution.py:88
  60.4 7.8 %collective-permute-start.27 = (bf16[16,6144]{1,0:T(8,128)(2,1)S(1)}, bf16[16,6144]{1,0:T(8,128)(2,1)S(1)}, u32[]{:S(2)}, u32[]{:S(2)}) collective-permute-start(bf16[16,6144]{1,0:T(8,128)(2,1)S(1)} %fusion.13), channel_id=1, source_target_pairs={{4,0},{5,1},{8,4},{9,5},{12,8},{13,9},{14,12},{15,13},{10,14},{11,... | collective-permute-start | bytes 589832 | tf_op jit(solution)/shard_map/ppermute | solution.py:88
  62.1 7.8 %collective-permute-start.28 = (bf16[16,6144]{1,0:T(8,128)(2,1)S(1)}, bf16[16,6144]{1,0:T(8,128)(2,1)S(1)}, u32[]{:S(2)}, u32[]{:S(2)}) collective-permute-start(bf16[16,6144]{1,0:T(8,128)(2,1)S(1)} %fusion.12), channel_id=1, source_target_pairs={{0,4},{1,5},{4,8},{5,9},{8,12},{9,13},{12,14},{13,15},{14,10},{15,... | collective-permute-start | bytes 589832 | tf_op jit(solution)/shard_map/ppermute | solution.py:88
  62.7 11.6 %collective-permute-start.25 = (bf16[16,6144]{1,0:T(8,128)(2,1)S(1)}, bf16[16,6144]{1,0:T(8,128)(2,1)S(1)}, u32[]{:S(2)}, u32[]{:S(2)}) collective-permute-start(bf16[16,6144]{1,0:T(8,128)(2,1)S(1)} %get-tuple-element.54), channel_id=1, source_target_pairs={{4,0},{5,1},{8,4},{9,5},{12,8},{13,9},{14,12},{15,13},{10,14},{11,... | collective-permute-start | bytes 589832 | tf_op jit(solution)/shard_map/ppermute | solution.py:88
  64.3 9.7 %collective-permute-start.26 = (bf16[16,6144]{1,0:T(8,128)(2,1)S(1)}, bf16[16,6144]{1,0:T(8,128)(2,1)S(1)}, u32[]{:S(2)}, u32[]{:S(2)}) collective-permute-start(bf16[16,6144]{1,0:T(8,128)(2,1)S(1)} %get-tuple-element.55), channel_id=1, source_target_pairs={{0,4},{1,5},{4,8},{5,9},{8,12},{9,13},{12,14},{13,15},{14,10},{15,... | collective-permute-start | bytes 589832 | tf_op jit(solution)/shard_map/ppermute | solution.py:88
  69.9 9.9 %collective-permute-start.29 = (bf16[16,6144]{1,0:T(8,128)(2,1)S(1)}, bf16[16,6144]{1,0:T(8,128)(2,1)S(1)}, u32[]{:S(2)}, u32[]{:S(2)}) collective-permute-start(bf16[16,6144]{1,0:T(8,128)(2,1)S(1)} %get-tuple-element.69), channel_id=1, source_target_pairs={{4,0},{5,1},{8,4},{9,5},{12,8},{13,9},{14,12},{15,13},{10,14},{11,... | collective-permute-start | bytes 589832 | tf_op jit(solution)/shard_map/ppermute | solution.py:88
  71.6 8.2 %collective-permute-start.30 = (bf16[16,6144]{1,0:T(8,128)(2,1)S(1)}, bf16[16,6144]{1,0:T(8,128)(2,1)S(1)}, u32[]{:S(2)}, u32[]{:S(2)}) collective-permute-start(bf16[16,6144]{1,0:T(8,128)(2,1)S(1)} %get-tuple-element.70), channel_id=1, source_target_pairs={{0,4},{1,5},{4,8},{5,9},{8,12},{9,13},{12,14},{13,15},{14,10},{15,... | collective-permute-start | bytes 589832 | tf_op jit(solution)/shard_map/ppermute | solution.py:88
  74.4 5.7 %collective-permute-start.32 = (bf16[16,6144]{1,0:T(8,128)(2,1)S(1)}, bf16[16,6144]{1,0:T(8,128)(2,1)S(1)}, u32[]{:S(2)}, u32[]{:S(2)}) collective-permute-start(bf16[16,6144]{1,0:T(8,128)(2,1)S(1)} %fusion.15), channel_id=1, source_target_pairs={{4,0},{5,1},{8,4},{9,5},{12,8},{13,9},{14,12},{15,13},{10,14},{11,... | collective-permute-start | bytes 589832 | tf_op jit(solution)/shard_map/ppermute | solution.py:88
  76.0 5.7 %collective-permute-start.33 = (bf16[16,6144]{1,0:T(8,128)(2,1)S(1)}, bf16[16,6144]{1,0:T(8,128)(2,1)S(1)}, u32[]{:S(2)}, u32[]{:S(2)}) collective-permute-start(bf16[16,6144]{1,0:T(8,128)(2,1)S(1)} %fusion.14), channel_id=1, source_target_pairs={{0,4},{1,5},{4,8},{5,9},{8,12},{9,13},{12,14},{13,15},{14,10},{15,... | collective-permute-start | bytes 589832 | tf_op jit(solution)/shard_map/ppermute | solution.py:88
  81.8 6.1 %collective-permute-start.35 = (bf16[16,6144]{1,0:T(8,128)(2,1)S(1)}, bf16[16,6144]{1,0:T(8,128)(2,1)S(1)}, u32[]{:S(2)}, u32[]{:S(2)}) collective-permute-start(bf16[16,6144]{1,0:T(8,128)(2,1)S(1)} %get-tuple-element.76), channel_id=1, source_target_pairs={{0,4},{1,5},{4,8},{5,9},{8,12},{9,13},{12,14},{13,15},{14,10},{15,... | collective-permute-start | bytes 589832 | tf_op jit(solution)/shard_map/ppermute | solution.py:88
  82.3 6.4 %collective-permute-start.31 = (bf16[16,6144]{1,0:T(8,128)(2,1)S(1)}, bf16[16,6144]{1,0:T(8,128)(2,1)S(1)}, u32[]{:S(2)}, u32[]{:S(2)}) collective-permute-start(bf16[16,6144]{1,0:T(8,128)(2,1)S(1)} %fusion.16), channel_id=1, source_target_pairs={{4,0},{5,1},{8,4},{9,5},{12,8},{13,9},{14,12},{15,13},{10,14},{11,... | collective-permute-start | bytes 589832 | tf_op jit(solution)/shard_map/ppermute | solution.py:88
  84.0 10.4 %collective-permute-start.34 = (bf16[16,6144]{1,0:T(8,128)(2,1)S(1)}, bf16[16,6144]{1,0:T(8,128)(2,1)S(1)}, u32[]{:S(2)}, u32[]{:S(2)}) collective-permute-start(bf16[16,6144]{1,0:T(8,128)(2,1)S(1)} %get-tuple-element.75), channel_id=1, source_target_pairs={{4,0},{5,1},{8,4},{9,5},{12,8},{13,9},{14,12},{15,13},{10,14},{11,... | collective-permute-start | bytes 589832 | tf_op jit(solution)/shard_map/ppermute | solution.py:88
  87.9 6.5 %collective-permute-start.36 = (bf16[16,6144]{1,0:T(8,128)(2,1)S(1)}, bf16[16,6144]{1,0:T(8,128)(2,1)S(1)}, u32[]{:S(2)}, u32[]{:S(2)}) collective-permute-start(bf16[16,6144]{1,0:T(8,128)(2,1)S(1)} %fusion.5), channel_id=1, source_target_pairs={{0,4},{1,5},{4,8},{5,9},{8,12},{9,13},{12,14},{13,15},{14,10},{15,... | collective-permute-start | bytes 589832 | tf_op jit(solution)/shard_map/ppermute | solution.py:88
  88.8 7.4 %copy-start.1 = (bf16[128,6144]{1,0:T(8,128)(2,1)S(1)}, bf16[128,6144]{1,0:T(8,128)(2,1)}, u32[]{:S(2)}) copy-start(bf16[128,6144]{1,0:T(8,128)(2,1)} %param.8) | copy-start | bytes 4718596

commit v7 on v6

--- a/solution.py
+++ b/solution.py
@@ -108,16 +108,23 @@
         far_x = far_block(held_xr, held_xl)
         early_x = permute(jnp.concatenate(got_x, axis=0), core_pairs)
         late_x = permute(far_x, core_pairs)
+        chip_d = jnp.concatenate(got_d, axis=0)
+        chip_d, late_x = lax.optimization_barrier((chip_d, late_x))
         rows_x = jnp.concatenate(got_x + [far_x, early_x, late_x], axis=0)
-        chip_d = jnp.concatenate(got_d, axis=0)
         return rows_x, jnp.concatenate([chip_d, permute(chip_d, core_pairs)], axis=0)
 
+    half = 2 * steps * CAP
     cut = max(2 * steps - 3, 1) * CAP
 
-    def pair_sum(own, sent):
-        far = own[cut:] + permute(sent[cut:], core_pairs).astype(jnp.float32)
-        near = own[:cut] + permute(sent[:cut], core_pairs).astype(jnp.float32)
-        return near, far
+    def far_sum(own, sent):
+        return own[cut:half] + permute(sent[cut:], core_pairs).astype(jnp.float32)
+
+    def near_sums(owns, sents):
+        near = permute(jnp.concatenate([sent[:cut] for sent in sents], axis=0), core_pairs)
+        return [
+            own[:cut] + near[i * cut : (i + 1) * cut].astype(jnp.float32)
+            for i, own in enumerate(owns)
+        ]
 
     def block_of(total, at):
         at = at * CAP
@@ -167,47 +174,44 @@
         )
         rows_x = rows_wide[:, :d]
         coef_rows = rows_wide[:, d : d + 1].astype(jnp.float32)
-        half = rows_wide.shape[0] // 2
 
         gate = jnp.dot(rows_x, w_gate, preferred_element_type=jnp.float32)
         up = jnp.dot(rows_x, w_up, preferred_element_type=jnp.float32)
         sig = jax.nn.sigmoid(gate)
         act = gate * sig
         hidden = (coef_rows * act * up).astype(jnp.bfloat16)
-        out_rows = jnp.dot(hidden, w_down, preferred_element_type=jnp.float32)
-        out_sent = out_rows[half:].astype(jnp.bfloat16)
-        rows_dy, out_sent = lax.optimization_barrier((rows_dy, out_sent))
-        out_total = pair_sum(out_rows[:half], out_sent)
-
         dhid = jnp.dot(rows_dy, w_down.T, preferred_element_type=jnp.float32)
         scaled = coef_rows * dhid
         dgate = (scaled * up * sig * (1.0 + gate * (1.0 - sig))).astype(jnp.bfloat16)
         dup = (scaled * act).astype(jnp.bfloat16)
-        dgate, blocks = tie(dgate, wave(out_total, {}, 1, "l"))
-        out_carry = send(blocks)
         dx_rows = jnp.dot(dgate, w_gate.T, preferred_element_type=jnp.float32) + jnp.dot(
             dup, w_up.T, preferred_element_type=jnp.float32
         )
         dx_sent = dx_rows[half:].astype(jnp.bfloat16)
-        dx_sent, out_carry = tie(dx_sent, out_carry)
-        dx_total = pair_sum(dx_rows[:half], dx_sent)
-        dx_carry = {}
-
+        hidden, dx_sent = lax.optimization_barrier((hidden, dx_sent))
+        dx_far = far_sum(dx_rows, dx_sent)
+        out_rows = jnp.dot(hidden, w_down, preferred_element_type=jnp.float32)
+        out_sent = out_rows[half:].astype(jnp.bfloat16)
+        out_far = far_sum(out_rows, out_sent)
+        dx_near, out_near = near_sums([dx_rows, out_rows], [dx_sent, out_sent])
+        dx_total, out_total = (dx_near, dx_far), (out_near, out_far)
+
+        dx_carry, out_carry = {}, {}
         grads, marks = [], []
         work = [(dgate, rows_wide), (dup, rows_wide), (hidden, rows_dy)]
-        for at in range(2, steps + 2):
-            if at <= steps:
-                out_carry.update(send(wave(out_total, out_carry, at, "l")))
-            dx_blocks = wave(dx_total, dx_carry, at - 1, "r")
-            if work and at in (2, 3, steps + 1):
+        for at in range(1, steps + 1):
+            dx_blocks = wave(dx_total, dx_carry, at, "r")
+            out_blocks = wave(out_total, out_carry, at, "l")
+            if work:
                 side, rows = work.pop(0)
                 side, dx_blocks = tie(side, dx_blocks)
                 grad, mark = weight_grad(side, rows, d, marks)
                 grads.append(grad)
-                if work and at <= steps:
-                    mark, out_carry = tie(mark, out_carry)
+                if work and at < steps:
+                    mark, dx_carry = tie(mark, dx_carry)
                 marks = [mark]
             dx_carry.update(send(dx_blocks))
+            out_carry.update(send(out_blocks))
         for side, rows in work:
             grads.append(weight_grad(side, rows, d, marks)[0])
         grad_gate, grad_up, grad_down = grads

time: 96.5 us -> 102 us (1.057)
  waiting for transfers between devices: 29.6 us -> 35.1 us
  matrix products: 15 us -> 13.6 us
  local copies, waits for them, and re-layouts: 3.59 us -> 4.9 us
    ppermute x37 -> x36, waiting for transfers between devices: 29.6 us -> 35.1 us  [permute(): return lax.ppermute(x, 'et', pairs)]
    unnamed x26 -> x27, local copies, waits for them, and re-layouts: 2.54 us -> 4.06 us
    dot_general x3, matrix products: 2.15 us -> 0.75 us  [per_device(): jnp.dot(select, a, preferred_element_type=jnp.float32).astype(jnp.bfloat16)]
    ppermute x37 -> x36, starting transfers between devices: 34 us -> 34.3 us  [permute(): return lax.ppermute(x, 'et', pairs)]
  transfers between devices with their start and end apart: 37 -> 36, of which waited for: 21 -> 19; matrix products, arithmetic and copies ran while one was open for 16% -> 7% of each run, Pallas kernels for 11% -> 10%
where the time goes in v7:
time: 102 us
  waiting for transfers between devices  35.1 us (34%)
  starting transfers between devices  34.3 us (34%)
  matrix products  13.6 us (13%)
  Pallas kernels  10.4 us (10%)
  local copies, waits for them, and re-layouts  4.9 us (5%)
  other arithmetic  2.76 us (3%)
  between operations  1.07 us (1%)
    ppermute x36, waiting for transfers between devices, permute(): return lax.ppermute(x, 'et', pairs)  35.1 us
    ppermute x36, starting transfers between devices, permute(): return lax.ppermute(x, 'et', pairs)  34.3 us
    pallas_call x3, Pallas kernels, weight_grad(): pl.pallas_call(lambda *refs: grad_kernel(parts, width, len(marks), *refs)...  10.4 us
    unnamed x27, local copies, waits for them, and re-layouts  4.06 us
    dot_general x2, matrix products, per_device(): jnp.dot(select.T, final(total[0], carry), preferred_element_type=jnp.floa...  3.53 us
  transfers between devices with their start and end apart: 36, of which 19 were waited for; matrix products, arithmetic and copies ran while one was open for 7% of the time, Pallas kernels for 10%

profile of v7, /device:TPU:0, one launch (start us, length us, event | category | flops | bytes accessed | tf_op | source)
XLA Modules:
  0.0 102.2 jit_solution(13840059800225179433)
XLA Ops:
  0.7 0.9 select_reduce_fusion
  2.4 3.1 %collective-permute-start.9 = (bf16[16,6144]{1,0:T(8,128)(2,1)S(1)}, bf16[16,6144]{1,0:T(8,128)(2,1)S(1)}, u32[]{:S(2)}, u32[]{:S(2)}) collective-permute-start(bf16[16,6144]{1,0:T(8,128)(2,1)S(1)} %get-tuple-element.102), channel_id=1, source_target_pairs={{0,4},{1,5},{4,8},{5,9},{8,12},{9,13},{12,14},{13,15},{14,10},{15,... | collective-permute-start | bytes 589832 | tf_op jit(solution)/shard_map/ppermute | solution.py:88
  6.0 1.6 %collective-permute-start = (bf16[16,6272]{1,0:T(8,128)(2,1)S(1)}, bf16[16,6272]{1,0:T(8,128)(2,1)S(1)}, u32[]{:S(2)}, u32[]{:S(2)}) collective-permute-start(bf16[16,6272]{1,0:T(8,128)(2,1)S(1)} %get-tuple-element.100), channel_id=1, source_target_pairs={{0,4},{1,5},{4,8},{5,9},{8,12},{9,13},{12,14},{13,15},{14,10},{15,... | collective-permute-start | bytes 602120 | tf_op jit(solution)/shard_map/ppermute | solution.py:88
  7.7 0.4 collective-permute-start.1
  8.2 3.0 %collective-permute-done.9 = bf16[16,6144]{1,0:T(8,128)(2,1)S(1)} collective-permute-done((bf16[16,6144]{1,0:T(8,128)(2,1)S(1)}, bf16[16,6144]{1,0:T(8,128)(2,1)S(1)}, u32[]{:S(2)}, u32[]{:S(2)}) %collective-permute-start.9) | collective-permute-done | bytes 196640 | tf_op jit(solution)/shard_map/ppermute | solution.py:88
  11.1 2.1 %collective-permute-start.11 = (bf16[16,6144]{1,0:T(8,128)(2,1)S(1)}, bf16[16,6144]{1,0:T(8,128)(2,1)S(1)}, u32[]{:S(2)}, u32[]{:S(2)}) collective-permute-start(bf16[16,6144]{1,0:T(8,128)(2,1)S(1)} %collective-permute-done.9), channel_id=1, source_target_pairs={{0,4},{1,5},{4,8},{5,9},{8,12},{9,13},{12,14},{13,15},{14,10},{15,... | collective-permute-start | bytes 589832 | tf_op jit(solution)/shard_map/ppermute | solution.py:88
  13.3 4.8 %collective-permute-done.10 = bf16[16,6144]{1,0:T(8,128)(2,1)S(1)} collective-permute-done((bf16[16,6144]{1,0:T(8,128)(2,1)S(1)}, bf16[16,6144]{1,0:T(8,128)(2,1)S(1)}, u32[]{:S(2)}, u32[]{:S(2)}) %collective-permute-start.10) | collective-permute-done | bytes 196640 | tf_op jit(solution)/shard_map/ppermute | solution.py:88
  18.1 0.4 collective-permute-start.12
  18.5 1.6 %collective-permute-start.2 = (bf16[16,6272]{1,0:T(8,128)(2,1)S(1)}, bf16[16,6272]{1,0:T(8,128)(2,1)S(1)}, u32[]{:S(2)}, u32[]{:S(2)}) collective-permute-start(bf16[16,6272]{1,0:T(8,128)(2,1)S(1)} %collective-permute-done), channel_id=1, source_target_pairs={{0,4},{1,5},{4,8},{5,9},{8,12},{9,13},{12,14},{13,15},{14,10},{15,... | collective-permute-start | bytes 602120 | tf_op jit(solution)/shard_map/ppermute | solution.py:88
  20.2 0.4 collective-permute-start.3
  20.7 1.6 %collective-permute-start.13 = (bf16[16,6144]{1,0:T(8,128)(2,1)S(1)}, bf16[16,6144]{1,0:T(8,128)(2,1)S(1)}, u32[]{:S(2)}, u32[]{:S(2)}) collective-permute-start(bf16[16,6144]{1,0:T(8,128)(2,1)S(1)} %collective-permute-done.11), channel_id=1, source_target_pairs={{0,4},{1,5},{4,8},{5,9},{8,12},{9,13},{12,14},{13,15},{14,10},{15,... | collective-permute-start | bytes 589832 | tf_op jit(solution)/shard_map/ppermute | solution.py:88
  22.3 3.5 %collective-permute-done.12 = bf16[16,6144]{1,0:T(8,128)(2,1)S(1)} collective-permute-done((bf16[16,6144]{1,0:T(8,128)(2,1)S(1)}, bf16[16,6144]{1,0:T(8,128)(2,1)S(1)}, u32[]{:S(2)}, u32[]{:S(2)}) %collective-permute-start.12) | collective-permute-done | bytes 196640 | tf_op jit(solution)/shard_map/ppermute | solution.py:88
  25.9 0.4 collective-permute-start.14
  26.5 1.6 %collective-permute-start.4 = (bf16[16,6272]{1,0:T(8,128)(2,1)S(1)}, bf16[16,6272]{1,0:T(8,128)(2,1)S(1)}, u32[]{:S(2)}, u32[]{:S(2)}) collective-permute-start(bf16[16,6272]{1,0:T(8,128)(2,1)S(1)} %collective-permute-done.2), channel_id=1, source_target_pairs={{0,4},{1,5},{4,8},{5,9},{8,12},{9,13},{12,14},{13,15},{14,10},{15,... | collective-permute-start | bytes 602120 | tf_op jit(solution)/shard_map/ppermute | solution.py:88
  28.1 2.1 %collective-permute-done.3 = bf16[16,6272]{1,0:T(8,128)(2,1)S(1)} collective-permute-done((bf16[16,6272]{1,0:T(8,128)(2,1)S(1)}, bf16[16,6272]{1,0:T(8,128)(2,1)S(1)}, u32[]{:S(2)}, u32[]{:S(2)}) %collective-permute-start.3) | collective-permute-done | bytes 200736 | tf_op jit(solution)/shard_map/ppermute | solution.py:88
  30.2 0.4 collective-permute-start.5
  30.7 3.7 %collective-permute-done.14 = bf16[16,6144]{1,0:T(8,128)(2,1)S(1)} collective-permute-done((bf16[16,6144]{1,0:T(8,128)(2,1)S(1)}, bf16[16,6144]{1,0:T(8,128)(2,1)S(1)}, u32[]{:S(2)}, u32[]{:S(2)}) %collective-permute-start.14) | collective-permute-done | bytes 196640 | tf_op jit(solution)/shard_map/ppermute | solution.py:88
  34.4 0.5 collective-permute-start.16
  34.9 1.6 %collective-permute-start.15 = (bf16[16,3072]{1,0:T(8,128)(2,1)S(1)}, bf16[16,3072]{1,0:T(8,128)(2,1)S(1)}, u32[]{:S(2)}, u32[]{:S(2)}) collective-permute-start(bf16[16,3072]{1,0:T(8,128)(2,1)S(1)} %slice.143), channel_id=1, source_target_pairs={{0,4},{1,5},{4,8},{5,9},{8,12},{9,13},{12,14},{13,15},{14,10},{15,... | collective-permute-start | bytes 294920 | tf_op jit(solution)/shard_map/ppermute | solution.py:88
  36.6 1.6 %collective-permute-start.6 = (bf16[16,3072]{1,0:T(8,128)(2,1)S(1)}, bf16[16,3072]{1,0:T(8,128)(2,1)S(1)}, u32[]{:S(2)}, u32[]{:S(2)}) collective-permute-start(bf16[16,3072]{1,0:T(8,128)(2,1)S(1)} %slice.141), channel_id=1, source_target_pairs={{0,4},{1,5},{4,8},{5,9},{8,12},{9,13},{12,14},{13,15},{14,10},{15,... | collective-permute-start | bytes 294920 | tf_op jit(solution)/shard_map/ppermute | solution.py:88
  38.3 0.7 collective-permute-start.7
  39.2 0.4 collective-permute-done.15
  39.6 1.7 %collective-permute-done.6 = bf16[16,3072]{1,0:T(8,128)(2,1)S(1)} collective-permute-done((bf16[16,3072]{1,0:T(8,128)(2,1)S(1)}, bf16[16,3072]{1,0:T(8,128)(2,1)S(1)}, u32[]{:S(2)}, u32[]{:S(2)}) %collective-permute-start.6) | collective-permute-done | bytes 98336 | tf_op jit(solution)/shard_map/ppermute | solution.py:88
  41.3 1.9 %collective-permute-done.7 = bf16[16,3200]{1,0:T(8,128)(2,1)S(1)} collective-permute-done((bf16[16,3200]{1,0:T(8,128)(2,1)S(1)}, bf16[16,3200]{1,0:T(8,128)(2,1)S(1)}, u32[]{:S(2)}, u32[]{:S(2)}) %collective-permute-start.7) | collective-permute-done | bytes 102432 | tf_op jit(solution)/shard_map/ppermute | solution.py:88
  43.3 1.4 %collective-permute-done.17 = bf16[16,6272]{1,0:T(8,128)(2,1)S(1)} collective-permute-done((bf16[16,6272]{1,0:T(8,128)(2,1)S(1)}, bf16[16,6272]{1,0:T(8,128)(2,1)S(1)}, u32[]{:S(2)}, u32[]{:S(2)}) %collective-permute-start.17) | collective-permute-done | bytes 200736 | tf_op jit(solution)/shard_map/ppermute | solution.py:88
  45.3 1.7 %copy-done.2 = bf16[6144,336]{0,1:T(8,128)(2,1)S(1)} copy-done((bf16[6144,336]{0,1:T(8,128)(2,1)S(1)}, bf16[6144,336]{0,1:T(8,128)(2,1)}, u32[]{:S(2)}) %copy-start.2) | copy-done | bytes 4128792
  47.0 1.3 %fusion.2 = f32[256,336]{0,1:T(8,128)S(1)} fusion(bf16[6144,336]{0,1:T(8,128)(2,1)S(1)} %copy-done.2, bf16[256,6272]{1,0:T(8,128)(2,1)S(1)} %constant_dynamic-update-slice_fusion.14.refs_1_), kind=kOutput, calls=%fused_computation.8 | convolution fusion | flops 1056964608 | bytes 7618560 | tf_op jit(solution)/shard_map/dot_general | solution.py:178
  48.3 0.9 copy-done.4
  49.2 1.3 %fusion = f32[256,336]{0,1:T(8,128)S(1)} fusion(bf16[6144,336]{0,1:T(8,128)(2,1)S(1)} %copy-done.4, bf16[256,6272]{1,0:T(8,128)(2,1)S(1)} %constant_dynamic-update-slice_fusion.14.refs_1_), kind=kOutput, calls=%fused_computation.6 | convolution fusion | flops 1056964608 | bytes 7618560 | tf_op jit(solution)/shard_map/dot_general | solution.py:179
  50.6 0.8 copy-done.3
  51.4 1.3 %multiply_convert_fusion = (bf16[256,336]{0,1:T(8,128)(2,1)S(1)}, bf16[256,336]{0,1:T(8,128)(2,1)S(1)}, bf16[256,336]{0,1:T(8,128)(2,1)S(1)}) fusion(f32[256,336]{0,1:T(8,128)S(1)} %fusion.2, f32[256,336]{0,1:T(8,128)S(1)} %fusion, f32[256]{0:T(256)S(1)} %convert_reduce_fusion, bf16[256,6144]{1,0:T(8,128)(2,1)S(1)} %constant_dynamic-update-slice_fusion.24.refs_1_, ...), kind=kOutput, calls=%fused_computation.44 | convolution fusion | flops 1058426880 | bytes 8479744 | tf_op jit(solution)/shard_map/dot_general | solution.py:183
  52.7 1.8 %fusion.43 = f32[256,6144]{1,0:T(8,128)S(1)} fusion(bf16[256,336]{0,1:T(8,128)(2,1)S(1)} %get-tuple-element.58, bf16[6144,336]{0,1:T(8,128)(2,1)S(1)} %copy-done.2), kind=kOutput, calls=%fused_computation.102 | convolution fusion | flops 1056964608 | bytes 10592256 | tf_op jit(solution)/shard_map/dot_general | solution.py:187
  54.5 1.8 %convolution_add_fusion = f32[256,6144]{1,0:T(8,128)S(1)} fusion(f32[256,6144]{1,0:T(8,128)S(1)} %fusion.43, bf16[256,336]{0,1:T(8,128)(2,1)S(1)} %get-tuple-element.60, bf16[6144,336]{0,1:T(8,128)(2,1)S(1)} %copy-done.4), kind=kOutput, calls=%fused_computation | convolution fusion | flops 1058537472 | bytes 16883712 | tf_op jit(solution)/shard_map/dot_general | solution.py:187
  56.5 1.8 %fusion.42 = (bf16[256,6144]{1,0:T(8,128)(2,1)S(1)}, f32[256,6144]{1,0:T(8,128)S(1)}) fusion(bf16[256,336]{0,1:T(8,128)(2,1)S(1)} %get-tuple-element.63, bf16[336,6144]{1,0:T(8,128)(2,1)S(1)} %copy-done.3), kind=kOutput, calls=%fused_computation.101 | convolution fusion | flops 1058537472 | bytes 13737984 | tf_op jit(solution)/shard_map/dot_general | solution.py:193
  58.6 0.4 collective-permute-start.20
  59.4 0.4 collective-permute-start.28
  59.8 0.9 collective-permute-done.20
  60.9 0.5 collective-permute-start.21
  61.4 1.6 %collective-permute-start.22 = (bf16[16,6144]{1,0:T(8,128)(2,1)S(1)}, bf16[16,6144]{1,0:T(8,128)(2,1)S(1)}, u32[]{:S(2)}, u32[]{:S(2)}) collective-permute-start(bf16[16,6144]{1,0:T(8,128)(2,1)S(1)} %get-tuple-element.41), channel_id=1, source_target_pairs={{0,4},{1,5},{4,8},{5,9},{8,12},{9,13},{12,14},{13,15},{14,10},{15,... | collective-permute-start | bytes 589832 | tf_op jit(solution)/shard_map/ppermute | solution.py:88
  63.0 1.4 %collective-permute-done.28 = bf16[48,6144]{1,0:T(8,128)(2,1)S(1)} collective-permute-done((bf16[48,6144]{1,0:T(8,128)(2,1)S(1)}, bf16[48,6144]{1,0:T(8,128)(2,1)S(1)}, u32[]{:S(2)}, u32[]{:S(2)}) %collective-permute-start.28) | collective-permute-done | bytes 589856 | tf_op jit(solution)/shard_map/ppermute | solution.py:88
  64.5 0.5 collective-permute-start.29
  65.1 1.6 %collective-permute-start.30 = (bf16[16,6144]{1,0:T(8,128)(2,1)S(1)}, bf16[16,6144]{1,0:T(8,128)(2,1)S(1)}, u32[]{:S(2)}, u32[]{:S(2)}) collective-permute-start(bf16[16,6144]{1,0:T(8,128)(2,1)S(1)} %get-tuple-element.49), channel_id=1, source_target_pairs={{0,4},{1,5},{4,8},{5,9},{8,12},{9,13},{12,14},{13,15},{14,10},{15,... | collective-permute-start | bytes 589832 | tf_op jit(solution)/shard_map/ppermute | solution.py:88
  66.6 3.3 %shard_map.110 = (bf16[336,6144]{1,0:T(8,128)(2,1)}, f32[8,128]{1,0:T(8,128)S(1)}) custom-call(bf16[336,256]{1,0:T(8,128)(2,1)S(1)} %bitcast.26, bf16[256,6272]{1,0:T(8,128)(2,1)S(1)} %constant_dynamic-update-slice_fusion.14.refs_1_), custom_call_target="tpu_custom_call" | custom-call | flops 1056964608 | bytes 7274496 | tf_op jit(solution)/shard_map/pallas_call | solution.py:54
  70.0 2.5 %collective-permute-done.30 = bf16[16,6144]{1,0:T(8,128)(2,1)S(1)} collective-permute-done((bf16[16,6144]{1,0:T(8,128)(2,1)S(1)}, bf16[16,6144]{1,0:T(8,128)(2,1)S(1)}, u32[]{:S(2)}, u32[]{:S(2)}) %collective-permute-start.30) | collective-permute-done | bytes 196640 | tf_op jit(solution)/shard_map/ppermute | solution.py:88
  72.5 0.6 slice_add_fusion
  73.2 1.6 %collective-permute-start.24 = (bf16[16,6144]{1,0:T(8,128)(2,1)S(1)}, bf16[16,6144]{1,0:T(8,128)(2,1)S(1)}, u32[]{:S(2)}, u32[]{:S(2)}) collective-permute-start(bf16[16,6144]{1,0:T(8,128)(2,1)S(1)} %fusion.13), channel_id=1, source_target_pairs={{0,4},{1,5},{4,8},{5,9},{8,12},{9,13},{12,14},{13,15},{14,10},{15,... | collective-permute-start | bytes 589832 | tf_op jit(solution)/shard_map/ppermute | solution.py:88
  74.8 0.4 collective-permute-start.23
  75.3 1.6 %collective-permute-start.32 = (bf16[16,6144]{1,0:T(8,128)(2,1)S(1)}, bf16[16,6144]{1,0:T(8,128)(2,1)S(1)}, u32[]{:S(2)}, u32[]{:S(2)}) collective-permute-start(bf16[16,6144]{1,0:T(8,128)(2,1)S(1)} %fusion.7), channel_id=1, source_target_pairs={{0,4},{1,5},{4,8},{5,9},{8,12},{9,13},{12,14},{13,15},{14,10},{15,... | collective-permute-start | bytes 589832 | tf_op jit(solution)/shard_map/ppermute | solution.py:88
  76.9 0.4 collective-permute-start.31
  77.4 3.3 %shard_map.111 = (bf16[336,6144]{1,0:T(8,128)(2,1)}, f32[8,128]{1,0:T(8,128)S(1)}) custom-call(bf16[336,256]{1,0:T(8,128)(2,1)S(1)} %bitcast.28, bf16[256,6272]{1,0:T(8,128)(2,1)S(1)} %constant_dynamic-update-slice_fusion.14.refs_1_, f32[8,128]{1,0:T(8,128)S(1)} %get-tuple-element.61.refs_2_), custom_call_target="tpu_custom_call" | custom-call | flops 1056964608 | bytes 7274496 | tf_op jit(solution)/shard_map/pallas_call | solution.py:54
  80.7 0.4 collective-permute-done.24
  81.0 1.6 %collective-permute-done.23 = bf16[16,6144]{1,0:T(8,128)(2,1)S(1)} collective-permute-done((bf16[16,6144]{1,0:T(8,128)(2,1)S(1)}, bf16[16,6144]{1,0:T(8,128)(2,1)S(1)}, u32[]{:S(2)}, u32[]{:S(2)}) %collective-permute-start.23) | collective-permute-done | bytes 196640 | tf_op jit(solution)/shard_map/ppermute | solution.py:88
  82.7 1.6 %collective-permute-start.27 = (bf16[16,6144]{1,0:T(8,128)(2,1)S(1)}, bf16[16,6144]{1,0:T(8,128)(2,1)S(1)}, u32[]{:S(2)}, u32[]{:S(2)}) collective-permute-start(bf16[16,6144]{1,0:T(8,128)(2,1)S(1)} %get-tuple-element.45), channel_id=1, source_target_pairs={{0,4},{1,5},{4,8},{5,9},{8,12},{9,13},{12,14},{13,15},{14,10},{15,... | collective-permute-start | bytes 589832 | tf_op jit(solution)/shard_map/ppermute | solution.py:88
  84.3 0.5 collective-permute-start.25
  84.8 0.4 collective-permute-done.32
  85.2 1.6 %collective-permute-done.31 = bf16[16,6144]{1,0:T(8,128)(2,1)S(1)} collective-permute-done((bf16[16,6144]{1,0:T(8,128)(2,1)S(1)}, bf16[16,6144]{1,0:T(8,128)(2,1)S(1)}, u32[]{:S(2)}, u32[]{:S(2)}) %collective-permute-start.31) | collective-permute-done | bytes 196640 | tf_op jit(solution)/shard_map/ppermute | solution.py:88
  86.9 1.6 %collective-permute-start.34 = (bf16[16,6144]{1,0:T(8,128)(2,1)S(1)}, bf16[16,6144]{1,0:T(8,128)(2,1)S(1)}, u32[]{:S(2)}, u32[]{:S(2)}) collective-permute-start(bf16[16,6144]{1,0:T(8,128)(2,1)S(1)} %get-tuple-element.57), channel_id=1, source_target_pairs={{0,4},{1,5},{4,8},{5,9},{8,12},{9,13},{12,14},{13,15},{14,10},{15,... | collective-permute-start | bytes 589832 | tf_op jit(solution)/shard_map/ppermute | solution.py:88
  88.5 0.5 collective-permute-start.33
  89.0 3.9 %shard_map.112 = (bf16[336,6144]{1,0:T(8,128)(2,1)}, f32[8,128]{1,0:T(8,128)}) custom-call(bf16[336,256]{1,0:T(8,128)(2,1)S(1)} %bitcast.27, bf16[256,6144]{1,0:T(8,128)(2,1)S(1)} %constant_dynamic-update-slice_fusion.24.refs_1_, f32[8,128]{1,0:T(8,128)S(1)} %get-tuple-element.65.refs_2_), custom_call_target="tpu_custom_call" | custom-call | flops 1056964608 | bytes 7274496 | tf_op jit(solution)/shard_map/pallas_call | solution.py:54
  92.9 0.5 collective-permute-start.26
  93.5 1.6 %collective-permute-start.35 = (bf16[16,6144]{1,0:T(8,128)(2,1)S(1)}, bf16[16,6144]{1,0:T(8,128)(2,1)S(1)}, u32[]{:S(2)}, u32[]{:S(2)}) collective-permute-start(bf16[16,6144]{1,0:T(8,128)(2,1)S(1)} %fusion.5), channel_id=1, source_target_pairs={{0,4},{1,5},{4,8},{5,9},{8,12},{9,13},{12,14},{13,15},{14,10},{15,... | collective-permute-start | bytes 589832 | tf_op jit(solution)/shard_map/ppermute | solution.py:88
  95.1 3.5 %collective-permute-done.26 = bf16[16,6144]{1,0:T(8,128)(2,1)S(1)} collective-permute-done((bf16[16,6144]{1,0:T(8,128)(2,1)S(1)}, bf16[16,6144]{1,0:T(8,128)(2,1)S(1)}, u32[]{:S(2)}, u32[]{:S(2)}) %collective-permute-start.26) | collective-permute-done | bytes 196640 | tf_op jit(solution)/shard_map/ppermute | solution.py:88
  98.7 1.8 %convolution_convert_fusion.1 = bf16[128,6144]{1,0:T(8,128)(2,1)} fusion(f32[80,6144]{1,0:T(8,128)S(1)} %get-tuple-element.76, bf16[16,6144]{1,0:T(8,128)(2,1)S(1)} %collective-permute-done.27, bf16[16,6144]{1,0:T(8,128)(2,1)S(1)} %collective-permute-done.26, s32[128]{0:T(128)S(1)} %add_reduce_fusion, pred[128]{0:T(512)(128)(4,1)S(1)} %reduce_or.9), kind=kOutput, calls=%fused_computation.2 | convolution fusion | flops 26447872 | bytes 2360320 | tf_op jit(solution)/shard_map/dot_general | solution.py:219
  100.4 1.8 %convolution_convert_fusion = bf16[128,6144]{1,0:T(8,128)(2,1)} fusion(f32[80,6144]{1,0:T(8,128)S(1)} %get-tuple-element.75, bf16[16,6144]{1,0:T(8,128)(2,1)S(1)} %collective-permute-done.35, bf16[16,6144]{1,0:T(8,128)(2,1)S(1)} %collective-permute-done.33, s32[128]{0:T(128)S(1)} %add_reduce_fusion, pred[128]{0:T(512)(128)(4,1)S(1)} %reduce_or.9), kind=kOutput, calls=%fused_computation.1 | convolution fusion | flops 26447872 | bytes 2360320 | tf_op jit(solution)/shard_map/dot_general | solution.py:219
  (86 shorter events, 4.5 us)
Async XLA Ops:
  0.6 1.4 %copy-start = (bf16[128,6144]{1,0:T(8,128)(2,1)S(1)}, bf16[128,6144]{1,0:T(8,128)(2,1)}, u32[]{:S(2)}) copy-start(bf16[128,6144]{1,0:T(8,128)(2,1)} %param.8) | copy-start | bytes 4718596
  0.6 4.9 %copy-start.5 = (bf16[128,6144]{1,0:T(8,128)(2,1)S(1)}, bf16[128,6144]{1,0:T(8,128)(2,1)}, u32[]{:S(2)}) copy-start(bf16[128,6144]{1,0:T(8,128)(2,1)} %param.7) | copy-start | bytes 4718596
  2.4 8.7 %collective-permute-start.9 = (bf16[16,6144]{1,0:T(8,128)(2,1)S(1)}, bf16[16,6144]{1,0:T(8,128)(2,1)S(1)}, u32[]{:S(2)}, u32[]{:S(2)}) collective-permute-start(bf16[16,6144]{1,0:T(8,128)(2,1)S(1)} %get-tuple-element.102), channel_id=1, source_target_pairs={{0,4},{1,5},{4,8},{5,9},{8,12},{9,13},{12,14},{13,15},{14,10},{15,... | collective-permute-start | bytes 589832 | tf_op jit(solution)/shard_map/ppermute | solution.py:88
  6.0 12.5 %collective-permute-start = (bf16[16,6272]{1,0:T(8,128)(2,1)S(1)}, bf16[16,6272]{1,0:T(8,128)(2,1)S(1)}, u32[]{:S(2)}, u32[]{:S(2)}) collective-permute-start(bf16[16,6272]{1,0:T(8,128)(2,1)S(1)} %get-tuple-element.100), channel_id=1, source_target_pairs={{0,4},{1,5},{4,8},{5,9},{8,12},{9,13},{12,14},{13,15},{14,10},{15,... | collective-permute-start | bytes 602120 | tf_op jit(solution)/shard_map/ppermute | solution.py:88
  7.7 12.5 %collective-permute-start.1 = (bf16[16,6272]{1,0:T(8,128)(2,1)S(1)}, bf16[16,6272]{1,0:T(8,128)(2,1)S(1)}, u32[]{:S(2)}, u32[]{:S(2)}) collective-permute-start(bf16[16,6272]{1,0:T(8,128)(2,1)S(1)} %get-tuple-element.100), channel_id=1, source_target_pairs={{4,0},{5,1},{8,4},{9,5},{12,8},{13,9},{14,12},{15,13},{10,14},{11,... | collective-permute-start | bytes 602120 | tf_op jit(solution)/shard_map/ppermute | solution.py:88
  8.1 9.9 %collective-permute-start.10 = (bf16[16,6144]{1,0:T(8,128)(2,1)S(1)}, bf16[16,6144]{1,0:T(8,128)(2,1)S(1)}, u32[]{:S(2)}, u32[]{:S(2)}) collective-permute-start(bf16[16,6144]{1,0:T(8,128)(2,1)S(1)} %get-tuple-element.102), channel_id=1, source_target_pairs={{4,0},{5,1},{8,4},{9,5},{12,8},{13,9},{14,12},{15,13},{10,14},{11,... | collective-permute-start | bytes 589832 | tf_op jit(solution)/shard_map/ppermute | solution.py:88
  11.1 9.5 %collective-permute-start.11 = (bf16[16,6144]{1,0:T(8,128)(2,1)S(1)}, bf16[16,6144]{1,0:T(8,128)(2,1)S(1)}, u32[]{:S(2)}, u32[]{:S(2)}) collective-permute-start(bf16[16,6144]{1,0:T(8,128)(2,1)S(1)} %collective-permute-done.9), channel_id=1, source_target_pairs={{0,4},{1,5},{4,8},{5,9},{8,12},{9,13},{12,14},{13,15},{14,10},{15,... | collective-permute-start | bytes 589832 | tf_op jit(solution)/shard_map/ppermute | solution.py:88
  18.1 7.8 %collective-permute-start.12 = (bf16[16,6144]{1,0:T(8,128)(2,1)S(1)}, bf16[16,6144]{1,0:T(8,128)(2,1)S(1)}, u32[]{:S(2)}, u32[]{:S(2)}) collective-permute-start(bf16[16,6144]{1,0:T(8,128)(2,1)S(1)} %collective-permute-done.10), channel_id=1, source_target_pairs={{4,0},{5,1},{8,4},{9,5},{12,8},{13,9},{14,12},{15,13},{10,14},{11,... | collective-permute-start | bytes 589832 | tf_op jit(solution)/shard_map/ppermute | solution.py:88
  18.5 8.0 %collective-permute-start.2 = (bf16[16,6272]{1,0:T(8,128)(2,1)S(1)}, bf16[16,6272]{1,0:T(8,128)(2,1)S(1)}, u32[]{:S(2)}, u32[]{:S(2)}) collective-permute-start(bf16[16,6272]{1,0:T(8,128)(2,1)S(1)} %collective-permute-done), channel_id=1, source_target_pairs={{0,4},{1,5},{4,8},{5,9},{8,12},{9,13},{12,14},{13,15},{14,10},{15,... | collective-permute-start | bytes 602120 | tf_op jit(solution)/shard_map/ppermute | solution.py:88
  20.2 10.0 %collective-permute-start.3 = (bf16[16,6272]{1,0:T(8,128)(2,1)S(1)}, bf16[16,6272]{1,0:T(8,128)(2,1)S(1)}, u32[]{:S(2)}, u32[]{:S(2)}) collective-permute-start(bf16[16,6272]{1,0:T(8,128)(2,1)S(1)} %collective-permute-done.1), channel_id=1, source_target_pairs={{4,0},{5,1},{8,4},{9,5},{12,8},{13,9},{14,12},{15,13},{10,14},{11,... | collective-permute-start | bytes 602120 | tf_op jit(solution)/shard_map/ppermute | solution.py:88
  20.7 14.2 %collective-permute-start.13 = (bf16[16,6144]{1,0:T(8,128)(2,1)S(1)}, bf16[16,6144]{1,0:T(8,128)(2,1)S(1)}, u32[]{:S(2)}, u32[]{:S(2)}) collective-permute-start(bf16[16,6144]{1,0:T(8,128)(2,1)S(1)} %collective-permute-done.11), channel_id=1, source_target_pairs={{0,4},{1,5},{4,8},{5,9},{8,12},{9,13},{12,14},{13,15},{14,10},{15,... | collective-permute-start | bytes 589832 | tf_op jit(solution)/shard_map/ppermute | solution.py:88
  25.9 8.5 %collective-permute-start.14 = (bf16[16,6144]{1,0:T(8,128)(2,1)S(1)}, bf16[16,6144]{1,0:T(8,128)(2,1)S(1)}, u32[]{:S(2)}, u32[]{:S(2)}) collective-permute-start(bf16[16,6144]{1,0:T(8,128)(2,1)S(1)} %collective-permute-done.12), channel_id=1, source_target_pairs={{4,0},{5,1},{8,4},{9,5},{12,8},{13,9},{14,12},{15,13},{10,14},{11,... | collective-permute-start | bytes 589832 | tf_op jit(solution)/shard_map/ppermute | solution.py:88
  26.5 10.1 %collective-permute-start.4 = (bf16[16,6272]{1,0:T(8,128)(2,1)S(1)}, bf16[16,6272]{1,0:T(8,128)(2,1)S(1)}, u32[]{:S(2)}, u32[]{:S(2)}) collective-permute-start(bf16[16,6272]{1,0:T(8,128)(2,1)S(1)} %collective-permute-done.2), channel_id=1, source_target_pairs={{0,4},{1,5},{4,8},{5,9},{8,12},{9,13},{12,14},{13,15},{14,10},{15,... | collective-permute-start | bytes 602120 | tf_op jit(solution)/shard_map/ppermute | solution.py:88
  30.2 8.1 %collective-permute-start.5 = (bf16[16,6272]{1,0:T(8,128)(2,1)S(1)}, bf16[16,6272]{1,0:T(8,128)(2,1)S(1)}, u32[]{:S(2)}, u32[]{:S(2)}) collective-permute-start(bf16[16,6272]{1,0:T(8,128)(2,1)S(1)} %collective-permute-done.3), channel_id=1, source_target_pairs={{4,0},{5,1},{8,4},{9,5},{12,8},{13,9},{14,12},{15,13},{10,14},{11,... | collective-permute-start | bytes 602120 | tf_op jit(solution)/shard_map/ppermute | solution.py:88
  34.4 4.8 %collective-permute-start.16 = (bf16[16,3072]{1,0:T(8,128)(2,1)S(1)}, bf16[16,3072]{1,0:T(8,128)(2,1)S(1)}, u32[]{:S(2)}, u32[]{:S(2)}) collective-permute-start(bf16[16,3072]{1,0:T(8,128)(2,1)S(1)} %slice.144), channel_id=1, source_target_pairs={{4,0},{5,1},{8,4},{9,5},{12,8},{13,9},{14,12},{15,13},{10,14},{11,... | collective-permute-start | bytes 294920 | tf_op jit(solution)/shard_map/ppermute | solution.py:88
  34.9 4.7 %collective-permute-start.15 = (bf16[16,3072]{1,0:T(8,128)(2,1)S(1)}, bf16[16,3072]{1,0:T(8,128)(2,1)S(1)}, u32[]{:S(2)}, u32[]{:S(2)}) collective-permute-start(bf16[16,3072]{1,0:T(8,128)(2,1)S(1)} %slice.143), channel_id=1, source_target_pairs={{0,4},{1,5},{4,8},{5,9},{8,12},{9,13},{12,14},{13,15},{14,10},{15,... | collective-permute-start | bytes 294920 | tf_op jit(solution)/shard_map/ppermute | solution.py:88
  36.6 4.7 %collective-permute-start.6 = (bf16[16,3072]{1,0:T(8,128)(2,1)S(1)}, bf16[16,3072]{1,0:T(8,128)(2,1)S(1)}, u32[]{:S(2)}, u32[]{:S(2)}) collective-permute-start(bf16[16,3072]{1,0:T(8,128)(2,1)S(1)} %slice.141), channel_id=1, source_target_pairs={{0,4},{1,5},{4,8},{5,9},{8,12},{9,13},{12,14},{13,15},{14,10},{15,... | collective-permute-start | bytes 294920 | tf_op jit(solution)/shard_map/ppermute | solution.py:88
  38.3 4.9 %collective-permute-start.7 = (bf16[16,3200]{1,0:T(8,128)(2,1)S(1)}, bf16[16,3200]{1,0:T(8,128)(2,1)S(1)}, u32[]{:S(2)}, u32[]{:S(2)}) collective-permute-start(bf16[16,3200]{1,0:T(8,128)(2,1)S(1)} %slice.142), channel_id=1, source_target_pairs={{4,0},{5,1},{8,4},{9,5},{12,8},{13,9},{14,12},{15,13},{10,14},{11,... | collective-permute-start | bytes 307208 | tf_op jit(solution)/shard_map/ppermute | solution.py:88
  39.0 5.9 %collective-permute-start.8 = (bf16[112,6272]{1,0:T(8,128)(2,1)S(1)}, bf16[112,6272]{1,0:T(8,128)(2,1)S(1)}, u32[]{:S(2)}, u32[]{:S(2)}) collective-permute-start(bf16[112,6272]{1,0:T(8,128)(2,1)S(1)} %get-tuple-element.86), channel_id=1, source_target_pairs={{0,1},{1,0},{2,3},{3,2},{4,5},{5,4},{6,7},{7,6},{8,9},{9,8},{10,11... | collective-permute-start | bytes 4214792 | tf_op jit(solution)/shard_map/ppermute | solution.py:88
  43.2 1.5 %collective-permute-start.17 = (bf16[16,6272]{1,0:T(8,128)(2,1)S(1)}, bf16[16,6272]{1,0:T(8,128)(2,1)S(1)}, u32[]{:S(2)}, u32[]{:S(2)}) collective-permute-start(bf16[16,6272]{1,0:T(8,128)(2,1)S(1)} %pad_maximum_fusion.1), channel_id=1, source_target_pairs={{0,1},{1,0},{2,3},{3,2},{4,5},{5,4},{6,7},{7,6},{8,9},{9,8},{10,11... | collective-permute-start | bytes 602120 | tf_op jit(solution)/shard_map/ppermute | solution.py:88
  44.7 5.8 %collective-permute-start.18 = (bf16[128,6144]{1,0:T(8,128)(2,1)S(1)}, bf16[128,6144]{1,0:T(8,128)(2,1)S(1)}, u32[]{:S(2)}, u32[]{:S(2)}) collective-permute-start(bf16[128,6144]{1,0:T(8,128)(2,1)S(1)} %maximum_dynamic-update-slice_fusion), channel_id=1, source_target_pairs={{0,1},{1,0},{2,3},{3,2},{4,5},{5,4},{6,7},{7,6},{8,9},{9,8},{10,11... | collective-permute-start | bytes 4718600 | tf_op jit(solution)/shard_map/ppermute | solution.py:88
  44.8 2.2 %copy-start.2 = (bf16[6144,336]{0,1:T(8,128)(2,1)S(1)}, bf16[6144,336]{0,1:T(8,128)(2,1)}, u32[]{:S(2)}) copy-start(bf16[6144,336]{0,1:T(8,128)(2,1)} %param.11) | copy-start | bytes 12386308
  47.0 2.2 %copy-start.4 = (bf16[6144,336]{0,1:T(8,128)(2,1)S(1)}, bf16[6144,336]{0,1:T(8,128)(2,1)}, u32[]{:S(2)}) copy-start(bf16[6144,336]{0,1:T(8,128)(2,1)} %param.12) | copy-start | bytes 12386308
  49.2 2.2 %copy-start.3 = (bf16[336,6144]{1,0:T(8,128)(2,1)S(1)}, bf16[336,6144]{1,0:T(8,128)(2,1)}, u32[]{:S(2)}) copy-start(bf16[336,6144]{1,0:T(8,128)(2,1)} %param.13) | copy-start | bytes 12386308
  58.6 2.1 %collective-permute-start.20 = (bf16[48,6144]{1,0:T(8,128)(2,1)S(1)}, bf16[48,6144]{1,0:T(8,128)(2,1)S(1)}, u32[]{:S(2)}, u32[]{:S(2)}) collective-permute-start(bf16[48,6144]{1,0:T(8,128)(2,1)S(1)} %slice.155), channel_id=1, source_target_pairs={{0,1},{1,0},{2,3},{3,2},{4,5},{5,4},{6,7},{7,6},{8,9},{9,8},{10,11... | collective-permute-start | bytes 1769480 | tf_op jit(solution)/shard_map/ppermute | solution.py:88
  59.2 13.3 %collective-permute-start.19 = (bf16[160,6144]{1,0:T(8,128)(2,1)S(1)}, bf16[160,6144]{1,0:T(8,128)(2,1)S(1)}, u32[]{:S(2)}, u32[]{:S(2)}) collective-permute-start(bf16[160,6144]{1,0:T(8,128)(2,1)S(1)} %pad_maximum_fusion), channel_id=1, source_target_pairs={{0,1},{1,0},{2,3},{3,2},{4,5},{5,4},{6,7},{7,6},{8,9},{9,8},{10,11... | collective-permute-start | bytes 5898248 | tf_op jit(solution)/shard_map/ppermute | solution.py:88
  59.4 5.0 %collective-permute-start.28 = (bf16[48,6144]{1,0:T(8,128)(2,1)S(1)}, bf16[48,6144]{1,0:T(8,128)(2,1)S(1)}, u32[]{:S(2)}, u32[]{:S(2)}) collective-permute-start(bf16[48,6144]{1,0:T(8,128)(2,1)S(1)} %slice.135), channel_id=1, source_target_pairs={{0,1},{1,0},{2,3},{3,2},{4,5},{5,4},{6,7},{7,6},{8,9},{9,8},{10,11... | collective-permute-start | bytes 1769480 | tf_op jit(solution)/shard_map/ppermute | solution.py:88
  60.9 9.0 %collective-permute-start.21 = (bf16[16,6144]{1,0:T(8,128)(2,1)S(1)}, bf16[16,6144]{1,0:T(8,128)(2,1)S(1)}, u32[]{:S(2)}, u32[]{:S(2)}) collective-permute-start(bf16[16,6144]{1,0:T(8,128)(2,1)S(1)} %get-tuple-element.40), channel_id=1, source_target_pairs={{4,0},{5,1},{8,4},{9,5},{12,8},{13,9},{14,12},{15,13},{10,14},{11,... | collective-permute-start | bytes 589832 | tf_op jit(solution)/shard_map/ppermute | solution.py:88
  61.4 11.7 %collective-permute-start.22 = (bf16[16,6144]{1,0:T(8,128)(2,1)S(1)}, bf16[16,6144]{1,0:T(8,128)(2,1)S(1)}, u32[]{:S(2)}, u32[]{:S(2)}) collective-permute-start(bf16[16,6144]{1,0:T(8,128)(2,1)S(1)} %get-tuple-element.41), channel_id=1, source_target_pairs={{0,4},{1,5},{4,8},{5,9},{8,12},{9,13},{12,14},{13,15},{14,10},{15,... | collective-permute-start | bytes 589832 | tf_op jit(solution)/shard_map/ppermute | solution.py:88
  64.5 10.7 %collective-permute-start.29 = (bf16[16,6144]{1,0:T(8,128)(2,1)S(1)}, bf16[16,6144]{1,0:T(8,128)(2,1)S(1)}, u32[]{:S(2)}, u32[]{:S(2)}) collective-permute-start(bf16[16,6144]{1,0:T(8,128)(2,1)S(1)} %get-tuple-element.48), channel_id=1, source_target_pairs={{4,0},{5,1},{8,4},{9,5},{12,8},{13,9},{14,12},{15,13},{10,14},{11,... | collective-permute-start | bytes 589832 | tf_op jit(solution)/shard_map/ppermute | solution.py:88
  65.1 7.4 %collective-permute-start.30 = (bf16[16,6144]{1,0:T(8,128)(2,1)S(1)}, bf16[16,6144]{1,0:T(8,128)(2,1)S(1)}, u32[]{:S(2)}, u32[]{:S(2)}) collective-permute-start(bf16[16,6144]{1,0:T(8,128)(2,1)S(1)} %get-tuple-element.49), channel_id=1, source_target_pairs={{0,4},{1,5},{4,8},{5,9},{8,12},{9,13},{12,14},{13,15},{14,10},{15,... | collective-permute-start | bytes 589832 | tf_op jit(solution)/shard_map/ppermute | solution.py:88
  73.2 7.9 %collective-permute-start.24 = (bf16[16,6144]{1,0:T(8,128)(2,1)S(1)}, bf16[16,6144]{1,0:T(8,128)(2,1)S(1)}, u32[]{:S(2)}, u32[]{:S(2)}) collective-permute-start(bf16[16,6144]{1,0:T(8,128)(2,1)S(1)} %fusion.13), channel_id=1, source_target_pairs={{0,4},{1,5},{4,8},{5,9},{8,12},{9,13},{12,14},{13,15},{14,10},{15,... | collective-permute-start | bytes 589832 | tf_op jit(solution)/shard_map/ppermute | solution.py:88
  74.8 7.8 %collective-permute-start.23 = (bf16[16,6144]{1,0:T(8,128)(2,1)S(1)}, bf16[16,6144]{1,0:T(8,128)(2,1)S(1)}, u32[]{:S(2)}, u32[]{:S(2)}) collective-permute-start(bf16[16,6144]{1,0:T(8,128)(2,1)S(1)} %fusion.14), channel_id=1, source_target_pairs={{4,0},{5,1},{8,4},{9,5},{12,8},{13,9},{14,12},{15,13},{10,14},{11,... | collective-permute-start | bytes 589832 | tf_op jit(solution)/shard_map/ppermute | solution.py:88
  75.3 9.9 %collective-permute-start.32 = (bf16[16,6144]{1,0:T(8,128)(2,1)S(1)}, bf16[16,6144]{1,0:T(8,128)(2,1)S(1)}, u32[]{:S(2)}, u32[]{:S(2)}) collective-permute-start(bf16[16,6144]{1,0:T(8,128)(2,1)S(1)} %fusion.7), channel_id=1, source_target_pairs={{0,4},{1,5},{4,8},{5,9},{8,12},{9,13},{12,14},{13,15},{14,10},{15,... | collective-permute-start | bytes 589832 | tf_op jit(solution)/shard_map/ppermute | solution.py:88
  76.9 9.9 %collective-permute-start.31 = (bf16[16,6144]{1,0:T(8,128)(2,1)S(1)}, bf16[16,6144]{1,0:T(8,128)(2,1)S(1)}, u32[]{:S(2)}, u32[]{:S(2)}) collective-permute-start(bf16[16,6144]{1,0:T(8,128)(2,1)S(1)} %fusion.8), channel_id=1, source_target_pairs={{4,0},{5,1},{8,4},{9,5},{12,8},{13,9},{14,12},{15,13},{10,14},{11,... | collective-permute-start | bytes 589832 | tf_op jit(solution)/shard_map/ppermute | solution.py:88
  82.7 12.4 %collective-permute-start.27 = (bf16[16,6144]{1,0:T(8,128)(2,1)S(1)}, bf16[16,6144]{1,0:T(8,128)(2,1)S(1)}, u32[]{:S(2)}, u32[]{:S(2)}) collective-permute-start(bf16[16,6144]{1,0:T(8,128)(2,1)S(1)} %get-tuple-element.45), channel_id=1, source_target_pairs={{0,4},{1,5},{4,8},{5,9},{8,12},{9,13},{12,14},{13,15},{14,10},{15,... | collective-permute-start | bytes 589832 | tf_op jit(solution)/shard_map/ppermute | solution.py:88
  84.3 8.6 %collective-permute-start.25 = (bf16[16,6144]{1,0:T(8,128)(2,1)S(1)}, bf16[16,6144]{1,0:T(8,128)(2,1)S(1)}, u32[]{:S(2)}, u32[]{:S(2)}) collective-permute-start(bf16[16,6144]{1,0:T(8,128)(2,1)S(1)} %get-tuple-element.44), channel_id=1, source_target_pairs={{4,0},{5,1},{8,4},{9,5},{12,8},{13,9},{14,12},{15,13},{10,14},{11,... | collective-permute-start | bytes 589832 | tf_op jit(solution)/shard_map/ppermute | solution.py:88
  86.9 6.5 %collective-permute-start.34 = (bf16[16,6144]{1,0:T(8,128)(2,1)S(1)}, bf16[16,6144]{1,0:T(8,128)(2,1)S(1)}, u32[]{:S(2)}, u32[]{:S(2)}) collective-permute-start(bf16[16,6144]{1,0:T(8,128)(2,1)S(1)} %get-tuple-element.57), channel_id=1, source_target_pairs={{0,4},{1,5},{4,8},{5,9},{8,12},{9,13},{12,14},{13,15},{14,10},{15,... | collective-permute-start | bytes 589832 | tf_op jit(solution)/shard_map/ppermute | solution.py:88
  88.5 11.9 %collective-permute-start.33 = (bf16[16,6144]{1,0:T(8,128)(2,1)S(1)}, bf16[16,6144]{1,0:T(8,128)(2,1)S(1)}, u32[]{:S(2)}, u32[]{:S(2)}) collective-permute-start(bf16[16,6144]{1,0:T(8,128)(2,1)S(1)} %get-tuple-element.56), channel_id=1, source_target_pairs={{4,0},{5,1},{8,4},{9,5},{12,8},{13,9},{14,12},{15,13},{10,14},{11,... | collective-permute-start | bytes 589832 | tf_op jit(solution)/shard_map/ppermute | solution.py:88
  92.9 5.7 %collective-permute-start.26 = (bf16[16,6144]{1,0:T(8,128)(2,1)S(1)}, bf16[16,6144]{1,0:T(8,128)(2,1)S(1)}, u32[]{:S(2)}, u32[]{:S(2)}) collective-permute-start(bf16[16,6144]{1,0:T(8,128)(2,1)S(1)} %fusion.16), channel_id=1, source_target_pairs={{4,0},{5,1},{8,4},{9,5},{12,8},{13,9},{14,12},{15,13},{10,14},{11,... | collective-permute-start | bytes 589832 | tf_op jit(solution)/shard_map/ppermute | solution.py:88
  93.4 8.8 %copy-start.1 = (bf16[128,6144]{1,0:T(8,128)(2,1)S(1)}, bf16[128,6144]{1,0:T(8,128)(2,1)}, u32[]{:S(2)}) copy-start(bf16[128,6144]{1,0:T(8,128)(2,1)} %param.8) | copy-start | bytes 4718596
  93.5 6.9 %collective-permute-start.35 = (bf16[16,6144]{1,0:T(8,128)(2,1)S(1)}, bf16[16,6144]{1,0:T(8,128)(2,1)S(1)}, u32[]{:S(2)}, u32[]{:S(2)}) collective-permute-start(bf16[16,6144]{1,0:T(8,128)(2,1)S(1)} %fusion.5), channel_id=1, source_target_pairs={{0,4},{1,5},{4,8},{5,9},{8,12},{9,13},{12,14},{13,15},{14,10},{15,... | collective-permute-start | bytes 589832 | tf_op jit(solution)/shard_map/ppermute | solution.py:88

commit v8 on v7

v8 whole, which is shorter than its diff:
```python
import jax
import jax.numpy as jnp
from jax import lax
from jax.experimental import pallas as pl
from jax.experimental.pallas import tpu as pltpu
from jax.sharding import PartitionSpec as P

CAP = 16
LANES = 128
ANY = pl.BlockSpec(memory_space=pl.ANY)
MARK = jax.ShapeDtypeStruct((8, LANES), jnp.float32)


def parts_of(d, most):
    width = LANES
    for w in range(LANES, most + 1, LANES):
        if d % w == 0:
            width = w
    return d // width, width


def params(megabytes):
    return pltpu.CompilerParams(vmem_limit_bytes=megabytes << 20)


def grad_kernel(parts, width, offset, marks, side_ref, rows_ref, *refs):
    out_ref, mark_ref, rows_buf, out_buf, load_sem, store_sem = refs[marks:]
    spans = [pl.ds(j * width, width) for j in range(parts)]
    loads = [
        pltpu.make_async_copy(
            rows_ref.at[:, pl.ds(offset + j * width, width)], rows_buf.at[:, at], load_sem.at[j]
        )
        for j, at in enumerate(spans)
    ]
    stores = [
        pltpu.make_async_copy(out_buf.at[:, at], out_ref.at[:, at], store_sem.at[j])
        for j, at in enumerate(spans)
    ]
    for load in loads:
        load.start()
    mark_ref[...] = jnp.zeros(mark_ref.shape, jnp.float32)
    side = side_ref[...]
    for j, at in enumerate(spans):
        loads[j].wait()
        out_buf[:, at] = jnp.dot(
            side, rows_buf[:, at], preferred_element_type=jnp.float32
        ).astype(jnp.bfloat16)
        stores[j].start()
    for store in stores:
        store.wait()


def weight_grad(side, rows, offset, d, marks):
    r, f = side.shape
    parts, width = parts_of(d, 1024)
    return pl.pallas_call(
        lambda *refs: grad_kernel(parts, width, offset, len(marks), *refs),
        in_specs=[pl.BlockSpec(memory_space=pltpu.VMEM), ANY] + [ANY] * len(marks),
        out_specs=[ANY, pl.BlockSpec(memory_space=pltpu.VMEM)],
        out_shape=[jax.ShapeDtypeStruct((f, d), jnp.bfloat16), MARK],
        scratch_shapes=[
            pltpu.VMEM((r, d), jnp.bfloat16),
            pltpu.VMEM((f, d), jnp.bfloat16),
            pltpu.SemaphoreType.DMA((parts,)),
            pltpu.SemaphoreType.DMA((parts,)),
        ],
        compiler_params=params(20),
        cost_estimate=pl.CostEstimate(
            flops=2 * r * f * d, bytes_accessed=2 * d * (r + f), transcendentals=0
        ),
    )(side.T, rows, *marks)


def ring_of(n):
    chips = n // 2
    order = list(range(0, chips, 2)) + list(range(chips - 1, 0, -2))
    right = []
    for at, chip in enumerate(order):
        nxt = order[(at + 1) % chips]
        right += [(2 * chip + core, 2 * nxt + core) for core in (0, 1)]
    return right, [(b, a) for a, b in right]


def make_per_device(n):
    steps = n // 4
    core_pairs = [(i, i ^ 1) for i in range(n)]
    right_pairs, left_pairs = ring_of(n)
    blocks = 2 * steps
    near = max(blocks - 3, 1)

    def permute(x, pairs):
        return lax.ppermute(x, "et", pairs)

    def both_ways(right, left):
        return permute(right, right_pairs), permute(left, left_pairs)

    def gather(first, held, wide):
        got = [first, *held]
        for _ in range(2, steps):
            held = both_ways(*held)
            got += held
        far = both_ways(held[0][:, :wide], held[1][:, wide:])
        return got, far

    def early_of(got):
        return permute(jnp.concatenate(got, axis=0), core_pairs)

    def all_rows(got, far, early):
        far = jnp.concatenate(far, axis=1)
        return jnp.concatenate([*got, far, early, permute(far, core_pairs)], axis=0)

    def products(rows, wide, w_gate, w_up, w_down):
        rows_x, rows_dy = rows[:, : wide - LANES], rows[:, wide:]
        coef = rows[:, wide - LANES : wide - LANES + 1].astype(jnp.float32)
        gate = jnp.dot(rows_x, w_gate, preferred_element_type=jnp.float32)
        up = jnp.dot(rows_x, w_up, preferred_element_type=jnp.float32)
        sig = jax.nn.sigmoid(gate)
        act = gate * sig
        hidden = (coef * act * up).astype(jnp.bfloat16)
        scaled = coef * jnp.dot(rows_dy, w_down.T, preferred_element_type=jnp.float32)
        dgate = (scaled * up * sig * (1.0 + gate * (1.0 - sig))).astype(jnp.bfloat16)
        dup = (scaled * act).astype(jnp.bfloat16)
        return hidden, dgate, dup

    def rows_of(hidden, dgate, dup, w_gate, w_up, w_down):
        out_rows = jnp.dot(hidden, w_down, preferred_element_type=jnp.float32)
        dx_rows = jnp.dot(dgate, w_gate.T, preferred_element_type=jnp.float32) + jnp.dot(
            dup, w_up.T, preferred_element_type=jnp.float32
        )
        return out_rows, dx_rows

    def to_send(own):
        rows = own[0].shape[0] // 2
        return jnp.concatenate([a[rows:].astype(jnp.bfloat16) for a in own], axis=1)

    def pair_sums(own, sent):
        size = sent.shape[0] // blocks
        d = own[0].shape[1]
        pieces = []
        for at, to in ((near * size, blocks * size), (0, near * size)):
            got = permute(sent[at:to], core_pairs)
            pieces.append(
                [
                    a[at:to] + got[:, k * d : (k + 1) * d].astype(jnp.float32)
                    for k, a in enumerate(own)
                ]
            )
        return size, pieces[1], pieces[0]

    def block_of(total, part, at):
        size, close, far = total
        if at < near:
            return close[part][at * size : (at + 1) * size]
        return far[part][(at - near) * size : (at - near + 1) * size]

    def wave(total, carry, at):
        if at == 1:
            values = (block_of(total, 1, blocks - 1), block_of(total, 0, blocks - 1))
            values = [v.astype(jnp.bfloat16) for v in values]
        else:
            k = steps - at + 1
            values = []
            for way, index in ((0, 2 * k), (1, 2 * k - 1)):
                out_part, dx_part = (block_of(total, part, index) for part in (0, 1))
                got = carry[way].astype(jnp.float32)
                if at == 2 and way == 0:
                    dx_part = dx_part + got
                elif at == 2:
                    out_part = out_part + got
                else:
                    d = out_part.shape[1]
                    out_part, dx_part = out_part + got[:, :d], dx_part + got[:, d:]
                values.append(
                    jnp.concatenate(
                        [out_part.astype(jnp.bfloat16), dx_part.astype(jnp.bfloat16)], axis=1
                    )
                )
        return lax.optimization_barrier(tuple(values))

    def final(total, carry, part):
        d = total[1][part].shape[1]
        done = block_of(total, part, 0)
        for got in carry:
            done = done + got[:, part * d : (part + 1) * d].astype(jnp.float32)
        return done.astype(jnp.bfloat16)

    def per_device(tokens, out_grad, expert_ids, gate_vals, w_gate, w_up, w_down):
        d = tokens.shape[1]
        wide = d + LANES
        landed = expert_ids == 0
        coef = jnp.sum(jnp.where(landed, gate_vals.astype(jnp.float32), 0.0), axis=1).astype(
            jnp.bfloat16
        )
        routed = jnp.any(landed, axis=1)
        slot = jnp.cumsum(routed.astype(jnp.int32)) - 1
        select = (slot[None, :] == jnp.arange(CAP, dtype=jnp.int32)[:, None]) & routed[None, :]
        select = select.astype(jnp.bfloat16)
        slot_x, slot_dy, slot_coef = (
            jnp.dot(select, a, preferred_element_type=jnp.float32).astype(jnp.bfloat16)
            for a in (tokens, out_grad, coef[:, None])
        )
        slots = jnp.concatenate(
            [slot_x, jnp.broadcast_to(slot_coef, (CAP, LANES)), slot_dy], axis=1
        )
        first_a, first_b = slots[: CAP // 2], slots[CAP // 2 :]

        held_a = both_ways(first_a, first_a)
        first_b, *held_a = lax.optimization_barrier((first_b, *held_a))
        got_a, far_a = gather(first_a, tuple(held_a), wide)
        got_b, far_b = gather(first_b, both_ways(first_b, first_b), wide)
        weights = (w_gate, w_up, w_down)

        rows_a = all_rows(got_a, far_a, early_of(got_a))
        early_b = early_of(got_b)
        sides_a = products(rows_a, wide, *weights)
        out_a, dx_a = rows_of(*sides_a, *weights)
        sent_a = to_send((out_a, dx_a))
        early_b, dx_a, *far_b = lax.optimization_barrier((early_b, dx_a, *far_b))
        total_a = pair_sums((out_a, dx_a), sent_a)
        carry_a = both_ways(*wave(total_a, None, 1))

        rows_b = all_rows(got_b, far_b, early_b)
        hidden_b, dgate_b, dup_b = products(rows_b, wide, *weights)
        dgate_b, *carry_a = lax.optimization_barrier((dgate_b, *carry_a))
        sides_b = (hidden_b, dgate_b, dup_b)
        out_b, dx_b = rows_of(*sides_b, *weights)
        sent_b = to_send((out_b, dx_b))
        carry_a = both_ways(*wave(total_a, carry_a, 2))
        dx_b, *carry_a = lax.optimization_barrier((dx_b, *carry_a))
        total_b = pair_sums((out_b, dx_b), sent_b)

        sides = [jnp.concatenate(pair, axis=0) for pair in zip(sides_a, sides_b)]
        rows = jnp.concatenate([rows_a, rows_b], axis=0)
        hidden, dgate, dup = sides
        work = [(dgate, 0), (dup, 0), (hidden, wide)]
        carry_b = None
        grads, marks = [], []
        for at in range(1, steps + 1):
            if at + 2 <= steps:
                carry_a = both_ways(*wave(total_a, carry_a, at + 2))
            blocks_b = wave(total_b, carry_b, at)
            if work:
                side, offset = work.pop(0)
                side, *blocks_b = lax.optimization_barrier((side, *blocks_b))
                grad, mark = weight_grad(side, rows, offset, d, marks)
                grads.append(grad)
                carry_b = both_ways(*blocks_b)
                if work and at < steps:
                    mark, *carry_b = lax.optimization_barrier((mark, *carry_b))
                marks = [mark]
            else:
                carry_b = both_ways(*blocks_b)
        for side, offset in work:
            grads.append(weight_grad(side, rows, offset, d, marks)[0])
        grad_gate, grad_up, grad_down = grads
        mixed, grad_tokens = (
            jnp.dot(
                select.T,
                jnp.concatenate(
                    [final(total_a, carry_a, part), final(total_b, carry_b, part)], axis=0
                ),
                preferred_element_type=jnp.float32,
            ).astype(jnp.bfloat16)
            for part in (0, 1)
        )
        return (mixed, grad_tokens, grad_gate.T, grad_up.T, grad_down)

    return per_device


def solution(mesh):
    placed = (
        P(("groups", "et"), None),
        P(("groups", "et"), None),
        P(("groups", "et"), None),
        P(("groups", "et"), None),
        P(None, "et"),
        P(None, "et"),
        P("et", None),
    )
    return jax.shard_map(
        make_per_device(mesh.shape["et"]),
        mesh=mesh,
        in_specs=placed,
        out_specs=(
            P(("groups", "et"), None),
            P(("groups", "et"), None),
            P("groups", "et"),
            P("groups", "et"),
            P(("groups", "et"), None),
        ),
        check_vma=False,
    )
```

time: 102 us -> 112 us (1.098)
  matrix products: 13.6 us -> 19.3 us
  starting transfers between devices: 34.3 us -> 35.6 us
  waiting for transfers between devices: 35.1 us -> 36.4 us
    dot_general x8 -> x14, matrix products: 12.9 us -> 17.1 us  [the longest x2 3.53 us: per_device(): jnp.dot(select.T, jnp.concatenate([final(total_a, carry_a, part), final(t...]
    dot_general x3, matrix products: 0.75 us -> 2.16 us  [per_device(): jnp.dot(select, a, preferred_element_type=jnp.float32).astype(jnp.bfloat16)]
    ppermute x36 -> x40, starting transfers between devices: 34.3 us -> 35.6 us  [permute(): return lax.ppermute(x, 'et', pairs)]
    ppermute x36 -> x40, waiting for transfers between devices: 35.1 us -> 36.4 us  [permute(): return lax.ppermute(x, 'et', pairs)]
    unnamed x27 -> x31, local copies, waits for them, and re-layouts: 4.06 us -> 4.33 us
  transfers between devices with their start and end apart: 36 -> 40, of which waited for: 19 -> 17; matrix products, arithmetic and copies ran while one was open for 7% -> 16% of each run, Pallas kernels for 10% -> 9%
where the time goes in v8:
time: 112 us
  waiting for transfers between devices  36.4 us (32%)
  starting transfers between devices  35.6 us (32%)
  matrix products  19.3 us (17%)
  Pallas kernels  10.5 us (9%)
  local copies, waits for them, and re-layouts  4.97 us (4%)
  other arithmetic  3.39 us (3%)
  between operations  1.33 us (1%)
    ppermute x40, waiting for transfers between devices, permute(): return lax.ppermute(x, 'et', pairs)  36.4 us
    ppermute x40, starting transfers between devices, permute(): return lax.ppermute(x, 'et', pairs)  35.6 us
    pallas_call x3, Pallas kernels, weight_grad(): pl.pallas_call(lambda *refs: grad_kernel(parts, width, offset, len(marks)...  10.5 us
    unnamed x31, local copies, waits for them, and re-layouts  4.33 us
    dot_general x2, matrix products, per_device(): jnp.dot(select.T, jnp.concatenate([final(total_a, carry_a, part), final(t...  3.53 us
    dot_general x2, matrix products, products(): gate = jnp.dot(rows_x, w_gate, preferred_element_type=jnp.float32)  2.49 us
    dot_general x2, matrix products, products(): jnp.dot(rows_dy, w_down.T, preferred_element_type=jnp.float32)  2.49 us
    dot_general x2, matrix products, products(): up = jnp.dot(rows_x, w_up, preferred_element_type=jnp.float32)  2.47 us
  transfers between devices with their start and end apart: 40, of which 17 were waited for; matrix products, arithmetic and copies ran while one was open for 16% of the time, Pallas kernels for 9%

profile of v8, /device:TPU:0, one launch (start us, length us, event | category | flops | bytes accessed | tf_op | source)
XLA Modules:
  0.0 111.5 jit_solution(16349964954532051572)
XLA Ops:
  0.6 0.8 select_reduce_fusion
  2.5 1.7 %convolution_convert_fusion.3 = bf16[16,6144]{1,0:T(8,128)(2,1)S(1)} fusion(bf16[128,6144]{1,0:T(8,128)(2,1)} %param.7, s32[128]{0:T(128)S(1)} %add_reduce_fusion, pred[128]{0:T(512)(128)(4,1)S(1)} %reduce_or.9), kind=kOutput, calls=%fused_computation.5 | convolution fusion | flops 25268224 | bytes 1770112 | tf_op jit(solution)/shard_map/dot_general | solution.py:199
  4.4 3.1 %collective-permute-start = (bf16[8,12416]{1,0:T(8,128)(2,1)S(1)}, bf16[8,12416]{1,0:T(8,128)(2,1)S(1)}, u32[]{:S(2)}, u32[]{:S(2)}) collective-permute-start(bf16[8,12416]{1,0:T(8,128)(2,1)S(1)} %get-tuple-element.153), channel_id=1, source_target_pairs={{0,4},{1,5},{4,8},{5,9},{8,12},{9,13},{12,14},{13,15},{14,10},{15,... | collective-permute-start | bytes 595976 | tf_op jit(solution)/shard_map/ppermute | solution.py:92
  7.5 4.9 %collective-permute-done = bf16[8,12416]{1,0:T(8,128)(2,1)S(1)} collective-permute-done((bf16[8,12416]{1,0:T(8,128)(2,1)S(1)}, bf16[8,12416]{1,0:T(8,128)(2,1)S(1)}, u32[]{:S(2)}, u32[]{:S(2)}) %collective-permute-start) | collective-permute-done | bytes 198688 | tf_op jit(solution)/shard_map/ppermute | solution.py:92
  12.4 1.5 %collective-permute-done.1 = bf16[8,12416]{1,0:T(8,128)(2,1)S(1)} collective-permute-done((bf16[8,12416]{1,0:T(8,128)(2,1)S(1)}, bf16[8,12416]{1,0:T(8,128)(2,1)S(1)}, u32[]{:S(2)}, u32[]{:S(2)}) %collective-permute-start.1) | collective-permute-done | bytes 198688 | tf_op jit(solution)/shard_map/ppermute | solution.py:92
  13.9 1.6 %collective-permute-start.11 = (bf16[8,12416]{1,0:T(8,128)(2,1)S(1)}, bf16[8,12416]{1,0:T(8,128)(2,1)S(1)}, u32[]{:S(2)}, u32[]{:S(2)}) collective-permute-start(bf16[8,12416]{1,0:T(8,128)(2,1)S(1)} %get-tuple-element.56), channel_id=1, source_target_pairs={{0,4},{1,5},{4,8},{5,9},{8,12},{9,13},{12,14},{13,15},{14,10},{15,... | collective-permute-start | bytes 595976 | tf_op jit(solution)/shard_map/ppermute | solution.py:92
  15.9 1.6 %collective-permute-start.2 = (bf16[8,12416]{1,0:T(8,128)(2,1)S(1)}, bf16[8,12416]{1,0:T(8,128)(2,1)S(1)}, u32[]{:S(2)}, u32[]{:S(2)}) collective-permute-start(bf16[8,12416]{1,0:T(8,128)(2,1)S(1)} %collective-permute-done), channel_id=1, source_target_pairs={{0,4},{1,5},{4,8},{5,9},{8,12},{9,13},{12,14},{13,15},{14,10},{15,... | collective-permute-start | bytes 595976 | tf_op jit(solution)/shard_map/ppermute | solution.py:92
  18.1 5.6 %collective-permute-done.2 = bf16[8,12416]{1,0:T(8,128)(2,1)S(1)} collective-permute-done((bf16[8,12416]{1,0:T(8,128)(2,1)S(1)}, bf16[8,12416]{1,0:T(8,128)(2,1)S(1)}, u32[]{:S(2)}, u32[]{:S(2)}) %collective-permute-start.2) | collective-permute-done | bytes 198688 | tf_op jit(solution)/shard_map/ppermute | solution.py:92
  23.7 1.6 %collective-permute-start.4 = (bf16[8,12416]{1,0:T(8,128)(2,1)S(1)}, bf16[8,12416]{1,0:T(8,128)(2,1)S(1)}, u32[]{:S(2)}, u32[]{:S(2)}) collective-permute-start(bf16[8,12416]{1,0:T(8,128)(2,1)S(1)} %collective-permute-done.2), channel_id=1, source_target_pairs={{0,4},{1,5},{4,8},{5,9},{8,12},{9,13},{12,14},{13,15},{14,10},{15,... | collective-permute-start | bytes 595976 | tf_op jit(solution)/shard_map/ppermute | solution.py:92
  25.3 0.4 collective-permute-start.5
  25.7 1.6 %collective-permute-start.13 = (bf16[8,12416]{1,0:T(8,128)(2,1)S(1)}, bf16[8,12416]{1,0:T(8,128)(2,1)S(1)}, u32[]{:S(2)}, u32[]{:S(2)}) collective-permute-start(bf16[8,12416]{1,0:T(8,128)(2,1)S(1)} %collective-permute-done.11), channel_id=1, source_target_pairs={{0,4},{1,5},{4,8},{5,9},{8,12},{9,13},{12,14},{13,15},{14,10},{15,... | collective-permute-start | bytes 595976 | tf_op jit(solution)/shard_map/ppermute | solution.py:92
  27.3 0.4 collective-permute-start.14
  27.8 3.6 %collective-permute-done.4 = bf16[8,12416]{1,0:T(8,128)(2,1)S(1)} collective-permute-done((bf16[8,12416]{1,0:T(8,128)(2,1)S(1)}, bf16[8,12416]{1,0:T(8,128)(2,1)S(1)}, u32[]{:S(2)}, u32[]{:S(2)}) %collective-permute-start.4) | collective-permute-done | bytes 198688 | tf_op jit(solution)/shard_map/ppermute | solution.py:92
  31.5 1.6 %collective-permute-start.6 = (bf16[8,6272]{1,0:T(8,128)(2,1)S(1)}, bf16[8,6272]{1,0:T(8,128)(2,1)S(1)}, u32[]{:S(2)}, u32[]{:S(2)}) collective-permute-start(bf16[8,6272]{1,0:T(8,128)(2,1)S(1)} %slice.382), channel_id=1, source_target_pairs={{0,4},{1,5},{4,8},{5,9},{8,12},{9,13},{12,14},{13,15},{14,10},{15,... | collective-permute-start | bytes 301064 | tf_op jit(solution)/shard_map/ppermute | solution.py:92
  33.1 0.5 collective-permute-start.7
  33.8 1.6 %collective-permute-start.15 = (bf16[8,12416]{1,0:T(8,128)(2,1)S(1)}, bf16[8,12416]{1,0:T(8,128)(2,1)S(1)}, u32[]{:S(2)}, u32[]{:S(2)}) collective-permute-start(bf16[8,12416]{1,0:T(8,128)(2,1)S(1)} %collective-permute-done.13), channel_id=1, source_target_pairs={{0,4},{1,5},{4,8},{5,9},{8,12},{9,13},{12,14},{13,15},{14,10},{15,... | collective-permute-start | bytes 595976 | tf_op jit(solution)/shard_map/ppermute | solution.py:92
  35.9 1.9 %collective-permute-done.7 = bf16[8,6144]{1,0:T(8,128)(2,1)S(1)} collective-permute-done((bf16[8,6144]{1,0:T(8,128)(2,1)S(1)}, bf16[8,6144]{1,0:T(8,128)(2,1)S(1)}, u32[]{:S(2)}, u32[]{:S(2)}) %collective-permute-start.7) | collective-permute-done | bytes 98336 | tf_op jit(solution)/shard_map/ppermute | solution.py:92
  37.9 3.2 %collective-permute-done.15 = bf16[8,12416]{1,0:T(8,128)(2,1)S(1)} collective-permute-done((bf16[8,12416]{1,0:T(8,128)(2,1)S(1)}, bf16[8,12416]{1,0:T(8,128)(2,1)S(1)}, u32[]{:S(2)}, u32[]{:S(2)}) %collective-permute-start.15) | collective-permute-done | bytes 198688 | tf_op jit(solution)/shard_map/ppermute | solution.py:92
  41.1 1.6 %collective-permute-start.18 = (bf16[8,6272]{1,0:T(8,128)(2,1)S(1)}, bf16[8,6272]{1,0:T(8,128)(2,1)S(1)}, u32[]{:S(2)}, u32[]{:S(2)}) collective-permute-start(bf16[8,6272]{1,0:T(8,128)(2,1)S(1)} %slice.396), channel_id=1, source_target_pairs={{0,4},{1,5},{4,8},{5,9},{8,12},{9,13},{12,14},{13,15},{14,10},{15,... | collective-permute-start | bytes 301064 | tf_op jit(solution)/shard_map/ppermute | solution.py:92
  42.8 0.5 collective-permute-start.19
  44.3 1.5 %copy-done.4 = bf16[6144,336]{0,1:T(8,128)(2,1)S(1)} copy-done((bf16[6144,336]{0,1:T(8,128)(2,1)S(1)}, bf16[6144,336]{0,1:T(8,128)(2,1)}, u32[]{:S(2)}) %copy-start.4) | copy-done | bytes 4128792
  45.9 1.2 %fusion.10 = f32[128,336]{0,1:T(8,128)S(1)} fusion(bf16[6144,336]{0,1:T(8,128)(2,1)S(1)} %copy-done.4, bf16[128,12416]{1,0:T(8,128)(2,1)S(1)} %get-tuple-element.196), kind=kOutput, calls=%fused_computation.24 | convolution fusion | flops 528482304 | bytes 5873664 | tf_op jit(solution)/shard_map/dot_general | solution.py:115
  47.2 1.2 %fusion.12 = f32[128,336]{0,1:T(8,128)S(1)} fusion(bf16[336,6144]{1,0:T(8,128)(2,1)S(1)} %copy-done.2, bf16[128,12416]{1,0:T(8,128)(2,1)S(1)} %get-tuple-element.196, f32[128]{0:T(128)S(1)} %convert_reduce_fusion.1), kind=kOutput, calls=%fused_computation.26 | convolution fusion | flops 528525312 | bytes 5874176 | tf_op jit(solution)/shard_map/dot_general | solution.py:120
  48.5 0.9 copy-done.3
  49.4 1.2 %multiply_convert_fusion.5 = (bf16[128,336]{0,1:T(8,128)(2,1)S(1)}, bf16[128,336]{0,1:T(8,128)(2,1)S(1)}, bf16[128,336]{0,1:T(8,128)(2,1)S(1)}) fusion(f32[128]{0:T(128)S(1)} %convert_reduce_fusion.1, f32[128,336]{0,1:T(8,128)S(1)} %fusion.10, f32[128,336]{0,1:T(8,128)S(1)} %fusion.12, bf16[6144,336]{0,1:T(8,128)(2,1)S(1)} %copy-done.3, ...), kind=kOutput, calls=%fused_computation.125 | convolution fusion | flops 529170432 | bytes 6304256 | tf_op jit(solution)/shard_map/dot_general | solution.py:116
  50.6 1.0 fusion.84
  51.6 1.0 convolution_add_fusion.1
  52.8 1.0 fusion.83
  54.1 0.5 collective-permute-start.10
  54.8 1.3 %collective-permute-done.21 = bf16[24,12288]{1,0:T(8,128)(2,1)S(1)} collective-permute-done((bf16[24,12288]{1,0:T(8,128)(2,1)S(1)}, bf16[24,12288]{1,0:T(8,128)(2,1)S(1)}, u32[]{:S(2)}, u32[]{:S(2)}) %collective-permute-start.21) | collective-permute-done | bytes 589856 | tf_op jit(solution)/shard_map/ppermute | solution.py:92
  56.3 1.6 %collective-permute-start.22 = (bf16[8,6144]{1,0:T(8,128)(2,1)S(1)}, bf16[8,6144]{1,0:T(8,128)(2,1)S(1)}, u32[]{:S(2)}, u32[]{:S(2)}) collective-permute-start(bf16[8,6144]{1,0:T(8,128)(2,1)S(1)} %get-tuple-element.61), channel_id=1, source_target_pairs={{0,4},{1,5},{4,8},{5,9},{8,12},{9,13},{12,14},{13,15},{14,10},{15,... | collective-permute-start | bytes 294920 | tf_op jit(solution)/shard_map/ppermute | solution.py:92
  57.9 0.5 collective-permute-start.23
  59.1 1.2 %fusion.6 = f32[128,336]{0,1:T(8,128)S(1)} fusion(bf16[6144,336]{0,1:T(8,128)(2,1)S(1)} %copy-done.3, bf16[128,12416]{1,0:T(8,128)(2,1)S(1)} %get-tuple-element.173), kind=kOutput, calls=%fused_computation.20 | convolution fusion | flops 528482304 | bytes 5873664 | tf_op jit(solution)/shard_map/dot_general | solution.py:116
  60.4 1.2 %fusion.15 = f32[128,336]{0,1:T(8,128)S(1)} fusion(bf16[336,6144]{1,0:T(8,128)(2,1)S(1)} %copy-done.2, bf16[128,12416]{1,0:T(8,128)(2,1)S(1)} %get-tuple-element.173, f32[128]{0:T(128)S(1)} %convert_reduce_fusion), kind=kOutput, calls=%fused_computation.27 | convolution fusion | flops 528525312 | bytes 5874176 | tf_op jit(solution)/shard_map/dot_general | solution.py:120
  61.6 1.3 %multiply_convert_fusion.2 = (bf16[128,336]{0,1:T(8,128)(2,1)S(1)}, bf16[128,336]{0,1:T(8,128)(2,1)S(1)}, bf16[128,336]{0,1:T(8,128)(2,1)S(1)}) fusion(f32[128,336]{0,1:T(8,128)S(1)} %fusion.15, f32[128,336]{0,1:T(8,128)S(1)} %fusion.6, f32[128]{0:T(128)S(1)} %convert_reduce_fusion, bf16[6144,336]{0,1:T(8,128)(2,1)S(1)} %copy-done.4, ...), kind=kOutput, calls=%fused_computation.120 | convolution fusion | flops 529170432 | bytes 6304256 | tf_op jit(solution)/shard_map/dot_general | solution.py:115
  62.9 1.0 fusion.85
  64.0 1.6 %collective-permute-start.24 = (bf16[8,12288]{1,0:T(8,128)(2,1)S(1)}, bf16[8,12288]{1,0:T(8,128)(2,1)S(1)}, u32[]{:S(2)}, u32[]{:S(2)}) collective-permute-start(bf16[8,12288]{1,0:T(8,128)(2,1)S(1)} %pad_maximum_fusion.5), channel_id=1, source_target_pairs={{0,4},{1,5},{4,8},{5,9},{8,12},{9,13},{12,14},{13,15},{14,10},{15,... | collective-permute-start | bytes 589832 | tf_op jit(solution)/shard_map/ppermute | solution.py:92
  66.1 1.0 fusion.86
  67.2 1.0 convolution_add_fusion
  68.6 0.5 collective-permute-start.31
  69.1 1.4 %collective-permute-done.24 = bf16[8,12288]{1,0:T(8,128)(2,1)S(1)} collective-permute-done((bf16[8,12288]{1,0:T(8,128)(2,1)S(1)}, bf16[8,12288]{1,0:T(8,128)(2,1)S(1)}, u32[]{:S(2)}, u32[]{:S(2)}) %collective-permute-start.24) | collective-permute-done | bytes 196640 | tf_op jit(solution)/shard_map/ppermute | solution.py:92
  70.5 1.3 %collective-permute-done.25 = bf16[8,12288]{1,0:T(8,128)(2,1)S(1)} collective-permute-done((bf16[8,12288]{1,0:T(8,128)(2,1)S(1)}, bf16[8,12288]{1,0:T(8,128)(2,1)S(1)}, u32[]{:S(2)}, u32[]{:S(2)}) %collective-permute-start.25) | collective-permute-done | bytes 196640 | tf_op jit(solution)/shard_map/ppermute | solution.py:92
  72.0 0.5 collective-permute-start.27
  72.5 1.6 %collective-permute-start.26 = (bf16[8,12288]{1,0:T(8,128)(2,1)S(1)}, bf16[8,12288]{1,0:T(8,128)(2,1)S(1)}, u32[]{:S(2)}, u32[]{:S(2)}) collective-permute-start(bf16[8,12288]{1,0:T(8,128)(2,1)S(1)} %pad_maximum_fusion.7), channel_id=1, source_target_pairs={{0,4},{1,5},{4,8},{5,9},{8,12},{9,13},{12,14},{13,15},{14,10},{15,... | collective-permute-start | bytes 589832 | tf_op jit(solution)/shard_map/ppermute | solution.py:92
  74.1 3.6 %collective-permute-done.27 = bf16[8,12288]{1,0:T(8,128)(2,1)S(1)} collective-permute-done((bf16[8,12288]{1,0:T(8,128)(2,1)S(1)}, bf16[8,12288]{1,0:T(8,128)(2,1)S(1)}, u32[]{:S(2)}, u32[]{:S(2)}) %collective-permute-start.27) | collective-permute-done | bytes 196640 | tf_op jit(solution)/shard_map/ppermute | solution.py:92
  78.5 1.6 %collective-permute-start.32 = (bf16[8,6144]{1,0:T(8,128)(2,1)S(1)}, bf16[8,6144]{1,0:T(8,128)(2,1)S(1)}, u32[]{:S(2)}, u32[]{:S(2)}) collective-permute-start(bf16[8,6144]{1,0:T(8,128)(2,1)S(1)} %get-tuple-element.79), channel_id=1, source_target_pairs={{0,4},{1,5},{4,8},{5,9},{8,12},{9,13},{12,14},{13,15},{14,10},{15,... | collective-permute-start | bytes 294920 | tf_op jit(solution)/shard_map/ppermute | solution.py:92
  80.6 3.3 %shard_map.110 = (bf16[336,6144]{1,0:T(8,128)(2,1)}, f32[8,128]{1,0:T(8,128)S(1)}) custom-call(bf16[336,256]{1,0:T(8,128)(2,1)S(1)} %bitcast.36, bf16[256,12416]{1,0:T(8,128)(2,1)S(1)} %get-tuple-element.172.refs_1_), custom_call_target="tpu_custom_call" | custom-call | flops 1056964608 | bytes 7274496 | tf_op jit(solution)/shard_map/pallas_call | solution.py:56
  83.9 1.3 %collective-permute-done.33 = bf16[8,6144]{1,0:T(8,128)(2,1)S(1)} collective-permute-done((bf16[8,6144]{1,0:T(8,128)(2,1)S(1)}, bf16[8,6144]{1,0:T(8,128)(2,1)S(1)}, u32[]{:S(2)}, u32[]{:S(2)}) %collective-permute-start.33) | collective-permute-done | bytes 98336 | tf_op jit(solution)/shard_map/ppermute | solution.py:92
  85.3 1.5 %collective-permute-start.34 = (bf16[8,12288]{1,0:T(8,128)(2,1)S(1)}, bf16[8,12288]{1,0:T(8,128)(2,1)S(1)}, u32[]{:S(2)}, u32[]{:S(2)}) collective-permute-start(bf16[8,12288]{1,0:T(8,128)(2,1)S(1)} %pad_maximum_fusion.11), channel_id=1, source_target_pairs={{0,4},{1,5},{4,8},{5,9},{8,12},{9,13},{12,14},{13,15},{14,10},{15,... | collective-permute-start | bytes 589832 | tf_op jit(solution)/shard_map/ppermute | solution.py:92
  86.7 0.6 collective-permute-start.35
  87.4 3.3 %shard_map.111 = (bf16[336,6144]{1,0:T(8,128)(2,1)}, f32[8,128]{1,0:T(8,128)S(1)}) custom-call(bf16[336,256]{1,0:T(8,128)(2,1)S(1)} %bitcast.35, bf16[256,12416]{1,0:T(8,128)(2,1)S(1)} %get-tuple-element.172.refs_1_, f32[8,128]{1,0:T(8,128)S(1)} %get-tuple-element.86.refs_2_), custom_call_target="tpu_custom_call" | custom-call | flops 1056964608 | bytes 7274496 | tf_op jit(solution)/shard_map/pallas_call | solution.py:56
  90.7 1.4 %collective-permute-done.34 = bf16[8,12288]{1,0:T(8,128)(2,1)S(1)} collective-permute-done((bf16[8,12288]{1,0:T(8,128)(2,1)S(1)}, bf16[8,12288]{1,0:T(8,128)(2,1)S(1)}, u32[]{:S(2)}, u32[]{:S(2)}) %collective-permute-start.34) | collective-permute-done | bytes 196640 | tf_op jit(solution)/shard_map/ppermute | solution.py:92
  92.1 2.4 %collective-permute-done.35 = bf16[8,12288]{1,0:T(8,128)(2,1)S(1)} collective-permute-done((bf16[8,12288]{1,0:T(8,128)(2,1)S(1)}, bf16[8,12288]{1,0:T(8,128)(2,1)S(1)}, u32[]{:S(2)}, u32[]{:S(2)}) %collective-permute-start.35) | collective-permute-done | bytes 196640 | tf_op jit(solution)/shard_map/ppermute | solution.py:92
  94.9 0.7 collective-permute-start.37
  95.6 1.4 %collective-permute-start.36 = (bf16[8,12288]{1,0:T(8,128)(2,1)S(1)}, bf16[8,12288]{1,0:T(8,128)(2,1)S(1)}, u32[]{:S(2)}, u32[]{:S(2)}) collective-permute-start(bf16[8,12288]{1,0:T(8,128)(2,1)S(1)} %pad_maximum_fusion.13), channel_id=1, source_target_pairs={{0,4},{1,5},{4,8},{5,9},{8,12},{9,13},{12,14},{13,15},{14,10},{15,... | collective-permute-start | bytes 589832 | tf_op jit(solution)/shard_map/ppermute | solution.py:92
  97.0 0.7 collective-permute-start.29
  97.7 1.4 %collective-permute-start.28 = (bf16[8,12288]{1,0:T(8,128)(2,1)S(1)}, bf16[8,12288]{1,0:T(8,128)(2,1)S(1)}, u32[]{:S(2)}, u32[]{:S(2)}) collective-permute-start(bf16[8,12288]{1,0:T(8,128)(2,1)S(1)} %pad_maximum_fusion.9), channel_id=1, source_target_pairs={{0,4},{1,5},{4,8},{5,9},{8,12},{9,13},{12,14},{13,15},{14,10},{15,... | collective-permute-start | bytes 589832 | tf_op jit(solution)/shard_map/ppermute | solution.py:92
  99.1 1.6 %collective-permute-done.37 = bf16[8,12288]{1,0:T(8,128)(2,1)S(1)} collective-permute-done((bf16[8,12288]{1,0:T(8,128)(2,1)S(1)}, bf16[8,12288]{1,0:T(8,128)(2,1)S(1)}, u32[]{:S(2)}, u32[]{:S(2)}) %collective-permute-start.37) | collective-permute-done | bytes 196640 | tf_op jit(solution)/shard_map/ppermute | solution.py:92
  100.7 0.5 collective-permute-done.36
  101.4 0.8 collective-permute-start.39
  102.3 1.3 %collective-permute-start.38 = (bf16[8,12288]{1,0:T(8,128)(2,1)S(1)}, bf16[8,12288]{1,0:T(8,128)(2,1)S(1)}, u32[]{:S(2)}, u32[]{:S(2)}) collective-permute-start(bf16[8,12288]{1,0:T(8,128)(2,1)S(1)} %pad_maximum_fusion.15), channel_id=1, source_target_pairs={{0,4},{1,5},{4,8},{5,9},{8,12},{9,13},{12,14},{13,15},{14,10},{15,... | collective-permute-start | bytes 589832 | tf_op jit(solution)/shard_map/ppermute | solution.py:92
  103.6 3.9 %shard_map.112 = (bf16[336,6144]{1,0:T(8,128)(2,1)}, f32[8,128]{1,0:T(8,128)}) custom-call(bf16[336,256]{1,0:T(8,128)(2,1)S(1)} %bitcast.34, bf16[256,12416]{1,0:T(8,128)(2,1)S(1)} %get-tuple-element.172.refs_1_, f32[8,128]{1,0:T(8,128)S(1)} %get-tuple-element.101.refs_2_), custom_call_target="tpu_custom_call" | custom-call | flops 1056964608 | bytes 7274496 | tf_op jit(solution)/shard_map/pallas_call | solution.py:56
  108.0 1.8 %convolution_convert_fusion.1 = bf16[128,6144]{1,0:T(8,128)(2,1)} fusion(bf16[8,6144]{1,0:T(8,128)(2,1)S(1)} %get-tuple-element.157, bf16[8,6144]{1,0:T(8,128)(2,1)S(1)} %get-tuple-element.155, s32[128]{0:T(128)S(1)} %add_reduce_fusion, pred[128]{0:T(512)(128)(4,1)S(1)} %reduce_or.9), kind=kOutput, calls=%fused_computation.3 | convolution fusion | flops 26349568 | bytes 1770112 | tf_op jit(solution)/shard_map/dot_general | solution.py:257
  109.8 1.8 %convolution_convert_fusion = bf16[128,6144]{1,0:T(8,128)(2,1)} fusion(bf16[8,6144]{1,0:T(8,128)(2,1)S(1)} %get-tuple-element.156, bf16[8,6144]{1,0:T(8,128)(2,1)S(1)} %get-tuple-element.154, s32[128]{0:T(128)S(1)} %add_reduce_fusion, pred[128]{0:T(512)(128)(4,1)S(1)} %reduce_or.9), kind=kOutput, calls=%fused_computation.2 | convolution fusion | flops 26349568 | bytes 1770112 | tf_op jit(solution)/shard_map/dot_general | solution.py:257
  (131 shorter events, 9.2 us)
Async XLA Ops:
  0.6 1.4 %copy-start = (bf16[128,6144]{1,0:T(8,128)(2,1)S(1)}, bf16[128,6144]{1,0:T(8,128)(2,1)}, u32[]{:S(2)}) copy-start(bf16[128,6144]{1,0:T(8,128)(2,1)} %param.8) | copy-start | bytes 4718596
  4.4 8.0 %collective-permute-start = (bf16[8,12416]{1,0:T(8,128)(2,1)S(1)}, bf16[8,12416]{1,0:T(8,128)(2,1)S(1)}, u32[]{:S(2)}, u32[]{:S(2)}) collective-permute-start(bf16[8,12416]{1,0:T(8,128)(2,1)S(1)} %get-tuple-element.153), channel_id=1, source_target_pairs={{0,4},{1,5},{4,8},{5,9},{8,12},{9,13},{12,14},{13,15},{14,10},{15,... | collective-permute-start | bytes 595976 | tf_op jit(solution)/shard_map/ppermute | solution.py:92
  7.5 6.4 %collective-permute-start.1 = (bf16[8,12416]{1,0:T(8,128)(2,1)S(1)}, bf16[8,12416]{1,0:T(8,128)(2,1)S(1)}, u32[]{:S(2)}, u32[]{:S(2)}) collective-permute-start(bf16[8,12416]{1,0:T(8,128)(2,1)S(1)} %get-tuple-element.153), channel_id=1, source_target_pairs={{4,0},{5,1},{8,4},{9,5},{12,8},{13,9},{14,12},{15,13},{10,14},{11,... | collective-permute-start | bytes 595976 | tf_op jit(solution)/shard_map/ppermute | solution.py:92
  13.9 11.8 %collective-permute-start.11 = (bf16[8,12416]{1,0:T(8,128)(2,1)S(1)}, bf16[8,12416]{1,0:T(8,128)(2,1)S(1)}, u32[]{:S(2)}, u32[]{:S(2)}) collective-permute-start(bf16[8,12416]{1,0:T(8,128)(2,1)S(1)} %get-tuple-element.56), channel_id=1, source_target_pairs={{0,4},{1,5},{4,8},{5,9},{8,12},{9,13},{12,14},{13,15},{14,10},{15,... | collective-permute-start | bytes 595976 | tf_op jit(solution)/shard_map/ppermute | solution.py:92
  15.5 11.8 %collective-permute-start.12 = (bf16[8,12416]{1,0:T(8,128)(2,1)S(1)}, bf16[8,12416]{1,0:T(8,128)(2,1)S(1)}, u32[]{:S(2)}, u32[]{:S(2)}) collective-permute-start(bf16[8,12416]{1,0:T(8,128)(2,1)S(1)} %get-tuple-element.56), channel_id=1, source_target_pairs={{4,0},{5,1},{8,4},{9,5},{12,8},{13,9},{14,12},{15,13},{10,14},{11,... | collective-permute-start | bytes 595976 | tf_op jit(solution)/shard_map/ppermute | solution.py:92
  15.9 7.7 %collective-permute-start.2 = (bf16[8,12416]{1,0:T(8,128)(2,1)S(1)}, bf16[8,12416]{1,0:T(8,128)(2,1)S(1)}, u32[]{:S(2)}, u32[]{:S(2)}) collective-permute-start(bf16[8,12416]{1,0:T(8,128)(2,1)S(1)} %collective-permute-done), channel_id=1, source_target_pairs={{0,4},{1,5},{4,8},{5,9},{8,12},{9,13},{12,14},{13,15},{14,10},{15,... | collective-permute-start | bytes 595976 | tf_op jit(solution)/shard_map/ppermute | solution.py:92
  17.5 7.7 %collective-permute-start.3 = (bf16[8,12416]{1,0:T(8,128)(2,1)S(1)}, bf16[8,12416]{1,0:T(8,128)(2,1)S(1)}, u32[]{:S(2)}, u32[]{:S(2)}) collective-permute-start(bf16[8,12416]{1,0:T(8,128)(2,1)S(1)} %collective-permute-done.1), channel_id=1, source_target_pairs={{4,0},{5,1},{8,4},{9,5},{12,8},{13,9},{14,12},{15,13},{10,14},{11,... | collective-permute-start | bytes 595976 | tf_op jit(solution)/shard_map/ppermute | solution.py:92
  23.7 7.8 %collective-permute-start.4 = (bf16[8,12416]{1,0:T(8,128)(2,1)S(1)}, bf16[8,12416]{1,0:T(8,128)(2,1)S(1)}, u32[]{:S(2)}, u32[]{:S(2)}) collective-permute-start(bf16[8,12416]{1,0:T(8,128)(2,1)S(1)} %collective-permute-done.2), channel_id=1, source_target_pairs={{0,4},{1,5},{4,8},{5,9},{8,12},{9,13},{12,14},{13,15},{14,10},{15,... | collective-permute-start | bytes 595976 | tf_op jit(solution)/shard_map/ppermute | solution.py:92
  25.3 7.8 %collective-permute-start.5 = (bf16[8,12416]{1,0:T(8,128)(2,1)S(1)}, bf16[8,12416]{1,0:T(8,128)(2,1)S(1)}, u32[]{:S(2)}, u32[]{:S(2)}) collective-permute-start(bf16[8,12416]{1,0:T(8,128)(2,1)S(1)} %collective-permute-done.3), channel_id=1, source_target_pairs={{4,0},{5,1},{8,4},{9,5},{12,8},{13,9},{14,12},{15,13},{10,14},{11,... | collective-permute-start | bytes 595976 | tf_op jit(solution)/shard_map/ppermute | solution.py:92
  25.7 8.1 %collective-permute-start.13 = (bf16[8,12416]{1,0:T(8,128)(2,1)S(1)}, bf16[8,12416]{1,0:T(8,128)(2,1)S(1)}, u32[]{:S(2)}, u32[]{:S(2)}) collective-permute-start(bf16[8,12416]{1,0:T(8,128)(2,1)S(1)} %collective-permute-done.11), channel_id=1, source_target_pairs={{0,4},{1,5},{4,8},{5,9},{8,12},{9,13},{12,14},{13,15},{14,10},{15,... | collective-permute-start | bytes 595976 | tf_op jit(solution)/shard_map/ppermute | solution.py:92
  27.3 8.1 %collective-permute-start.14 = (bf16[8,12416]{1,0:T(8,128)(2,1)S(1)}, bf16[8,12416]{1,0:T(8,128)(2,1)S(1)}, u32[]{:S(2)}, u32[]{:S(2)}) collective-permute-start(bf16[8,12416]{1,0:T(8,128)(2,1)S(1)} %collective-permute-done.12), channel_id=1, source_target_pairs={{4,0},{5,1},{8,4},{9,5},{12,8},{13,9},{14,12},{15,13},{10,14},{11,... | collective-permute-start | bytes 595976 | tf_op jit(solution)/shard_map/ppermute | solution.py:92
  31.5 6.3 %collective-permute-start.6 = (bf16[8,6272]{1,0:T(8,128)(2,1)S(1)}, bf16[8,6272]{1,0:T(8,128)(2,1)S(1)}, u32[]{:S(2)}, u32[]{:S(2)}) collective-permute-start(bf16[8,6272]{1,0:T(8,128)(2,1)S(1)} %slice.382), channel_id=1, source_target_pairs={{0,4},{1,5},{4,8},{5,9},{8,12},{9,13},{12,14},{13,15},{14,10},{15,... | collective-permute-start | bytes 301064 | tf_op jit(solution)/shard_map/ppermute | solution.py:92
  33.1 4.7 %collective-permute-start.7 = (bf16[8,6144]{1,0:T(8,128)(2,1)S(1)}, bf16[8,6144]{1,0:T(8,128)(2,1)S(1)}, u32[]{:S(2)}, u32[]{:S(2)}) collective-permute-start(bf16[8,6144]{1,0:T(8,128)(2,1)S(1)} %slice.383), channel_id=1, source_target_pairs={{4,0},{5,1},{8,4},{9,5},{12,8},{13,9},{14,12},{15,13},{10,14},{11,... | collective-permute-start | bytes 294920 | tf_op jit(solution)/shard_map/ppermute | solution.py:92
  33.7 9.6 %collective-permute-start.8 = (bf16[56,12416]{1,0:T(8,128)(2,1)S(1)}, bf16[56,12416]{1,0:T(8,128)(2,1)S(1)}, u32[]{:S(2)}, u32[]{:S(2)}) collective-permute-start(bf16[56,12416]{1,0:T(8,128)(2,1)S(1)} %get-tuple-element.199), channel_id=1, source_target_pairs={{0,1},{1,0},{2,3},{3,2},{4,5},{5,4},{6,7},{7,6},{8,9},{9,8},{10,11... | collective-permute-start | bytes 4171784 | tf_op jit(solution)/shard_map/ppermute | solution.py:92
  33.8 7.3 %collective-permute-start.15 = (bf16[8,12416]{1,0:T(8,128)(2,1)S(1)}, bf16[8,12416]{1,0:T(8,128)(2,1)S(1)}, u32[]{:S(2)}, u32[]{:S(2)}) collective-permute-start(bf16[8,12416]{1,0:T(8,128)(2,1)S(1)} %collective-permute-done.13), channel_id=1, source_target_pairs={{0,4},{1,5},{4,8},{5,9},{8,12},{9,13},{12,14},{13,15},{14,10},{15,... | collective-permute-start | bytes 595976 | tf_op jit(solution)/shard_map/ppermute | solution.py:92
  35.4 7.4 %collective-permute-start.16 = (bf16[8,12416]{1,0:T(8,128)(2,1)S(1)}, bf16[8,12416]{1,0:T(8,128)(2,1)S(1)}, u32[]{:S(2)}, u32[]{:S(2)}) collective-permute-start(bf16[8,12416]{1,0:T(8,128)(2,1)S(1)} %collective-permute-done.14), channel_id=1, source_target_pairs={{4,0},{5,1},{8,4},{9,5},{12,8},{13,9},{14,12},{15,13},{10,14},{11,... | collective-permute-start | bytes 595976 | tf_op jit(solution)/shard_map/ppermute | solution.py:92
  37.8 5.9 %collective-permute-start.9 = (bf16[8,12416]{1,0:T(8,128)(2,1)S(1)}, bf16[8,12416]{1,0:T(8,128)(2,1)S(1)}, u32[]{:S(2)}, u32[]{:S(2)}) collective-permute-start(bf16[8,12416]{1,0:T(8,128)(2,1)S(1)} %pad_maximum_fusion.3), channel_id=1, source_target_pairs={{0,1},{1,0},{2,3},{3,2},{4,5},{5,4},{6,7},{7,6},{8,9},{9,8},{10,11... | collective-permute-start | bytes 595976 | tf_op jit(solution)/shard_map/ppermute | solution.py:92
  41.1 13.4 %collective-permute-start.18 = (bf16[8,6272]{1,0:T(8,128)(2,1)S(1)}, bf16[8,6272]{1,0:T(8,128)(2,1)S(1)}, u32[]{:S(2)}, u32[]{:S(2)}) collective-permute-start(bf16[8,6272]{1,0:T(8,128)(2,1)S(1)} %slice.396), channel_id=1, source_target_pairs={{0,4},{1,5},{4,8},{5,9},{8,12},{9,13},{12,14},{13,15},{14,10},{15,... | collective-permute-start | bytes 301064 | tf_op jit(solution)/shard_map/ppermute | solution.py:92
  42.8 11.8 %collective-permute-start.19 = (bf16[8,6144]{1,0:T(8,128)(2,1)S(1)}, bf16[8,6144]{1,0:T(8,128)(2,1)S(1)}, u32[]{:S(2)}, u32[]{:S(2)}) collective-permute-start(bf16[8,6144]{1,0:T(8,128)(2,1)S(1)} %slice.397), channel_id=1, source_target_pairs={{4,0},{5,1},{8,4},{9,5},{12,8},{13,9},{14,12},{15,13},{10,14},{11,... | collective-permute-start | bytes 294920 | tf_op jit(solution)/shard_map/ppermute | solution.py:92
  43.7 2.2 %copy-start.4 = (bf16[6144,336]{0,1:T(8,128)(2,1)S(1)}, bf16[6144,336]{0,1:T(8,128)(2,1)}, u32[]{:S(2)}) copy-start(bf16[6144,336]{0,1:T(8,128)(2,1)} %param.11) | copy-start | bytes 12386308
  44.1 3.2 %copy-start.2 = (bf16[336,6144]{1,0:T(8,128)(2,1)S(1)}, bf16[336,6144]{1,0:T(8,128)(2,1)}, u32[]{:S(2)}) copy-start(bf16[336,6144]{1,0:T(8,128)(2,1)} %param.13) | copy-start | bytes 12386308
  44.1 10.5 %collective-permute-start.17 = (bf16[56,12416]{1,0:T(8,128)(2,1)S(1)}, bf16[56,12416]{1,0:T(8,128)(2,1)S(1)}, u32[]{:S(2)}, u32[]{:S(2)}) collective-permute-start(bf16[56,12416]{1,0:T(8,128)(2,1)S(1)} %get-tuple-element.176), channel_id=1, source_target_pairs={{0,1},{1,0},{2,3},{3,2},{4,5},{5,4},{6,7},{7,6},{8,9},{9,8},{10,11... | collective-permute-start | bytes 4171784 | tf_op jit(solution)/shard_map/ppermute | solution.py:92
  47.2 2.2 %copy-start.3 = (bf16[6144,336]{0,1:T(8,128)(2,1)S(1)}, bf16[6144,336]{0,1:T(8,128)(2,1)}, u32[]{:S(2)}) copy-start(bf16[6144,336]{0,1:T(8,128)(2,1)} %param.12) | copy-start | bytes 12386308
  54.0 2.1 %collective-permute-start.21 = (bf16[24,12288]{1,0:T(8,128)(2,1)S(1)}, bf16[24,12288]{1,0:T(8,128)(2,1)S(1)}, u32[]{:S(2)}, u32[]{:S(2)}) collective-permute-start(bf16[24,12288]{1,0:T(8,128)(2,1)S(1)} %pad_maximum_fusion.1), channel_id=1, source_target_pairs={{0,1},{1,0},{2,3},{3,2},{4,5},{5,4},{6,7},{7,6},{8,9},{9,8},{10,11... | collective-permute-start | bytes 1769480 | tf_op jit(solution)/shard_map/ppermute | solution.py:92
  54.1 4.7 %collective-permute-start.10 = (bf16[40,12288]{1,0:T(8,128)(2,1)S(1)}, bf16[40,12288]{1,0:T(8,128)(2,1)S(1)}, u32[]{:S(2)}, u32[]{:S(2)}) collective-permute-start(bf16[40,12288]{1,0:T(8,128)(2,1)S(1)} %fusion.20), channel_id=1, source_target_pairs={{0,1},{1,0},{2,3},{3,2},{4,5},{5,4},{6,7},{7,6},{8,9},{9,8},{10,11... | collective-permute-start | bytes 2949128 | tf_op jit(solution)/shard_map/ppermute | solution.py:92
  54.6 4.4 %collective-permute-start.20 = (bf16[8,12416]{1,0:T(8,128)(2,1)S(1)}, bf16[8,12416]{1,0:T(8,128)(2,1)S(1)}, u32[]{:S(2)}, u32[]{:S(2)}) collective-permute-start(bf16[8,12416]{1,0:T(8,128)(2,1)S(1)} %pad_maximum_fusion.4), channel_id=1, source_target_pairs={{0,1},{1,0},{2,3},{3,2},{4,5},{5,4},{6,7},{7,6},{8,9},{9,8},{10,11... | collective-permute-start | bytes 595976 | tf_op jit(solution)/shard_map/ppermute | solution.py:92
  56.3 7.6 %collective-permute-start.22 = (bf16[8,6144]{1,0:T(8,128)(2,1)S(1)}, bf16[8,6144]{1,0:T(8,128)(2,1)S(1)}, u32[]{:S(2)}, u32[]{:S(2)}) collective-permute-start(bf16[8,6144]{1,0:T(8,128)(2,1)S(1)} %get-tuple-element.61), channel_id=1, source_target_pairs={{0,4},{1,5},{4,8},{5,9},{8,12},{9,13},{12,14},{13,15},{14,10},{15,... | collective-permute-start | bytes 294920 | tf_op jit(solution)/shard_map/ppermute | solution.py:92
  57.9 6.0 %collective-permute-start.23 = (bf16[8,6144]{1,0:T(8,128)(2,1)S(1)}, bf16[8,6144]{1,0:T(8,128)(2,1)S(1)}, u32[]{:S(2)}, u32[]{:S(2)}) collective-permute-start(bf16[8,6144]{1,0:T(8,128)(2,1)S(1)} %get-tuple-element.62), channel_id=1, source_target_pairs={{4,0},{5,1},{8,4},{9,5},{12,8},{13,9},{14,12},{15,13},{10,14},{11,... | collective-permute-start | bytes 294920 | tf_op jit(solution)/shard_map/ppermute | solution.py:92
  64.0 6.4 %collective-permute-start.24 = (bf16[8,12288]{1,0:T(8,128)(2,1)S(1)}, bf16[8,12288]{1,0:T(8,128)(2,1)S(1)}, u32[]{:S(2)}, u32[]{:S(2)}) collective-permute-start(bf16[8,12288]{1,0:T(8,128)(2,1)S(1)} %pad_maximum_fusion.5), channel_id=1, source_target_pairs={{0,4},{1,5},{4,8},{5,9},{8,12},{9,13},{12,14},{13,15},{14,10},{15,... | collective-permute-start | bytes 589832 | tf_op jit(solution)/shard_map/ppermute | solution.py:92
  65.7 6.1 %collective-permute-start.25 = (bf16[8,12288]{1,0:T(8,128)(2,1)S(1)}, bf16[8,12288]{1,0:T(8,128)(2,1)S(1)}, u32[]{:S(2)}, u32[]{:S(2)}) collective-permute-start(bf16[8,12288]{1,0:T(8,128)(2,1)S(1)} %pad_maximum_fusion.6), channel_id=1, source_target_pairs={{4,0},{5,1},{8,4},{9,5},{12,8},{13,9},{14,12},{15,13},{10,14},{11,... | collective-permute-start | bytes 589832 | tf_op jit(solution)/shard_map/ppermute | solution.py:92
  68.5 26.0 %collective-permute-start.30 = (bf16[40,12288]{1,0:T(8,128)(2,1)S(1)}, bf16[40,12288]{1,0:T(8,128)(2,1)S(1)}, u32[]{:S(2)}, u32[]{:S(2)}) collective-permute-start(bf16[40,12288]{1,0:T(8,128)(2,1)S(1)} %fusion.19), channel_id=1, source_target_pairs={{0,1},{1,0},{2,3},{3,2},{4,5},{5,4},{6,7},{7,6},{8,9},{9,8},{10,11... | collective-permute-start | bytes 2949128 | tf_op jit(solution)/shard_map/ppermute | solution.py:92
  68.6 9.7 %collective-permute-start.31 = (bf16[24,12288]{1,0:T(8,128)(2,1)S(1)}, bf16[24,12288]{1,0:T(8,128)(2,1)S(1)}, u32[]{:S(2)}, u32[]{:S(2)}) collective-permute-start(bf16[24,12288]{1,0:T(8,128)(2,1)S(1)} %pad_maximum_fusion), channel_id=1, source_target_pairs={{0,1},{1,0},{2,3},{3,2},{4,5},{5,4},{6,7},{7,6},{8,9},{9,8},{10,11... | collective-permute-start | bytes 1769480 | tf_op jit(solution)/shard_map/ppermute | solution.py:92
  72.0 5.7 %collective-permute-start.27 = (bf16[8,12288]{1,0:T(8,128)(2,1)S(1)}, bf16[8,12288]{1,0:T(8,128)(2,1)S(1)}, u32[]{:S(2)}, u32[]{:S(2)}) collective-permute-start(bf16[8,12288]{1,0:T(8,128)(2,1)S(1)} %pad_maximum_fusion.8), channel_id=1, source_target_pairs={{4,0},{5,1},{8,4},{9,5},{12,8},{13,9},{14,12},{15,13},{10,14},{11,... | collective-permute-start | bytes 589832 | tf_op jit(solution)/shard_map/ppermute | solution.py:92
  72.5 5.7 %collective-permute-start.26 = (bf16[8,12288]{1,0:T(8,128)(2,1)S(1)}, bf16[8,12288]{1,0:T(8,128)(2,1)S(1)}, u32[]{:S(2)}, u32[]{:S(2)}) collective-permute-start(bf16[8,12288]{1,0:T(8,128)(2,1)S(1)} %pad_maximum_fusion.7), channel_id=1, source_target_pairs={{0,4},{1,5},{4,8},{5,9},{8,12},{9,13},{12,14},{13,15},{14,10},{15,... | collective-permute-start | bytes 589832 | tf_op jit(solution)/shard_map/ppermute | solution.py:92
  78.5 5.4 %collective-permute-start.32 = (bf16[8,6144]{1,0:T(8,128)(2,1)S(1)}, bf16[8,6144]{1,0:T(8,128)(2,1)S(1)}, u32[]{:S(2)}, u32[]{:S(2)}) collective-permute-start(bf16[8,6144]{1,0:T(8,128)(2,1)S(1)} %get-tuple-element.79), channel_id=1, source_target_pairs={{0,4},{1,5},{4,8},{5,9},{8,12},{9,13},{12,14},{13,15},{14,10},{15,... | collective-permute-start | bytes 294920 | tf_op jit(solution)/shard_map/ppermute | solution.py:92
  80.1 5.0 %collective-permute-start.33 = (bf16[8,6144]{1,0:T(8,128)(2,1)S(1)}, bf16[8,6144]{1,0:T(8,128)(2,1)S(1)}, u32[]{:S(2)}, u32[]{:S(2)}) collective-permute-start(bf16[8,6144]{1,0:T(8,128)(2,1)S(1)} %get-tuple-element.80), channel_id=1, source_target_pairs={{4,0},{5,1},{8,4},{9,5},{12,8},{13,9},{14,12},{15,13},{10,14},{11,... | collective-permute-start | bytes 294920 | tf_op jit(solution)/shard_map/ppermute | solution.py:92
  85.3 6.8 %collective-permute-start.34 = (bf16[8,12288]{1,0:T(8,128)(2,1)S(1)}, bf16[8,12288]{1,0:T(8,128)(2,1)S(1)}, u32[]{:S(2)}, u32[]{:S(2)}) collective-permute-start(bf16[8,12288]{1,0:T(8,128)(2,1)S(1)} %pad_maximum_fusion.11), channel_id=1, source_target_pairs={{0,4},{1,5},{4,8},{5,9},{8,12},{9,13},{12,14},{13,15},{14,10},{15,... | collective-permute-start | bytes 589832 | tf_op jit(solution)/shard_map/ppermute | solution.py:92
  86.7 7.7 %collective-permute-start.35 = (bf16[8,12288]{1,0:T(8,128)(2,1)S(1)}, bf16[8,12288]{1,0:T(8,128)(2,1)S(1)}, u32[]{:S(2)}, u32[]{:S(2)}) collective-permute-start(bf16[8,12288]{1,0:T(8,128)(2,1)S(1)} %pad_maximum_fusion.12), channel_id=1, source_target_pairs={{4,0},{5,1},{8,4},{9,5},{12,8},{13,9},{14,12},{15,13},{10,14},{11,... | collective-permute-start | bytes 589832 | tf_op jit(solution)/shard_map/ppermute | solution.py:92
  94.9 5.8 %collective-permute-start.37 = (bf16[8,12288]{1,0:T(8,128)(2,1)S(1)}, bf16[8,12288]{1,0:T(8,128)(2,1)S(1)}, u32[]{:S(2)}, u32[]{:S(2)}) collective-permute-start(bf16[8,12288]{1,0:T(8,128)(2,1)S(1)} %pad_maximum_fusion.14), channel_id=1, source_target_pairs={{4,0},{5,1},{8,4},{9,5},{12,8},{13,9},{14,12},{15,13},{10,14},{11,... | collective-permute-start | bytes 589832 | tf_op jit(solution)/shard_map/ppermute | solution.py:92
  95.6 5.7 %collective-permute-start.36 = (bf16[8,12288]{1,0:T(8,128)(2,1)S(1)}, bf16[8,12288]{1,0:T(8,128)(2,1)S(1)}, u32[]{:S(2)}, u32[]{:S(2)}) collective-permute-start(bf16[8,12288]{1,0:T(8,128)(2,1)S(1)} %pad_maximum_fusion.13), channel_id=1, source_target_pairs={{0,4},{1,5},{4,8},{5,9},{8,12},{9,13},{12,14},{13,15},{14,10},{15,... | collective-permute-start | bytes 589832 | tf_op jit(solution)/shard_map/ppermute | solution.py:92
  97.0 6.5 %collective-permute-start.29 = (bf16[8,12288]{1,0:T(8,128)(2,1)S(1)}, bf16[8,12288]{1,0:T(8,128)(2,1)S(1)}, u32[]{:S(2)}, u32[]{:S(2)}) collective-permute-start(bf16[8,12288]{1,0:T(8,128)(2,1)S(1)} %pad_maximum_fusion.10), channel_id=1, source_target_pairs={{4,0},{5,1},{8,4},{9,5},{12,8},{13,9},{14,12},{15,13},{10,14},{11,... | collective-permute-start | bytes 589832 | tf_op jit(solution)/shard_map/ppermute | solution.py:92
  97.7 5.8 %collective-permute-start.28 = (bf16[8,12288]{1,0:T(8,128)(2,1)S(1)}, bf16[8,12288]{1,0:T(8,128)(2,1)S(1)}, u32[]{:S(2)}, u32[]{:S(2)}) collective-permute-start(bf16[8,12288]{1,0:T(8,128)(2,1)S(1)} %pad_maximum_fusion.9), channel_id=1, source_target_pairs={{0,4},{1,5},{4,8},{5,9},{8,12},{9,13},{12,14},{13,15},{14,10},{15,... | collective-permute-start | bytes 589832 | tf_op jit(solution)/shard_map/ppermute | solution.py:92
  101.4 6.1 %collective-permute-start.39 = (bf16[8,12288]{1,0:T(8,128)(2,1)S(1)}, bf16[8,12288]{1,0:T(8,128)(2,1)S(1)}, u32[]{:S(2)}, u32[]{:S(2)}) collective-permute-start(bf16[8,12288]{1,0:T(8,128)(2,1)S(1)} %pad_maximum_fusion.16), channel_id=1, source_target_pairs={{4,0},{5,1},{8,4},{9,5},{12,8},{13,9},{14,12},{15,13},{10,14},{11,... | collective-permute-start | bytes 589832 | tf_op jit(solution)/shard_map/ppermute | solution.py:92
  102.3 5.7 %collective-permute-start.38 = (bf16[8,12288]{1,0:T(8,128)(2,1)S(1)}, bf16[8,12288]{1,0:T(8,128)(2,1)S(1)}, u32[]{:S(2)}, u32[]{:S(2)}) collective-permute-start(bf16[8,12288]{1,0:T(8,128)(2,1)S(1)} %pad_maximum_fusion.15), channel_id=1, source_target_pairs={{0,4},{1,5},{4,8},{5,9},{8,12},{9,13},{12,14},{13,15},{14,10},{15,... | collective-permute-start | bytes 589832 | tf_op jit(solution)/shard_map/ppermute | solution.py:92
  103.6 7.9 %copy-start.1 = (bf16[128,6144]{1,0:T(8,128)(2,1)S(1)}, bf16[128,6144]{1,0:T(8,128)(2,1)}, u32[]{:S(2)}) copy-start(bf16[128,6144]{1,0:T(8,128)(2,1)} %param.8) | copy-start | bytes 4718596

commit v9 on v6

--- a/solution.py
+++ b/solution.py
@@ -108,9 +108,9 @@
         far_x = far_block(held_xr, held_xl)
         early_x = permute(jnp.concatenate(got_x, axis=0), core_pairs)
         late_x = permute(far_x, core_pairs)
+        chip_d, late_x = lax.optimization_barrier((jnp.concatenate(got_d, axis=0), late_x))
         rows_x = jnp.concatenate(got_x + [far_x, early_x, late_x], axis=0)
-        chip_d = jnp.concatenate(got_d, axis=0)
-        return rows_x, jnp.concatenate([chip_d, permute(chip_d, core_pairs)], axis=0)
+        return rows_x, jnp.concatenate(got_d + [permute(chip_d, core_pairs)], axis=0)
 
     cut = max(2 * steps - 3, 1) * CAP
 
@@ -189,28 +189,29 @@
             dup, w_up.T, preferred_element_type=jnp.float32
         )
         dx_sent = dx_rows[half:].astype(jnp.bfloat16)
-        dx_sent, out_carry = tie(dx_sent, out_carry)
+        hidden, dx_sent = lax.optimization_barrier((hidden, dx_sent))
+        grad_down, mark = weight_grad(hidden, rows_dy, d, [])
+        mark, out_carry = tie(mark, out_carry)
         dx_total = pair_sum(dx_rows[:half], dx_sent)
         dx_carry = {}
 
-        grads, marks = [], []
-        work = [(dgate, rows_wide), (dup, rows_wide), (hidden, rows_dy)]
+        grads, marks = [], [mark]
+        work = [dgate, dup]
         for at in range(2, steps + 2):
             if at <= steps:
                 out_carry.update(send(wave(out_total, out_carry, at, "l")))
             dx_blocks = wave(dx_total, dx_carry, at - 1, "r")
-            if work and at in (2, 3, steps + 1):
-                side, rows = work.pop(0)
-                side, dx_blocks = tie(side, dx_blocks)
-                grad, mark = weight_grad(side, rows, d, marks)
+            if work:
+                side, dx_blocks = tie(work.pop(0), dx_blocks)
+                grad, mark = weight_grad(side, rows_wide, d, marks)
                 grads.append(grad)
                 if work and at <= steps:
                     mark, out_carry = tie(mark, out_carry)
                 marks = [mark]
             dx_carry.update(send(dx_blocks))
-        for side, rows in work:
-            grads.append(weight_grad(side, rows, d, marks)[0])
-        grad_gate, grad_up, grad_down = grads
+        for side in work:
+            grads.append(weight_grad(side, rows_wide, d, marks)[0])
+        grad_gate, grad_up = grads
         mixed, grad_tokens = (
             jnp.dot(select.T, final(total[0], carry), preferred_element_type=jnp.float32).astype(
                 jnp.bfloat16

time: 96.5 us -> 98.5 us (1.021)
  waiting for transfers between devices: 29.6 us -> 32.2 us
    ppermute x37, waiting for transfers between devices: 29.6 us -> 32.2 us  [permute(): return lax.ppermute(x, 'et', pairs)]
  transfers between devices with their start and end apart: 37 -> 37, of which waited for: 21 -> 17; matrix products, arithmetic and copies ran while one was open for 16% -> 16% of each run, Pallas kernels for 11% -> 11%
where the time goes in v9:
time: 98.5 us; the launch traced here: 98.3 us
  starting transfers between devices  33.5 us (34%)
  waiting for transfers between devices  32.2 us (33%)
  matrix products  15 us (15%)
  Pallas kernels  10.4 us (11%)
  local copies, waits for them, and re-layouts  3.53 us (4%)
  other arithmetic  2.39 us (2%)
  between operations  1.11 us (1%)
    ppermute x37, starting transfers between devices, permute(): return lax.ppermute(x, 'et', pairs)  33.5 us
    ppermute x37, waiting for transfers between devices, permute(): return lax.ppermute(x, 'et', pairs)  32.2 us
    pallas_call x3, Pallas kernels, weight_grad(): pl.pallas_call(lambda *refs: grad_kernel(parts, width, len(marks), *refs)...  10.4 us
    dot_general x2, matrix products, per_device(): jnp.dot(select.T, final(total[0], carry), preferred_element_type=jnp.floa...  3.53 us
    unnamed x26, local copies, waits for them, and re-layouts  2.48 us
    dot_general x3, matrix products, per_device(): jnp.dot(select, a, preferred_element_type=jnp.float32).astype(jnp.bfloat16)  2.15 us
  transfers between devices with their start and end apart: 37, of which 17 were waited for; matrix products, arithmetic and copies ran while one was open for 16% of the time, Pallas kernels for 11%

profile of v9, /device:TPU:0, one launch (start us, length us, event | category | flops | bytes accessed | tf_op | source)
XLA Modules:
  0.0 98.3 jit_solution(13345332430659661993)
XLA Ops:
  0.6 0.8 select_reduce_fusion
  2.1 0.3 constant_dynamic-update-slice_fusion.32
  2.4 3.0 %collective-permute-start.10 = (bf16[16,6144]{1,0:T(8,128)(2,1)S(1)}, bf16[16,6144]{1,0:T(8,128)(2,1)S(1)}, u32[]{:S(2)}, u32[]{:S(2)}) collective-permute-start(bf16[16,6144]{1,0:T(8,128)(2,1)S(1)} %get-tuple-element.126), channel_id=1, source_target_pairs={{4,0},{5,1},{8,4},{9,5},{12,8},{13,9},{14,12},{15,13},{10,14},{11,... | collective-permute-start | bytes 589832 | tf_op jit(solution)/shard_map/ppermute | solution.py:88
  5.7 1.7 %convolution_convert_fusion.3 = bf16[16,6144]{1,0:T(8,128)(2,1)S(1)} fusion(bf16[128,6144]{1,0:T(8,128)(2,1)} %param.7, s32[128]{0:T(128)S(1)} %add_reduce_fusion, pred[128]{0:T(512)(128)(4,1)S(1)} %reduce_or.9), kind=kOutput, calls=%fused_computation.4 | convolution fusion | flops 25268224 | bytes 1770112 | tf_op jit(solution)/shard_map/dot_general | solution.py:161
  7.5 2.0 %collective-permute-start = (bf16[16,6272]{1,0:T(8,128)(2,1)S(1)}, bf16[16,6272]{1,0:T(8,128)(2,1)S(1)}, u32[]{:S(2)}, u32[]{:S(2)}) collective-permute-start(bf16[16,6272]{1,0:T(8,128)(2,1)S(1)} %get-tuple-element.111), channel_id=1, source_target_pairs={{0,4},{1,5},{4,8},{5,9},{8,12},{9,13},{12,14},{13,15},{14,10},{15,... | collective-permute-start | bytes 602120 | tf_op jit(solution)/shard_map/ppermute | solution.py:88
  9.6 0.8 collective-permute-done.10
  10.4 2.2 %collective-permute-start.12 = (bf16[16,6144]{1,0:T(8,128)(2,1)S(1)}, bf16[16,6144]{1,0:T(8,128)(2,1)S(1)}, u32[]{:S(2)}, u32[]{:S(2)}) collective-permute-start(bf16[16,6144]{1,0:T(8,128)(2,1)S(1)} %collective-permute-done.10), channel_id=1, source_target_pairs={{4,0},{5,1},{8,4},{9,5},{12,8},{13,9},{14,12},{15,13},{10,14},{11,... | collective-permute-start | bytes 589832 | tf_op jit(solution)/shard_map/ppermute | solution.py:88
  12.6 0.7 collective-permute-done.9
  13.3 4.2 %collective-permute-done = bf16[16,6272]{1,0:T(8,128)(2,1)S(1)} collective-permute-done((bf16[16,6272]{1,0:T(8,128)(2,1)S(1)}, bf16[16,6272]{1,0:T(8,128)(2,1)S(1)}, u32[]{:S(2)}, u32[]{:S(2)}) %collective-permute-start) | collective-permute-done | bytes 200736 | tf_op jit(solution)/shard_map/ppermute | solution.py:88
  17.5 2.0 %collective-permute-start.3 = (bf16[16,6272]{1,0:T(8,128)(2,1)S(1)}, bf16[16,6272]{1,0:T(8,128)(2,1)S(1)}, u32[]{:S(2)}, u32[]{:S(2)}) collective-permute-start(bf16[16,6272]{1,0:T(8,128)(2,1)S(1)} %collective-permute-done.1), channel_id=1, source_target_pairs={{4,0},{5,1},{8,4},{9,5},{12,8},{13,9},{14,12},{15,13},{10,14},{11,... | collective-permute-start | bytes 602120 | tf_op jit(solution)/shard_map/ppermute | solution.py:88
  19.6 1.5 %collective-permute-done.12 = bf16[16,6144]{1,0:T(8,128)(2,1)S(1)} collective-permute-done((bf16[16,6144]{1,0:T(8,128)(2,1)S(1)}, bf16[16,6144]{1,0:T(8,128)(2,1)S(1)}, u32[]{:S(2)}, u32[]{:S(2)}) %collective-permute-start.12) | collective-permute-done | bytes 196640 | tf_op jit(solution)/shard_map/ppermute | solution.py:88
  21.2 0.6 collective-permute-start.14
  21.8 1.4 %collective-permute-start.13 = (bf16[16,6144]{1,0:T(8,128)(2,1)S(1)}, bf16[16,6144]{1,0:T(8,128)(2,1)S(1)}, u32[]{:S(2)}, u32[]{:S(2)}) collective-permute-start(bf16[16,6144]{1,0:T(8,128)(2,1)S(1)} %collective-permute-done.11), channel_id=1, source_target_pairs={{0,4},{1,5},{4,8},{5,9},{8,12},{9,13},{12,14},{13,15},{14,10},{15,... | collective-permute-start | bytes 589832 | tf_op jit(solution)/shard_map/ppermute | solution.py:88
  23.3 2.8 %collective-permute-done.2 = bf16[16,6272]{1,0:T(8,128)(2,1)S(1)} collective-permute-done((bf16[16,6272]{1,0:T(8,128)(2,1)S(1)}, bf16[16,6272]{1,0:T(8,128)(2,1)S(1)}, u32[]{:S(2)}, u32[]{:S(2)}) %collective-permute-start.2) | collective-permute-done | bytes 200736 | tf_op jit(solution)/shard_map/ppermute | solution.py:88
  26.1 2.0 %collective-permute-start.5 = (bf16[16,6272]{1,0:T(8,128)(2,1)S(1)}, bf16[16,6272]{1,0:T(8,128)(2,1)S(1)}, u32[]{:S(2)}, u32[]{:S(2)}) collective-permute-start(bf16[16,6272]{1,0:T(8,128)(2,1)S(1)} %collective-permute-done.3), channel_id=1, source_target_pairs={{4,0},{5,1},{8,4},{9,5},{12,8},{13,9},{14,12},{15,13},{10,14},{11,... | collective-permute-start | bytes 602120 | tf_op jit(solution)/shard_map/ppermute | solution.py:88
  28.2 1.5 %collective-permute-done.14 = bf16[16,6144]{1,0:T(8,128)(2,1)S(1)} collective-permute-done((bf16[16,6144]{1,0:T(8,128)(2,1)S(1)}, bf16[16,6144]{1,0:T(8,128)(2,1)S(1)}, u32[]{:S(2)}, u32[]{:S(2)}) %collective-permute-start.14) | collective-permute-done | bytes 196640 | tf_op jit(solution)/shard_map/ppermute | solution.py:88
  29.7 0.9 collective-permute-start.16
  30.6 1.2 %collective-permute-start.15 = (bf16[16,3072]{1,0:T(8,128)(2,1)S(1)}, bf16[16,3072]{1,0:T(8,128)(2,1)S(1)}, u32[]{:S(2)}, u32[]{:S(2)}) collective-permute-start(bf16[16,3072]{1,0:T(8,128)(2,1)S(1)} %slice.142), channel_id=1, source_target_pairs={{0,4},{1,5},{4,8},{5,9},{8,12},{9,13},{12,14},{13,15},{14,10},{15,... | collective-permute-start | bytes 294920 | tf_op jit(solution)/shard_map/ppermute | solution.py:88
  31.9 2.3 %collective-permute-done.4 = bf16[16,6272]{1,0:T(8,128)(2,1)S(1)} collective-permute-done((bf16[16,6272]{1,0:T(8,128)(2,1)S(1)}, bf16[16,6272]{1,0:T(8,128)(2,1)S(1)}, u32[]{:S(2)}, u32[]{:S(2)}) %collective-permute-start.4) | collective-permute-done | bytes 200736 | tf_op jit(solution)/shard_map/ppermute | solution.py:88
  34.2 0.5 collective-permute-start.6
  34.7 1.7 %collective-permute-start.7 = (bf16[16,3200]{1,0:T(8,128)(2,1)S(1)}, bf16[16,3200]{1,0:T(8,128)(2,1)S(1)}, u32[]{:S(2)}, u32[]{:S(2)}) collective-permute-start(bf16[16,3200]{1,0:T(8,128)(2,1)S(1)} %slice.141), channel_id=1, source_target_pairs={{4,0},{5,1},{8,4},{9,5},{12,8},{13,9},{14,12},{15,13},{10,14},{11,... | collective-permute-start | bytes 307208 | tf_op jit(solution)/shard_map/ppermute | solution.py:88
  36.6 2.3 %collective-permute-done.6 = bf16[16,3072]{1,0:T(8,128)(2,1)S(1)} collective-permute-done((bf16[16,3072]{1,0:T(8,128)(2,1)S(1)}, bf16[16,3072]{1,0:T(8,128)(2,1)S(1)}, u32[]{:S(2)}, u32[]{:S(2)}) %collective-permute-start.6) | collective-permute-done | bytes 98336 | tf_op jit(solution)/shard_map/ppermute | solution.py:88
  38.9 0.5 collective-permute-done.7
  39.5 1.4 %collective-permute-done.17 = bf16[16,6272]{1,0:T(8,128)(2,1)S(1)} collective-permute-done((bf16[16,6272]{1,0:T(8,128)(2,1)S(1)}, bf16[16,6272]{1,0:T(8,128)(2,1)S(1)}, u32[]{:S(2)}, u32[]{:S(2)}) %collective-permute-start.17) | collective-permute-done | bytes 200736 | tf_op jit(solution)/shard_map/ppermute | solution.py:88
  41.0 0.2 constant_dynamic-update-slice_fusion.15
  41.4 1.3 %fusion.2 = f32[256,336]{0,1:T(8,128)S(1)} fusion(bf16[6144,336]{0,1:T(8,128)(2,1)S(1)} %copy-done.3, bf16[256,6272]{1,0:T(8,128)(2,1)S(1)} %constant_dynamic-update-slice_fusion.14.refs_1_), kind=kOutput, calls=%fused_computation.9 | convolution fusion | flops 1056964608 | bytes 7618560 | tf_op jit(solution)/shard_map/dot_general | solution.py:172
  42.7 0.8 copy-done.4
  43.5 1.3 %multiply_convert_fusion.2 = (bf16[256,336]{0,1:T(8,128)(2,1)S(1)}, f32[256,336]{0,1:T(8,128)S(1)}) fusion(f32[256]{0:T(256)S(1)} %convert_reduce_fusion, f32[256,336]{0,1:T(8,128)S(1)} %fusion.2, bf16[6144,336]{0,1:T(8,128)(2,1)S(1)} %copy-done.4, bf16[256,6272]{1,0:T(8,128)(2,1)S(1)} %constant_dynamic-update-slice_fusion.14.refs_1_), kind=kOutput, calls=%fused_computation.46 | convolution fusion | flops 1057566720 | bytes 8135680 | tf_op jit(solution)/shard_map/dot_general | solution.py:173
  44.8 0.9 copy-done.2
  45.7 1.8 %fusion.42 = f32[256,6144]{1,0:T(8,128)S(1)} fusion(bf16[256,336]{0,1:T(8,128)(2,1)S(1)} %get-tuple-element.54, bf16[336,6144]{1,0:T(8,128)(2,1)S(1)} %copy-done.2), kind=kOutput, calls=%fused_computation.109 | convolution fusion | flops 1056964608 | bytes 10592256 | tf_op jit(solution)/shard_map/dot_general | solution.py:177
  47.5 0.2 slice.222
  47.9 0.4 collective-permute-start.20
  48.4 0.2 collective-permute-start.19
  48.6 1.3 %multiply_convert_fusion = (bf16[256,336]{0,1:T(8,128)(2,1)S(1)}, bf16[256,336]{0,1:T(8,128)(2,1)S(1)}) fusion(f32[256,336]{0,1:T(8,128)S(1)} %fusion.2, f32[256,336]{0,1:T(8,128)S(1)} %get-tuple-element.128, bf16[256,6144]{1,0:T(8,128)(2,1)S(1)} %constant_dynamic-update-slice_fusion.24.refs_1_, bf16[336,6144]{1,0:T(8,128)(2,1)S(1)} %copy-done.2, ...), kind=kOutput, calls=%fused_computation.44 | convolution fusion | flops 1058168832 | bytes 8307712 | tf_op jit(solution)/shard_map/dot_general | solution.py:182
  50.2 1.7 %collective-permute-start.22 = (bf16[16,6144]{1,0:T(8,128)(2,1)S(1)}, bf16[16,6144]{1,0:T(8,128)(2,1)S(1)}, u32[]{:S(2)}, u32[]{:S(2)}) collective-permute-start(bf16[16,6144]{1,0:T(8,128)(2,1)S(1)} %get-tuple-element.56), channel_id=1, source_target_pairs={{4,0},{5,1},{8,4},{9,5},{12,8},{13,9},{14,12},{15,13},{10,14},{11,... | collective-permute-start | bytes 589832 | tf_op jit(solution)/shard_map/ppermute | solution.py:88
  51.9 0.4 collective-permute-start.23
  52.3 1.8 %fusion.43 = f32[256,6144]{1,0:T(8,128)S(1)} fusion(bf16[256,336]{0,1:T(8,128)(2,1)S(1)} %get-tuple-element.53, bf16[6144,336]{0,1:T(8,128)(2,1)S(1)} %copy-done.3), kind=kOutput, calls=%fused_computation.110 | convolution fusion | flops 1056964608 | bytes 10592256 | tf_op jit(solution)/shard_map/dot_general | solution.py:188
  54.1 1.8 %convolution_add_fusion = f32[256,6144]{1,0:T(8,128)S(1)} fusion(f32[256,6144]{1,0:T(8,128)S(1)} %fusion.43, bf16[256,336]{0,1:T(8,128)(2,1)S(1)} %get-tuple-element.77, bf16[6144,336]{0,1:T(8,128)(2,1)S(1)} %copy-done.4), kind=kOutput, calls=%fused_computation | convolution fusion | flops 1058537472 | bytes 16883712 | tf_op jit(solution)/shard_map/dot_general | solution.py:188
  55.9 0.2 slice.221
  56.3 3.3 %shard_map.110 = (bf16[336,6144]{1,0:T(8,128)(2,1)}, f32[8,128]{1,0:T(8,128)S(1)}) custom-call(bf16[336,256]{1,0:T(8,128)(2,1)S(1)} %bitcast.27, bf16[256,6144]{1,0:T(8,128)(2,1)S(1)} %constant_dynamic-update-slice_fusion.24.refs_1_), custom_call_target="tpu_custom_call" | custom-call | flops 1056964608 | bytes 7274496 | tf_op jit(solution)/shard_map/pallas_call | solution.py:54
  59.8 1.7 %collective-permute-start.24 = (bf16[16,6144]{1,0:T(8,128)(2,1)S(1)}, bf16[16,6144]{1,0:T(8,128)(2,1)S(1)}, u32[]{:S(2)}, u32[]{:S(2)}) collective-permute-start(bf16[16,6144]{1,0:T(8,128)(2,1)S(1)} %fusion.14), channel_id=1, source_target_pairs={{4,0},{5,1},{8,4},{9,5},{12,8},{13,9},{14,12},{15,13},{10,14},{11,... | collective-permute-start | bytes 589832 | tf_op jit(solution)/shard_map/ppermute | solution.py:88
  61.5 0.4 collective-permute-start.25
  62.1 1.7 %collective-permute-start.31 = (bf16[16,6144]{1,0:T(8,128)(2,1)S(1)}, bf16[16,6144]{1,0:T(8,128)(2,1)S(1)}, u32[]{:S(2)}, u32[]{:S(2)}) collective-permute-start(bf16[16,6144]{1,0:T(8,128)(2,1)S(1)} %get-tuple-element.69), channel_id=1, source_target_pairs={{0,4},{1,5},{4,8},{5,9},{8,12},{9,13},{12,14},{13,15},{14,10},{15,... | collective-permute-start | bytes 589832 | tf_op jit(solution)/shard_map/ppermute | solution.py:88
  64.0 0.4 collective-permute-start.30
  64.4 3.3 %shard_map.111 = (bf16[336,6144]{1,0:T(8,128)(2,1)}, f32[8,128]{1,0:T(8,128)S(1)}) custom-call(bf16[336,256]{1,0:T(8,128)(2,1)S(1)} %bitcast.26, bf16[256,6272]{1,0:T(8,128)(2,1)S(1)} %constant_dynamic-update-slice_fusion.14.refs_1_, f32[8,128]{1,0:T(8,128)S(1)} %get-tuple-element.58.refs_2_), custom_call_target="tpu_custom_call" | custom-call | flops 1056964608 | bytes 7274496 | tf_op jit(solution)/shard_map/pallas_call | solution.py:54
  67.7 1.5 %collective-permute-done.25 = bf16[16,6144]{1,0:T(8,128)(2,1)S(1)} collective-permute-done((bf16[16,6144]{1,0:T(8,128)(2,1)S(1)}, bf16[16,6144]{1,0:T(8,128)(2,1)S(1)}, u32[]{:S(2)}, u32[]{:S(2)}) %collective-permute-start.25) | collective-permute-done | bytes 196640 | tf_op jit(solution)/shard_map/ppermute | solution.py:88
  69.3 3.5 %collective-permute-done.31 = bf16[16,6144]{1,0:T(8,128)(2,1)S(1)} collective-permute-done((bf16[16,6144]{1,0:T(8,128)(2,1)S(1)}, bf16[16,6144]{1,0:T(8,128)(2,1)S(1)}, u32[]{:S(2)}, u32[]{:S(2)}) %collective-permute-start.31) | collective-permute-done | bytes 196640 | tf_op jit(solution)/shard_map/ppermute | solution.py:88
  72.8 0.2 slice_add_fusion
  73.1 1.6 %collective-permute-start.32 = (bf16[16,6144]{1,0:T(8,128)(2,1)S(1)}, bf16[16,6144]{1,0:T(8,128)(2,1)S(1)}, u32[]{:S(2)}, u32[]{:S(2)}) collective-permute-start(bf16[16,6144]{1,0:T(8,128)(2,1)S(1)} %fusion.8), channel_id=1, source_target_pairs={{4,0},{5,1},{8,4},{9,5},{12,8},{13,9},{14,12},{15,13},{10,14},{11,... | collective-permute-start | bytes 589832 | tf_op jit(solution)/shard_map/ppermute | solution.py:88
  74.7 0.4 collective-permute-start.33
  75.2 1.6 %collective-permute-start.26 = (bf16[16,6144]{1,0:T(8,128)(2,1)S(1)}, bf16[16,6144]{1,0:T(8,128)(2,1)S(1)}, u32[]{:S(2)}, u32[]{:S(2)}) collective-permute-start(bf16[16,6144]{1,0:T(8,128)(2,1)S(1)} %get-tuple-element.66), channel_id=1, source_target_pairs={{4,0},{5,1},{8,4},{9,5},{12,8},{13,9},{14,12},{15,13},{10,14},{11,... | collective-permute-start | bytes 589832 | tf_op jit(solution)/shard_map/ppermute | solution.py:88
  76.9 0.4 collective-permute-start.28
  77.3 3.7 %collective-permute-done.32 = bf16[16,6144]{1,0:T(8,128)(2,1)S(1)} collective-permute-done((bf16[16,6144]{1,0:T(8,128)(2,1)S(1)}, bf16[16,6144]{1,0:T(8,128)(2,1)S(1)}, u32[]{:S(2)}, u32[]{:S(2)}) %collective-permute-start.32) | collective-permute-done | bytes 196640 | tf_op jit(solution)/shard_map/ppermute | solution.py:88
  81.0 1.6 %collective-permute-done.33 = bf16[16,6144]{1,0:T(8,128)(2,1)S(1)} collective-permute-done((bf16[16,6144]{1,0:T(8,128)(2,1)S(1)}, bf16[16,6144]{1,0:T(8,128)(2,1)S(1)}, u32[]{:S(2)}, u32[]{:S(2)}) %collective-permute-start.33) | collective-permute-done | bytes 196640 | tf_op jit(solution)/shard_map/ppermute | solution.py:88
  82.6 0.5 collective-permute-start.35
  83.1 0.4 collective-permute-done.26
  83.6 1.6 %collective-permute-start.27 = (bf16[16,6144]{1,0:T(8,128)(2,1)S(1)}, bf16[16,6144]{1,0:T(8,128)(2,1)S(1)}, u32[]{:S(2)}, u32[]{:S(2)}) collective-permute-start(bf16[16,6144]{1,0:T(8,128)(2,1)S(1)} %fusion.16), channel_id=1, source_target_pairs={{4,0},{5,1},{8,4},{9,5},{12,8},{13,9},{14,12},{15,13},{10,14},{11,... | collective-permute-start | bytes 589832 | tf_op jit(solution)/shard_map/ppermute | solution.py:88
  85.2 3.9 %shard_map.112 = (bf16[336,6144]{1,0:T(8,128)(2,1)}, f32[8,128]{1,0:T(8,128)}) custom-call(bf16[336,256]{1,0:T(8,128)(2,1)S(1)} %bitcast.28, bf16[256,6272]{1,0:T(8,128)(2,1)S(1)} %constant_dynamic-update-slice_fusion.14.refs_1_, f32[8,128]{1,0:T(8,128)S(1)} %get-tuple-element.78.refs_2_), custom_call_target="tpu_custom_call" | custom-call | flops 1056964608 | bytes 7274496 | tf_op jit(solution)/shard_map/pallas_call | solution.py:54
  89.1 1.6 %collective-permute-start.34 = (bf16[16,6144]{1,0:T(8,128)(2,1)S(1)}, bf16[16,6144]{1,0:T(8,128)(2,1)S(1)}, u32[]{:S(2)}, u32[]{:S(2)}) collective-permute-start(bf16[16,6144]{1,0:T(8,128)(2,1)S(1)} %get-tuple-element.74), channel_id=1, source_target_pairs={{4,0},{5,1},{8,4},{9,5},{12,8},{13,9},{14,12},{15,13},{10,14},{11,... | collective-permute-start | bytes 589832 | tf_op jit(solution)/shard_map/ppermute | solution.py:88
  90.8 0.5 collective-permute-start.36
  91.3 1.8 %convolution_convert_fusion.1 = bf16[128,6144]{1,0:T(8,128)(2,1)} fusion(f32[80,6144]{1,0:T(8,128)S(1)} %slice_add_fusion.1, bf16[16,6144]{1,0:T(8,128)(2,1)S(1)} %collective-permute-done.28, bf16[16,6144]{1,0:T(8,128)(2,1)S(1)} %collective-permute-done.27, s32[128]{0:T(128)S(1)} %add_reduce_fusion, pred[128]{0:T(512)(128)(4,1)S(1)} %reduce_or.9), kind=kOutput, calls=%fused_computation.2 | convolution fusion | flops 26447872 | bytes 2360320 | tf_op jit(solution)/shard_map/dot_general | solution.py:216
  93.1 1.8 %collective-permute-done.34 = bf16[16,6144]{1,0:T(8,128)(2,1)S(1)} collective-permute-done((bf16[16,6144]{1,0:T(8,128)(2,1)S(1)}, bf16[16,6144]{1,0:T(8,128)(2,1)S(1)}, u32[]{:S(2)}, u32[]{:S(2)}) %collective-permute-start.34) | collective-permute-done | bytes 196640 | tf_op jit(solution)/shard_map/ppermute | solution.py:88
  94.8 1.7 %collective-permute-done.36 = bf16[16,6144]{1,0:T(8,128)(2,1)S(1)} collective-permute-done((bf16[16,6144]{1,0:T(8,128)(2,1)S(1)}, bf16[16,6144]{1,0:T(8,128)(2,1)S(1)}, u32[]{:S(2)}, u32[]{:S(2)}) %collective-permute-start.36) | collective-permute-done | bytes 196640 | tf_op jit(solution)/shard_map/ppermute | solution.py:88
  96.5 1.8 %convolution_convert_fusion = bf16[128,6144]{1,0:T(8,128)(2,1)} fusion(f32[80,6144]{1,0:T(8,128)S(1)} %slice_add_fusion, bf16[16,6144]{1,0:T(8,128)(2,1)S(1)} %collective-permute-done.36, bf16[16,6144]{1,0:T(8,128)(2,1)S(1)} %collective-permute-done.34, s32[128]{0:T(128)S(1)} %add_reduce_fusion, pred[128]{0:T(512)(128)(4,1)S(1)} %reduce_or.9), kind=kOutput, calls=%fused_computation.1 | convolution fusion | flops 26447872 | bytes 2360320 | tf_op jit(solution)/shard_map/dot_general | solution.py:216
  (88 shorter events, 3.4 us)
Async XLA Ops:
  0.6 1.4 %copy-start = (bf16[128,6144]{1,0:T(8,128)(2,1)S(1)}, bf16[128,6144]{1,0:T(8,128)(2,1)}, u32[]{:S(2)}) copy-start(bf16[128,6144]{1,0:T(8,128)(2,1)} %param.8) | copy-start | bytes 4718596
  2.4 8.0 %collective-permute-start.10 = (bf16[16,6144]{1,0:T(8,128)(2,1)S(1)}, bf16[16,6144]{1,0:T(8,128)(2,1)S(1)}, u32[]{:S(2)}, u32[]{:S(2)}) collective-permute-start(bf16[16,6144]{1,0:T(8,128)(2,1)S(1)} %get-tuple-element.126), channel_id=1, source_target_pairs={{4,0},{5,1},{8,4},{9,5},{12,8},{13,9},{14,12},{15,13},{10,14},{11,... | collective-permute-start | bytes 589832 | tf_op jit(solution)/shard_map/ppermute | solution.py:88
  5.4 7.8 %collective-permute-start.9 = (bf16[16,6144]{1,0:T(8,128)(2,1)S(1)}, bf16[16,6144]{1,0:T(8,128)(2,1)S(1)}, u32[]{:S(2)}, u32[]{:S(2)}) collective-permute-start(bf16[16,6144]{1,0:T(8,128)(2,1)S(1)} %get-tuple-element.126), channel_id=1, source_target_pairs={{0,4},{1,5},{4,8},{5,9},{8,12},{9,13},{12,14},{13,15},{14,10},{15,... | collective-permute-start | bytes 589832 | tf_op jit(solution)/shard_map/ppermute | solution.py:88
  7.5 10.0 %collective-permute-start = (bf16[16,6272]{1,0:T(8,128)(2,1)S(1)}, bf16[16,6272]{1,0:T(8,128)(2,1)S(1)}, u32[]{:S(2)}, u32[]{:S(2)}) collective-permute-start(bf16[16,6272]{1,0:T(8,128)(2,1)S(1)} %get-tuple-element.111), channel_id=1, source_target_pairs={{0,4},{1,5},{4,8},{5,9},{8,12},{9,13},{12,14},{13,15},{14,10},{15,... | collective-permute-start | bytes 602120 | tf_op jit(solution)/shard_map/ppermute | solution.py:88
  9.5 8.0 %collective-permute-start.1 = (bf16[16,6272]{1,0:T(8,128)(2,1)S(1)}, bf16[16,6272]{1,0:T(8,128)(2,1)S(1)}, u32[]{:S(2)}, u32[]{:S(2)}) collective-permute-start(bf16[16,6272]{1,0:T(8,128)(2,1)S(1)} %get-tuple-element.111), channel_id=1, source_target_pairs={{4,0},{5,1},{8,4},{9,5},{12,8},{13,9},{14,12},{15,13},{10,14},{11,... | collective-permute-start | bytes 602120 | tf_op jit(solution)/shard_map/ppermute | solution.py:88
  10.4 10.8 %collective-permute-start.12 = (bf16[16,6144]{1,0:T(8,128)(2,1)S(1)}, bf16[16,6144]{1,0:T(8,128)(2,1)S(1)}, u32[]{:S(2)}, u32[]{:S(2)}) collective-permute-start(bf16[16,6144]{1,0:T(8,128)(2,1)S(1)} %collective-permute-done.10), channel_id=1, source_target_pairs={{4,0},{5,1},{8,4},{9,5},{12,8},{13,9},{14,12},{15,13},{10,14},{11,... | collective-permute-start | bytes 589832 | tf_op jit(solution)/shard_map/ppermute | solution.py:88
  13.2 8.5 %collective-permute-start.11 = (bf16[16,6144]{1,0:T(8,128)(2,1)S(1)}, bf16[16,6144]{1,0:T(8,128)(2,1)S(1)}, u32[]{:S(2)}, u32[]{:S(2)}) collective-permute-start(bf16[16,6144]{1,0:T(8,128)(2,1)S(1)} %collective-permute-done.9), channel_id=1, source_target_pairs={{0,4},{1,5},{4,8},{5,9},{8,12},{9,13},{12,14},{13,15},{14,10},{15,... | collective-permute-start | bytes 589832 | tf_op jit(solution)/shard_map/ppermute | solution.py:88
  17.5 8.5 %collective-permute-start.2 = (bf16[16,6272]{1,0:T(8,128)(2,1)S(1)}, bf16[16,6272]{1,0:T(8,128)(2,1)S(1)}, u32[]{:S(2)}, u32[]{:S(2)}) collective-permute-start(bf16[16,6272]{1,0:T(8,128)(2,1)S(1)} %collective-permute-done), channel_id=1, source_target_pairs={{0,4},{1,5},{4,8},{5,9},{8,12},{9,13},{12,14},{13,15},{14,10},{15,... | collective-permute-start | bytes 602120 | tf_op jit(solution)/shard_map/ppermute | solution.py:88
  17.5 8.5 %collective-permute-start.3 = (bf16[16,6272]{1,0:T(8,128)(2,1)S(1)}, bf16[16,6272]{1,0:T(8,128)(2,1)S(1)}, u32[]{:S(2)}, u32[]{:S(2)}) collective-permute-start(bf16[16,6272]{1,0:T(8,128)(2,1)S(1)} %collective-permute-done.1), channel_id=1, source_target_pairs={{4,0},{5,1},{8,4},{9,5},{12,8},{13,9},{14,12},{15,13},{10,14},{11,... | collective-permute-start | bytes 602120 | tf_op jit(solution)/shard_map/ppermute | solution.py:88
  21.2 8.5 %collective-permute-start.14 = (bf16[16,6144]{1,0:T(8,128)(2,1)S(1)}, bf16[16,6144]{1,0:T(8,128)(2,1)S(1)}, u32[]{:S(2)}, u32[]{:S(2)}) collective-permute-start(bf16[16,6144]{1,0:T(8,128)(2,1)S(1)} %collective-permute-done.12), channel_id=1, source_target_pairs={{4,0},{5,1},{8,4},{9,5},{12,8},{13,9},{14,12},{15,13},{10,14},{11,... | collective-permute-start | bytes 589832 | tf_op jit(solution)/shard_map/ppermute | solution.py:88
  21.8 8.8 %collective-permute-start.13 = (bf16[16,6144]{1,0:T(8,128)(2,1)S(1)}, bf16[16,6144]{1,0:T(8,128)(2,1)S(1)}, u32[]{:S(2)}, u32[]{:S(2)}) collective-permute-start(bf16[16,6144]{1,0:T(8,128)(2,1)S(1)} %collective-permute-done.11), channel_id=1, source_target_pairs={{0,4},{1,5},{4,8},{5,9},{8,12},{9,13},{12,14},{13,15},{14,10},{15,... | collective-permute-start | bytes 589832 | tf_op jit(solution)/shard_map/ppermute | solution.py:88
  26.1 8.1 %collective-permute-start.4 = (bf16[16,6272]{1,0:T(8,128)(2,1)S(1)}, bf16[16,6272]{1,0:T(8,128)(2,1)S(1)}, u32[]{:S(2)}, u32[]{:S(2)}) collective-permute-start(bf16[16,6272]{1,0:T(8,128)(2,1)S(1)} %collective-permute-done.2), channel_id=1, source_target_pairs={{0,4},{1,5},{4,8},{5,9},{8,12},{9,13},{12,14},{13,15},{14,10},{15,... | collective-permute-start | bytes 602120 | tf_op jit(solution)/shard_map/ppermute | solution.py:88
  26.1 8.6 %collective-permute-start.5 = (bf16[16,6272]{1,0:T(8,128)(2,1)S(1)}, bf16[16,6272]{1,0:T(8,128)(2,1)S(1)}, u32[]{:S(2)}, u32[]{:S(2)}) collective-permute-start(bf16[16,6272]{1,0:T(8,128)(2,1)S(1)} %collective-permute-done.3), channel_id=1, source_target_pairs={{4,0},{5,1},{8,4},{9,5},{12,8},{13,9},{14,12},{15,13},{10,14},{11,... | collective-permute-start | bytes 602120 | tf_op jit(solution)/shard_map/ppermute | solution.py:88
  29.7 6.8 %collective-permute-start.16 = (bf16[16,3072]{1,0:T(8,128)(2,1)S(1)}, bf16[16,3072]{1,0:T(8,128)(2,1)S(1)}, u32[]{:S(2)}, u32[]{:S(2)}) collective-permute-start(bf16[16,3072]{1,0:T(8,128)(2,1)S(1)} %slice.143), channel_id=1, source_target_pairs={{4,0},{5,1},{8,4},{9,5},{12,8},{13,9},{14,12},{15,13},{10,14},{11,... | collective-permute-start | bytes 294920 | tf_op jit(solution)/shard_map/ppermute | solution.py:88
  30.6 5.9 %collective-permute-start.15 = (bf16[16,3072]{1,0:T(8,128)(2,1)S(1)}, bf16[16,3072]{1,0:T(8,128)(2,1)S(1)}, u32[]{:S(2)}, u32[]{:S(2)}) collective-permute-start(bf16[16,3072]{1,0:T(8,128)(2,1)S(1)} %slice.142), channel_id=1, source_target_pairs={{0,4},{1,5},{4,8},{5,9},{8,12},{9,13},{12,14},{13,15},{14,10},{15,... | collective-permute-start | bytes 294920 | tf_op jit(solution)/shard_map/ppermute | solution.py:88
  34.2 7.2 %copy-start.3 = (bf16[6144,336]{0,1:T(8,128)(2,1)S(1)}, bf16[6144,336]{0,1:T(8,128)(2,1)}, u32[]{:S(2)}) copy-start(bf16[6144,336]{0,1:T(8,128)(2,1)} %param.11) | copy-start | bytes 12386308
  34.2 4.7 %collective-permute-start.6 = (bf16[16,3072]{1,0:T(8,128)(2,1)S(1)}, bf16[16,3072]{1,0:T(8,128)(2,1)S(1)}, u32[]{:S(2)}, u32[]{:S(2)}) collective-permute-start(bf16[16,3072]{1,0:T(8,128)(2,1)S(1)} %slice.140), channel_id=1, source_target_pairs={{0,4},{1,5},{4,8},{5,9},{8,12},{9,13},{12,14},{13,15},{14,10},{15,... | collective-permute-start | bytes 294920 | tf_op jit(solution)/shard_map/ppermute | solution.py:88
  34.7 4.7 %collective-permute-start.7 = (bf16[16,3200]{1,0:T(8,128)(2,1)S(1)}, bf16[16,3200]{1,0:T(8,128)(2,1)S(1)}, u32[]{:S(2)}, u32[]{:S(2)}) collective-permute-start(bf16[16,3200]{1,0:T(8,128)(2,1)S(1)} %slice.141), channel_id=1, source_target_pairs={{4,0},{5,1},{8,4},{9,5},{12,8},{13,9},{14,12},{15,13},{10,14},{11,... | collective-permute-start | bytes 307208 | tf_op jit(solution)/shard_map/ppermute | solution.py:88
  36.4 4.6 %collective-permute-start.8 = (bf16[112,6272]{1,0:T(8,128)(2,1)S(1)}, bf16[112,6272]{1,0:T(8,128)(2,1)S(1)}, u32[]{:S(2)}, u32[]{:S(2)}) collective-permute-start(bf16[112,6272]{1,0:T(8,128)(2,1)S(1)} %get-tuple-element.97), channel_id=1, source_target_pairs={{0,1},{1,0},{2,3},{3,2},{4,5},{5,4},{6,7},{7,6},{8,9},{9,8},{10,11... | collective-permute-start | bytes 4214792 | tf_op jit(solution)/shard_map/ppermute | solution.py:88
  39.4 1.5 %collective-permute-start.17 = (bf16[16,6272]{1,0:T(8,128)(2,1)S(1)}, bf16[16,6272]{1,0:T(8,128)(2,1)S(1)}, u32[]{:S(2)}, u32[]{:S(2)}) collective-permute-start(bf16[16,6272]{1,0:T(8,128)(2,1)S(1)} %pad_maximum_fusion), channel_id=1, source_target_pairs={{0,1},{1,0},{2,3},{3,2},{4,5},{5,4},{6,7},{7,6},{8,9},{9,8},{10,11... | collective-permute-start | bytes 602120 | tf_op jit(solution)/shard_map/ppermute | solution.py:88
  40.9 6.8 %collective-permute-start.18 = (bf16[128,6144]{1,0:T(8,128)(2,1)S(1)}, bf16[128,6144]{1,0:T(8,128)(2,1)S(1)}, u32[]{:S(2)}, u32[]{:S(2)}) collective-permute-start(bf16[128,6144]{1,0:T(8,128)(2,1)S(1)} %maximum_dynamic-update-slice_fusion), channel_id=1, source_target_pairs={{0,1},{1,0},{2,3},{3,2},{4,5},{5,4},{6,7},{7,6},{8,9},{9,8},{10,11... | collective-permute-start | bytes 4718600 | tf_op jit(solution)/shard_map/ppermute | solution.py:88
  41.4 2.2 %copy-start.4 = (bf16[6144,336]{0,1:T(8,128)(2,1)S(1)}, bf16[6144,336]{0,1:T(8,128)(2,1)}, u32[]{:S(2)}) copy-start(bf16[6144,336]{0,1:T(8,128)(2,1)} %param.12) | copy-start | bytes 12386308
  43.5 2.2 %copy-start.2 = (bf16[336,6144]{1,0:T(8,128)(2,1)S(1)}, bf16[336,6144]{1,0:T(8,128)(2,1)}, u32[]{:S(2)}) copy-start(bf16[336,6144]{1,0:T(8,128)(2,1)} %param.13) | copy-start | bytes 12386308
  47.9 2.1 %collective-permute-start.20 = (bf16[48,6144]{1,0:T(8,128)(2,1)S(1)}, bf16[48,6144]{1,0:T(8,128)(2,1)S(1)}, u32[]{:S(2)}, u32[]{:S(2)}) collective-permute-start(bf16[48,6144]{1,0:T(8,128)(2,1)S(1)} %slice.121), channel_id=1, source_target_pairs={{0,1},{1,0},{2,3},{3,2},{4,5},{5,4},{6,7},{7,6},{8,9},{9,8},{10,11... | collective-permute-start | bytes 1769480 | tf_op jit(solution)/shard_map/ppermute | solution.py:88
  48.4 11.2 %collective-permute-start.19 = (bf16[80,6144]{1,0:T(8,128)(2,1)S(1)}, bf16[80,6144]{1,0:T(8,128)(2,1)S(1)}, u32[]{:S(2)}, u32[]{:S(2)}) collective-permute-start(bf16[80,6144]{1,0:T(8,128)(2,1)S(1)} %slice.116), channel_id=1, source_target_pairs={{0,1},{1,0},{2,3},{3,2},{4,5},{5,4},{6,7},{7,6},{8,9},{9,8},{10,11... | collective-permute-start | bytes 2949128 | tf_op jit(solution)/shard_map/ppermute | solution.py:88
  50.2 9.4 %collective-permute-start.22 = (bf16[16,6144]{1,0:T(8,128)(2,1)S(1)}, bf16[16,6144]{1,0:T(8,128)(2,1)S(1)}, u32[]{:S(2)}, u32[]{:S(2)}) collective-permute-start(bf16[16,6144]{1,0:T(8,128)(2,1)S(1)} %get-tuple-element.56), channel_id=1, source_target_pairs={{4,0},{5,1},{8,4},{9,5},{12,8},{13,9},{14,12},{15,13},{10,14},{11,... | collective-permute-start | bytes 589832 | tf_op jit(solution)/shard_map/ppermute | solution.py:88
  51.9 7.7 %collective-permute-start.23 = (bf16[16,6144]{1,0:T(8,128)(2,1)S(1)}, bf16[16,6144]{1,0:T(8,128)(2,1)S(1)}, u32[]{:S(2)}, u32[]{:S(2)}) collective-permute-start(bf16[16,6144]{1,0:T(8,128)(2,1)S(1)} %get-tuple-element.57), channel_id=1, source_target_pairs={{0,4},{1,5},{4,8},{5,9},{8,12},{9,13},{12,14},{13,15},{14,10},{15,... | collective-permute-start | bytes 589832 | tf_op jit(solution)/shard_map/ppermute | solution.py:88
  56.2 5.7 %collective-permute-start.21 = (bf16[48,6144]{1,0:T(8,128)(2,1)S(1)}, bf16[48,6144]{1,0:T(8,128)(2,1)S(1)}, u32[]{:S(2)}, u32[]{:S(2)}) collective-permute-start(bf16[48,6144]{1,0:T(8,128)(2,1)S(1)} %slice.126), channel_id=1, source_target_pairs={{0,1},{1,0},{2,3},{3,2},{4,5},{5,4},{6,7},{7,6},{8,9},{9,8},{10,11... | collective-permute-start | bytes 1769480 | tf_op jit(solution)/shard_map/ppermute | solution.py:88
  59.8 7.9 %collective-permute-start.24 = (bf16[16,6144]{1,0:T(8,128)(2,1)S(1)}, bf16[16,6144]{1,0:T(8,128)(2,1)S(1)}, u32[]{:S(2)}, u32[]{:S(2)}) collective-permute-start(bf16[16,6144]{1,0:T(8,128)(2,1)S(1)} %fusion.14), channel_id=1, source_target_pairs={{4,0},{5,1},{8,4},{9,5},{12,8},{13,9},{14,12},{15,13},{10,14},{11,... | collective-permute-start | bytes 589832 | tf_op jit(solution)/shard_map/ppermute | solution.py:88
  61.5 7.7 %collective-permute-start.25 = (bf16[16,6144]{1,0:T(8,128)(2,1)S(1)}, bf16[16,6144]{1,0:T(8,128)(2,1)S(1)}, u32[]{:S(2)}, u32[]{:S(2)}) collective-permute-start(bf16[16,6144]{1,0:T(8,128)(2,1)S(1)} %fusion.13), channel_id=1, source_target_pairs={{0,4},{1,5},{4,8},{5,9},{8,12},{9,13},{12,14},{13,15},{14,10},{15,... | collective-permute-start | bytes 589832 | tf_op jit(solution)/shard_map/ppermute | solution.py:88
  62.1 10.6 %collective-permute-start.31 = (bf16[16,6144]{1,0:T(8,128)(2,1)S(1)}, bf16[16,6144]{1,0:T(8,128)(2,1)S(1)}, u32[]{:S(2)}, u32[]{:S(2)}) collective-permute-start(bf16[16,6144]{1,0:T(8,128)(2,1)S(1)} %get-tuple-element.69), channel_id=1, source_target_pairs={{0,4},{1,5},{4,8},{5,9},{8,12},{9,13},{12,14},{13,15},{14,10},{15,... | collective-permute-start | bytes 589832 | tf_op jit(solution)/shard_map/ppermute | solution.py:88
  63.9 8.9 %collective-permute-start.29 = (bf16[80,6144]{1,0:T(8,128)(2,1)S(1)}, bf16[80,6144]{1,0:T(8,128)(2,1)S(1)}, u32[]{:S(2)}, u32[]{:S(2)}) collective-permute-start(bf16[80,6144]{1,0:T(8,128)(2,1)S(1)} %slice.133), channel_id=1, source_target_pairs={{0,1},{1,0},{2,3},{3,2},{4,5},{5,4},{6,7},{7,6},{8,9},{9,8},{10,11... | collective-permute-start | bytes 2949128 | tf_op jit(solution)/shard_map/ppermute | solution.py:88
  64.0 9.0 %collective-permute-start.30 = (bf16[16,6144]{1,0:T(8,128)(2,1)S(1)}, bf16[16,6144]{1,0:T(8,128)(2,1)S(1)}, u32[]{:S(2)}, u32[]{:S(2)}) collective-permute-start(bf16[16,6144]{1,0:T(8,128)(2,1)S(1)} %get-tuple-element.68), channel_id=1, source_target_pairs={{4,0},{5,1},{8,4},{9,5},{12,8},{13,9},{14,12},{15,13},{10,14},{11,... | collective-permute-start | bytes 589832 | tf_op jit(solution)/shard_map/ppermute | solution.py:88
  73.1 7.9 %collective-permute-start.32 = (bf16[16,6144]{1,0:T(8,128)(2,1)S(1)}, bf16[16,6144]{1,0:T(8,128)(2,1)S(1)}, u32[]{:S(2)}, u32[]{:S(2)}) collective-permute-start(bf16[16,6144]{1,0:T(8,128)(2,1)S(1)} %fusion.8), channel_id=1, source_target_pairs={{4,0},{5,1},{8,4},{9,5},{12,8},{13,9},{14,12},{15,13},{10,14},{11,... | collective-permute-start | bytes 589832 | tf_op jit(solution)/shard_map/ppermute | solution.py:88
  74.7 7.8 %collective-permute-start.33 = (bf16[16,6144]{1,0:T(8,128)(2,1)S(1)}, bf16[16,6144]{1,0:T(8,128)(2,1)S(1)}, u32[]{:S(2)}, u32[]{:S(2)}) collective-permute-start(bf16[16,6144]{1,0:T(8,128)(2,1)S(1)} %fusion.7), channel_id=1, source_target_pairs={{0,4},{1,5},{4,8},{5,9},{8,12},{9,13},{12,14},{13,15},{14,10},{15,... | collective-permute-start | bytes 589832 | tf_op jit(solution)/shard_map/ppermute | solution.py:88
  75.2 8.3 %collective-permute-start.26 = (bf16[16,6144]{1,0:T(8,128)(2,1)S(1)}, bf16[16,6144]{1,0:T(8,128)(2,1)S(1)}, u32[]{:S(2)}, u32[]{:S(2)}) collective-permute-start(bf16[16,6144]{1,0:T(8,128)(2,1)S(1)} %get-tuple-element.66), channel_id=1, source_target_pairs={{4,0},{5,1},{8,4},{9,5},{12,8},{13,9},{14,12},{15,13},{10,14},{11,... | collective-permute-start | bytes 589832 | tf_op jit(solution)/shard_map/ppermute | solution.py:88
  76.9 14.4 %collective-permute-start.28 = (bf16[16,6144]{1,0:T(8,128)(2,1)S(1)}, bf16[16,6144]{1,0:T(8,128)(2,1)S(1)}, u32[]{:S(2)}, u32[]{:S(2)}) collective-permute-start(bf16[16,6144]{1,0:T(8,128)(2,1)S(1)} %get-tuple-element.67), channel_id=1, source_target_pairs={{0,4},{1,5},{4,8},{5,9},{8,12},{9,13},{12,14},{13,15},{14,10},{15,... | collective-permute-start | bytes 589832 | tf_op jit(solution)/shard_map/ppermute | solution.py:88
  82.6 8.1 %collective-permute-start.35 = (bf16[16,6144]{1,0:T(8,128)(2,1)S(1)}, bf16[16,6144]{1,0:T(8,128)(2,1)S(1)}, u32[]{:S(2)}, u32[]{:S(2)}) collective-permute-start(bf16[16,6144]{1,0:T(8,128)(2,1)S(1)} %get-tuple-element.75), channel_id=1, source_target_pairs={{0,4},{1,5},{4,8},{5,9},{8,12},{9,13},{12,14},{13,15},{14,10},{15,... | collective-permute-start | bytes 589832 | tf_op jit(solution)/shard_map/ppermute | solution.py:88
  83.6 7.7 %collective-permute-start.27 = (bf16[16,6144]{1,0:T(8,128)(2,1)S(1)}, bf16[16,6144]{1,0:T(8,128)(2,1)S(1)}, u32[]{:S(2)}, u32[]{:S(2)}) collective-permute-start(bf16[16,6144]{1,0:T(8,128)(2,1)S(1)} %fusion.16), channel_id=1, source_target_pairs={{4,0},{5,1},{8,4},{9,5},{12,8},{13,9},{14,12},{15,13},{10,14},{11,... | collective-permute-start | bytes 589832 | tf_op jit(solution)/shard_map/ppermute | solution.py:88
  85.2 13.1 %copy-start.1 = (bf16[128,6144]{1,0:T(8,128)(2,1)S(1)}, bf16[128,6144]{1,0:T(8,128)(2,1)}, u32[]{:S(2)}) copy-start(bf16[128,6144]{1,0:T(8,128)(2,1)} %param.8) | copy-start | bytes 4718596
  89.1 5.7 %collective-permute-start.34 = (bf16[16,6144]{1,0:T(8,128)(2,1)S(1)}, bf16[16,6144]{1,0:T(8,128)(2,1)S(1)}, u32[]{:S(2)}, u32[]{:S(2)}) collective-permute-start(bf16[16,6144]{1,0:T(8,128)(2,1)S(1)} %get-tuple-element.74), channel_id=1, source_target_pairs={{4,0},{5,1},{8,4},{9,5},{12,8},{13,9},{14,12},{15,13},{10,14},{11,... | collective-permute-start | bytes 589832 | tf_op jit(solution)/shard_map/ppermute | solution.py:88
  90.8 5.7 %collective-permute-start.36 = (bf16[16,6144]{1,0:T(8,128)(2,1)S(1)}, bf16[16,6144]{1,0:T(8,128)(2,1)S(1)}, u32[]{:S(2)}, u32[]{:S(2)}) collective-permute-start(bf16[16,6144]{1,0:T(8,128)(2,1)S(1)} %fusion.5), channel_id=1, source_target_pairs={{0,4},{1,5},{4,8},{5,9},{8,12},{9,13},{12,14},{13,15},{14,10},{15,... | collective-permute-start | bytes 589832 | tf_op jit(solution)/shard_map/ppermute | solution.py:88

commit v10 on v6

--- a/solution.py
+++ b/solution.py
@@ -108,9 +108,9 @@
         far_x = far_block(held_xr, held_xl)
         early_x = permute(jnp.concatenate(got_x, axis=0), core_pairs)
         late_x = permute(far_x, core_pairs)
+        chip_d, late_x = lax.optimization_barrier((jnp.concatenate(got_d, axis=0), late_x))
         rows_x = jnp.concatenate(got_x + [far_x, early_x, late_x], axis=0)
-        chip_d = jnp.concatenate(got_d, axis=0)
-        return rows_x, jnp.concatenate([chip_d, permute(chip_d, core_pairs)], axis=0)
+        return rows_x, jnp.concatenate(got_d + [permute(chip_d, core_pairs)], axis=0)
 
     cut = max(2 * steps - 3, 1) * CAP
 
@@ -199,7 +199,7 @@
             if at <= steps:
                 out_carry.update(send(wave(out_total, out_carry, at, "l")))
             dx_blocks = wave(dx_total, dx_carry, at - 1, "r")
-            if work and at in (2, 3, steps + 1):
+            if work:
                 side, rows = work.pop(0)
                 side, dx_blocks = tie(side, dx_blocks)
                 grad, mark = weight_grad(side, rows, d, marks)

time: 96.5 us -> 96.6 us (level)
  transfers between devices with their start and end apart: 37 -> 37, of which waited for: 21 -> 19; matrix products, arithmetic and copies ran while one was open for 16% -> 16% of each run, Pallas kernels for 11% -> 11%
where the time goes in v10:
time: 96.6 us; the launch traced here: 96.3 us
  starting transfers between devices  33.9 us (35%)
  waiting for transfers between devices  29.9 us (31%)
  matrix products  15 us (16%)
  Pallas kernels  10.4 us (11%)
  local copies, waits for them, and re-layouts  3.59 us (4%)
  other arithmetic  2.47 us (3%)
  between operations  1.1 us (1%)
    ppermute x37, starting transfers between devices, permute(): return lax.ppermute(x, 'et', pairs)  33.9 us
    ppermute x37, waiting for transfers between devices, permute(): return lax.ppermute(x, 'et', pairs)  29.9 us
    pallas_call x3, Pallas kernels, weight_grad(): pl.pallas_call(lambda *refs: grad_kernel(parts, width, len(marks), *refs)...  10.4 us
    dot_general x2, matrix products, per_device(): jnp.dot(select.T, final(total[0], carry), preferred_element_type=jnp.floa...  3.53 us
    unnamed x26, local copies, waits for them, and re-layouts  2.54 us
    dot_general x3, matrix products, per_device(): jnp.dot(select, a, preferred_element_type=jnp.float32).astype(jnp.bfloat16)  2.15 us
  transfers between devices with their start and end apart: 37, of which 19 were waited for; matrix products, arithmetic and copies ran while one was open for 16% of the time, Pallas kernels for 11%

profile of v10, /device:TPU:0, one launch (start us, length us, event | category | flops | bytes accessed | tf_op | source)
XLA Modules:
  0.0 96.3 jit_solution(9068269745051893149)
XLA Ops:
  0.6 0.8 select_reduce_fusion
  2.1 0.3 constant_dynamic-update-slice_fusion.32
  2.4 3.0 %collective-permute-start.10 = (bf16[16,6144]{1,0:T(8,128)(2,1)S(1)}, bf16[16,6144]{1,0:T(8,128)(2,1)S(1)}, u32[]{:S(2)}, u32[]{:S(2)}) collective-permute-start(bf16[16,6144]{1,0:T(8,128)(2,1)S(1)} %get-tuple-element.134), channel_id=1, source_target_pairs={{4,0},{5,1},{8,4},{9,5},{12,8},{13,9},{14,12},{15,13},{10,14},{11,... | collective-permute-start | bytes 589832 | tf_op jit(solution)/shard_map/ppermute | solution.py:88
  5.7 1.7 %convolution_convert_fusion.3 = bf16[16,6144]{1,0:T(8,128)(2,1)S(1)} fusion(bf16[128,6144]{1,0:T(8,128)(2,1)} %param.7, s32[128]{0:T(128)S(1)} %add_reduce_fusion, pred[128]{0:T(512)(128)(4,1)S(1)} %reduce_or.9), kind=kOutput, calls=%fused_computation.4 | convolution fusion | flops 25268224 | bytes 1770112 | tf_op jit(solution)/shard_map/dot_general | solution.py:161
  7.5 2.0 %collective-permute-start = (bf16[16,6272]{1,0:T(8,128)(2,1)S(1)}, bf16[16,6272]{1,0:T(8,128)(2,1)S(1)}, u32[]{:S(2)}, u32[]{:S(2)}) collective-permute-start(bf16[16,6272]{1,0:T(8,128)(2,1)S(1)} %get-tuple-element.119), channel_id=1, source_target_pairs={{0,4},{1,5},{4,8},{5,9},{8,12},{9,13},{12,14},{13,15},{14,10},{15,... | collective-permute-start | bytes 602120 | tf_op jit(solution)/shard_map/ppermute | solution.py:88
  9.6 0.8 collective-permute-done.10
  10.4 2.2 %collective-permute-start.12 = (bf16[16,6144]{1,0:T(8,128)(2,1)S(1)}, bf16[16,6144]{1,0:T(8,128)(2,1)S(1)}, u32[]{:S(2)}, u32[]{:S(2)}) collective-permute-start(bf16[16,6144]{1,0:T(8,128)(2,1)S(1)} %collective-permute-done.10), channel_id=1, source_target_pairs={{4,0},{5,1},{8,4},{9,5},{12,8},{13,9},{14,12},{15,13},{10,14},{11,... | collective-permute-start | bytes 589832 | tf_op jit(solution)/shard_map/ppermute | solution.py:88
  12.6 0.7 collective-permute-done.9
  13.3 4.2 %collective-permute-done = bf16[16,6272]{1,0:T(8,128)(2,1)S(1)} collective-permute-done((bf16[16,6272]{1,0:T(8,128)(2,1)S(1)}, bf16[16,6272]{1,0:T(8,128)(2,1)S(1)}, u32[]{:S(2)}, u32[]{:S(2)}) %collective-permute-start) | collective-permute-done | bytes 200736 | tf_op jit(solution)/shard_map/ppermute | solution.py:88
  17.5 2.0 %collective-permute-start.3 = (bf16[16,6272]{1,0:T(8,128)(2,1)S(1)}, bf16[16,6272]{1,0:T(8,128)(2,1)S(1)}, u32[]{:S(2)}, u32[]{:S(2)}) collective-permute-start(bf16[16,6272]{1,0:T(8,128)(2,1)S(1)} %collective-permute-done.1), channel_id=1, source_target_pairs={{4,0},{5,1},{8,4},{9,5},{12,8},{13,9},{14,12},{15,13},{10,14},{11,... | collective-permute-start | bytes 602120 | tf_op jit(solution)/shard_map/ppermute | solution.py:88
  19.6 1.5 %collective-permute-done.12 = bf16[16,6144]{1,0:T(8,128)(2,1)S(1)} collective-permute-done((bf16[16,6144]{1,0:T(8,128)(2,1)S(1)}, bf16[16,6144]{1,0:T(8,128)(2,1)S(1)}, u32[]{:S(2)}, u32[]{:S(2)}) %collective-permute-start.12) | collective-permute-done | bytes 196640 | tf_op jit(solution)/shard_map/ppermute | solution.py:88
  21.2 0.6 collective-permute-start.14
  21.8 1.4 %collective-permute-start.13 = (bf16[16,6144]{1,0:T(8,128)(2,1)S(1)}, bf16[16,6144]{1,0:T(8,128)(2,1)S(1)}, u32[]{:S(2)}, u32[]{:S(2)}) collective-permute-start(bf16[16,6144]{1,0:T(8,128)(2,1)S(1)} %collective-permute-done.11), channel_id=1, source_target_pairs={{0,4},{1,5},{4,8},{5,9},{8,12},{9,13},{12,14},{13,15},{14,10},{15,... | collective-permute-start | bytes 589832 | tf_op jit(solution)/shard_map/ppermute | solution.py:88
  23.3 2.8 %collective-permute-done.2 = bf16[16,6272]{1,0:T(8,128)(2,1)S(1)} collective-permute-done((bf16[16,6272]{1,0:T(8,128)(2,1)S(1)}, bf16[16,6272]{1,0:T(8,128)(2,1)S(1)}, u32[]{:S(2)}, u32[]{:S(2)}) %collective-permute-start.2) | collective-permute-done | bytes 200736 | tf_op jit(solution)/shard_map/ppermute | solution.py:88
  26.1 2.0 %collective-permute-start.5 = (bf16[16,6272]{1,0:T(8,128)(2,1)S(1)}, bf16[16,6272]{1,0:T(8,128)(2,1)S(1)}, u32[]{:S(2)}, u32[]{:S(2)}) collective-permute-start(bf16[16,6272]{1,0:T(8,128)(2,1)S(1)} %collective-permute-done.3), channel_id=1, source_target_pairs={{4,0},{5,1},{8,4},{9,5},{12,8},{13,9},{14,12},{15,13},{10,14},{11,... | collective-permute-start | bytes 602120 | tf_op jit(solution)/shard_map/ppermute | solution.py:88
  28.2 1.5 %collective-permute-done.14 = bf16[16,6144]{1,0:T(8,128)(2,1)S(1)} collective-permute-done((bf16[16,6144]{1,0:T(8,128)(2,1)S(1)}, bf16[16,6144]{1,0:T(8,128)(2,1)S(1)}, u32[]{:S(2)}, u32[]{:S(2)}) %collective-permute-start.14) | collective-permute-done | bytes 196640 | tf_op jit(solution)/shard_map/ppermute | solution.py:88
  29.7 0.9 collective-permute-start.16
  30.6 1.2 %collective-permute-start.15 = (bf16[16,3072]{1,0:T(8,128)(2,1)S(1)}, bf16[16,3072]{1,0:T(8,128)(2,1)S(1)}, u32[]{:S(2)}, u32[]{:S(2)}) collective-permute-start(bf16[16,3072]{1,0:T(8,128)(2,1)S(1)} %slice.142), channel_id=1, source_target_pairs={{0,4},{1,5},{4,8},{5,9},{8,12},{9,13},{12,14},{13,15},{14,10},{15,... | collective-permute-start | bytes 294920 | tf_op jit(solution)/shard_map/ppermute | solution.py:88
  31.9 2.3 %collective-permute-done.4 = bf16[16,6272]{1,0:T(8,128)(2,1)S(1)} collective-permute-done((bf16[16,6272]{1,0:T(8,128)(2,1)S(1)}, bf16[16,6272]{1,0:T(8,128)(2,1)S(1)}, u32[]{:S(2)}, u32[]{:S(2)}) %collective-permute-start.4) | collective-permute-done | bytes 200736 | tf_op jit(solution)/shard_map/ppermute | solution.py:88
  34.2 0.5 collective-permute-start.6
  34.7 1.7 %collective-permute-start.7 = (bf16[16,3200]{1,0:T(8,128)(2,1)S(1)}, bf16[16,3200]{1,0:T(8,128)(2,1)S(1)}, u32[]{:S(2)}, u32[]{:S(2)}) collective-permute-start(bf16[16,3200]{1,0:T(8,128)(2,1)S(1)} %slice.141), channel_id=1, source_target_pairs={{4,0},{5,1},{8,4},{9,5},{12,8},{13,9},{14,12},{15,13},{10,14},{11,... | collective-permute-start | bytes 307208 | tf_op jit(solution)/shard_map/ppermute | solution.py:88
  36.6 2.3 %collective-permute-done.6 = bf16[16,3072]{1,0:T(8,128)(2,1)S(1)} collective-permute-done((bf16[16,3072]{1,0:T(8,128)(2,1)S(1)}, bf16[16,3072]{1,0:T(8,128)(2,1)S(1)}, u32[]{:S(2)}, u32[]{:S(2)}) %collective-permute-start.6) | collective-permute-done | bytes 98336 | tf_op jit(solution)/shard_map/ppermute | solution.py:88
  38.9 0.5 collective-permute-done.7
  39.5 1.4 %collective-permute-done.17 = bf16[16,6272]{1,0:T(8,128)(2,1)S(1)} collective-permute-done((bf16[16,6272]{1,0:T(8,128)(2,1)S(1)}, bf16[16,6272]{1,0:T(8,128)(2,1)S(1)}, u32[]{:S(2)}, u32[]{:S(2)}) %collective-permute-start.17) | collective-permute-done | bytes 200736 | tf_op jit(solution)/shard_map/ppermute | solution.py:88
  41.4 1.3 %fusion.2 = f32[256,336]{0,1:T(8,128)S(1)} fusion(bf16[6144,336]{0,1:T(8,128)(2,1)S(1)} %copy-done.3, bf16[256,6272]{1,0:T(8,128)(2,1)S(1)} %constant_dynamic-update-slice_fusion.14.refs_1_), kind=kOutput, calls=%fused_computation.9 | convolution fusion | flops 1056964608 | bytes 7618560 | tf_op jit(solution)/shard_map/dot_general | solution.py:172
  42.6 0.9 copy-done.4
  43.5 1.3 %multiply_convert_fusion.2 = (bf16[256,336]{0,1:T(8,128)(2,1)S(1)}, f32[256,336]{0,1:T(8,128)S(1)}) fusion(f32[256]{0:T(256)S(1)} %convert_reduce_fusion, f32[256,336]{0,1:T(8,128)S(1)} %fusion.2, bf16[6144,336]{0,1:T(8,128)(2,1)S(1)} %copy-done.4, bf16[256,6272]{1,0:T(8,128)(2,1)S(1)} %constant_dynamic-update-slice_fusion.14.refs_1_), kind=kOutput, calls=%fused_computation.46 | convolution fusion | flops 1057566720 | bytes 8135680 | tf_op jit(solution)/shard_map/dot_general | solution.py:173
  44.8 0.9 copy-done.2
  45.7 1.8 %fusion.42 = f32[256,6144]{1,0:T(8,128)S(1)} fusion(bf16[256,336]{0,1:T(8,128)(2,1)S(1)} %get-tuple-element.86, bf16[336,6144]{1,0:T(8,128)(2,1)S(1)} %copy-done.2), kind=kOutput, calls=%fused_computation.109 | convolution fusion | flops 1056964608 | bytes 10592256 | tf_op jit(solution)/shard_map/dot_general | solution.py:177
  47.5 0.2 slice.222
  47.9 0.4 collective-permute-start.20
  48.5 0.2 collective-permute-start.19
  48.7 1.3 %multiply_convert_fusion = (bf16[256,336]{0,1:T(8,128)(2,1)S(1)}, bf16[256,336]{0,1:T(8,128)(2,1)S(1)}) fusion(f32[256,336]{0,1:T(8,128)S(1)} %fusion.2, f32[256,336]{0,1:T(8,128)S(1)} %get-tuple-element.136, bf16[256,6144]{1,0:T(8,128)(2,1)S(1)} %constant_dynamic-update-slice_fusion.24.refs_1_, bf16[336,6144]{1,0:T(8,128)(2,1)S(1)} %copy-done.2, ...), kind=kOutput, calls=%fused_computation.44 | convolution fusion | flops 1058168832 | bytes 8307712 | tf_op jit(solution)/shard_map/dot_general | solution.py:182
  50.2 1.7 %collective-permute-start.21 = (bf16[16,6144]{1,0:T(8,128)(2,1)S(1)}, bf16[16,6144]{1,0:T(8,128)(2,1)S(1)}, u32[]{:S(2)}, u32[]{:S(2)}) collective-permute-start(bf16[16,6144]{1,0:T(8,128)(2,1)S(1)} %get-tuple-element.54), channel_id=1, source_target_pairs={{4,0},{5,1},{8,4},{9,5},{12,8},{13,9},{14,12},{15,13},{10,14},{11,... | collective-permute-start | bytes 589832 | tf_op jit(solution)/shard_map/ppermute | solution.py:88
  51.9 0.4 collective-permute-start.22
  52.3 1.8 %fusion.43 = f32[256,6144]{1,0:T(8,128)S(1)} fusion(bf16[256,336]{0,1:T(8,128)(2,1)S(1)} %get-tuple-element.64, bf16[6144,336]{0,1:T(8,128)(2,1)S(1)} %copy-done.3), kind=kOutput, calls=%fused_computation.110 | convolution fusion | flops 1056964608 | bytes 10592256 | tf_op jit(solution)/shard_map/dot_general | solution.py:188
  54.1 1.8 %convolution_add_fusion = f32[256,6144]{1,0:T(8,128)S(1)} fusion(f32[256,6144]{1,0:T(8,128)S(1)} %fusion.43, bf16[256,336]{0,1:T(8,128)(2,1)S(1)} %get-tuple-element.63, bf16[6144,336]{0,1:T(8,128)(2,1)S(1)} %copy-done.4), kind=kOutput, calls=%fused_computation | convolution fusion | flops 1058537472 | bytes 16883712 | tf_op jit(solution)/shard_map/dot_general | solution.py:188
  56.0 0.2 slice.221
  56.1 1.3 %collective-permute-done.21 = bf16[16,6144]{1,0:T(8,128)(2,1)S(1)} collective-permute-done((bf16[16,6144]{1,0:T(8,128)(2,1)S(1)}, bf16[16,6144]{1,0:T(8,128)(2,1)S(1)}, u32[]{:S(2)}, u32[]{:S(2)}) %collective-permute-start.21) | collective-permute-done | bytes 196640 | tf_op jit(solution)/shard_map/ppermute | solution.py:88
  57.4 1.3 %collective-permute-done.22 = bf16[16,6144]{1,0:T(8,128)(2,1)S(1)} collective-permute-done((bf16[16,6144]{1,0:T(8,128)(2,1)S(1)}, bf16[16,6144]{1,0:T(8,128)(2,1)S(1)}, u32[]{:S(2)}, u32[]{:S(2)}) %collective-permute-start.22) | collective-permute-done | bytes 196640 | tf_op jit(solution)/shard_map/ppermute | solution.py:88
  59.0 0.5 collective-permute-start.23
  59.8 1.6 %collective-permute-start.27 = (bf16[16,6144]{1,0:T(8,128)(2,1)S(1)}, bf16[16,6144]{1,0:T(8,128)(2,1)S(1)}, u32[]{:S(2)}, u32[]{:S(2)}) collective-permute-start(bf16[16,6144]{1,0:T(8,128)(2,1)S(1)} %fusion.13), channel_id=1, source_target_pairs={{4,0},{5,1},{8,4},{9,5},{12,8},{13,9},{14,12},{15,13},{10,14},{11,... | collective-permute-start | bytes 589832 | tf_op jit(solution)/shard_map/ppermute | solution.py:88
  61.4 0.4 collective-permute-start.28
  62.0 1.6 %collective-permute-start.25 = (bf16[16,6144]{1,0:T(8,128)(2,1)S(1)}, bf16[16,6144]{1,0:T(8,128)(2,1)S(1)}, u32[]{:S(2)}, u32[]{:S(2)}) collective-permute-start(bf16[16,6144]{1,0:T(8,128)(2,1)S(1)} %get-tuple-element.59), channel_id=1, source_target_pairs={{4,0},{5,1},{8,4},{9,5},{12,8},{13,9},{14,12},{15,13},{10,14},{11,... | collective-permute-start | bytes 589832 | tf_op jit(solution)/shard_map/ppermute | solution.py:88
  63.7 0.4 collective-permute-start.26
  64.1 3.3 %shard_map.110 = (bf16[336,6144]{1,0:T(8,128)(2,1)}, f32[8,128]{1,0:T(8,128)S(1)}) custom-call(bf16[336,256]{1,0:T(8,128)(2,1)S(1)} %bitcast.27, bf16[256,6272]{1,0:T(8,128)(2,1)S(1)} %constant_dynamic-update-slice_fusion.14.refs_1_), custom_call_target="tpu_custom_call" | custom-call | flops 1056964608 | bytes 7274496 | tf_op jit(solution)/shard_map/pallas_call | solution.py:54
  67.6 1.6 %collective-permute-done.28 = bf16[16,6144]{1,0:T(8,128)(2,1)S(1)} collective-permute-done((bf16[16,6144]{1,0:T(8,128)(2,1)S(1)}, bf16[16,6144]{1,0:T(8,128)(2,1)S(1)}, u32[]{:S(2)}, u32[]{:S(2)}) %collective-permute-start.28) | collective-permute-done | bytes 196640 | tf_op jit(solution)/shard_map/ppermute | solution.py:88
  69.3 1.6 %collective-permute-start.29 = (bf16[16,6144]{1,0:T(8,128)(2,1)S(1)}, bf16[16,6144]{1,0:T(8,128)(2,1)S(1)}, u32[]{:S(2)}, u32[]{:S(2)}) collective-permute-start(bf16[16,6144]{1,0:T(8,128)(2,1)S(1)} %get-tuple-element.74), channel_id=1, source_target_pairs={{4,0},{5,1},{8,4},{9,5},{12,8},{13,9},{14,12},{15,13},{10,14},{11,... | collective-permute-start | bytes 589832 | tf_op jit(solution)/shard_map/ppermute | solution.py:88
  70.9 0.4 collective-permute-start.30
  71.3 2.1 %collective-permute-done.26 = bf16[16,6144]{1,0:T(8,128)(2,1)S(1)} collective-permute-done((bf16[16,6144]{1,0:T(8,128)(2,1)S(1)}, bf16[16,6144]{1,0:T(8,128)(2,1)S(1)}, u32[]{:S(2)}, u32[]{:S(2)}) %collective-permute-start.26) | collective-permute-done | bytes 196640 | tf_op jit(solution)/shard_map/ppermute | solution.py:88
  73.4 0.2 slice_add_fusion
  73.7 1.6 %collective-permute-start.32 = (bf16[16,6144]{1,0:T(8,128)(2,1)S(1)}, bf16[16,6144]{1,0:T(8,128)(2,1)S(1)}, u32[]{:S(2)}, u32[]{:S(2)}) collective-permute-start(bf16[16,6144]{1,0:T(8,128)(2,1)S(1)} %fusion.15), channel_id=1, source_target_pairs={{4,0},{5,1},{8,4},{9,5},{12,8},{13,9},{14,12},{15,13},{10,14},{11,... | collective-permute-start | bytes 589832 | tf_op jit(solution)/shard_map/ppermute | solution.py:88
  75.4 0.4 collective-permute-start.33
  75.8 3.3 %shard_map.111 = (bf16[336,6144]{1,0:T(8,128)(2,1)}, f32[8,128]{1,0:T(8,128)S(1)}) custom-call(bf16[336,256]{1,0:T(8,128)(2,1)S(1)} %bitcast.28, bf16[256,6272]{1,0:T(8,128)(2,1)S(1)} %constant_dynamic-update-slice_fusion.14.refs_1_, f32[8,128]{1,0:T(8,128)S(1)} %get-tuple-element.70.refs_2_), custom_call_target="tpu_custom_call" | custom-call | flops 1056964608 | bytes 7274496 | tf_op jit(solution)/shard_map/pallas_call | solution.py:54
  79.1 0.3 collective-permute-done.32
  79.5 1.6 %collective-permute-done.33 = bf16[16,6144]{1,0:T(8,128)(2,1)S(1)} collective-permute-done((bf16[16,6144]{1,0:T(8,128)(2,1)S(1)}, bf16[16,6144]{1,0:T(8,128)(2,1)S(1)}, u32[]{:S(2)}, u32[]{:S(2)}) %collective-permute-start.33) | collective-permute-done | bytes 196640 | tf_op jit(solution)/shard_map/ppermute | solution.py:88
  81.1 0.5 collective-permute-start.35
  81.7 1.6 %collective-permute-start.31 = (bf16[16,6144]{1,0:T(8,128)(2,1)S(1)}, bf16[16,6144]{1,0:T(8,128)(2,1)S(1)}, u32[]{:S(2)}, u32[]{:S(2)}) collective-permute-start(bf16[16,6144]{1,0:T(8,128)(2,1)S(1)} %fusion.16), channel_id=1, source_target_pairs={{4,0},{5,1},{8,4},{9,5},{12,8},{13,9},{14,12},{15,13},{10,14},{11,... | collective-permute-start | bytes 589832 | tf_op jit(solution)/shard_map/ppermute | solution.py:88
  83.3 1.6 %collective-permute-start.34 = (bf16[16,6144]{1,0:T(8,128)(2,1)S(1)}, bf16[16,6144]{1,0:T(8,128)(2,1)S(1)}, u32[]{:S(2)}, u32[]{:S(2)}) collective-permute-start(bf16[16,6144]{1,0:T(8,128)(2,1)S(1)} %get-tuple-element.82), channel_id=1, source_target_pairs={{4,0},{5,1},{8,4},{9,5},{12,8},{13,9},{14,12},{15,13},{10,14},{11,... | collective-permute-start | bytes 589832 | tf_op jit(solution)/shard_map/ppermute | solution.py:88
  84.9 3.9 %shard_map.112 = (bf16[336,6144]{1,0:T(8,128)(2,1)}, f32[8,128]{1,0:T(8,128)}) custom-call(bf16[336,256]{1,0:T(8,128)(2,1)S(1)} %bitcast.26, bf16[256,6144]{1,0:T(8,128)(2,1)S(1)} %constant_dynamic-update-slice_fusion.24.refs_1_, f32[8,128]{1,0:T(8,128)S(1)} %get-tuple-element.87.refs_2_), custom_call_target="tpu_custom_call" | custom-call | flops 1056964608 | bytes 7274496 | tf_op jit(solution)/shard_map/pallas_call | solution.py:54
  88.8 0.5 collective-permute-start.36
  89.3 1.8 %convolution_convert_fusion.1 = bf16[128,6144]{1,0:T(8,128)(2,1)} fusion(f32[80,6144]{1,0:T(8,128)S(1)} %slice_add_fusion.1, bf16[16,6144]{1,0:T(8,128)(2,1)S(1)} %collective-permute-done.30, bf16[16,6144]{1,0:T(8,128)(2,1)S(1)} %collective-permute-done.31, s32[128]{0:T(128)S(1)} %add_reduce_fusion, pred[128]{0:T(512)(128)(4,1)S(1)} %reduce_or.9), kind=kOutput, calls=%fused_computation.2 | convolution fusion | flops 26447872 | bytes 2360320 | tf_op jit(solution)/shard_map/dot_general | solution.py:215
  91.1 3.5 %collective-permute-done.36 = bf16[16,6144]{1,0:T(8,128)(2,1)S(1)} collective-permute-done((bf16[16,6144]{1,0:T(8,128)(2,1)S(1)}, bf16[16,6144]{1,0:T(8,128)(2,1)S(1)}, u32[]{:S(2)}, u32[]{:S(2)}) %collective-permute-start.36) | collective-permute-done | bytes 196640 | tf_op jit(solution)/shard_map/ppermute | solution.py:88
  94.5 1.8 %convolution_convert_fusion = bf16[128,6144]{1,0:T(8,128)(2,1)} fusion(f32[80,6144]{1,0:T(8,128)S(1)} %slice_add_fusion, bf16[16,6144]{1,0:T(8,128)(2,1)S(1)} %collective-permute-done.36, bf16[16,6144]{1,0:T(8,128)(2,1)S(1)} %collective-permute-done.34, s32[128]{0:T(128)S(1)} %add_reduce_fusion, pred[128]{0:T(512)(128)(4,1)S(1)} %reduce_or.9), kind=kOutput, calls=%fused_computation.1 | convolution fusion | flops 26447872 | bytes 2360320 | tf_op jit(solution)/shard_map/dot_general | solution.py:215
  (88 shorter events, 3.8 us)
Async XLA Ops:
  0.6 1.4 %copy-start = (bf16[128,6144]{1,0:T(8,128)(2,1)S(1)}, bf16[128,6144]{1,0:T(8,128)(2,1)}, u32[]{:S(2)}) copy-start(bf16[128,6144]{1,0:T(8,128)(2,1)} %param.8) | copy-start | bytes 4718596
  2.4 8.0 %collective-permute-start.10 = (bf16[16,6144]{1,0:T(8,128)(2,1)S(1)}, bf16[16,6144]{1,0:T(8,128)(2,1)S(1)}, u32[]{:S(2)}, u32[]{:S(2)}) collective-permute-start(bf16[16,6144]{1,0:T(8,128)(2,1)S(1)} %get-tuple-element.134), channel_id=1, source_target_pairs={{4,0},{5,1},{8,4},{9,5},{12,8},{13,9},{14,12},{15,13},{10,14},{11,... | collective-permute-start | bytes 589832 | tf_op jit(solution)/shard_map/ppermute | solution.py:88
  5.4 7.8 %collective-permute-start.9 = (bf16[16,6144]{1,0:T(8,128)(2,1)S(1)}, bf16[16,6144]{1,0:T(8,128)(2,1)S(1)}, u32[]{:S(2)}, u32[]{:S(2)}) collective-permute-start(bf16[16,6144]{1,0:T(8,128)(2,1)S(1)} %get-tuple-element.134), channel_id=1, source_target_pairs={{0,4},{1,5},{4,8},{5,9},{8,12},{9,13},{12,14},{13,15},{14,10},{15,... | collective-permute-start | bytes 589832 | tf_op jit(solution)/shard_map/ppermute | solution.py:88
  7.5 10.0 %collective-permute-start = (bf16[16,6272]{1,0:T(8,128)(2,1)S(1)}, bf16[16,6272]{1,0:T(8,128)(2,1)S(1)}, u32[]{:S(2)}, u32[]{:S(2)}) collective-permute-start(bf16[16,6272]{1,0:T(8,128)(2,1)S(1)} %get-tuple-element.119), channel_id=1, source_target_pairs={{0,4},{1,5},{4,8},{5,9},{8,12},{9,13},{12,14},{13,15},{14,10},{15,... | collective-permute-start | bytes 602120 | tf_op jit(solution)/shard_map/ppermute | solution.py:88
  9.5 8.0 %collective-permute-start.1 = (bf16[16,6272]{1,0:T(8,128)(2,1)S(1)}, bf16[16,6272]{1,0:T(8,128)(2,1)S(1)}, u32[]{:S(2)}, u32[]{:S(2)}) collective-permute-start(bf16[16,6272]{1,0:T(8,128)(2,1)S(1)} %get-tuple-element.119), channel_id=1, source_target_pairs={{4,0},{5,1},{8,4},{9,5},{12,8},{13,9},{14,12},{15,13},{10,14},{11,... | collective-permute-start | bytes 602120 | tf_op jit(solution)/shard_map/ppermute | solution.py:88
  10.4 10.8 %collective-permute-start.12 = (bf16[16,6144]{1,0:T(8,128)(2,1)S(1)}, bf16[16,6144]{1,0:T(8,128)(2,1)S(1)}, u32[]{:S(2)}, u32[]{:S(2)}) collective-permute-start(bf16[16,6144]{1,0:T(8,128)(2,1)S(1)} %collective-permute-done.10), channel_id=1, source_target_pairs={{4,0},{5,1},{8,4},{9,5},{12,8},{13,9},{14,12},{15,13},{10,14},{11,... | collective-permute-start | bytes 589832 | tf_op jit(solution)/shard_map/ppermute | solution.py:88
  13.2 8.5 %collective-permute-start.11 = (bf16[16,6144]{1,0:T(8,128)(2,1)S(1)}, bf16[16,6144]{1,0:T(8,128)(2,1)S(1)}, u32[]{:S(2)}, u32[]{:S(2)}) collective-permute-start(bf16[16,6144]{1,0:T(8,128)(2,1)S(1)} %collective-permute-done.9), channel_id=1, source_target_pairs={{0,4},{1,5},{4,8},{5,9},{8,12},{9,13},{12,14},{13,15},{14,10},{15,... | collective-permute-start | bytes 589832 | tf_op jit(solution)/shard_map/ppermute | solution.py:88
  17.5 8.5 %collective-permute-start.2 = (bf16[16,6272]{1,0:T(8,128)(2,1)S(1)}, bf16[16,6272]{1,0:T(8,128)(2,1)S(1)}, u32[]{:S(2)}, u32[]{:S(2)}) collective-permute-start(bf16[16,6272]{1,0:T(8,128)(2,1)S(1)} %collective-permute-done), channel_id=1, source_target_pairs={{0,4},{1,5},{4,8},{5,9},{8,12},{9,13},{12,14},{13,15},{14,10},{15,... | collective-permute-start | bytes 602120 | tf_op jit(solution)/shard_map/ppermute | solution.py:88
  17.5 8.5 %collective-permute-start.3 = (bf16[16,6272]{1,0:T(8,128)(2,1)S(1)}, bf16[16,6272]{1,0:T(8,128)(2,1)S(1)}, u32[]{:S(2)}, u32[]{:S(2)}) collective-permute-start(bf16[16,6272]{1,0:T(8,128)(2,1)S(1)} %collective-permute-done.1), channel_id=1, source_target_pairs={{4,0},{5,1},{8,4},{9,5},{12,8},{13,9},{14,12},{15,13},{10,14},{11,... | collective-permute-start | bytes 602120 | tf_op jit(solution)/shard_map/ppermute | solution.py:88
  21.2 8.5 %collective-permute-start.14 = (bf16[16,6144]{1,0:T(8,128)(2,1)S(1)}, bf16[16,6144]{1,0:T(8,128)(2,1)S(1)}, u32[]{:S(2)}, u32[]{:S(2)}) collective-permute-start(bf16[16,6144]{1,0:T(8,128)(2,1)S(1)} %collective-permute-done.12), channel_id=1, source_target_pairs={{4,0},{5,1},{8,4},{9,5},{12,8},{13,9},{14,12},{15,13},{10,14},{11,... | collective-permute-start | bytes 589832 | tf_op jit(solution)/shard_map/ppermute | solution.py:88
  21.8 8.8 %collective-permute-start.13 = (bf16[16,6144]{1,0:T(8,128)(2,1)S(1)}, bf16[16,6144]{1,0:T(8,128)(2,1)S(1)}, u32[]{:S(2)}, u32[]{:S(2)}) collective-permute-start(bf16[16,6144]{1,0:T(8,128)(2,1)S(1)} %collective-permute-done.11), channel_id=1, source_target_pairs={{0,4},{1,5},{4,8},{5,9},{8,12},{9,13},{12,14},{13,15},{14,10},{15,... | collective-permute-start | bytes 589832 | tf_op jit(solution)/shard_map/ppermute | solution.py:88
  26.1 8.1 %collective-permute-start.4 = (bf16[16,6272]{1,0:T(8,128)(2,1)S(1)}, bf16[16,6272]{1,0:T(8,128)(2,1)S(1)}, u32[]{:S(2)}, u32[]{:S(2)}) collective-permute-start(bf16[16,6272]{1,0:T(8,128)(2,1)S(1)} %collective-permute-done.2), channel_id=1, source_target_pairs={{0,4},{1,5},{4,8},{5,9},{8,12},{9,13},{12,14},{13,15},{14,10},{15,... | collective-permute-start | bytes 602120 | tf_op jit(solution)/shard_map/ppermute | solution.py:88
  26.1 8.6 %collective-permute-start.5 = (bf16[16,6272]{1,0:T(8,128)(2,1)S(1)}, bf16[16,6272]{1,0:T(8,128)(2,1)S(1)}, u32[]{:S(2)}, u32[]{:S(2)}) collective-permute-start(bf16[16,6272]{1,0:T(8,128)(2,1)S(1)} %collective-permute-done.3), channel_id=1, source_target_pairs={{4,0},{5,1},{8,4},{9,5},{12,8},{13,9},{14,12},{15,13},{10,14},{11,... | collective-permute-start | bytes 602120 | tf_op jit(solution)/shard_map/ppermute | solution.py:88
  29.7 6.8 %collective-permute-start.16 = (bf16[16,3072]{1,0:T(8,128)(2,1)S(1)}, bf16[16,3072]{1,0:T(8,128)(2,1)S(1)}, u32[]{:S(2)}, u32[]{:S(2)}) collective-permute-start(bf16[16,3072]{1,0:T(8,128)(2,1)S(1)} %slice.143), channel_id=1, source_target_pairs={{4,0},{5,1},{8,4},{9,5},{12,8},{13,9},{14,12},{15,13},{10,14},{11,... | collective-permute-start | bytes 294920 | tf_op jit(solution)/shard_map/ppermute | solution.py:88
  30.6 5.9 %collective-permute-start.15 = (bf16[16,3072]{1,0:T(8,128)(2,1)S(1)}, bf16[16,3072]{1,0:T(8,128)(2,1)S(1)}, u32[]{:S(2)}, u32[]{:S(2)}) collective-permute-start(bf16[16,3072]{1,0:T(8,128)(2,1)S(1)} %slice.142), channel_id=1, source_target_pairs={{0,4},{1,5},{4,8},{5,9},{8,12},{9,13},{12,14},{13,15},{14,10},{15,... | collective-permute-start | bytes 294920 | tf_op jit(solution)/shard_map/ppermute | solution.py:88
  34.2 7.2 %copy-start.3 = (bf16[6144,336]{0,1:T(8,128)(2,1)S(1)}, bf16[6144,336]{0,1:T(8,128)(2,1)}, u32[]{:S(2)}) copy-start(bf16[6144,336]{0,1:T(8,128)(2,1)} %param.11) | copy-start | bytes 12386308
  34.2 4.7 %collective-permute-start.6 = (bf16[16,3072]{1,0:T(8,128)(2,1)S(1)}, bf16[16,3072]{1,0:T(8,128)(2,1)S(1)}, u32[]{:S(2)}, u32[]{:S(2)}) collective-permute-start(bf16[16,3072]{1,0:T(8,128)(2,1)S(1)} %slice.140), channel_id=1, source_target_pairs={{0,4},{1,5},{4,8},{5,9},{8,12},{9,13},{12,14},{13,15},{14,10},{15,... | collective-permute-start | bytes 294920 | tf_op jit(solution)/shard_map/ppermute | solution.py:88
  34.7 4.7 %collective-permute-start.7 = (bf16[16,3200]{1,0:T(8,128)(2,1)S(1)}, bf16[16,3200]{1,0:T(8,128)(2,1)S(1)}, u32[]{:S(2)}, u32[]{:S(2)}) collective-permute-start(bf16[16,3200]{1,0:T(8,128)(2,1)S(1)} %slice.141), channel_id=1, source_target_pairs={{4,0},{5,1},{8,4},{9,5},{12,8},{13,9},{14,12},{15,13},{10,14},{11,... | collective-permute-start | bytes 307208 | tf_op jit(solution)/shard_map/ppermute | solution.py:88
  36.4 4.6 %collective-permute-start.8 = (bf16[112,6272]{1,0:T(8,128)(2,1)S(1)}, bf16[112,6272]{1,0:T(8,128)(2,1)S(1)}, u32[]{:S(2)}, u32[]{:S(2)}) collective-permute-start(bf16[112,6272]{1,0:T(8,128)(2,1)S(1)} %get-tuple-element.105), channel_id=1, source_target_pairs={{0,1},{1,0},{2,3},{3,2},{4,5},{5,4},{6,7},{7,6},{8,9},{9,8},{10,11... | collective-permute-start | bytes 4214792 | tf_op jit(solution)/shard_map/ppermute | solution.py:88
  39.4 1.5 %collective-permute-start.17 = (bf16[16,6272]{1,0:T(8,128)(2,1)S(1)}, bf16[16,6272]{1,0:T(8,128)(2,1)S(1)}, u32[]{:S(2)}, u32[]{:S(2)}) collective-permute-start(bf16[16,6272]{1,0:T(8,128)(2,1)S(1)} %pad_maximum_fusion), channel_id=1, source_target_pairs={{0,1},{1,0},{2,3},{3,2},{4,5},{5,4},{6,7},{7,6},{8,9},{9,8},{10,11... | collective-permute-start | bytes 602120 | tf_op jit(solution)/shard_map/ppermute | solution.py:88
  40.9 6.8 %collective-permute-start.18 = (bf16[128,6144]{1,0:T(8,128)(2,1)S(1)}, bf16[128,6144]{1,0:T(8,128)(2,1)S(1)}, u32[]{:S(2)}, u32[]{:S(2)}) collective-permute-start(bf16[128,6144]{1,0:T(8,128)(2,1)S(1)} %maximum_dynamic-update-slice_fusion), channel_id=1, source_target_pairs={{0,1},{1,0},{2,3},{3,2},{4,5},{5,4},{6,7},{7,6},{8,9},{9,8},{10,11... | collective-permute-start | bytes 4718600 | tf_op jit(solution)/shard_map/ppermute | solution.py:88
  41.4 2.2 %copy-start.4 = (bf16[6144,336]{0,1:T(8,128)(2,1)S(1)}, bf16[6144,336]{0,1:T(8,128)(2,1)}, u32[]{:S(2)}) copy-start(bf16[6144,336]{0,1:T(8,128)(2,1)} %param.12) | copy-start | bytes 12386308
  43.5 2.2 %copy-start.2 = (bf16[336,6144]{1,0:T(8,128)(2,1)S(1)}, bf16[336,6144]{1,0:T(8,128)(2,1)}, u32[]{:S(2)}) copy-start(bf16[336,6144]{1,0:T(8,128)(2,1)} %param.13) | copy-start | bytes 12386308
  47.9 2.1 %collective-permute-start.20 = (bf16[48,6144]{1,0:T(8,128)(2,1)S(1)}, bf16[48,6144]{1,0:T(8,128)(2,1)S(1)}, u32[]{:S(2)}, u32[]{:S(2)}) collective-permute-start(bf16[48,6144]{1,0:T(8,128)(2,1)S(1)} %slice.120), channel_id=1, source_target_pairs={{0,1},{1,0},{2,3},{3,2},{4,5},{5,4},{6,7},{7,6},{8,9},{9,8},{10,11... | collective-permute-start | bytes 1769480 | tf_op jit(solution)/shard_map/ppermute | solution.py:88
  48.5 11.1 %collective-permute-start.19 = (bf16[80,6144]{1,0:T(8,128)(2,1)S(1)}, bf16[80,6144]{1,0:T(8,128)(2,1)S(1)}, u32[]{:S(2)}, u32[]{:S(2)}) collective-permute-start(bf16[80,6144]{1,0:T(8,128)(2,1)S(1)} %slice.116), channel_id=1, source_target_pairs={{0,1},{1,0},{2,3},{3,2},{4,5},{5,4},{6,7},{7,6},{8,9},{9,8},{10,11... | collective-permute-start | bytes 2949128 | tf_op jit(solution)/shard_map/ppermute | solution.py:88
  50.2 7.2 %collective-permute-start.21 = (bf16[16,6144]{1,0:T(8,128)(2,1)S(1)}, bf16[16,6144]{1,0:T(8,128)(2,1)S(1)}, u32[]{:S(2)}, u32[]{:S(2)}) collective-permute-start(bf16[16,6144]{1,0:T(8,128)(2,1)S(1)} %get-tuple-element.54), channel_id=1, source_target_pairs={{4,0},{5,1},{8,4},{9,5},{12,8},{13,9},{14,12},{15,13},{10,14},{11,... | collective-permute-start | bytes 589832 | tf_op jit(solution)/shard_map/ppermute | solution.py:88
  51.9 6.9 %collective-permute-start.22 = (bf16[16,6144]{1,0:T(8,128)(2,1)S(1)}, bf16[16,6144]{1,0:T(8,128)(2,1)S(1)}, u32[]{:S(2)}, u32[]{:S(2)}) collective-permute-start(bf16[16,6144]{1,0:T(8,128)(2,1)S(1)} %get-tuple-element.55), channel_id=1, source_target_pairs={{0,4},{1,5},{4,8},{5,9},{8,12},{9,13},{12,14},{13,15},{14,10},{15,... | collective-permute-start | bytes 589832 | tf_op jit(solution)/shard_map/ppermute | solution.py:88
  58.9 2.9 %collective-permute-start.24 = (bf16[48,6144]{1,0:T(8,128)(2,1)S(1)}, bf16[48,6144]{1,0:T(8,128)(2,1)S(1)}, u32[]{:S(2)}, u32[]{:S(2)}) collective-permute-start(bf16[48,6144]{1,0:T(8,128)(2,1)S(1)} %slice.128), channel_id=1, source_target_pairs={{0,1},{1,0},{2,3},{3,2},{4,5},{5,4},{6,7},{7,6},{8,9},{9,8},{10,11... | collective-permute-start | bytes 1769480 | tf_op jit(solution)/shard_map/ppermute | solution.py:88
  59.0 14.5 %collective-permute-start.23 = (bf16[80,6144]{1,0:T(8,128)(2,1)S(1)}, bf16[80,6144]{1,0:T(8,128)(2,1)S(1)}, u32[]{:S(2)}, u32[]{:S(2)}) collective-permute-start(bf16[80,6144]{1,0:T(8,128)(2,1)S(1)} %slice.125), channel_id=1, source_target_pairs={{0,1},{1,0},{2,3},{3,2},{4,5},{5,4},{6,7},{7,6},{8,9},{9,8},{10,11... | collective-permute-start | bytes 2949128 | tf_op jit(solution)/shard_map/ppermute | solution.py:88
  59.8 7.8 %collective-permute-start.27 = (bf16[16,6144]{1,0:T(8,128)(2,1)S(1)}, bf16[16,6144]{1,0:T(8,128)(2,1)S(1)}, u32[]{:S(2)}, u32[]{:S(2)}) collective-permute-start(bf16[16,6144]{1,0:T(8,128)(2,1)S(1)} %fusion.13), channel_id=1, source_target_pairs={{4,0},{5,1},{8,4},{9,5},{12,8},{13,9},{14,12},{15,13},{10,14},{11,... | collective-permute-start | bytes 589832 | tf_op jit(solution)/shard_map/ppermute | solution.py:88
  61.4 7.8 %collective-permute-start.28 = (bf16[16,6144]{1,0:T(8,128)(2,1)S(1)}, bf16[16,6144]{1,0:T(8,128)(2,1)S(1)}, u32[]{:S(2)}, u32[]{:S(2)}) collective-permute-start(bf16[16,6144]{1,0:T(8,128)(2,1)S(1)} %fusion.12), channel_id=1, source_target_pairs={{0,4},{1,5},{4,8},{5,9},{8,12},{9,13},{12,14},{13,15},{14,10},{15,... | collective-permute-start | bytes 589832 | tf_op jit(solution)/shard_map/ppermute | solution.py:88
  62.0 11.6 %collective-permute-start.25 = (bf16[16,6144]{1,0:T(8,128)(2,1)S(1)}, bf16[16,6144]{1,0:T(8,128)(2,1)S(1)}, u32[]{:S(2)}, u32[]{:S(2)}) collective-permute-start(bf16[16,6144]{1,0:T(8,128)(2,1)S(1)} %get-tuple-element.59), channel_id=1, source_target_pairs={{4,0},{5,1},{8,4},{9,5},{12,8},{13,9},{14,12},{15,13},{10,14},{11,... | collective-permute-start | bytes 589832 | tf_op jit(solution)/shard_map/ppermute | solution.py:88
  63.7 9.7 %collective-permute-start.26 = (bf16[16,6144]{1,0:T(8,128)(2,1)S(1)}, bf16[16,6144]{1,0:T(8,128)(2,1)S(1)}, u32[]{:S(2)}, u32[]{:S(2)}) collective-permute-start(bf16[16,6144]{1,0:T(8,128)(2,1)S(1)} %get-tuple-element.60), channel_id=1, source_target_pairs={{0,4},{1,5},{4,8},{5,9},{8,12},{9,13},{12,14},{13,15},{14,10},{15,... | collective-permute-start | bytes 589832 | tf_op jit(solution)/shard_map/ppermute | solution.py:88
  69.3 9.9 %collective-permute-start.29 = (bf16[16,6144]{1,0:T(8,128)(2,1)S(1)}, bf16[16,6144]{1,0:T(8,128)(2,1)S(1)}, u32[]{:S(2)}, u32[]{:S(2)}) collective-permute-start(bf16[16,6144]{1,0:T(8,128)(2,1)S(1)} %get-tuple-element.74), channel_id=1, source_target_pairs={{4,0},{5,1},{8,4},{9,5},{12,8},{13,9},{14,12},{15,13},{10,14},{11,... | collective-permute-start | bytes 589832 | tf_op jit(solution)/shard_map/ppermute | solution.py:88
  70.9 8.2 %collective-permute-start.30 = (bf16[16,6144]{1,0:T(8,128)(2,1)S(1)}, bf16[16,6144]{1,0:T(8,128)(2,1)S(1)}, u32[]{:S(2)}, u32[]{:S(2)}) collective-permute-start(bf16[16,6144]{1,0:T(8,128)(2,1)S(1)} %get-tuple-element.75), channel_id=1, source_target_pairs={{0,4},{1,5},{4,8},{5,9},{8,12},{9,13},{12,14},{13,15},{14,10},{15,... | collective-permute-start | bytes 589832 | tf_op jit(solution)/shard_map/ppermute | solution.py:88
  73.7 5.7 %collective-permute-start.32 = (bf16[16,6144]{1,0:T(8,128)(2,1)S(1)}, bf16[16,6144]{1,0:T(8,128)(2,1)S(1)}, u32[]{:S(2)}, u32[]{:S(2)}) collective-permute-start(bf16[16,6144]{1,0:T(8,128)(2,1)S(1)} %fusion.15), channel_id=1, source_target_pairs={{4,0},{5,1},{8,4},{9,5},{12,8},{13,9},{14,12},{15,13},{10,14},{11,... | collective-permute-start | bytes 589832 | tf_op jit(solution)/shard_map/ppermute | solution.py:88
  75.4 5.7 %collective-permute-start.33 = (bf16[16,6144]{1,0:T(8,128)(2,1)S(1)}, bf16[16,6144]{1,0:T(8,128)(2,1)S(1)}, u32[]{:S(2)}, u32[]{:S(2)}) collective-permute-start(bf16[16,6144]{1,0:T(8,128)(2,1)S(1)} %fusion.14), channel_id=1, source_target_pairs={{0,4},{1,5},{4,8},{5,9},{8,12},{9,13},{12,14},{13,15},{14,10},{15,... | collective-permute-start | bytes 589832 | tf_op jit(solution)/shard_map/ppermute | solution.py:88
  81.1 7.6 %collective-permute-start.35 = (bf16[16,6144]{1,0:T(8,128)(2,1)S(1)}, bf16[16,6144]{1,0:T(8,128)(2,1)S(1)}, u32[]{:S(2)}, u32[]{:S(2)}) collective-permute-start(bf16[16,6144]{1,0:T(8,128)(2,1)S(1)} %get-tuple-element.83), channel_id=1, source_target_pairs={{0,4},{1,5},{4,8},{5,9},{8,12},{9,13},{12,14},{13,15},{14,10},{15,... | collective-permute-start | bytes 589832 | tf_op jit(solution)/shard_map/ppermute | solution.py:88
  81.7 7.6 %collective-permute-start.31 = (bf16[16,6144]{1,0:T(8,128)(2,1)S(1)}, bf16[16,6144]{1,0:T(8,128)(2,1)S(1)}, u32[]{:S(2)}, u32[]{:S(2)}) collective-permute-start(bf16[16,6144]{1,0:T(8,128)(2,1)S(1)} %fusion.16), channel_id=1, source_target_pairs={{4,0},{5,1},{8,4},{9,5},{12,8},{13,9},{14,12},{15,13},{10,14},{11,... | collective-permute-start | bytes 589832 | tf_op jit(solution)/shard_map/ppermute | solution.py:88
  83.3 7.8 %collective-permute-start.34 = (bf16[16,6144]{1,0:T(8,128)(2,1)S(1)}, bf16[16,6144]{1,0:T(8,128)(2,1)S(1)}, u32[]{:S(2)}, u32[]{:S(2)}) collective-permute-start(bf16[16,6144]{1,0:T(8,128)(2,1)S(1)} %get-tuple-element.82), channel_id=1, source_target_pairs={{4,0},{5,1},{8,4},{9,5},{12,8},{13,9},{14,12},{15,13},{10,14},{11,... | collective-permute-start | bytes 589832 | tf_op jit(solution)/shard_map/ppermute | solution.py:88
  84.9 11.4 %copy-start.1 = (bf16[128,6144]{1,0:T(8,128)(2,1)S(1)}, bf16[128,6144]{1,0:T(8,128)(2,1)}, u32[]{:S(2)}) copy-start(bf16[128,6144]{1,0:T(8,128)(2,1)} %param.8) | copy-start | bytes 4718596
  88.8 5.7 %collective-permute-start.36 = (bf16[16,6144]{1,0:T(8,128)(2,1)S(1)}, bf16[16,6144]{1,0:T(8,128)(2,1)S(1)}, u32[]{:S(2)}, u32[]{:S(2)}) collective-permute-start(bf16[16,6144]{1,0:T(8,128)(2,1)S(1)} %fusion.5), channel_id=1, source_target_pairs={{0,4},{1,5},{4,8},{5,9},{8,12},{9,13},{12,14},{13,15},{14,10},{15,... | collective-permute-start | bytes 589832 | tf_op jit(solution)/shard_map/ppermute | solution.py:88

commit v11 on v10

--- a/solution.py
+++ b/solution.py
@@ -189,28 +189,26 @@
             dup, w_up.T, preferred_element_type=jnp.float32
         )
         dx_sent = dx_rows[half:].astype(jnp.bfloat16)
-        dx_sent, out_carry = tie(dx_sent, out_carry)
         dx_total = pair_sum(dx_rows[:half], dx_sent)
         dx_carry = {}
 
-        grads, marks = [], []
-        work = [(dgate, rows_wide), (dup, rows_wide), (hidden, rows_dy)]
-        for at in range(2, steps + 2):
-            if at <= steps:
+        grads = []
+        work = [(hidden, rows_dy), (dgate, rows_wide), (dup, rows_wide)]
+        for at in range(1, steps + 1):
+            if at > 1:
                 out_carry.update(send(wave(out_total, out_carry, at, "l")))
-            dx_blocks = wave(dx_total, dx_carry, at - 1, "r")
+            dx_blocks = wave(dx_total, dx_carry, at, "r")
             if work:
                 side, rows = work.pop(0)
                 side, dx_blocks = tie(side, dx_blocks)
-                grad, mark = weight_grad(side, rows, d, marks)
+                grad, mark = weight_grad(side, rows, d, [])
                 grads.append(grad)
-                if work and at <= steps:
-                    mark, out_carry = tie(mark, out_carry)
-                marks = [mark]
+                zero = mark[0, 0].astype(jnp.bfloat16)
+                out_carry = {w: c + zero for w, c in out_carry.items()}
             dx_carry.update(send(dx_blocks))
         for side, rows in work:
-            grads.append(weight_grad(side, rows, d, marks)[0])
-        grad_gate, grad_up, grad_down = grads
+            grads.append(weight_grad(side, rows, d, [])[0])
+        grad_down, grad_gate, grad_up = grads
         mixed, grad_tokens = (
             jnp.dot(select.T, final(total[0], carry), preferred_element_type=jnp.float32).astype(
                 jnp.bfloat16

time: 96.6 us -> 97.5 us (level)
  waiting for transfers between devices: 29.9 us -> 24.3 us
  local copies, waits for them, and re-layouts: 3.59 us -> 7.44 us
  other arithmetic: 2.47 us -> 5.08 us
    ppermute x37, waiting for transfers between devices: 29.9 us -> 24.3 us  [permute(): return lax.ppermute(x, 'et', pairs)]
    convert_element_type x8, other arithmetic: 0.43 us -> 3.14 us  [wave(): blocks[way] = block.astype(jnp.bfloat16)]
    slice x1 -> x3, local copies, waits for them, and re-layouts: 0.19 us -> 1.54 us  [per_device(): zero = mark[0, 0].astype(jnp.bfloat16)]
    unnamed x26 -> x30, local copies, waits for them, and re-layouts: 2.54 us -> 3.34 us
  transfers between devices with their start and end apart: 37 -> 37, of which waited for: 19 -> 14; matrix products, arithmetic and copies ran while one was open for 16% -> 22% of each run, Pallas kernels for 11% -> 10%
where the time goes in v11:
time: 97.5 us; the launch traced here: 97.2 us
  starting transfers between devices  33.9 us (35%)
  waiting for transfers between devices  24.3 us (25%)
  matrix products  15.6 us (16%)
  Pallas kernels  9.84 us (10%)
  local copies, waits for them, and re-layouts  7.44 us (8%)
  other arithmetic  5.08 us (5%)
  between operations  1.12 us (1%)
    ppermute x37, starting transfers between devices, permute(): return lax.ppermute(x, 'et', pairs)  33.9 us
    ppermute x37, waiting for transfers between devices, permute(): return lax.ppermute(x, 'et', pairs)  24.3 us
    pallas_call x3, Pallas kernels, weight_grad(): pl.pallas_call(lambda *refs: grad_kernel(parts, width, len(marks), *refs)...  9.84 us
    dot_general x2, matrix products, per_device(): jnp.dot(select.T, final(total[0], carry), preferred_element_type=jnp.floa...  4.17 us
    unnamed x30, local copies, waits for them, and re-layouts  3.34 us
    convert_element_type x8, other arithmetic, wave(): blocks[way] = block.astype(jnp.bfloat16)  3.14 us
    dot_general x3, matrix products, per_device(): jnp.dot(select, a, preferred_element_type=jnp.float32).astype(jnp.bfloat16)  2.15 us
  transfers between devices with their start and end apart: 37, of which 14 were waited for; matrix products, arithmetic and copies ran while one was open for 22% of the time, Pallas kernels for 10%

profile of v11, /device:TPU:0, one launch (start us, length us, event | category | flops | bytes accessed | tf_op | source)
XLA Modules:
  0.0 97.2 jit_solution(315249291381262894)
XLA Ops:
  0.6 0.8 select_reduce_fusion
  2.4 3.0 %collective-permute-start.10 = (bf16[16,6144]{1,0:T(8,128)(2,1)S(1)}, bf16[16,6144]{1,0:T(8,128)(2,1)S(1)}, u32[]{:S(2)}, u32[]{:S(2)}) collective-permute-start(bf16[16,6144]{1,0:T(8,128)(2,1)S(1)} %get-tuple-element.118), channel_id=1, source_target_pairs={{4,0},{5,1},{8,4},{9,5},{12,8},{13,9},{14,12},{15,13},{10,14},{11,... | collective-permute-start | bytes 589832 | tf_op jit(solution)/shard_map/ppermute | solution.py:88
  5.7 1.7 %convolution_convert_fusion.3 = bf16[16,6144]{1,0:T(8,128)(2,1)S(1)} fusion(bf16[128,6144]{1,0:T(8,128)(2,1)} %param.7, s32[128]{0:T(128)S(1)} %add_reduce_fusion, pred[128]{0:T(512)(128)(4,1)S(1)} %reduce_or.9), kind=kOutput, calls=%fused_computation.4 | convolution fusion | flops 25268224 | bytes 1770112 | tf_op jit(solution)/shard_map/dot_general | solution.py:161
  7.5 2.0 %collective-permute-start = (bf16[16,6272]{1,0:T(8,128)(2,1)S(1)}, bf16[16,6272]{1,0:T(8,128)(2,1)S(1)}, u32[]{:S(2)}, u32[]{:S(2)}) collective-permute-start(bf16[16,6272]{1,0:T(8,128)(2,1)S(1)} %get-tuple-element.103), channel_id=1, source_target_pairs={{0,4},{1,5},{4,8},{5,9},{8,12},{9,13},{12,14},{13,15},{14,10},{15,... | collective-permute-start | bytes 602120 | tf_op jit(solution)/shard_map/ppermute | solution.py:88
  9.6 0.8 collective-permute-done.10
  10.4 2.2 %collective-permute-start.12 = (bf16[16,6144]{1,0:T(8,128)(2,1)S(1)}, bf16[16,6144]{1,0:T(8,128)(2,1)S(1)}, u32[]{:S(2)}, u32[]{:S(2)}) collective-permute-start(bf16[16,6144]{1,0:T(8,128)(2,1)S(1)} %collective-permute-done.10), channel_id=1, source_target_pairs={{4,0},{5,1},{8,4},{9,5},{12,8},{13,9},{14,12},{15,13},{10,14},{11,... | collective-permute-start | bytes 589832 | tf_op jit(solution)/shard_map/ppermute | solution.py:88
  12.6 0.7 collective-permute-done.9
  13.3 4.2 %collective-permute-done = bf16[16,6272]{1,0:T(8,128)(2,1)S(1)} collective-permute-done((bf16[16,6272]{1,0:T(8,128)(2,1)S(1)}, bf16[16,6272]{1,0:T(8,128)(2,1)S(1)}, u32[]{:S(2)}, u32[]{:S(2)}) %collective-permute-start) | collective-permute-done | bytes 200736 | tf_op jit(solution)/shard_map/ppermute | solution.py:88
  17.5 2.0 %collective-permute-start.3 = (bf16[16,6272]{1,0:T(8,128)(2,1)S(1)}, bf16[16,6272]{1,0:T(8,128)(2,1)S(1)}, u32[]{:S(2)}, u32[]{:S(2)}) collective-permute-start(bf16[16,6272]{1,0:T(8,128)(2,1)S(1)} %collective-permute-done.1), channel_id=1, source_target_pairs={{4,0},{5,1},{8,4},{9,5},{12,8},{13,9},{14,12},{15,13},{10,14},{11,... | collective-permute-start | bytes 602120 | tf_op jit(solution)/shard_map/ppermute | solution.py:88
  19.6 1.5 %collective-permute-done.12 = bf16[16,6144]{1,0:T(8,128)(2,1)S(1)} collective-permute-done((bf16[16,6144]{1,0:T(8,128)(2,1)S(1)}, bf16[16,6144]{1,0:T(8,128)(2,1)S(1)}, u32[]{:S(2)}, u32[]{:S(2)}) %collective-permute-start.12) | collective-permute-done | bytes 196640 | tf_op jit(solution)/shard_map/ppermute | solution.py:88
  21.2 0.6 collective-permute-start.14
  21.8 1.4 %collective-permute-start.13 = (bf16[16,6144]{1,0:T(8,128)(2,1)S(1)}, bf16[16,6144]{1,0:T(8,128)(2,1)S(1)}, u32[]{:S(2)}, u32[]{:S(2)}) collective-permute-start(bf16[16,6144]{1,0:T(8,128)(2,1)S(1)} %collective-permute-done.11), channel_id=1, source_target_pairs={{0,4},{1,5},{4,8},{5,9},{8,12},{9,13},{12,14},{13,15},{14,10},{15,... | collective-permute-start | bytes 589832 | tf_op jit(solution)/shard_map/ppermute | solution.py:88
  23.3 2.8 %collective-permute-done.2 = bf16[16,6272]{1,0:T(8,128)(2,1)S(1)} collective-permute-done((bf16[16,6272]{1,0:T(8,128)(2,1)S(1)}, bf16[16,6272]{1,0:T(8,128)(2,1)S(1)}, u32[]{:S(2)}, u32[]{:S(2)}) %collective-permute-start.2) | collective-permute-done | bytes 200736 | tf_op jit(solution)/shard_map/ppermute | solution.py:88
  26.1 2.0 %collective-permute-start.5 = (bf16[16,6272]{1,0:T(8,128)(2,1)S(1)}, bf16[16,6272]{1,0:T(8,128)(2,1)S(1)}, u32[]{:S(2)}, u32[]{:S(2)}) collective-permute-start(bf16[16,6272]{1,0:T(8,128)(2,1)S(1)} %collective-permute-done.3), channel_id=1, source_target_pairs={{4,0},{5,1},{8,4},{9,5},{12,8},{13,9},{14,12},{15,13},{10,14},{11,... | collective-permute-start | bytes 602120 | tf_op jit(solution)/shard_map/ppermute | solution.py:88
  28.2 1.5 %collective-permute-done.14 = bf16[16,6144]{1,0:T(8,128)(2,1)S(1)} collective-permute-done((bf16[16,6144]{1,0:T(8,128)(2,1)S(1)}, bf16[16,6144]{1,0:T(8,128)(2,1)S(1)}, u32[]{:S(2)}, u32[]{:S(2)}) %collective-permute-start.14) | collective-permute-done | bytes 196640 | tf_op jit(solution)/shard_map/ppermute | solution.py:88
  29.7 0.9 collective-permute-start.16
  30.6 1.2 %collective-permute-start.15 = (bf16[16,3072]{1,0:T(8,128)(2,1)S(1)}, bf16[16,3072]{1,0:T(8,128)(2,1)S(1)}, u32[]{:S(2)}, u32[]{:S(2)}) collective-permute-start(bf16[16,3072]{1,0:T(8,128)(2,1)S(1)} %slice.156), channel_id=1, source_target_pairs={{0,4},{1,5},{4,8},{5,9},{8,12},{9,13},{12,14},{13,15},{14,10},{15,... | collective-permute-start | bytes 294920 | tf_op jit(solution)/shard_map/ppermute | solution.py:88
  31.9 2.3 %collective-permute-done.4 = bf16[16,6272]{1,0:T(8,128)(2,1)S(1)} collective-permute-done((bf16[16,6272]{1,0:T(8,128)(2,1)S(1)}, bf16[16,6272]{1,0:T(8,128)(2,1)S(1)}, u32[]{:S(2)}, u32[]{:S(2)}) %collective-permute-start.4) | collective-permute-done | bytes 200736 | tf_op jit(solution)/shard_map/ppermute | solution.py:88
  34.2 0.5 collective-permute-start.6
  34.7 1.9 %collective-permute-start.7 = (bf16[16,3200]{1,0:T(8,128)(2,1)S(1)}, bf16[16,3200]{1,0:T(8,128)(2,1)S(1)}, u32[]{:S(2)}, u32[]{:S(2)}) collective-permute-start(bf16[16,3200]{1,0:T(8,128)(2,1)S(1)} %slice.155), channel_id=1, source_target_pairs={{4,0},{5,1},{8,4},{9,5},{12,8},{13,9},{14,12},{15,13},{10,14},{11,... | collective-permute-start | bytes 307208 | tf_op jit(solution)/shard_map/ppermute | solution.py:88
  36.7 2.1 %collective-permute-done.6 = bf16[16,3072]{1,0:T(8,128)(2,1)S(1)} collective-permute-done((bf16[16,3072]{1,0:T(8,128)(2,1)S(1)}, bf16[16,3072]{1,0:T(8,128)(2,1)S(1)}, u32[]{:S(2)}, u32[]{:S(2)}) %collective-permute-start.6) | collective-permute-done | bytes 98336 | tf_op jit(solution)/shard_map/ppermute | solution.py:88
  38.9 0.7 collective-permute-done.7
  39.7 1.4 %collective-permute-done.17 = bf16[16,6272]{1,0:T(8,128)(2,1)S(1)} collective-permute-done((bf16[16,6272]{1,0:T(8,128)(2,1)S(1)}, bf16[16,6272]{1,0:T(8,128)(2,1)S(1)}, u32[]{:S(2)}, u32[]{:S(2)}) %collective-permute-start.17) | collective-permute-done | bytes 200736 | tf_op jit(solution)/shard_map/ppermute | solution.py:88
  41.6 1.3 %fusion.2 = f32[256,336]{0,1:T(8,128)S(1)} fusion(bf16[6144,336]{0,1:T(8,128)(2,1)S(1)} %copy-done.3, bf16[256,6272]{1,0:T(8,128)(2,1)S(1)} %constant_dynamic-update-slice_fusion.14.refs_1_), kind=kOutput, calls=%fused_computation.8 | convolution fusion | flops 1056964608 | bytes 7618560 | tf_op jit(solution)/shard_map/dot_general | solution.py:172
  42.8 0.9 copy-done.4
  43.7 1.3 %multiply_convert_fusion.2 = (bf16[256,336]{0,1:T(8,128)(2,1)S(1)}, f32[256,336]{0,1:T(8,128)S(1)}) fusion(f32[256]{0:T(256)S(1)} %convert_reduce_fusion, f32[256,336]{0,1:T(8,128)S(1)} %fusion.2, bf16[6144,336]{0,1:T(8,128)(2,1)S(1)} %copy-done.4, bf16[256,6272]{1,0:T(8,128)(2,1)S(1)} %constant_dynamic-update-slice_fusion.14.refs_1_), kind=kOutput, calls=%fused_computation.45 | convolution fusion | flops 1057566720 | bytes 8135680 | tf_op jit(solution)/shard_map/dot_general | solution.py:173
  45.0 0.9 copy-done.2
  45.9 1.8 %fusion.45 = f32[256,6144]{1,0:T(8,128)S(1)} fusion(bf16[256,336]{0,1:T(8,128)(2,1)S(1)} %get-tuple-element.49, bf16[336,6144]{1,0:T(8,128)(2,1)S(1)} %copy-done.2), kind=kOutput, calls=%fused_computation.111 | convolution fusion | flops 1056964608 | bytes 10592256 | tf_op jit(solution)/shard_map/dot_general | solution.py:177
  48.1 0.4 collective-permute-start.20
  48.5 1.0 %slice.128 = bf16[80,6144]{1,0:T(8,128)(2,1)} slice(bf16[128,6144]{1,0:T(8,128)(2,1)S(1)} %slice.235), slice={[0:80], [0:6144]} | slice | bytes 1966080 | tf_op jit(solution)/shard_map/slice | solution.py:119
  49.7 1.3 %multiply_convert_fusion = (bf16[256,336]{0,1:T(8,128)(2,1)S(1)}, bf16[256,336]{0,1:T(8,128)(2,1)S(1)}) fusion(f32[256,336]{0,1:T(8,128)S(1)} %fusion.2, f32[256,336]{0,1:T(8,128)S(1)} %get-tuple-element.120, bf16[256,6144]{1,0:T(8,128)(2,1)S(1)} %constant_dynamic-update-slice_fusion.24.refs_1_, bf16[336,6144]{1,0:T(8,128)(2,1)S(1)} %copy-done.2, ...), kind=kOutput, calls=%fused_computation.43 | convolution fusion | flops 1058168832 | bytes 8307712 | tf_op jit(solution)/shard_map/dot_general | solution.py:182
  51.2 0.8 fusion.43
  51.9 1.8 %fusion.46 = f32[256,6144]{1,0:T(8,128)S(1)} fusion(bf16[256,336]{0,1:T(8,128)(2,1)S(1)} %get-tuple-element.57, bf16[6144,336]{0,1:T(8,128)(2,1)S(1)} %copy-done.3), kind=kOutput, calls=%fused_computation.112 | convolution fusion | flops 1056964608 | bytes 10592256 | tf_op jit(solution)/shard_map/dot_general | solution.py:188
  53.7 1.8 %fusion.44 = (bf16[256,6144]{1,0:T(8,128)(2,1)S(1)}, f32[256,6144]{1,0:T(8,128)S(1)}) fusion(f32[256,6144]{1,0:T(8,128)S(1)} %fusion.46, bf16[256,336]{0,1:T(8,128)(2,1)S(1)} %get-tuple-element.65, bf16[6144,336]{0,1:T(8,128)(2,1)S(1)} %copy-done.4), kind=kOutput, calls=%fused_computation.110 | convolution fusion | flops 1060110336 | bytes 20029440 | tf_op jit(solution)/shard_map/dot_general | solution.py:188
  55.7 0.8 copy-done.6
  56.5 1.6 %collective-permute-start.21 = (bf16[16,6144]{1,0:T(8,128)(2,1)S(1)}, bf16[16,6144]{1,0:T(8,128)(2,1)S(1)}, u32[]{:S(2)}, u32[]{:S(2)}) collective-permute-start(bf16[16,6144]{1,0:T(8,128)(2,1)S(1)} %copy-done.6), channel_id=1, source_target_pairs={{4,0},{5,1},{8,4},{9,5},{12,8},{13,9},{14,12},{15,13},{10,14},{11,... | collective-permute-start | bytes 589832 | tf_op jit(solution)/shard_map/ppermute | solution.py:88
  58.6 0.5 collective-permute-start.25
  59.2 1.3 %collective-permute-done.22 = bf16[48,6144]{1,0:T(8,128)(2,1)S(1)} collective-permute-done((bf16[48,6144]{1,0:T(8,128)(2,1)S(1)}, bf16[48,6144]{1,0:T(8,128)(2,1)S(1)}, u32[]{:S(2)}, u32[]{:S(2)}) %collective-permute-start.22) | collective-permute-done | bytes 589856 | tf_op jit(solution)/shard_map/ppermute | solution.py:88
  60.7 1.7 %collective-permute-start.26 = (bf16[16,6144]{1,0:T(8,128)(2,1)S(1)}, bf16[16,6144]{1,0:T(8,128)(2,1)S(1)}, u32[]{:S(2)}, u32[]{:S(2)}) collective-permute-start(bf16[16,6144]{1,0:T(8,128)(2,1)S(1)} %get-tuple-element.53), channel_id=1, source_target_pairs={{4,0},{5,1},{8,4},{9,5},{12,8},{13,9},{14,12},{15,13},{10,14},{11,... | collective-permute-start | bytes 589832 | tf_op jit(solution)/shard_map/ppermute | solution.py:88
  62.4 0.4 collective-permute-start.27
  62.8 3.3 %shard_map.110 = (bf16[336,6144]{1,0:T(8,128)(2,1)}, f32[8,128]{1,0:T(8,128)S(1)}) custom-call(bf16[336,256]{1,0:T(8,128)(2,1)S(1)} %bitcast.30, bf16[256,6144]{1,0:T(8,128)(2,1)S(1)} %constant_dynamic-update-slice_fusion.24.refs_1_), custom_call_target="tpu_custom_call" | custom-call | flops 1056964608 | bytes 7274496 | tf_op jit(solution)/shard_map/pallas_call | solution.py:54
  66.1 0.5 slice.141
  66.6 0.7 fusion.14
  67.3 0.7 fusion.13
  68.0 1.7 %collective-permute-start.24 = (bf16[16,6144]{1,0:T(8,128)(2,1)S(1)}, bf16[16,6144]{1,0:T(8,128)(2,1)S(1)}, u32[]{:S(2)}, u32[]{:S(2)}) collective-permute-start(bf16[16,6144]{1,0:T(8,128)(2,1)S(1)} %fusion.14), channel_id=1, source_target_pairs={{4,0},{5,1},{8,4},{9,5},{12,8},{13,9},{14,12},{15,13},{10,14},{11,... | collective-permute-start | bytes 589832 | tf_op jit(solution)/shard_map/ppermute | solution.py:88
  69.7 0.4 collective-permute-start.28
  70.4 1.7 %collective-permute-start.30 = (bf16[16,6144]{1,0:T(8,128)(2,1)S(1)}, bf16[16,6144]{1,0:T(8,128)(2,1)S(1)}, u32[]{:S(2)}, u32[]{:S(2)}) collective-permute-start(bf16[16,6144]{1,0:T(8,128)(2,1)S(1)} %fusion.12), channel_id=1, source_target_pairs={{4,0},{5,1},{8,4},{9,5},{12,8},{13,9},{14,12},{15,13},{10,14},{11,... | collective-permute-start | bytes 589832 | tf_op jit(solution)/shard_map/ppermute | solution.py:88
  72.1 0.4 collective-permute-start.31
  72.5 3.3 %shard_map.111 = (bf16[336,6144]{1,0:T(8,128)(2,1)}, f32[8,128]{1,0:T(8,128)S(1)}) custom-call(bf16[336,256]{1,0:T(8,128)(2,1)S(1)} %bitcast.29, bf16[256,6272]{1,0:T(8,128)(2,1)S(1)} %constant_dynamic-update-slice_fusion.14.refs_1_), custom_call_target="tpu_custom_call" | custom-call | flops 1056964608 | bytes 7274496 | tf_op jit(solution)/shard_map/pallas_call | solution.py:54
  75.8 0.5 slice.147
  76.3 1.3 %collective-permute-done.28 = bf16[16,6144]{1,0:T(8,128)(2,1)S(1)} collective-permute-done((bf16[16,6144]{1,0:T(8,128)(2,1)S(1)}, bf16[16,6144]{1,0:T(8,128)(2,1)S(1)}, u32[]{:S(2)}, u32[]{:S(2)}) %collective-permute-start.28) | collective-permute-done | bytes 196640 | tf_op jit(solution)/shard_map/ppermute | solution.py:88
  77.6 0.7 fusion.10
  78.3 1.6 %collective-permute-start.29 = (bf16[16,6144]{1,0:T(8,128)(2,1)S(1)}, bf16[16,6144]{1,0:T(8,128)(2,1)S(1)}, u32[]{:S(2)}, u32[]{:S(2)}) collective-permute-start(bf16[16,6144]{1,0:T(8,128)(2,1)S(1)} %get-tuple-element.60), channel_id=1, source_target_pairs={{4,0},{5,1},{8,4},{9,5},{12,8},{13,9},{14,12},{15,13},{10,14},{11,... | collective-permute-start | bytes 589832 | tf_op jit(solution)/shard_map/ppermute | solution.py:88
  79.9 0.4 collective-permute-start.33
  80.6 1.6 %collective-permute-start.34 = (bf16[16,6144]{1,0:T(8,128)(2,1)S(1)}, bf16[16,6144]{1,0:T(8,128)(2,1)S(1)}, u32[]{:S(2)}, u32[]{:S(2)}) collective-permute-start(bf16[16,6144]{1,0:T(8,128)(2,1)S(1)} %get-tuple-element.68), channel_id=1, source_target_pairs={{4,0},{5,1},{8,4},{9,5},{12,8},{13,9},{14,12},{15,13},{10,14},{11,... | collective-permute-start | bytes 589832 | tf_op jit(solution)/shard_map/ppermute | solution.py:88
  82.2 0.4 collective-permute-start.35
  82.7 3.3 %shard_map.112 = (bf16[336,6144]{1,0:T(8,128)(2,1)}, f32[8,128]{1,0:T(8,128)S(1)}) custom-call(bf16[336,256]{1,0:T(8,128)(2,1)S(1)} %bitcast.31, bf16[256,6272]{1,0:T(8,128)(2,1)S(1)} %constant_dynamic-update-slice_fusion.14.refs_1_), custom_call_target="tpu_custom_call" | custom-call | flops 1056964608 | bytes 7274496 | tf_op jit(solution)/shard_map/pallas_call | solution.py:54
  86.0 0.5 slice.151
  86.5 0.8 fusion.16
  87.3 1.6 %collective-permute-start.32 = (bf16[16,6144]{1,0:T(8,128)(2,1)S(1)}, bf16[16,6144]{1,0:T(8,128)(2,1)S(1)}, u32[]{:S(2)}, u32[]{:S(2)}) collective-permute-start(bf16[16,6144]{1,0:T(8,128)(2,1)S(1)} %fusion.16), channel_id=1, source_target_pairs={{4,0},{5,1},{8,4},{9,5},{12,8},{13,9},{14,12},{15,13},{10,14},{11,... | collective-permute-start | bytes 589832 | tf_op jit(solution)/shard_map/ppermute | solution.py:88
  89.0 0.5 collective-permute-start.36
  89.5 3.5 %collective-permute-done.32 = bf16[16,6144]{1,0:T(8,128)(2,1)S(1)} collective-permute-done((bf16[16,6144]{1,0:T(8,128)(2,1)S(1)}, bf16[16,6144]{1,0:T(8,128)(2,1)S(1)}, u32[]{:S(2)}, u32[]{:S(2)}) %collective-permute-start.32) | collective-permute-done | bytes 196640 | tf_op jit(solution)/shard_map/ppermute | solution.py:88
  93.0 2.4 %convolution_convert_fusion.1 = bf16[128,6144]{1,0:T(8,128)(2,1)} fusion(f32[80,6144]{1,0:T(8,128)S(1)} %slice_add_fusion.1, bf16[16,6144]{1,0:T(8,128)(2,1)S(1)} %collective-permute-done.32, bf16[16,6144]{1,0:T(8,128)(2,1)S(1)} %collective-permute-done.33, bf16[]{:T(256)} %bitcast.8, s32[128]{0:T(128)S(1)} %add_reduce_fusion, pred[128]{0:T(512)(128)(4,1)S(1)} %reduce_or.9), kind=kOutput, calls=%fused_computation.2 | convolution fusion | flops 26546176 | bytes 2360322 | tf_op jit(solution)/shard_map/dot_general | solution.py:213
  95.5 1.8 %convolution_convert_fusion = bf16[128,6144]{1,0:T(8,128)(2,1)} fusion(f32[80,6144]{1,0:T(8,128)S(1)} %slice_add_fusion, bf16[16,6144]{1,0:T(8,128)(2,1)S(1)} %collective-permute-done.36, bf16[16,6144]{1,0:T(8,128)(2,1)S(1)} %collective-permute-done.34, s32[128]{0:T(128)S(1)} %add_reduce_fusion, pred[128]{0:T(512)(128)(4,1)S(1)} %reduce_or.9), kind=kOutput, calls=%fused_computation.1 | convolution fusion | flops 26447872 | bytes 2360320 | tf_op jit(solution)/shard_map/dot_general | solution.py:213
  (97 shorter events, 4.5 us)
Async XLA Ops:
  0.6 1.4 %copy-start = (bf16[128,6144]{1,0:T(8,128)(2,1)S(1)}, bf16[128,6144]{1,0:T(8,128)(2,1)}, u32[]{:S(2)}) copy-start(bf16[128,6144]{1,0:T(8,128)(2,1)} %param.8) | copy-start | bytes 4718596
  2.4 8.0 %collective-permute-start.10 = (bf16[16,6144]{1,0:T(8,128)(2,1)S(1)}, bf16[16,6144]{1,0:T(8,128)(2,1)S(1)}, u32[]{:S(2)}, u32[]{:S(2)}) collective-permute-start(bf16[16,6144]{1,0:T(8,128)(2,1)S(1)} %get-tuple-element.118), channel_id=1, source_target_pairs={{4,0},{5,1},{8,4},{9,5},{12,8},{13,9},{14,12},{15,13},{10,14},{11,... | collective-permute-start | bytes 589832 | tf_op jit(solution)/shard_map/ppermute | solution.py:88
  5.4 7.8 %collective-permute-start.9 = (bf16[16,6144]{1,0:T(8,128)(2,1)S(1)}, bf16[16,6144]{1,0:T(8,128)(2,1)S(1)}, u32[]{:S(2)}, u32[]{:S(2)}) collective-permute-start(bf16[16,6144]{1,0:T(8,128)(2,1)S(1)} %get-tuple-element.118), channel_id=1, source_target_pairs={{0,4},{1,5},{4,8},{5,9},{8,12},{9,13},{12,14},{13,15},{14,10},{15,... | collective-permute-start | bytes 589832 | tf_op jit(solution)/shard_map/ppermute | solution.py:88
  7.5 10.0 %collective-permute-start = (bf16[16,6272]{1,0:T(8,128)(2,1)S(1)}, bf16[16,6272]{1,0:T(8,128)(2,1)S(1)}, u32[]{:S(2)}, u32[]{:S(2)}) collective-permute-start(bf16[16,6272]{1,0:T(8,128)(2,1)S(1)} %get-tuple-element.103), channel_id=1, source_target_pairs={{0,4},{1,5},{4,8},{5,9},{8,12},{9,13},{12,14},{13,15},{14,10},{15,... | collective-permute-start | bytes 602120 | tf_op jit(solution)/shard_map/ppermute | solution.py:88
  9.5 8.0 %collective-permute-start.1 = (bf16[16,6272]{1,0:T(8,128)(2,1)S(1)}, bf16[16,6272]{1,0:T(8,128)(2,1)S(1)}, u32[]{:S(2)}, u32[]{:S(2)}) collective-permute-start(bf16[16,6272]{1,0:T(8,128)(2,1)S(1)} %get-tuple-element.103), channel_id=1, source_target_pairs={{4,0},{5,1},{8,4},{9,5},{12,8},{13,9},{14,12},{15,13},{10,14},{11,... | collective-permute-start | bytes 602120 | tf_op jit(solution)/shard_map/ppermute | solution.py:88
  10.4 10.8 %collective-permute-start.12 = (bf16[16,6144]{1,0:T(8,128)(2,1)S(1)}, bf16[16,6144]{1,0:T(8,128)(2,1)S(1)}, u32[]{:S(2)}, u32[]{:S(2)}) collective-permute-start(bf16[16,6144]{1,0:T(8,128)(2,1)S(1)} %collective-permute-done.10), channel_id=1, source_target_pairs={{4,0},{5,1},{8,4},{9,5},{12,8},{13,9},{14,12},{15,13},{10,14},{11,... | collective-permute-start | bytes 589832 | tf_op jit(solution)/shard_map/ppermute | solution.py:88
  13.2 8.5 %collective-permute-start.11 = (bf16[16,6144]{1,0:T(8,128)(2,1)S(1)}, bf16[16,6144]{1,0:T(8,128)(2,1)S(1)}, u32[]{:S(2)}, u32[]{:S(2)}) collective-permute-start(bf16[16,6144]{1,0:T(8,128)(2,1)S(1)} %collective-permute-done.9), channel_id=1, source_target_pairs={{0,4},{1,5},{4,8},{5,9},{8,12},{9,13},{12,14},{13,15},{14,10},{15,... | collective-permute-start | bytes 589832 | tf_op jit(solution)/shard_map/ppermute | solution.py:88
  17.5 8.5 %collective-permute-start.2 = (bf16[16,6272]{1,0:T(8,128)(2,1)S(1)}, bf16[16,6272]{1,0:T(8,128)(2,1)S(1)}, u32[]{:S(2)}, u32[]{:S(2)}) collective-permute-start(bf16[16,6272]{1,0:T(8,128)(2,1)S(1)} %collective-permute-done), channel_id=1, source_target_pairs={{0,4},{1,5},{4,8},{5,9},{8,12},{9,13},{12,14},{13,15},{14,10},{15,... | collective-permute-start | bytes 602120 | tf_op jit(solution)/shard_map/ppermute | solution.py:88
  17.5 8.5 %collective-permute-start.3 = (bf16[16,6272]{1,0:T(8,128)(2,1)S(1)}, bf16[16,6272]{1,0:T(8,128)(2,1)S(1)}, u32[]{:S(2)}, u32[]{:S(2)}) collective-permute-start(bf16[16,6272]{1,0:T(8,128)(2,1)S(1)} %collective-permute-done.1), channel_id=1, source_target_pairs={{4,0},{5,1},{8,4},{9,5},{12,8},{13,9},{14,12},{15,13},{10,14},{11,... | collective-permute-start | bytes 602120 | tf_op jit(solution)/shard_map/ppermute | solution.py:88
  21.2 8.5 %collective-permute-start.14 = (bf16[16,6144]{1,0:T(8,128)(2,1)S(1)}, bf16[16,6144]{1,0:T(8,128)(2,1)S(1)}, u32[]{:S(2)}, u32[]{:S(2)}) collective-permute-start(bf16[16,6144]{1,0:T(8,128)(2,1)S(1)} %collective-permute-done.12), channel_id=1, source_target_pairs={{4,0},{5,1},{8,4},{9,5},{12,8},{13,9},{14,12},{15,13},{10,14},{11,... | collective-permute-start | bytes 589832 | tf_op jit(solution)/shard_map/ppermute | solution.py:88
  21.8 8.8 %collective-permute-start.13 = (bf16[16,6144]{1,0:T(8,128)(2,1)S(1)}, bf16[16,6144]{1,0:T(8,128)(2,1)S(1)}, u32[]{:S(2)}, u32[]{:S(2)}) collective-permute-start(bf16[16,6144]{1,0:T(8,128)(2,1)S(1)} %collective-permute-done.11), channel_id=1, source_target_pairs={{0,4},{1,5},{4,8},{5,9},{8,12},{9,13},{12,14},{13,15},{14,10},{15,... | collective-permute-start | bytes 589832 | tf_op jit(solution)/shard_map/ppermute | solution.py:88
  26.1 8.1 %collective-permute-start.4 = (bf16[16,6272]{1,0:T(8,128)(2,1)S(1)}, bf16[16,6272]{1,0:T(8,128)(2,1)S(1)}, u32[]{:S(2)}, u32[]{:S(2)}) collective-permute-start(bf16[16,6272]{1,0:T(8,128)(2,1)S(1)} %collective-permute-done.2), channel_id=1, source_target_pairs={{0,4},{1,5},{4,8},{5,9},{8,12},{9,13},{12,14},{13,15},{14,10},{15,... | collective-permute-start | bytes 602120 | tf_op jit(solution)/shard_map/ppermute | solution.py:88
  26.1 8.6 %collective-permute-start.5 = (bf16[16,6272]{1,0:T(8,128)(2,1)S(1)}, bf16[16,6272]{1,0:T(8,128)(2,1)S(1)}, u32[]{:S(2)}, u32[]{:S(2)}) collective-permute-start(bf16[16,6272]{1,0:T(8,128)(2,1)S(1)} %collective-permute-done.3), channel_id=1, source_target_pairs={{4,0},{5,1},{8,4},{9,5},{12,8},{13,9},{14,12},{15,13},{10,14},{11,... | collective-permute-start | bytes 602120 | tf_op jit(solution)/shard_map/ppermute | solution.py:88
  29.7 7.0 %collective-permute-start.16 = (bf16[16,3072]{1,0:T(8,128)(2,1)S(1)}, bf16[16,3072]{1,0:T(8,128)(2,1)S(1)}, u32[]{:S(2)}, u32[]{:S(2)}) collective-permute-start(bf16[16,3072]{1,0:T(8,128)(2,1)S(1)} %slice.157), channel_id=1, source_target_pairs={{4,0},{5,1},{8,4},{9,5},{12,8},{13,9},{14,12},{15,13},{10,14},{11,... | collective-permute-start | bytes 294920 | tf_op jit(solution)/shard_map/ppermute | solution.py:88
  30.6 6.1 %collective-permute-start.15 = (bf16[16,3072]{1,0:T(8,128)(2,1)S(1)}, bf16[16,3072]{1,0:T(8,128)(2,1)S(1)}, u32[]{:S(2)}, u32[]{:S(2)}) collective-permute-start(bf16[16,3072]{1,0:T(8,128)(2,1)S(1)} %slice.156), channel_id=1, source_target_pairs={{0,4},{1,5},{4,8},{5,9},{8,12},{9,13},{12,14},{13,15},{14,10},{15,... | collective-permute-start | bytes 294920 | tf_op jit(solution)/shard_map/ppermute | solution.py:88
  34.2 7.4 %copy-start.3 = (bf16[6144,336]{0,1:T(8,128)(2,1)S(1)}, bf16[6144,336]{0,1:T(8,128)(2,1)}, u32[]{:S(2)}) copy-start(bf16[6144,336]{0,1:T(8,128)(2,1)} %param.11) | copy-start | bytes 12386308
  34.2 4.7 %collective-permute-start.6 = (bf16[16,3072]{1,0:T(8,128)(2,1)S(1)}, bf16[16,3072]{1,0:T(8,128)(2,1)S(1)}, u32[]{:S(2)}, u32[]{:S(2)}) collective-permute-start(bf16[16,3072]{1,0:T(8,128)(2,1)S(1)} %slice.154), channel_id=1, source_target_pairs={{0,4},{1,5},{4,8},{5,9},{8,12},{9,13},{12,14},{13,15},{14,10},{15,... | collective-permute-start | bytes 294920 | tf_op jit(solution)/shard_map/ppermute | solution.py:88
  34.7 4.9 %collective-permute-start.7 = (bf16[16,3200]{1,0:T(8,128)(2,1)S(1)}, bf16[16,3200]{1,0:T(8,128)(2,1)S(1)}, u32[]{:S(2)}, u32[]{:S(2)}) collective-permute-start(bf16[16,3200]{1,0:T(8,128)(2,1)S(1)} %slice.155), channel_id=1, source_target_pairs={{4,0},{5,1},{8,4},{9,5},{12,8},{13,9},{14,12},{15,13},{10,14},{11,... | collective-permute-start | bytes 307208 | tf_op jit(solution)/shard_map/ppermute | solution.py:88
  36.6 4.6 %collective-permute-start.8 = (bf16[112,6272]{1,0:T(8,128)(2,1)S(1)}, bf16[112,6272]{1,0:T(8,128)(2,1)S(1)}, u32[]{:S(2)}, u32[]{:S(2)}) collective-permute-start(bf16[112,6272]{1,0:T(8,128)(2,1)S(1)} %get-tuple-element.89), channel_id=1, source_target_pairs={{0,1},{1,0},{2,3},{3,2},{4,5},{5,4},{6,7},{7,6},{8,9},{9,8},{10,11... | collective-permute-start | bytes 4214792 | tf_op jit(solution)/shard_map/ppermute | solution.py:88
  39.6 1.5 %collective-permute-start.17 = (bf16[16,6272]{1,0:T(8,128)(2,1)S(1)}, bf16[16,6272]{1,0:T(8,128)(2,1)S(1)}, u32[]{:S(2)}, u32[]{:S(2)}) collective-permute-start(bf16[16,6272]{1,0:T(8,128)(2,1)S(1)} %pad_maximum_fusion), channel_id=1, source_target_pairs={{0,1},{1,0},{2,3},{3,2},{4,5},{5,4},{6,7},{7,6},{8,9},{9,8},{10,11... | collective-permute-start | bytes 602120 | tf_op jit(solution)/shard_map/ppermute | solution.py:88
  41.1 6.8 %collective-permute-start.18 = (bf16[128,6144]{1,0:T(8,128)(2,1)S(1)}, bf16[128,6144]{1,0:T(8,128)(2,1)S(1)}, u32[]{:S(2)}, u32[]{:S(2)}) collective-permute-start(bf16[128,6144]{1,0:T(8,128)(2,1)S(1)} %maximum_dynamic-update-slice_fusion), channel_id=1, source_target_pairs={{0,1},{1,0},{2,3},{3,2},{4,5},{5,4},{6,7},{7,6},{8,9},{9,8},{10,11... | collective-permute-start | bytes 4718600 | tf_op jit(solution)/shard_map/ppermute | solution.py:88
  41.5 2.2 %copy-start.4 = (bf16[6144,336]{0,1:T(8,128)(2,1)S(1)}, bf16[6144,336]{0,1:T(8,128)(2,1)}, u32[]{:S(2)}) copy-start(bf16[6144,336]{0,1:T(8,128)(2,1)} %param.12) | copy-start | bytes 12386308
  43.7 2.2 %copy-start.2 = (bf16[336,6144]{1,0:T(8,128)(2,1)S(1)}, bf16[336,6144]{1,0:T(8,128)(2,1)}, u32[]{:S(2)}) copy-start(bf16[336,6144]{1,0:T(8,128)(2,1)} %param.13) | copy-start | bytes 12386308
  48.1 2.9 %collective-permute-start.20 = (bf16[48,6144]{1,0:T(8,128)(2,1)S(1)}, bf16[48,6144]{1,0:T(8,128)(2,1)S(1)}, u32[]{:S(2)}, u32[]{:S(2)}) collective-permute-start(bf16[48,6144]{1,0:T(8,128)(2,1)S(1)} %slice.133), channel_id=1, source_target_pairs={{0,1},{1,0},{2,3},{3,2},{4,5},{5,4},{6,7},{7,6},{8,9},{9,8},{10,11... | collective-permute-start | bytes 1769480 | tf_op jit(solution)/shard_map/ppermute | solution.py:88
  49.6 9.5 %collective-permute-start.19 = (bf16[80,6144]{1,0:T(8,128)(2,1)}, bf16[80,6144]{1,0:T(8,128)(2,1)S(1)}, u32[]{:S(2)}, u32[]{:S(2)}) collective-permute-start(bf16[80,6144]{1,0:T(8,128)(2,1)} %slice.128), channel_id=1, source_target_pairs={{0,1},{1,0},{2,3},{3,2},{4,5},{5,4},{6,7},{7,6},{8,9},{9,8},{10,11... | collective-permute-start | bytes 2949128 | tf_op jit(solution)/shard_map/ppermute | solution.py:88
  55.6 0.9 copy-start.6
  55.6 2.6 %copy-start.5 = (bf16[16,6144]{1,0:T(8,128)(2,1)S(1)}, bf16[16,6144]{1,0:T(8,128)(2,1)}, u32[]{:S(2)}) copy-start(bf16[16,6144]{1,0:T(8,128)(2,1)} %get-tuple-element.51) | copy-start | bytes 589828
  56.5 10.1 %collective-permute-start.21 = (bf16[16,6144]{1,0:T(8,128)(2,1)S(1)}, bf16[16,6144]{1,0:T(8,128)(2,1)S(1)}, u32[]{:S(2)}, u32[]{:S(2)}) collective-permute-start(bf16[16,6144]{1,0:T(8,128)(2,1)S(1)} %copy-done.6), channel_id=1, source_target_pairs={{4,0},{5,1},{8,4},{9,5},{12,8},{13,9},{14,12},{15,13},{10,14},{11,... | collective-permute-start | bytes 589832 | tf_op jit(solution)/shard_map/ppermute | solution.py:88
  58.2 9.2 %collective-permute-start.23 = (bf16[16,6144]{1,0:T(8,128)(2,1)S(1)}, bf16[16,6144]{1,0:T(8,128)(2,1)S(1)}, u32[]{:S(2)}, u32[]{:S(2)}) collective-permute-start(bf16[16,6144]{1,0:T(8,128)(2,1)S(1)} %copy-done.5), channel_id=1, source_target_pairs={{0,4},{1,5},{4,8},{5,9},{8,12},{9,13},{12,14},{13,15},{14,10},{15,... | collective-permute-start | bytes 589832 | tf_op jit(solution)/shard_map/ppermute | solution.py:88
  58.6 2.0 %collective-permute-start.22 = (bf16[48,6144]{1,0:T(8,128)(2,1)S(1)}, bf16[48,6144]{1,0:T(8,128)(2,1)S(1)}, u32[]{:S(2)}, u32[]{:S(2)}) collective-permute-start(bf16[48,6144]{1,0:T(8,128)(2,1)S(1)} %slice.170), channel_id=1, source_target_pairs={{0,1},{1,0},{2,3},{3,2},{4,5},{5,4},{6,7},{7,6},{8,9},{9,8},{10,11... | collective-permute-start | bytes 1769480 | tf_op jit(solution)/shard_map/ppermute | solution.py:88
  58.6 11.6 %collective-permute-start.25 = (bf16[80,6144]{1,0:T(8,128)(2,1)S(1)}, bf16[80,6144]{1,0:T(8,128)(2,1)S(1)}, u32[]{:S(2)}, u32[]{:S(2)}) collective-permute-start(bf16[80,6144]{1,0:T(8,128)(2,1)S(1)} %slice.175), channel_id=1, source_target_pairs={{0,1},{1,0},{2,3},{3,2},{4,5},{5,4},{6,7},{7,6},{8,9},{9,8},{10,11... | collective-permute-start | bytes 2949128 | tf_op jit(solution)/shard_map/ppermute | solution.py:88
  60.7 9.6 %collective-permute-start.26 = (bf16[16,6144]{1,0:T(8,128)(2,1)S(1)}, bf16[16,6144]{1,0:T(8,128)(2,1)S(1)}, u32[]{:S(2)}, u32[]{:S(2)}) collective-permute-start(bf16[16,6144]{1,0:T(8,128)(2,1)S(1)} %get-tuple-element.53), channel_id=1, source_target_pairs={{4,0},{5,1},{8,4},{9,5},{12,8},{13,9},{14,12},{15,13},{10,14},{11,... | collective-permute-start | bytes 589832 | tf_op jit(solution)/shard_map/ppermute | solution.py:88
  62.4 7.7 %collective-permute-start.27 = (bf16[16,6144]{1,0:T(8,128)(2,1)S(1)}, bf16[16,6144]{1,0:T(8,128)(2,1)S(1)}, u32[]{:S(2)}, u32[]{:S(2)}) collective-permute-start(bf16[16,6144]{1,0:T(8,128)(2,1)S(1)} %get-tuple-element.54), channel_id=1, source_target_pairs={{0,4},{1,5},{4,8},{5,9},{8,12},{9,13},{12,14},{13,15},{14,10},{15,... | collective-permute-start | bytes 589832 | tf_op jit(solution)/shard_map/ppermute | solution.py:88
  68.0 8.3 %collective-permute-start.24 = (bf16[16,6144]{1,0:T(8,128)(2,1)S(1)}, bf16[16,6144]{1,0:T(8,128)(2,1)S(1)}, u32[]{:S(2)}, u32[]{:S(2)}) collective-permute-start(bf16[16,6144]{1,0:T(8,128)(2,1)S(1)} %fusion.14), channel_id=1, source_target_pairs={{4,0},{5,1},{8,4},{9,5},{12,8},{13,9},{14,12},{15,13},{10,14},{11,... | collective-permute-start | bytes 589832 | tf_op jit(solution)/shard_map/ppermute | solution.py:88
  69.7 7.8 %collective-permute-start.28 = (bf16[16,6144]{1,0:T(8,128)(2,1)S(1)}, bf16[16,6144]{1,0:T(8,128)(2,1)S(1)}, u32[]{:S(2)}, u32[]{:S(2)}) collective-permute-start(bf16[16,6144]{1,0:T(8,128)(2,1)S(1)} %fusion.13), channel_id=1, source_target_pairs={{0,4},{1,5},{4,8},{5,9},{8,12},{9,13},{12,14},{13,15},{14,10},{15,... | collective-permute-start | bytes 589832 | tf_op jit(solution)/shard_map/ppermute | solution.py:88
  70.4 10.0 %collective-permute-start.30 = (bf16[16,6144]{1,0:T(8,128)(2,1)S(1)}, bf16[16,6144]{1,0:T(8,128)(2,1)S(1)}, u32[]{:S(2)}, u32[]{:S(2)}) collective-permute-start(bf16[16,6144]{1,0:T(8,128)(2,1)S(1)} %fusion.12), channel_id=1, source_target_pairs={{4,0},{5,1},{8,4},{9,5},{12,8},{13,9},{14,12},{15,13},{10,14},{11,... | collective-permute-start | bytes 589832 | tf_op jit(solution)/shard_map/ppermute | solution.py:88
  72.1 8.4 %collective-permute-start.31 = (bf16[16,6144]{1,0:T(8,128)(2,1)S(1)}, bf16[16,6144]{1,0:T(8,128)(2,1)S(1)}, u32[]{:S(2)}, u32[]{:S(2)}) collective-permute-start(bf16[16,6144]{1,0:T(8,128)(2,1)S(1)} %fusion.11), channel_id=1, source_target_pairs={{0,4},{1,5},{4,8},{5,9},{8,12},{9,13},{12,14},{13,15},{14,10},{15,... | collective-permute-start | bytes 589832 | tf_op jit(solution)/shard_map/ppermute | solution.py:88
  78.3 8.2 %collective-permute-start.29 = (bf16[16,6144]{1,0:T(8,128)(2,1)S(1)}, bf16[16,6144]{1,0:T(8,128)(2,1)S(1)}, u32[]{:S(2)}, u32[]{:S(2)}) collective-permute-start(bf16[16,6144]{1,0:T(8,128)(2,1)S(1)} %get-tuple-element.60), channel_id=1, source_target_pairs={{4,0},{5,1},{8,4},{9,5},{12,8},{13,9},{14,12},{15,13},{10,14},{11,... | collective-permute-start | bytes 589832 | tf_op jit(solution)/shard_map/ppermute | solution.py:88
  79.9 9.6 %collective-permute-start.33 = (bf16[16,6144]{1,0:T(8,128)(2,1)S(1)}, bf16[16,6144]{1,0:T(8,128)(2,1)S(1)}, u32[]{:S(2)}, u32[]{:S(2)}) collective-permute-start(bf16[16,6144]{1,0:T(8,128)(2,1)S(1)} %get-tuple-element.67), channel_id=1, source_target_pairs={{0,4},{1,5},{4,8},{5,9},{8,12},{9,13},{12,14},{13,15},{14,10},{15,... | collective-permute-start | bytes 589832 | tf_op jit(solution)/shard_map/ppermute | solution.py:88
  80.6 14.9 %collective-permute-start.34 = (bf16[16,6144]{1,0:T(8,128)(2,1)S(1)}, bf16[16,6144]{1,0:T(8,128)(2,1)S(1)}, u32[]{:S(2)}, u32[]{:S(2)}) collective-permute-start(bf16[16,6144]{1,0:T(8,128)(2,1)S(1)} %get-tuple-element.68), channel_id=1, source_target_pairs={{4,0},{5,1},{8,4},{9,5},{12,8},{13,9},{14,12},{15,13},{10,14},{11,... | collective-permute-start | bytes 589832 | tf_op jit(solution)/shard_map/ppermute | solution.py:88
  82.2 6.7 %collective-permute-start.35 = (bf16[16,6144]{1,0:T(8,128)(2,1)S(1)}, bf16[16,6144]{1,0:T(8,128)(2,1)S(1)}, u32[]{:S(2)}, u32[]{:S(2)}) collective-permute-start(bf16[16,6144]{1,0:T(8,128)(2,1)S(1)} %get-tuple-element.69), channel_id=1, source_target_pairs={{0,4},{1,5},{4,8},{5,9},{8,12},{9,13},{12,14},{13,15},{14,10},{15,... | collective-permute-start | bytes 589832 | tf_op jit(solution)/shard_map/ppermute | solution.py:88
  86.5 10.7 %copy-start.1 = (bf16[128,6144]{1,0:T(8,128)(2,1)S(1)}, bf16[128,6144]{1,0:T(8,128)(2,1)}, u32[]{:S(2)}) copy-start(bf16[128,6144]{1,0:T(8,128)(2,1)} %param.8) | copy-start | bytes 4718596
  87.3 5.7 %collective-permute-start.32 = (bf16[16,6144]{1,0:T(8,128)(2,1)S(1)}, bf16[16,6144]{1,0:T(8,128)(2,1)S(1)}, u32[]{:S(2)}, u32[]{:S(2)}) collective-permute-start(bf16[16,6144]{1,0:T(8,128)(2,1)S(1)} %fusion.16), channel_id=1, source_target_pairs={{4,0},{5,1},{8,4},{9,5},{12,8},{13,9},{14,12},{15,13},{10,14},{11,... | collective-permute-start | bytes 589832 | tf_op jit(solution)/shard_map/ppermute | solution.py:88
  89.0 6.5 %collective-permute-start.36 = (bf16[16,6144]{1,0:T(8,128)(2,1)S(1)}, bf16[16,6144]{1,0:T(8,128)(2,1)S(1)}, u32[]{:S(2)}, u32[]{:S(2)}) collective-permute-start(bf16[16,6144]{1,0:T(8,128)(2,1)S(1)} %fusion.5), channel_id=1, source_target_pairs={{0,4},{1,5},{4,8},{5,9},{8,12},{9,13},{12,14},{13,15},{14,10},{15,... | collective-permute-start | bytes 589832 | tf_op jit(solution)/shard_map/ppermute | solution.py:88

commit v12 on v9

--- a/solution.py
+++ b/solution.py
@@ -207,6 +207,9 @@
                 grads.append(grad)
                 if work and at <= steps:
                     mark, out_carry = tie(mark, out_carry)
+                elif at <= steps:
+                    zero = mark[0, 0].astype(jnp.bfloat16)
+                    out_carry = {w: c + zero for w, c in out_carry.items()}
                 marks = [mark]
             dx_carry.update(send(dx_blocks))
         for side in work:

time: 98.5 us -> 96.9 us (0.984)
  waiting for transfers between devices: 32.2 us -> 29.3 us
    ppermute x37, waiting for transfers between devices: 32.2 us -> 29.3 us  [permute(): return lax.ppermute(x, 'et', pairs)]
  transfers between devices with their start and end apart: 37 -> 37, of which waited for: 17 -> 17; matrix products, arithmetic and copies ran while one was open for 16% -> 18% of each run, Pallas kernels for 11% -> 10%
where the time goes in v12:
time: 96.9 us; the launch traced here: 96.6 us
  starting transfers between devices  33.5 us (35%)
  waiting for transfers between devices  29.3 us (30%)
  matrix products  15.7 us (16%)
  Pallas kernels  9.85 us (10%)
  local copies, waits for them, and re-layouts  4.05 us (4%)
  other arithmetic  3.16 us (3%)
  between operations  1.13 us (1%)
    ppermute x37, starting transfers between devices, permute(): return lax.ppermute(x, 'et', pairs)  33.5 us
    ppermute x37, waiting for transfers between devices, permute(): return lax.ppermute(x, 'et', pairs)  29.3 us
    pallas_call x3, Pallas kernels, weight_grad(): pl.pallas_call(lambda *refs: grad_kernel(parts, width, len(marks), *refs)...  9.85 us
    dot_general x2, matrix products, per_device(): jnp.dot(select.T, final(total[0], carry), preferred_element_type=jnp.floa...  4.17 us
    unnamed x26, local copies, waits for them, and re-layouts  2.48 us
    dot_general x3, matrix products, per_device(): jnp.dot(select, a, preferred_element_type=jnp.float32).astype(jnp.bfloat16)  2.15 us
  transfers between devices with their start and end apart: 37, of which 17 were waited for; matrix products, arithmetic and copies ran while one was open for 18% of the time, Pallas kernels for 10%

profile of v12, /device:TPU:0, one launch (start us, length us, event | category | flops | bytes accessed | tf_op | source)
XLA Modules:
  0.0 96.6 jit_solution(12349281984041724767)
XLA Ops:
  0.6 0.8 select_reduce_fusion
  2.1 0.3 constant_dynamic-update-slice_fusion.32
  2.4 3.0 %collective-permute-start.10 = (bf16[16,6144]{1,0:T(8,128)(2,1)S(1)}, bf16[16,6144]{1,0:T(8,128)(2,1)S(1)}, u32[]{:S(2)}, u32[]{:S(2)}) collective-permute-start(bf16[16,6144]{1,0:T(8,128)(2,1)S(1)} %get-tuple-element.128), channel_id=1, source_target_pairs={{4,0},{5,1},{8,4},{9,5},{12,8},{13,9},{14,12},{15,13},{10,14},{11,... | collective-permute-start | bytes 589832 | tf_op jit(solution)/shard_map/ppermute | solution.py:88
  5.7 1.7 %convolution_convert_fusion.3 = bf16[16,6144]{1,0:T(8,128)(2,1)S(1)} fusion(bf16[128,6144]{1,0:T(8,128)(2,1)} %param.7, s32[128]{0:T(128)S(1)} %add_reduce_fusion, pred[128]{0:T(512)(128)(4,1)S(1)} %reduce_or.9), kind=kOutput, calls=%fused_computation.4 | convolution fusion | flops 25268224 | bytes 1770112 | tf_op jit(solution)/shard_map/dot_general | solution.py:161
  7.5 2.0 %collective-permute-start = (bf16[16,6272]{1,0:T(8,128)(2,1)S(1)}, bf16[16,6272]{1,0:T(8,128)(2,1)S(1)}, u32[]{:S(2)}, u32[]{:S(2)}) collective-permute-start(bf16[16,6272]{1,0:T(8,128)(2,1)S(1)} %get-tuple-element.113), channel_id=1, source_target_pairs={{0,4},{1,5},{4,8},{5,9},{8,12},{9,13},{12,14},{13,15},{14,10},{15,... | collective-permute-start | bytes 602120 | tf_op jit(solution)/shard_map/ppermute | solution.py:88
  9.6 0.8 collective-permute-done.10
  10.4 2.2 %collective-permute-start.12 = (bf16[16,6144]{1,0:T(8,128)(2,1)S(1)}, bf16[16,6144]{1,0:T(8,128)(2,1)S(1)}, u32[]{:S(2)}, u32[]{:S(2)}) collective-permute-start(bf16[16,6144]{1,0:T(8,128)(2,1)S(1)} %collective-permute-done.10), channel_id=1, source_target_pairs={{4,0},{5,1},{8,4},{9,5},{12,8},{13,9},{14,12},{15,13},{10,14},{11,... | collective-permute-start | bytes 589832 | tf_op jit(solution)/shard_map/ppermute | solution.py:88
  12.6 0.7 collective-permute-done.9
  13.3 4.2 %collective-permute-done = bf16[16,6272]{1,0:T(8,128)(2,1)S(1)} collective-permute-done((bf16[16,6272]{1,0:T(8,128)(2,1)S(1)}, bf16[16,6272]{1,0:T(8,128)(2,1)S(1)}, u32[]{:S(2)}, u32[]{:S(2)}) %collective-permute-start) | collective-permute-done | bytes 200736 | tf_op jit(solution)/shard_map/ppermute | solution.py:88
  17.5 2.0 %collective-permute-start.3 = (bf16[16,6272]{1,0:T(8,128)(2,1)S(1)}, bf16[16,6272]{1,0:T(8,128)(2,1)S(1)}, u32[]{:S(2)}, u32[]{:S(2)}) collective-permute-start(bf16[16,6272]{1,0:T(8,128)(2,1)S(1)} %collective-permute-done.1), channel_id=1, source_target_pairs={{4,0},{5,1},{8,4},{9,5},{12,8},{13,9},{14,12},{15,13},{10,14},{11,... | collective-permute-start | bytes 602120 | tf_op jit(solution)/shard_map/ppermute | solution.py:88
  19.6 1.5 %collective-permute-done.12 = bf16[16,6144]{1,0:T(8,128)(2,1)S(1)} collective-permute-done((bf16[16,6144]{1,0:T(8,128)(2,1)S(1)}, bf16[16,6144]{1,0:T(8,128)(2,1)S(1)}, u32[]{:S(2)}, u32[]{:S(2)}) %collective-permute-start.12) | collective-permute-done | bytes 196640 | tf_op jit(solution)/shard_map/ppermute | solution.py:88
  21.2 0.6 collective-permute-start.14
  21.8 1.4 %collective-permute-start.13 = (bf16[16,6144]{1,0:T(8,128)(2,1)S(1)}, bf16[16,6144]{1,0:T(8,128)(2,1)S(1)}, u32[]{:S(2)}, u32[]{:S(2)}) collective-permute-start(bf16[16,6144]{1,0:T(8,128)(2,1)S(1)} %collective-permute-done.11), channel_id=1, source_target_pairs={{0,4},{1,5},{4,8},{5,9},{8,12},{9,13},{12,14},{13,15},{14,10},{15,... | collective-permute-start | bytes 589832 | tf_op jit(solution)/shard_map/ppermute | solution.py:88
  23.3 2.8 %collective-permute-done.2 = bf16[16,6272]{1,0:T(8,128)(2,1)S(1)} collective-permute-done((bf16[16,6272]{1,0:T(8,128)(2,1)S(1)}, bf16[16,6272]{1,0:T(8,128)(2,1)S(1)}, u32[]{:S(2)}, u32[]{:S(2)}) %collective-permute-start.2) | collective-permute-done | bytes 200736 | tf_op jit(solution)/shard_map/ppermute | solution.py:88
  26.1 2.0 %collective-permute-start.5 = (bf16[16,6272]{1,0:T(8,128)(2,1)S(1)}, bf16[16,6272]{1,0:T(8,128)(2,1)S(1)}, u32[]{:S(2)}, u32[]{:S(2)}) collective-permute-start(bf16[16,6272]{1,0:T(8,128)(2,1)S(1)} %collective-permute-done.3), channel_id=1, source_target_pairs={{4,0},{5,1},{8,4},{9,5},{12,8},{13,9},{14,12},{15,13},{10,14},{11,... | collective-permute-start | bytes 602120 | tf_op jit(solution)/shard_map/ppermute | solution.py:88
  28.2 1.5 %collective-permute-done.14 = bf16[16,6144]{1,0:T(8,128)(2,1)S(1)} collective-permute-done((bf16[16,6144]{1,0:T(8,128)(2,1)S(1)}, bf16[16,6144]{1,0:T(8,128)(2,1)S(1)}, u32[]{:S(2)}, u32[]{:S(2)}) %collective-permute-start.14) | collective-permute-done | bytes 196640 | tf_op jit(solution)/shard_map/ppermute | solution.py:88
  29.7 0.9 collective-permute-start.16
  30.6 1.2 %collective-permute-start.15 = (bf16[16,3072]{1,0:T(8,128)(2,1)S(1)}, bf16[16,3072]{1,0:T(8,128)(2,1)S(1)}, u32[]{:S(2)}, u32[]{:S(2)}) collective-permute-start(bf16[16,3072]{1,0:T(8,128)(2,1)S(1)} %slice.147), channel_id=1, source_target_pairs={{0,4},{1,5},{4,8},{5,9},{8,12},{9,13},{12,14},{13,15},{14,10},{15,... | collective-permute-start | bytes 294920 | tf_op jit(solution)/shard_map/ppermute | solution.py:88
  31.9 2.3 %collective-permute-done.4 = bf16[16,6272]{1,0:T(8,128)(2,1)S(1)} collective-permute-done((bf16[16,6272]{1,0:T(8,128)(2,1)S(1)}, bf16[16,6272]{1,0:T(8,128)(2,1)S(1)}, u32[]{:S(2)}, u32[]{:S(2)}) %collective-permute-start.4) | collective-permute-done | bytes 200736 | tf_op jit(solution)/shard_map/ppermute | solution.py:88
  34.2 0.5 collective-permute-start.6
  34.7 1.7 %collective-permute-start.7 = (bf16[16,3200]{1,0:T(8,128)(2,1)S(1)}, bf16[16,3200]{1,0:T(8,128)(2,1)S(1)}, u32[]{:S(2)}, u32[]{:S(2)}) collective-permute-start(bf16[16,3200]{1,0:T(8,128)(2,1)S(1)} %slice.146), channel_id=1, source_target_pairs={{4,0},{5,1},{8,4},{9,5},{12,8},{13,9},{14,12},{15,13},{10,14},{11,... | collective-permute-start | bytes 307208 | tf_op jit(solution)/shard_map/ppermute | solution.py:88
  36.6 2.3 %collective-permute-done.6 = bf16[16,3072]{1,0:T(8,128)(2,1)S(1)} collective-permute-done((bf16[16,3072]{1,0:T(8,128)(2,1)S(1)}, bf16[16,3072]{1,0:T(8,128)(2,1)S(1)}, u32[]{:S(2)}, u32[]{:S(2)}) %collective-permute-start.6) | collective-permute-done | bytes 98336 | tf_op jit(solution)/shard_map/ppermute | solution.py:88
  38.9 0.5 collective-permute-done.7
  39.5 1.4 %collective-permute-done.17 = bf16[16,6272]{1,0:T(8,128)(2,1)S(1)} collective-permute-done((bf16[16,6272]{1,0:T(8,128)(2,1)S(1)}, bf16[16,6272]{1,0:T(8,128)(2,1)S(1)}, u32[]{:S(2)}, u32[]{:S(2)}) %collective-permute-start.17) | collective-permute-done | bytes 200736 | tf_op jit(solution)/shard_map/ppermute | solution.py:88
  41.4 1.3 %fusion.2 = f32[256,336]{0,1:T(8,128)S(1)} fusion(bf16[6144,336]{0,1:T(8,128)(2,1)S(1)} %copy-done.3, bf16[256,6272]{1,0:T(8,128)(2,1)S(1)} %constant_dynamic-update-slice_fusion.14.refs_1_), kind=kOutput, calls=%fused_computation.9 | convolution fusion | flops 1056964608 | bytes 7618560 | tf_op jit(solution)/shard_map/dot_general | solution.py:172
  42.7 0.8 copy-done.4
  43.5 1.3 %multiply_convert_fusion.2 = (bf16[256,336]{0,1:T(8,128)(2,1)S(1)}, f32[256,336]{0,1:T(8,128)S(1)}) fusion(f32[256]{0:T(256)S(1)} %convert_reduce_fusion, f32[256,336]{0,1:T(8,128)S(1)} %fusion.2, bf16[6144,336]{0,1:T(8,128)(2,1)S(1)} %copy-done.4, bf16[256,6272]{1,0:T(8,128)(2,1)S(1)} %constant_dynamic-update-slice_fusion.14.refs_1_), kind=kOutput, calls=%fused_computation.46 | convolution fusion | flops 1057566720 | bytes 8135680 | tf_op jit(solution)/shard_map/dot_general | solution.py:173
  44.8 0.9 copy-done.2
  45.7 1.8 %fusion.44 = f32[256,6144]{1,0:T(8,128)S(1)} fusion(bf16[256,336]{0,1:T(8,128)(2,1)S(1)} %get-tuple-element.55, bf16[336,6144]{1,0:T(8,128)(2,1)S(1)} %copy-done.2), kind=kOutput, calls=%fused_computation.111 | convolution fusion | flops 1056964608 | bytes 10592256 | tf_op jit(solution)/shard_map/dot_general | solution.py:177
  47.5 0.2 slice.227
  47.9 0.4 collective-permute-start.20
  48.4 0.2 collective-permute-start.19
  48.6 1.3 %multiply_convert_fusion = (bf16[256,336]{0,1:T(8,128)(2,1)S(1)}, bf16[256,336]{0,1:T(8,128)(2,1)S(1)}) fusion(f32[256,336]{0,1:T(8,128)S(1)} %fusion.2, f32[256,336]{0,1:T(8,128)S(1)} %get-tuple-element.130, bf16[256,6144]{1,0:T(8,128)(2,1)S(1)} %constant_dynamic-update-slice_fusion.24.refs_1_, bf16[336,6144]{1,0:T(8,128)(2,1)S(1)} %copy-done.2, ...), kind=kOutput, calls=%fused_computation.44 | convolution fusion | flops 1058168832 | bytes 8307712 | tf_op jit(solution)/shard_map/dot_general | solution.py:182
  50.2 1.7 %collective-permute-start.22 = (bf16[16,6144]{1,0:T(8,128)(2,1)S(1)}, bf16[16,6144]{1,0:T(8,128)(2,1)S(1)}, u32[]{:S(2)}, u32[]{:S(2)}) collective-permute-start(bf16[16,6144]{1,0:T(8,128)(2,1)S(1)} %get-tuple-element.57), channel_id=1, source_target_pairs={{4,0},{5,1},{8,4},{9,5},{12,8},{13,9},{14,12},{15,13},{10,14},{11,... | collective-permute-start | bytes 589832 | tf_op jit(solution)/shard_map/ppermute | solution.py:88
  51.9 0.4 collective-permute-start.23
  52.3 1.8 %fusion.45 = f32[256,6144]{1,0:T(8,128)S(1)} fusion(bf16[256,336]{0,1:T(8,128)(2,1)S(1)} %get-tuple-element.54, bf16[6144,336]{0,1:T(8,128)(2,1)S(1)} %copy-done.3), kind=kOutput, calls=%fused_computation.112 | convolution fusion | flops 1056964608 | bytes 10592256 | tf_op jit(solution)/shard_map/dot_general | solution.py:188
  54.1 1.8 %convolution_add_fusion = f32[256,6144]{1,0:T(8,128)S(1)} fusion(f32[256,6144]{1,0:T(8,128)S(1)} %fusion.45, bf16[256,336]{0,1:T(8,128)(2,1)S(1)} %get-tuple-element.72, bf16[6144,336]{0,1:T(8,128)(2,1)S(1)} %copy-done.4), kind=kOutput, calls=%fused_computation | convolution fusion | flops 1058537472 | bytes 16883712 | tf_op jit(solution)/shard_map/dot_general | solution.py:188
  56.3 3.3 %shard_map.110 = (bf16[336,6144]{1,0:T(8,128)(2,1)}, f32[8,128]{1,0:T(8,128)S(1)}) custom-call(bf16[336,256]{1,0:T(8,128)(2,1)S(1)} %bitcast.28, bf16[256,6144]{1,0:T(8,128)(2,1)S(1)} %constant_dynamic-update-slice_fusion.24.refs_1_), custom_call_target="tpu_custom_call" | custom-call | flops 1056964608 | bytes 7274496 | tf_op jit(solution)/shard_map/pallas_call | solution.py:54
  59.8 1.7 %collective-permute-start.24 = (bf16[16,6144]{1,0:T(8,128)(2,1)S(1)}, bf16[16,6144]{1,0:T(8,128)(2,1)S(1)}, u32[]{:S(2)}, u32[]{:S(2)}) collective-permute-start(bf16[16,6144]{1,0:T(8,128)(2,1)S(1)} %fusion.14), channel_id=1, source_target_pairs={{4,0},{5,1},{8,4},{9,5},{12,8},{13,9},{14,12},{15,13},{10,14},{11,... | collective-permute-start | bytes 589832 | tf_op jit(solution)/shard_map/ppermute | solution.py:88
  61.5 0.4 collective-permute-start.25
  62.1 1.7 %collective-permute-start.29 = (bf16[16,6144]{1,0:T(8,128)(2,1)S(1)}, bf16[16,6144]{1,0:T(8,128)(2,1)S(1)}, u32[]{:S(2)}, u32[]{:S(2)}) collective-permute-start(bf16[16,6144]{1,0:T(8,128)(2,1)S(1)} %get-tuple-element.69), channel_id=1, source_target_pairs={{0,4},{1,5},{4,8},{5,9},{8,12},{9,13},{12,14},{13,15},{14,10},{15,... | collective-permute-start | bytes 589832 | tf_op jit(solution)/shard_map/ppermute | solution.py:88
  64.0 0.4 collective-permute-start.28
  64.4 3.3 %shard_map.111 = (bf16[336,6144]{1,0:T(8,128)(2,1)}, f32[8,128]{1,0:T(8,128)S(1)}) custom-call(bf16[336,256]{1,0:T(8,128)(2,1)S(1)} %bitcast.27, bf16[256,6272]{1,0:T(8,128)(2,1)S(1)} %constant_dynamic-update-slice_fusion.14.refs_1_, f32[8,128]{1,0:T(8,128)S(1)} %get-tuple-element.59.refs_2_), custom_call_target="tpu_custom_call" | custom-call | flops 1056964608 | bytes 7274496 | tf_op jit(solution)/shard_map/pallas_call | solution.py:54
  67.7 1.5 %collective-permute-done.25 = bf16[16,6144]{1,0:T(8,128)(2,1)S(1)} collective-permute-done((bf16[16,6144]{1,0:T(8,128)(2,1)S(1)}, bf16[16,6144]{1,0:T(8,128)(2,1)S(1)}, u32[]{:S(2)}, u32[]{:S(2)}) %collective-permute-start.25) | collective-permute-done | bytes 196640 | tf_op jit(solution)/shard_map/ppermute | solution.py:88
  69.3 3.5 %collective-permute-done.29 = bf16[16,6144]{1,0:T(8,128)(2,1)S(1)} collective-permute-done((bf16[16,6144]{1,0:T(8,128)(2,1)S(1)}, bf16[16,6144]{1,0:T(8,128)(2,1)S(1)}, u32[]{:S(2)}, u32[]{:S(2)}) %collective-permute-start.29) | collective-permute-done | bytes 196640 | tf_op jit(solution)/shard_map/ppermute | solution.py:88
  72.8 0.2 slice_add_fusion
  73.1 1.6 %collective-permute-start.32 = (bf16[16,6144]{1,0:T(8,128)(2,1)S(1)}, bf16[16,6144]{1,0:T(8,128)(2,1)S(1)}, u32[]{:S(2)}, u32[]{:S(2)}) collective-permute-start(bf16[16,6144]{1,0:T(8,128)(2,1)S(1)} %fusion.11), channel_id=1, source_target_pairs={{4,0},{5,1},{8,4},{9,5},{12,8},{13,9},{14,12},{15,13},{10,14},{11,... | collective-permute-start | bytes 589832 | tf_op jit(solution)/shard_map/ppermute | solution.py:88
  74.7 0.4 collective-permute-start.33
  75.2 1.6 %collective-permute-start.26 = (bf16[16,6144]{1,0:T(8,128)(2,1)S(1)}, bf16[16,6144]{1,0:T(8,128)(2,1)S(1)}, u32[]{:S(2)}, u32[]{:S(2)}) collective-permute-start(bf16[16,6144]{1,0:T(8,128)(2,1)S(1)} %get-tuple-element.67), channel_id=1, source_target_pairs={{4,0},{5,1},{8,4},{9,5},{12,8},{13,9},{14,12},{15,13},{10,14},{11,... | collective-permute-start | bytes 589832 | tf_op jit(solution)/shard_map/ppermute | solution.py:88
  76.9 0.4 collective-permute-start.31
  77.3 3.3 %shard_map.112 = (bf16[336,6144]{1,0:T(8,128)(2,1)}, f32[8,128]{1,0:T(8,128)S(1)}) custom-call(bf16[336,256]{1,0:T(8,128)(2,1)S(1)} %bitcast.29, bf16[256,6272]{1,0:T(8,128)(2,1)S(1)} %constant_dynamic-update-slice_fusion.14.refs_1_, f32[8,128]{1,0:T(8,128)S(1)} %get-tuple-element.73.refs_2_), custom_call_target="tpu_custom_call" | custom-call | flops 1056964608 | bytes 7274496 | tf_op jit(solution)/shard_map/pallas_call | solution.py:54
  80.6 0.5 slice.140
  81.1 1.4 %collective-permute-done.33 = bf16[16,6144]{1,0:T(8,128)(2,1)S(1)} collective-permute-done((bf16[16,6144]{1,0:T(8,128)(2,1)S(1)}, bf16[16,6144]{1,0:T(8,128)(2,1)S(1)}, u32[]{:S(2)}, u32[]{:S(2)}) %collective-permute-start.33) | collective-permute-done | bytes 196640 | tf_op jit(solution)/shard_map/ppermute | solution.py:88
  82.6 0.5 collective-permute-start.35
  83.1 0.4 collective-permute-done.26
  83.6 0.8 fusion.16
  84.4 1.6 %collective-permute-start.30 = (bf16[16,6144]{1,0:T(8,128)(2,1)S(1)}, bf16[16,6144]{1,0:T(8,128)(2,1)S(1)}, u32[]{:S(2)}, u32[]{:S(2)}) collective-permute-start(bf16[16,6144]{1,0:T(8,128)(2,1)S(1)} %fusion.16), channel_id=1, source_target_pairs={{4,0},{5,1},{8,4},{9,5},{12,8},{13,9},{14,12},{15,13},{10,14},{11,... | collective-permute-start | bytes 589832 | tf_op jit(solution)/shard_map/ppermute | solution.py:88
  86.0 1.6 %collective-permute-start.34 = (bf16[16,6144]{1,0:T(8,128)(2,1)S(1)}, bf16[16,6144]{1,0:T(8,128)(2,1)S(1)}, u32[]{:S(2)}, u32[]{:S(2)}) collective-permute-start(bf16[16,6144]{1,0:T(8,128)(2,1)S(1)} %get-tuple-element.78), channel_id=1, source_target_pairs={{4,0},{5,1},{8,4},{9,5},{12,8},{13,9},{14,12},{15,13},{10,14},{11,... | collective-permute-start | bytes 589832 | tf_op jit(solution)/shard_map/ppermute | solution.py:88
  87.6 1.5 %collective-permute-done.35 = bf16[16,6144]{1,0:T(8,128)(2,1)S(1)} collective-permute-done((bf16[16,6144]{1,0:T(8,128)(2,1)S(1)}, bf16[16,6144]{1,0:T(8,128)(2,1)S(1)}, u32[]{:S(2)}, u32[]{:S(2)}) %collective-permute-start.35) | collective-permute-done | bytes 196640 | tf_op jit(solution)/shard_map/ppermute | solution.py:88
  89.1 0.5 collective-permute-start.36
  89.6 2.2 %collective-permute-done.30 = bf16[16,6144]{1,0:T(8,128)(2,1)S(1)} collective-permute-done((bf16[16,6144]{1,0:T(8,128)(2,1)S(1)}, bf16[16,6144]{1,0:T(8,128)(2,1)S(1)}, u32[]{:S(2)}, u32[]{:S(2)}) %collective-permute-start.30) | collective-permute-done | bytes 196640 | tf_op jit(solution)/shard_map/ppermute | solution.py:88
  91.8 2.4 %convolution_convert_fusion.1 = bf16[128,6144]{1,0:T(8,128)(2,1)} fusion(f32[80,6144]{1,0:T(8,128)S(1)} %slice_add_fusion.1, bf16[16,6144]{1,0:T(8,128)(2,1)S(1)} %collective-permute-done.30, bf16[16,6144]{1,0:T(8,128)(2,1)S(1)} %collective-permute-done.31, bf16[]{:T(256)} %bitcast.6, s32[128]{0:T(128)S(1)} %add_reduce_fusion, pred[128]{0:T(512)(128)(4,1)S(1)} %reduce_or.9), kind=kOutput, calls=%fused_computation.2 | convolution fusion | flops 26546176 | bytes 2360322 | tf_op jit(solution)/shard_map/dot_general | solution.py:219
  94.2 0.6 collective-permute-done.36
  94.8 1.8 %convolution_convert_fusion = bf16[128,6144]{1,0:T(8,128)(2,1)} fusion(f32[80,6144]{1,0:T(8,128)S(1)} %slice_add_fusion, bf16[16,6144]{1,0:T(8,128)(2,1)S(1)} %collective-permute-done.36, bf16[16,6144]{1,0:T(8,128)(2,1)S(1)} %collective-permute-done.34, s32[128]{0:T(128)S(1)} %add_reduce_fusion, pred[128]{0:T(512)(128)(4,1)S(1)} %reduce_or.9), kind=kOutput, calls=%fused_computation.1 | convolution fusion | flops 26447872 | bytes 2360320 | tf_op jit(solution)/shard_map/dot_general | solution.py:219
  (90 shorter events, 3.8 us)
Async XLA Ops:
  0.6 1.4 %copy-start = (bf16[128,6144]{1,0:T(8,128)(2,1)S(1)}, bf16[128,6144]{1,0:T(8,128)(2,1)}, u32[]{:S(2)}) copy-start(bf16[128,6144]{1,0:T(8,128)(2,1)} %param.8) | copy-start | bytes 4718596
  2.4 8.0 %collective-permute-start.10 = (bf16[16,6144]{1,0:T(8,128)(2,1)S(1)}, bf16[16,6144]{1,0:T(8,128)(2,1)S(1)}, u32[]{:S(2)}, u32[]{:S(2)}) collective-permute-start(bf16[16,6144]{1,0:T(8,128)(2,1)S(1)} %get-tuple-element.128), channel_id=1, source_target_pairs={{4,0},{5,1},{8,4},{9,5},{12,8},{13,9},{14,12},{15,13},{10,14},{11,... | collective-permute-start | bytes 589832 | tf_op jit(solution)/shard_map/ppermute | solution.py:88
  5.4 7.8 %collective-permute-start.9 = (bf16[16,6144]{1,0:T(8,128)(2,1)S(1)}, bf16[16,6144]{1,0:T(8,128)(2,1)S(1)}, u32[]{:S(2)}, u32[]{:S(2)}) collective-permute-start(bf16[16,6144]{1,0:T(8,128)(2,1)S(1)} %get-tuple-element.128), channel_id=1, source_target_pairs={{0,4},{1,5},{4,8},{5,9},{8,12},{9,13},{12,14},{13,15},{14,10},{15,... | collective-permute-start | bytes 589832 | tf_op jit(solution)/shard_map/ppermute | solution.py:88
  7.5 10.0 %collective-permute-start = (bf16[16,6272]{1,0:T(8,128)(2,1)S(1)}, bf16[16,6272]{1,0:T(8,128)(2,1)S(1)}, u32[]{:S(2)}, u32[]{:S(2)}) collective-permute-start(bf16[16,6272]{1,0:T(8,128)(2,1)S(1)} %get-tuple-element.113), channel_id=1, source_target_pairs={{0,4},{1,5},{4,8},{5,9},{8,12},{9,13},{12,14},{13,15},{14,10},{15,... | collective-permute-start | bytes 602120 | tf_op jit(solution)/shard_map/ppermute | solution.py:88
  9.5 8.0 %collective-permute-start.1 = (bf16[16,6272]{1,0:T(8,128)(2,1)S(1)}, bf16[16,6272]{1,0:T(8,128)(2,1)S(1)}, u32[]{:S(2)}, u32[]{:S(2)}) collective-permute-start(bf16[16,6272]{1,0:T(8,128)(2,1)S(1)} %get-tuple-element.113), channel_id=1, source_target_pairs={{4,0},{5,1},{8,4},{9,5},{12,8},{13,9},{14,12},{15,13},{10,14},{11,... | collective-permute-start | bytes 602120 | tf_op jit(solution)/shard_map/ppermute | solution.py:88
  10.4 10.8 %collective-permute-start.12 = (bf16[16,6144]{1,0:T(8,128)(2,1)S(1)}, bf16[16,6144]{1,0:T(8,128)(2,1)S(1)}, u32[]{:S(2)}, u32[]{:S(2)}) collective-permute-start(bf16[16,6144]{1,0:T(8,128)(2,1)S(1)} %collective-permute-done.10), channel_id=1, source_target_pairs={{4,0},{5,1},{8,4},{9,5},{12,8},{13,9},{14,12},{15,13},{10,14},{11,... | collective-permute-start | bytes 589832 | tf_op jit(solution)/shard_map/ppermute | solution.py:88
  13.2 8.5 %collective-permute-start.11 = (bf16[16,6144]{1,0:T(8,128)(2,1)S(1)}, bf16[16,6144]{1,0:T(8,128)(2,1)S(1)}, u32[]{:S(2)}, u32[]{:S(2)}) collective-permute-start(bf16[16,6144]{1,0:T(8,128)(2,1)S(1)} %collective-permute-done.9), channel_id=1, source_target_pairs={{0,4},{1,5},{4,8},{5,9},{8,12},{9,13},{12,14},{13,15},{14,10},{15,... | collective-permute-start | bytes 589832 | tf_op jit(solution)/shard_map/ppermute | solution.py:88
  17.5 8.5 %collective-permute-start.2 = (bf16[16,6272]{1,0:T(8,128)(2,1)S(1)}, bf16[16,6272]{1,0:T(8,128)(2,1)S(1)}, u32[]{:S(2)}, u32[]{:S(2)}) collective-permute-start(bf16[16,6272]{1,0:T(8,128)(2,1)S(1)} %collective-permute-done), channel_id=1, source_target_pairs={{0,4},{1,5},{4,8},{5,9},{8,12},{9,13},{12,14},{13,15},{14,10},{15,... | collective-permute-start | bytes 602120 | tf_op jit(solution)/shard_map/ppermute | solution.py:88
  17.5 8.5 %collective-permute-start.3 = (bf16[16,6272]{1,0:T(8,128)(2,1)S(1)}, bf16[16,6272]{1,0:T(8,128)(2,1)S(1)}, u32[]{:S(2)}, u32[]{:S(2)}) collective-permute-start(bf16[16,6272]{1,0:T(8,128)(2,1)S(1)} %collective-permute-done.1), channel_id=1, source_target_pairs={{4,0},{5,1},{8,4},{9,5},{12,8},{13,9},{14,12},{15,13},{10,14},{11,... | collective-permute-start | bytes 602120 | tf_op jit(solution)/shard_map/ppermute | solution.py:88
  21.2 8.5 %collective-permute-start.14 = (bf16[16,6144]{1,0:T(8,128)(2,1)S(1)}, bf16[16,6144]{1,0:T(8,128)(2,1)S(1)}, u32[]{:S(2)}, u32[]{:S(2)}) collective-permute-start(bf16[16,6144]{1,0:T(8,128)(2,1)S(1)} %collective-permute-done.12), channel_id=1, source_target_pairs={{4,0},{5,1},{8,4},{9,5},{12,8},{13,9},{14,12},{15,13},{10,14},{11,... | collective-permute-start | bytes 589832 | tf_op jit(solution)/shard_map/ppermute | solution.py:88
  21.8 8.8 %collective-permute-start.13 = (bf16[16,6144]{1,0:T(8,128)(2,1)S(1)}, bf16[16,6144]{1,0:T(8,128)(2,1)S(1)}, u32[]{:S(2)}, u32[]{:S(2)}) collective-permute-start(bf16[16,6144]{1,0:T(8,128)(2,1)S(1)} %collective-permute-done.11), channel_id=1, source_target_pairs={{0,4},{1,5},{4,8},{5,9},{8,12},{9,13},{12,14},{13,15},{14,10},{15,... | collective-permute-start | bytes 589832 | tf_op jit(solution)/shard_map/ppermute | solution.py:88
  26.1 8.1 %collective-permute-start.4 = (bf16[16,6272]{1,0:T(8,128)(2,1)S(1)}, bf16[16,6272]{1,0:T(8,128)(2,1)S(1)}, u32[]{:S(2)}, u32[]{:S(2)}) collective-permute-start(bf16[16,6272]{1,0:T(8,128)(2,1)S(1)} %collective-permute-done.2), channel_id=1, source_target_pairs={{0,4},{1,5},{4,8},{5,9},{8,12},{9,13},{12,14},{13,15},{14,10},{15,... | collective-permute-start | bytes 602120 | tf_op jit(solution)/shard_map/ppermute | solution.py:88
  26.1 8.6 %collective-permute-start.5 = (bf16[16,6272]{1,0:T(8,128)(2,1)S(1)}, bf16[16,6272]{1,0:T(8,128)(2,1)S(1)}, u32[]{:S(2)}, u32[]{:S(2)}) collective-permute-start(bf16[16,6272]{1,0:T(8,128)(2,1)S(1)} %collective-permute-done.3), channel_id=1, source_target_pairs={{4,0},{5,1},{8,4},{9,5},{12,8},{13,9},{14,12},{15,13},{10,14},{11,... | collective-permute-start | bytes 602120 | tf_op jit(solution)/shard_map/ppermute | solution.py:88
  29.7 6.8 %collective-permute-start.16 = (bf16[16,3072]{1,0:T(8,128)(2,1)S(1)}, bf16[16,3072]{1,0:T(8,128)(2,1)S(1)}, u32[]{:S(2)}, u32[]{:S(2)}) collective-permute-start(bf16[16,3072]{1,0:T(8,128)(2,1)S(1)} %slice.148), channel_id=1, source_target_pairs={{4,0},{5,1},{8,4},{9,5},{12,8},{13,9},{14,12},{15,13},{10,14},{11,... | collective-permute-start | bytes 294920 | tf_op jit(solution)/shard_map/ppermute | solution.py:88
  30.6 5.9 %collective-permute-start.15 = (bf16[16,3072]{1,0:T(8,128)(2,1)S(1)}, bf16[16,3072]{1,0:T(8,128)(2,1)S(1)}, u32[]{:S(2)}, u32[]{:S(2)}) collective-permute-start(bf16[16,3072]{1,0:T(8,128)(2,1)S(1)} %slice.147), channel_id=1, source_target_pairs={{0,4},{1,5},{4,8},{5,9},{8,12},{9,13},{12,14},{13,15},{14,10},{15,... | collective-permute-start | bytes 294920 | tf_op jit(solution)/shard_map/ppermute | solution.py:88
  34.2 7.2 %copy-start.3 = (bf16[6144,336]{0,1:T(8,128)(2,1)S(1)}, bf16[6144,336]{0,1:T(8,128)(2,1)}, u32[]{:S(2)}) copy-start(bf16[6144,336]{0,1:T(8,128)(2,1)} %param.11) | copy-start | bytes 12386308
  34.2 4.7 %collective-permute-start.6 = (bf16[16,3072]{1,0:T(8,128)(2,1)S(1)}, bf16[16,3072]{1,0:T(8,128)(2,1)S(1)}, u32[]{:S(2)}, u32[]{:S(2)}) collective-permute-start(bf16[16,3072]{1,0:T(8,128)(2,1)S(1)} %slice.145), channel_id=1, source_target_pairs={{0,4},{1,5},{4,8},{5,9},{8,12},{9,13},{12,14},{13,15},{14,10},{15,... | collective-permute-start | bytes 294920 | tf_op jit(solution)/shard_map/ppermute | solution.py:88
  34.7 4.7 %collective-permute-start.7 = (bf16[16,3200]{1,0:T(8,128)(2,1)S(1)}, bf16[16,3200]{1,0:T(8,128)(2,1)S(1)}, u32[]{:S(2)}, u32[]{:S(2)}) collective-permute-start(bf16[16,3200]{1,0:T(8,128)(2,1)S(1)} %slice.146), channel_id=1, source_target_pairs={{4,0},{5,1},{8,4},{9,5},{12,8},{13,9},{14,12},{15,13},{10,14},{11,... | collective-permute-start | bytes 307208 | tf_op jit(solution)/shard_map/ppermute | solution.py:88
  36.4 4.6 %collective-permute-start.8 = (bf16[112,6272]{1,0:T(8,128)(2,1)S(1)}, bf16[112,6272]{1,0:T(8,128)(2,1)S(1)}, u32[]{:S(2)}, u32[]{:S(2)}) collective-permute-start(bf16[112,6272]{1,0:T(8,128)(2,1)S(1)} %get-tuple-element.99), channel_id=1, source_target_pairs={{0,1},{1,0},{2,3},{3,2},{4,5},{5,4},{6,7},{7,6},{8,9},{9,8},{10,11... | collective-permute-start | bytes 4214792 | tf_op jit(solution)/shard_map/ppermute | solution.py:88
  39.4 1.5 %collective-permute-start.17 = (bf16[16,6272]{1,0:T(8,128)(2,1)S(1)}, bf16[16,6272]{1,0:T(8,128)(2,1)S(1)}, u32[]{:S(2)}, u32[]{:S(2)}) collective-permute-start(bf16[16,6272]{1,0:T(8,128)(2,1)S(1)} %pad_maximum_fusion), channel_id=1, source_target_pairs={{0,1},{1,0},{2,3},{3,2},{4,5},{5,4},{6,7},{7,6},{8,9},{9,8},{10,11... | collective-permute-start | bytes 602120 | tf_op jit(solution)/shard_map/ppermute | solution.py:88
  40.9 6.8 %collective-permute-start.18 = (bf16[128,6144]{1,0:T(8,128)(2,1)S(1)}, bf16[128,6144]{1,0:T(8,128)(2,1)S(1)}, u32[]{:S(2)}, u32[]{:S(2)}) collective-permute-start(bf16[128,6144]{1,0:T(8,128)(2,1)S(1)} %maximum_dynamic-update-slice_fusion), channel_id=1, source_target_pairs={{0,1},{1,0},{2,3},{3,2},{4,5},{5,4},{6,7},{7,6},{8,9},{9,8},{10,11... | collective-permute-start | bytes 4718600 | tf_op jit(solution)/shard_map/ppermute | solution.py:88
  41.4 2.2 %copy-start.4 = (bf16[6144,336]{0,1:T(8,128)(2,1)S(1)}, bf16[6144,336]{0,1:T(8,128)(2,1)}, u32[]{:S(2)}) copy-start(bf16[6144,336]{0,1:T(8,128)(2,1)} %param.12) | copy-start | bytes 12386308
  43.5 2.2 %copy-start.2 = (bf16[336,6144]{1,0:T(8,128)(2,1)S(1)}, bf16[336,6144]{1,0:T(8,128)(2,1)}, u32[]{:S(2)}) copy-start(bf16[336,6144]{1,0:T(8,128)(2,1)} %param.13) | copy-start | bytes 12386308
  47.9 2.1 %collective-permute-start.20 = (bf16[48,6144]{1,0:T(8,128)(2,1)S(1)}, bf16[48,6144]{1,0:T(8,128)(2,1)S(1)}, u32[]{:S(2)}, u32[]{:S(2)}) collective-permute-start(bf16[48,6144]{1,0:T(8,128)(2,1)S(1)} %slice.125), channel_id=1, source_target_pairs={{0,1},{1,0},{2,3},{3,2},{4,5},{5,4},{6,7},{7,6},{8,9},{9,8},{10,11... | collective-permute-start | bytes 1769480 | tf_op jit(solution)/shard_map/ppermute | solution.py:88
  48.4 11.2 %collective-permute-start.19 = (bf16[80,6144]{1,0:T(8,128)(2,1)S(1)}, bf16[80,6144]{1,0:T(8,128)(2,1)S(1)}, u32[]{:S(2)}, u32[]{:S(2)}) collective-permute-start(bf16[80,6144]{1,0:T(8,128)(2,1)S(1)} %slice.120), channel_id=1, source_target_pairs={{0,1},{1,0},{2,3},{3,2},{4,5},{5,4},{6,7},{7,6},{8,9},{9,8},{10,11... | collective-permute-start | bytes 2949128 | tf_op jit(solution)/shard_map/ppermute | solution.py:88
  50.2 9.4 %collective-permute-start.22 = (bf16[16,6144]{1,0:T(8,128)(2,1)S(1)}, bf16[16,6144]{1,0:T(8,128)(2,1)S(1)}, u32[]{:S(2)}, u32[]{:S(2)}) collective-permute-start(bf16[16,6144]{1,0:T(8,128)(2,1)S(1)} %get-tuple-element.57), channel_id=1, source_target_pairs={{4,0},{5,1},{8,4},{9,5},{12,8},{13,9},{14,12},{15,13},{10,14},{11,... | collective-permute-start | bytes 589832 | tf_op jit(solution)/shard_map/ppermute | solution.py:88
  51.9 7.7 %collective-permute-start.23 = (bf16[16,6144]{1,0:T(8,128)(2,1)S(1)}, bf16[16,6144]{1,0:T(8,128)(2,1)S(1)}, u32[]{:S(2)}, u32[]{:S(2)}) collective-permute-start(bf16[16,6144]{1,0:T(8,128)(2,1)S(1)} %get-tuple-element.58), channel_id=1, source_target_pairs={{0,4},{1,5},{4,8},{5,9},{8,12},{9,13},{12,14},{13,15},{14,10},{15,... | collective-permute-start | bytes 589832 | tf_op jit(solution)/shard_map/ppermute | solution.py:88
  56.2 5.7 %collective-permute-start.21 = (bf16[48,6144]{1,0:T(8,128)(2,1)S(1)}, bf16[48,6144]{1,0:T(8,128)(2,1)S(1)}, u32[]{:S(2)}, u32[]{:S(2)}) collective-permute-start(bf16[48,6144]{1,0:T(8,128)(2,1)S(1)} %slice.130), channel_id=1, source_target_pairs={{0,1},{1,0},{2,3},{3,2},{4,5},{5,4},{6,7},{7,6},{8,9},{9,8},{10,11... | collective-permute-start | bytes 1769480 | tf_op jit(solution)/shard_map/ppermute | solution.py:88
  59.8 7.9 %collective-permute-start.24 = (bf16[16,6144]{1,0:T(8,128)(2,1)S(1)}, bf16[16,6144]{1,0:T(8,128)(2,1)S(1)}, u32[]{:S(2)}, u32[]{:S(2)}) collective-permute-start(bf16[16,6144]{1,0:T(8,128)(2,1)S(1)} %fusion.14), channel_id=1, source_target_pairs={{4,0},{5,1},{8,4},{9,5},{12,8},{13,9},{14,12},{15,13},{10,14},{11,... | collective-permute-start | bytes 589832 | tf_op jit(solution)/shard_map/ppermute | solution.py:88
  61.5 7.7 %collective-permute-start.25 = (bf16[16,6144]{1,0:T(8,128)(2,1)S(1)}, bf16[16,6144]{1,0:T(8,128)(2,1)S(1)}, u32[]{:S(2)}, u32[]{:S(2)}) collective-permute-start(bf16[16,6144]{1,0:T(8,128)(2,1)S(1)} %fusion.13), channel_id=1, source_target_pairs={{0,4},{1,5},{4,8},{5,9},{8,12},{9,13},{12,14},{13,15},{14,10},{15,... | collective-permute-start | bytes 589832 | tf_op jit(solution)/shard_map/ppermute | solution.py:88
  62.1 10.6 %collective-permute-start.29 = (bf16[16,6144]{1,0:T(8,128)(2,1)S(1)}, bf16[16,6144]{1,0:T(8,128)(2,1)S(1)}, u32[]{:S(2)}, u32[]{:S(2)}) collective-permute-start(bf16[16,6144]{1,0:T(8,128)(2,1)S(1)} %get-tuple-element.69), channel_id=1, source_target_pairs={{0,4},{1,5},{4,8},{5,9},{8,12},{9,13},{12,14},{13,15},{14,10},{15,... | collective-permute-start | bytes 589832 | tf_op jit(solution)/shard_map/ppermute | solution.py:88
  63.9 8.9 %collective-permute-start.27 = (bf16[80,6144]{1,0:T(8,128)(2,1)S(1)}, bf16[80,6144]{1,0:T(8,128)(2,1)S(1)}, u32[]{:S(2)}, u32[]{:S(2)}) collective-permute-start(bf16[80,6144]{1,0:T(8,128)(2,1)S(1)} %slice.137), channel_id=1, source_target_pairs={{0,1},{1,0},{2,3},{3,2},{4,5},{5,4},{6,7},{7,6},{8,9},{9,8},{10,11... | collective-permute-start | bytes 2949128 | tf_op jit(solution)/shard_map/ppermute | solution.py:88
  64.0 9.0 %collective-permute-start.28 = (bf16[16,6144]{1,0:T(8,128)(2,1)S(1)}, bf16[16,6144]{1,0:T(8,128)(2,1)S(1)}, u32[]{:S(2)}, u32[]{:S(2)}) collective-permute-start(bf16[16,6144]{1,0:T(8,128)(2,1)S(1)} %get-tuple-element.68), channel_id=1, source_target_pairs={{4,0},{5,1},{8,4},{9,5},{12,8},{13,9},{14,12},{15,13},{10,14},{11,... | collective-permute-start | bytes 589832 | tf_op jit(solution)/shard_map/ppermute | solution.py:88
  73.1 8.1 %collective-permute-start.32 = (bf16[16,6144]{1,0:T(8,128)(2,1)S(1)}, bf16[16,6144]{1,0:T(8,128)(2,1)S(1)}, u32[]{:S(2)}, u32[]{:S(2)}) collective-permute-start(bf16[16,6144]{1,0:T(8,128)(2,1)S(1)} %fusion.11), channel_id=1, source_target_pairs={{4,0},{5,1},{8,4},{9,5},{12,8},{13,9},{14,12},{15,13},{10,14},{11,... | collective-permute-start | bytes 589832 | tf_op jit(solution)/shard_map/ppermute | solution.py:88
  74.7 7.8 %collective-permute-start.33 = (bf16[16,6144]{1,0:T(8,128)(2,1)S(1)}, bf16[16,6144]{1,0:T(8,128)(2,1)S(1)}, u32[]{:S(2)}, u32[]{:S(2)}) collective-permute-start(bf16[16,6144]{1,0:T(8,128)(2,1)S(1)} %fusion.10), channel_id=1, source_target_pairs={{0,4},{1,5},{4,8},{5,9},{8,12},{9,13},{12,14},{13,15},{14,10},{15,... | collective-permute-start | bytes 589832 | tf_op jit(solution)/shard_map/ppermute | solution.py:88
  75.2 8.3 %collective-permute-start.26 = (bf16[16,6144]{1,0:T(8,128)(2,1)S(1)}, bf16[16,6144]{1,0:T(8,128)(2,1)S(1)}, u32[]{:S(2)}, u32[]{:S(2)}) collective-permute-start(bf16[16,6144]{1,0:T(8,128)(2,1)S(1)} %get-tuple-element.67), channel_id=1, source_target_pairs={{4,0},{5,1},{8,4},{9,5},{12,8},{13,9},{14,12},{15,13},{10,14},{11,... | collective-permute-start | bytes 589832 | tf_op jit(solution)/shard_map/ppermute | solution.py:88
  76.9 12.7 %collective-permute-start.31 = (bf16[16,6144]{1,0:T(8,128)(2,1)S(1)}, bf16[16,6144]{1,0:T(8,128)(2,1)S(1)}, u32[]{:S(2)}, u32[]{:S(2)}) collective-permute-start(bf16[16,6144]{1,0:T(8,128)(2,1)S(1)} %get-tuple-element.75), channel_id=1, source_target_pairs={{0,4},{1,5},{4,8},{5,9},{8,12},{9,13},{12,14},{13,15},{14,10},{15,... | collective-permute-start | bytes 589832 | tf_op jit(solution)/shard_map/ppermute | solution.py:88
  82.6 6.4 %collective-permute-start.35 = (bf16[16,6144]{1,0:T(8,128)(2,1)S(1)}, bf16[16,6144]{1,0:T(8,128)(2,1)S(1)}, u32[]{:S(2)}, u32[]{:S(2)}) collective-permute-start(bf16[16,6144]{1,0:T(8,128)(2,1)S(1)} %get-tuple-element.79), channel_id=1, source_target_pairs={{0,4},{1,5},{4,8},{5,9},{8,12},{9,13},{12,14},{13,15},{14,10},{15,... | collective-permute-start | bytes 589832 | tf_op jit(solution)/shard_map/ppermute | solution.py:88
  83.6 13.0 %copy-start.1 = (bf16[128,6144]{1,0:T(8,128)(2,1)S(1)}, bf16[128,6144]{1,0:T(8,128)(2,1)}, u32[]{:S(2)}) copy-start(bf16[128,6144]{1,0:T(8,128)(2,1)} %param.8) | copy-start | bytes 4718596
  84.4 7.4 %collective-permute-start.30 = (bf16[16,6144]{1,0:T(8,128)(2,1)S(1)}, bf16[16,6144]{1,0:T(8,128)(2,1)S(1)}, u32[]{:S(2)}, u32[]{:S(2)}) collective-permute-start(bf16[16,6144]{1,0:T(8,128)(2,1)S(1)} %fusion.16), channel_id=1, source_target_pairs={{4,0},{5,1},{8,4},{9,5},{12,8},{13,9},{14,12},{15,13},{10,14},{11,... | collective-permute-start | bytes 589832 | tf_op jit(solution)/shard_map/ppermute | solution.py:88
  86.0 8.2 %collective-permute-start.34 = (bf16[16,6144]{1,0:T(8,128)(2,1)S(1)}, bf16[16,6144]{1,0:T(8,128)(2,1)S(1)}, u32[]{:S(2)}, u32[]{:S(2)}) collective-permute-start(bf16[16,6144]{1,0:T(8,128)(2,1)S(1)} %get-tuple-element.78), channel_id=1, source_target_pairs={{4,0},{5,1},{8,4},{9,5},{12,8},{13,9},{14,12},{15,13},{10,14},{11,... | collective-permute-start | bytes 589832 | tf_op jit(solution)/shard_map/ppermute | solution.py:88
  89.1 5.7 %collective-permute-start.36 = (bf16[16,6144]{1,0:T(8,128)(2,1)S(1)}, bf16[16,6144]{1,0:T(8,128)(2,1)S(1)}, u32[]{:S(2)}, u32[]{:S(2)}) collective-permute-start(bf16[16,6144]{1,0:T(8,128)(2,1)S(1)} %fusion.5), channel_id=1, source_target_pairs={{0,4},{1,5},{4,8},{5,9},{8,12},{9,13},{12,14},{13,15},{14,10},{15,... | collective-permute-start | bytes 589832 | tf_op jit(solution)/shard_map/ppermute | solution.py:88
